TPU v7x, 32 devices: a whole 2x2x4 slice. The times are simulated.
32 devices in a mesh: dp: 16 (over z, x, core), seq: 2 (over y).
Axes of the slice: x: 2, y: 2, z: 4, core: 2. Of those that a mesh axis runs over, the one named last changes fastest.
Arguments:
- tokens: bfloat16 [32768, 1024], P(('dp', 'seq')), may hold values from -6 to 6
- doc_lengths: int32 [16, 2], P('dp'), may hold values from 256 to 1792, as said below
- variate_ids: int32 [16, 2048], P('dp'), may hold values from 0 to 3
- time_ids: int32 [32768], P(('dp', 'seq')), may hold values from 0 to 511
- in_proj: bfloat16 [1024, 3072], P('dp'), may hold values from -0.1875 to 0.1875
- out_proj: bfloat16 [1024, 1024], P('dp'), may hold values from -1.5 to 1.5
- gate_up: bfloat16 [1024, 8192], P('dp'), may hold values from -0.1875 to 0.1875
- down_proj: bfloat16 [4096, 1024], P('dp'), may hold values from -0.09375 to 0.09375
- attn_gain: bfloat16 [1024], P('dp'), may hold values from 0.5 to 1.5
- ffn_gain: bfloat16 [1024], P('dp'), may hold values from 0.5 to 1.5
- query_gain: float32 [64], replicated, may hold values from 0.5 to 1.5
- key_gain: float32 [64], replicated, may hold values from 0.5 to 1.5
- head_bias: float32 [16, 2], replicated, may hold values from -1 to 1
- cotangent: bfloat16 [32768, 1024], P(('dp', 'seq')), may hold values from -6 to 6
Outputs:
- layer_out: bfloat16 [32768, 1024], P(('dp', 'seq'))
- input_grad: float32 [32768, 1024], P(('dp', 'seq'))
- in_proj_grad: float32 [1024, 3072], P('dp')
- out_proj_grad: float32 [1024, 1024], P('dp')
- gate_up_grad: float32 [1024, 8192], P('dp')
- down_proj_grad: float32 [4096, 1024], P('dp')
- attn_gain_grad: float32 [1024], P('dp')
- ffn_gain_grad: float32 [1024], P('dp')
- query_gain_grad: float32 [64], replicated
- key_gain_grad: float32 [64], replicated
- head_bias_grad: float32 [16, 2], replicated
Inputs may be any that keep to these rules, and one draw needn't show every extreme that they name: `doc_lengths`: each pack holds two series, in either order, then padding slots. The longer has 1280 slots or more, the shorter 1024 // 4 to 512, the padding at most 256 slots.
All inputs are finite; a program needn't handle non-finite values.
Results may differ from a plain program's by a relative error of at most 0.018.
Values may be sent and summed in bfloat16 or wider, within the bound.
A program may use at most 320 MiB of HBM per device.

v0:
```python
import math

import jax
import jax.numpy as jnp
from jax import lax
from jax.sharding import PartitionSpec as P

EPSILON = 1e-06
ROPE_BASE = 10000.0
NEG_FILL = -1e30


def rms_forward(values, gain_vec):
    inv_rms = lax.rsqrt(jnp.mean(values * values, axis=-1, keepdims=True) + EPSILON)
    return (values * inv_rms * gain_vec, inv_rms)


def rms_backward(values, inv_rms, gain_vec, upstream):
    weighted = upstream * gain_vec
    inner_sum = jnp.mean(weighted * values, axis=-1, keepdims=True)
    value_grad = inv_rms * weighted - values * inv_rms * inv_rms * inv_rms * inner_sum
    return (value_grad, upstream * values * inv_rms)


def rotate_half(values, angles):
    half_dim = values.shape[-1] // 2
    cosine = jnp.cos(angles)
    sine = jnp.sin(angles)
    first = values[..., :half_dim]
    second = values[..., half_dim:]
    return jnp.concatenate(
        [first * cosine - second * sine, second * cosine + first * sine], axis=-1
    )


def rows_product(left, right):
    return lax.dot_general(
        left, right, (((0,), (0,)), ((), ())), preferred_element_type=jnp.float32
    )


def cols_product(left, right):
    return lax.dot_general(
        left, right, (((1,), (1,)), ((), ())), preferred_element_type=jnp.float32
    )


def body(
    tokens,
    doc_lengths,
    variate_ids,
    time_ids,
    in_proj,
    out_proj,
    gate_up,
    down_proj,
    attn_gain,
    ffn_gain,
    query_gain,
    key_gain,
    head_bias,
    cotangent,
):
    seq_count = lax.axis_size("seq")
    seq_rank = lax.axis_index("seq")
    local_rows = tokens.shape[0]
    model_width = tokens.shape[1]
    pack_rows = local_rows * seq_count
    head_dim = query_gain.shape[0]
    heads_all = head_bias.shape[0]
    heads_here = heads_all // seq_count
    hidden_width = gate_up.shape[1] // 2
    score_scale = head_dim ** (-0.5)
    block_rows = min(512, pack_rows)
    blocks = pack_rows // block_rows
    full_weights = (
        lax.all_gather(in_proj, "dp", axis=0, tiled=True),
        lax.all_gather(out_proj, "dp", axis=0, tiled=True),
        lax.all_gather(gate_up, "dp", axis=0, tiled=True),
        lax.all_gather(down_proj, "dp", axis=0, tiled=True),
        lax.all_gather(attn_gain, "dp", axis=0, tiled=True),
        lax.all_gather(ffn_gain, "dp", axis=0, tiled=True),
    )
    in_full, out_full, gate_full, down_full, attn_gain_full, ffn_gain_full = full_weights
    positions = jnp.arange(pack_rows, dtype=jnp.int32)
    first_end = doc_lengths[0, 0]
    second_end = first_end + doc_lengths[0, 1]
    seg_all = (positions >= first_end).astype(jnp.int32) + (positions >= second_end).astype(
        jnp.int32
    )
    local_positions = seq_rank * local_rows + jnp.arange(local_rows, dtype=jnp.int32)
    valid_rows = (local_positions < second_end).astype(jnp.float32)
    var_all = variate_ids[0]
    half_dim = head_dim // 2
    frequency = jnp.exp(jnp.arange(half_dim, dtype=jnp.float32) * (-math.log(ROPE_BASE) / half_dim))
    angles = (time_ids.astype(jnp.float32)[:, None] * frequency[None, :])[:, None, :]
    bias_here = lax.dynamic_slice_in_dim(head_bias, seq_rank * heads_here, heads_here, 0)
    inputs_f = tokens.astype(jnp.float32)
    attn_gain_f = attn_gain_full.astype(jnp.float32)
    normed, norm_scale = rms_forward(inputs_f, attn_gain_f)
    normed_low = normed.astype(jnp.bfloat16)
    merged_proj = jnp.dot(normed_low, in_full, preferred_element_type=jnp.float32).reshape(
        local_rows, 3, heads_all, head_dim
    )
    query_raw = merged_proj[:, 0]
    key_raw = merged_proj[:, 1]
    query_normed, query_scale = rms_forward(query_raw, query_gain)
    key_normed, key_scale = rms_forward(key_raw, key_gain)
    query_rot = rotate_half(query_normed, angles)
    key_rot = rotate_half(key_normed, angles)
    packed = (
        jnp.stack([query_rot, key_rot, merged_proj[:, 2]], axis=1)
        .astype(jnp.bfloat16)
        .reshape(local_rows, 3, model_width)
    )
    by_heads = lax.all_to_all(packed, "seq", split_axis=2, concat_axis=0, tiled=True).reshape(
        pack_rows, 3, heads_here, head_dim
    )
    head_query = by_heads[:, 0]
    head_key = by_heads[:, 1]
    head_value = by_heads[:, 2]

    def block_scores(query_block, start):
        seg_rows = lax.dynamic_slice_in_dim(seg_all, start, block_rows)
        var_rows = lax.dynamic_slice_in_dim(var_all, start, block_rows)
        same_doc = (seg_rows[:, None] == seg_all[None, :])[None]
        same_var = (var_rows[:, None] == var_all[None, :])[None]
        raw_scores = (
            jnp.einsum("qhd,khd->hqk", query_block, head_key, preferred_element_type=jnp.float32)
            * score_scale
        )
        biased = raw_scores + jnp.where(
            same_var, bias_here[:, 0][:, None, None], bias_here[:, 1][:, None, None]
        )
        return (jnp.where(same_doc, biased, NEG_FILL), same_var)

    query_blocks = head_query.reshape(blocks, block_rows, heads_here, head_dim)
    starts = jnp.arange(blocks, dtype=jnp.int32) * block_rows

    def forward_block(operands):
        query_block, start = operands
        scores, same_var = block_scores(query_block, start)
        row_top = jnp.max(scores, axis=-1, keepdims=True)
        log_total = row_top + jnp.log(jnp.sum(jnp.exp(scores - row_top), axis=-1, keepdims=True))
        attn_probs = jnp.exp(scores - log_total).astype(jnp.bfloat16)
        result = jnp.einsum(
            "hqk,khd->qhd", attn_probs, head_value, preferred_element_type=jnp.float32
        )
        return (result.astype(jnp.bfloat16), log_total[..., 0])

    attended_heads, log_totals = lax.map(forward_block, (query_blocks, starts))
    attended_heads = attended_heads.reshape(pack_rows, heads_here * head_dim)
    attended = lax.all_to_all(attended_heads, "seq", split_axis=0, concat_axis=1, tiled=True)
    mixed = jnp.dot(attended, out_full, preferred_element_type=jnp.float32)
    residual = inputs_f + mixed
    ffn_gain_f = ffn_gain_full.astype(jnp.float32)
    normed_ffn, ffn_scale = rms_forward(residual, ffn_gain_f)
    normed_ffn_low = normed_ffn.astype(jnp.bfloat16)
    gate_vals = jnp.dot(normed_ffn_low, gate_full, preferred_element_type=jnp.float32)
    gate_part = gate_vals[:, :hidden_width]
    up_part = gate_vals[:, hidden_width:]
    sigmoid_gate = jax.nn.sigmoid(gate_part)
    silu_gate = gate_part * sigmoid_gate
    hidden = (silu_gate * up_part).astype(jnp.bfloat16)
    branch = jnp.dot(hidden, down_full, preferred_element_type=jnp.float32)
    layer_out = (residual + branch).astype(jnp.bfloat16)
    back_weights = (
        lax.all_gather(in_proj, "dp", axis=0, tiled=True),
        lax.all_gather(out_proj, "dp", axis=0, tiled=True),
        lax.all_gather(gate_up, "dp", axis=0, tiled=True),
        lax.all_gather(down_proj, "dp", axis=0, tiled=True),
        lax.all_gather(attn_gain, "dp", axis=0, tiled=True),
        lax.all_gather(ffn_gain, "dp", axis=0, tiled=True),
    )
    in_back, out_back, gate_back, down_back, attn_gain_back, ffn_gain_back = back_weights
    seed_grad = cotangent.astype(jnp.float32) * valid_rows[:, None]
    seed_low = seed_grad.astype(jnp.bfloat16)
    down_grad = rows_product(hidden, seed_low)
    hidden_grad = cols_product(seed_low, down_back)
    gate_grad_part = hidden_grad * up_part * sigmoid_gate * (1.0 + gate_part * (1.0 - sigmoid_gate))
    up_grad_part = hidden_grad * silu_gate
    gate_vals_grad = jnp.concatenate([gate_grad_part, up_grad_part], axis=1).astype(jnp.bfloat16)
    gate_up_grad = rows_product(normed_ffn_low, gate_vals_grad)
    normed_ffn_grad = cols_product(gate_vals_grad, gate_back)
    resid_norm_grad, ffn_gain_terms = rms_backward(
        residual, ffn_scale, ffn_gain_back.astype(jnp.float32), normed_ffn_grad
    )
    residual_grad = seed_grad + resid_norm_grad
    mixed_low = residual_grad.astype(jnp.bfloat16)
    out_proj_grad = rows_product(attended, mixed_low)
    attended_grad = cols_product(mixed_low, out_back).astype(jnp.bfloat16)
    head_out_grad = lax.all_to_all(
        attended_grad, "seq", split_axis=1, concat_axis=0, tiled=True
    ).reshape(pack_rows, heads_here, head_dim)
    out_grad_blocks = head_out_grad.reshape(blocks, block_rows, heads_here, head_dim)

    def backward_block(running, operands):
        key_acc, value_acc, bias_acc = running
        query_block, out_block, log_total, start = operands
        scores, same_var = block_scores(query_block, start)
        attn_probs = jnp.exp(scores - log_total[..., None])
        value_acc = value_acc + jnp.einsum(
            "hqk,qhd->khd",
            attn_probs.astype(jnp.bfloat16),
            out_block,
            preferred_element_type=jnp.float32,
        )
        prob_grad = jnp.einsum(
            "qhd,khd->hqk", out_block, head_value, preferred_element_type=jnp.float32
        )
        row_total = jnp.sum(attn_probs * prob_grad, axis=-1, keepdims=True)
        score_grad = attn_probs * (prob_grad - row_total)
        same_terms = jnp.sum(jnp.where(same_var, score_grad, 0.0), axis=(1, 2))
        other_terms = jnp.sum(jnp.where(same_var, 0.0, score_grad), axis=(1, 2))
        bias_acc = bias_acc + jnp.stack([same_terms, other_terms], axis=-1)
        score_low = score_grad.astype(jnp.bfloat16)
        query_grad = (
            jnp.einsum("hqk,khd->qhd", score_low, head_key, preferred_element_type=jnp.float32)
            * score_scale
        )
        key_acc = (
            key_acc
            + jnp.einsum("hqk,qhd->khd", score_low, query_block, preferred_element_type=jnp.float32)
            * score_scale
        )
        return ((key_acc, value_acc, bias_acc), query_grad.astype(jnp.bfloat16))

    zero_rows = jnp.zeros((pack_rows, heads_here, head_dim), jnp.float32)
    zero_bias = jnp.zeros((heads_here, 2), jnp.float32)
    (key_acc, value_acc, bias_acc), query_grads = lax.scan(
        backward_block,
        (zero_rows, zero_rows, zero_bias),
        (query_blocks, out_grad_blocks, log_totals, starts),
    )
    grads_heads = jnp.stack(
        [
            query_grads.reshape(pack_rows, heads_here, head_dim),
            key_acc.astype(jnp.bfloat16),
            value_acc.astype(jnp.bfloat16),
        ],
        axis=1,
    ).reshape(pack_rows, 3, heads_here * head_dim)
    grads_tokens = (
        lax.all_to_all(grads_heads, "seq", split_axis=0, concat_axis=2, tiled=True)
        .reshape(local_rows, 3, heads_all, head_dim)
        .astype(jnp.float32)
    )
    query_rot_grad = rotate_half(grads_tokens[:, 0], -angles)
    key_rot_grad = rotate_half(grads_tokens[:, 1], -angles)
    query_raw_grad, query_gain_terms = rms_backward(
        query_raw, query_scale, query_gain, query_rot_grad
    )
    key_raw_grad, key_gain_terms = rms_backward(key_raw, key_scale, key_gain, key_rot_grad)
    merged_grad = (
        jnp.stack([query_raw_grad, key_raw_grad, grads_tokens[:, 2]], axis=1)
        .reshape(local_rows, 3 * model_width)
        .astype(jnp.bfloat16)
    )
    in_proj_grad = rows_product(normed_low, merged_grad)
    normed_grad = cols_product(merged_grad, in_back)
    input_norm_grad, attn_gain_terms = rms_backward(
        inputs_f, norm_scale, attn_gain_back.astype(jnp.float32), normed_grad
    )
    input_grad = residual_grad + input_norm_grad
    attn_gain_sum = jnp.sum(attn_gain_terms, axis=0)
    ffn_gain_sum = jnp.sum(ffn_gain_terms, axis=0)
    shards = (
        lax.psum_scatter(in_proj_grad, "dp", scatter_dimension=0, tiled=True),
        lax.psum_scatter(out_proj_grad, "dp", scatter_dimension=0, tiled=True),
        lax.psum_scatter(gate_up_grad, "dp", scatter_dimension=0, tiled=True),
        lax.psum_scatter(down_grad, "dp", scatter_dimension=0, tiled=True),
        lax.psum_scatter(attn_gain_sum, "dp", scatter_dimension=0, tiled=True),
        lax.psum_scatter(ffn_gain_sum, "dp", scatter_dimension=0, tiled=True),
    )
    summed = lax.psum((shards[0], shards[1], shards[2], shards[3], shards[4], shards[5]), "seq")
    bias_full = lax.dynamic_update_slice_in_dim(
        jnp.zeros((heads_all, 2), jnp.float32), bias_acc, seq_rank * heads_here, 0
    )
    small_sums = lax.psum(
        (jnp.sum(query_gain_terms, axis=(0, 1)), jnp.sum(key_gain_terms, axis=(0, 1)), bias_full),
        ("dp", "seq"),
    )
    return (
        layer_out,
        input_grad,
        summed[0],
        summed[1],
        summed[2],
        summed[3],
        summed[4],
        summed[5],
        small_sums[0],
        small_sums[1],
        small_sums[2],
    )


def solution(mesh):
    in_specs = (
        P(("dp", "seq"), None),
        P("dp", None),
        P("dp", None),
        P(("dp", "seq")),
        P("dp", None),
        P("dp", None),
        P("dp", None),
        P("dp", None),
        P("dp"),
        P("dp"),
        P(),
        P(),
        P(),
        P(("dp", "seq"), None),
    )
    out_specs = (
        P(("dp", "seq"), None),
        P(("dp", "seq"), None),
        P("dp", None),
        P("dp", None),
        P("dp", None),
        P("dp", None),
        P("dp"),
        P("dp"),
        P(),
        P(),
        P(),
    )
    return jax.shard_map(body, mesh=mesh, in_specs=in_specs, out_specs=out_specs, check_vma=False)
```

profile of v0, /device:TPU:0, one launch (start us, length us, event | category | flops | bytes accessed | tf_op | source)
XLA Modules:
  0.0 2082.4 jit_solution(10028968531954126580)
XLA Ops:
  14.2 36.1 %all-reduce.8 = (bf16[1024]{0:T(1024)(128)(2,1)S(1)}, bf16[1024]{0:T(1024)(128)(2,1)}) all-reduce(bf16[1024]{0:T(1024)(128)(2,1)S(1)} %dynamic-update-slice, bf16[1024]{0:T(1024)(128)(2,1)S(1)} %dynamic-update-slice.1), channel_id=1, replica_groups=mesh['dp'=16,'seq'=2] {'dp'}, use_global_device_ids=true, to_apply=%add | all-reduce | flops 2048 | bytes 8192
  52.6 22.4 %all-gather.5.cloned.1.call-done = bf16[1024,3072]{1,0:T(8,128)(2,1)} async-done(((bf16[64,3072]{1,0:T(8,128)(2,1)}), bf16[1024,3072]{1,0:T(8,128)(2,1)}) %all-gather.5.cloned.1.call-update) | async-done | bytes 6291472 | tf_op jit(solution)/shard_map/all_gather | solution.py:77
  122.4 89.8 %all-to-all-done = bf16[1024,3,1024]{0,1,2:T(4,128)(2,1)} async-done(((bf16[1024,3,1024]{0,1,2:T(4,128)(2,1)}), bf16[1024,3,1024]{0,1,2:T(4,128)(2,1)}, u32[]{:S(2)}, u32[]{:S(2)}) %all-to-all-start) | async-done | bytes 6291488 | tf_op jit(solution)/shard_map/all_to_all | solution.py:116
  267.0 200.1 %while.29 = (s32[]{:T(128)}, bf16[4,512,8,64]{1,3,2,0:T(8,128)(2,1)}, f32[4,8,512]{2,1,0:T(8,128)}, s32[4]{0:T(128)S(1)}, s32[2048]{0:T(1024)S(1)}, /*index=5*/b...) while((s32[]{:T(128)}, ...), condition=%wide.region_6.7_spmd, body=%wide.region_3.6_spmd.sunk | while | flops 2225336320 | bytes 110260616 | solution.py:151
  518.1 28.5 %fusion.90 = f32[1024,8192]{1,0:T(8,128)} fusion(bf16[1024,8192]{1,0:T(8,128)(2,1)} %all-gather.9.cloned.1.call-done, f32[1024,1024]{0,1:T(8,128)} %get-tuple-element.489, f32[1024]{0:T(1024)S(1)} %convert_element_type.103, f32[1024]{0:T(1024)S(1)} %add_rsqrt_fusion.2), kind=kOutput, calls=%fused_computation.162 | convolution fusion | flops 17183014912 | bytes 54534144 | tf_op jit(solution)/shard_map/dot_general | solution.py:159
  546.6 31.1 %multiply_convert_fusion.1 = (bf16[1024,4096]{1,0:T(8,128)(2,1)}, bf16[1024,4096]{1,0:T(8,128)(2,1)}, bf16[1024,4096]{1,0:T(8,128)(2,1)}) fusion(f32[1024,8192]{1,0:T(8,128)} %fusion.90, bf16[4096,1024]{1,0:T(8,128)(2,1)} %all-gather.11.cloned.1.call-done, bf16[1024,1024]{0,1:T(8,128)(2,1)} %copy.109, f32[1024]{0:T(1024)S(1)} %fusion.87), kind=kOutput, calls=%fused_computation.55 | convolution fusion | flops 8655994880 | bytes 69210112 | tf_op jit(solution)/shard_map/dot_general | solution.py:43
  577.7 27.6 %multiply_reduce_fusion.1 = (f32[1024]{0:T(1024)}, f32[1024]{0:T(1024)S(1)}, f32[1024,1024]{0,1:T(8,128)}) fusion(f32[1024,1024]{0,1:T(8,128)} %get-tuple-element.489, f32[1024]{0:T(1024)S(1)} %add_rsqrt_fusion.2, f32[1024]{0:T(1024)S(1)} %convert_element_type.103, bf16[1024,8192]{1,0:T(8,128)(2,1)} %all-gather.9.cloned.1.call-done, ...), kind=kOutput, calls=%fused_computation.111 | convolution fusion | flops 17219715072 | bytes 41959424 | tf_op jit(solution)/shard_map/dot_general | solution.py:43
  617.6 23.8 %all-to-all-done.2 = bf16[1024,2,512]{0,2,1:T(8,128)(2,1)} async-done(((bf16[1024,2,512]{0,2,1:T(8,128)(2,1)}), bf16[1024,2,512]{0,2,1:T(8,128)(2,1)}, u32[]{:S(2)}, u32[]{:S(2)}) %all-to-all-start.2) | async-done | bytes 2097184 | tf_op jit(solution)/shard_map/all_to_all | solution.py:192
  657.8 456.8 %while.30 = (s32[]{:T(128)}, f32[2048,8,64]{0,2,1:T(8,128)}, f32[2048,8,64]{0,2,1:T(8,128)}, f32[8,2]{0,1:T(2,128)S(1)}, bf16[4,512,8,64]{1,3,2,0:T(8,128)(2,1)}...) while((s32[]{:T(128)}, f32[2048,8,64]{0,2,1:T(8,128)}, ...), condition=%wide.region_13.14_spmd.clone, body=%wide.region_9.13_spmd.clone.sunk | while | flops 5502398464 | bytes 291091712 | solution.py:230
  677.9 27.6 %multiply_reduce_fusion.5 = (f32[8,512]{1,0:T(8,128)S(1)}, f32[8,512,2048]{2,1,0:T(8,128)}) fusion(f32[8,512,2048]{2,1,0:T(8,128)} %fusion.143, f32[8,512]{1,0:T(8,128)S(1)} %dynamic-slice_bitcast_fusion.2, f32[8]{0:T(128)S(1)} %get-tuple-element.681, f32[8]{0:T(128)S(1)} %get-tuple-element.682, pred[512,2048]{1,0:T(8,128)(4,1)S(1)} %get-tuple-element.680, ...), kind=kOutput, calls=%fused_computation.20.clone.1 | convolution fusion | flops 1132457984 | bytes 71860288 | tf_op jit(solution)/shard_map/while/body/eval_jaxpr/qhd,khd->hqk/dot_general | solution.py:129
  705.6 27.8 %select_reduce_fusion.3 = (f32[8]{0:T(128)S(1)}, f32[8]{0:T(128)S(1)}, bf16[8,512,2048]{2,1,0:T(8,128)(2,1)}) fusion(pred[512,2048]{1,0:T(8,128)(4,1)S(1)} %get-tuple-element.680, f32[8,512,2048]{2,1,0:T(8,128)} %get-tuple-element.684, f32[8,512,2048]{2,1,0:T(8,128)} %fusion.143, f32[8,512]{1,0:T(8,128)S(1)} %get-tuple-element.685), kind=kLoop, calls=%fused_computation.18.clone.1 | loop fusion | flops 58720240 | bytes 84951104 | tf_op jit(solution)/shard_map/while/body/eval_jaxpr/reduce_sum | solution.py:213
  790.1 27.6 %multiply_reduce_fusion.5 = (f32[8,512]{1,0:T(8,128)S(1)}, f32[8,512,2048]{2,1,0:T(8,128)}) fusion(f32[8,512,2048]{2,1,0:T(8,128)} %fusion.143, f32[8,512]{1,0:T(8,128)S(1)} %dynamic-slice_bitcast_fusion.2, f32[8]{0:T(128)S(1)} %get-tuple-element.681, f32[8]{0:T(128)S(1)} %get-tuple-element.682, pred[512,2048]{1,0:T(8,128)(4,1)S(1)} %get-tuple-element.680, ...), kind=kOutput, calls=%fused_computation.20.clone.1 | convolution fusion | flops 1132457984 | bytes 71860288 | tf_op jit(solution)/shard_map/while/body/eval_jaxpr/qhd,khd->hqk/dot_general | solution.py:129
  817.7 27.8 %select_reduce_fusion.3 = (f32[8]{0:T(128)S(1)}, f32[8]{0:T(128)S(1)}, bf16[8,512,2048]{2,1,0:T(8,128)(2,1)}) fusion(pred[512,2048]{1,0:T(8,128)(4,1)S(1)} %get-tuple-element.680, f32[8,512,2048]{2,1,0:T(8,128)} %get-tuple-element.684, f32[8,512,2048]{2,1,0:T(8,128)} %fusion.143, f32[8,512]{1,0:T(8,128)S(1)} %get-tuple-element.685), kind=kLoop, calls=%fused_computation.18.clone.1 | loop fusion | flops 58720240 | bytes 84951104 | tf_op jit(solution)/shard_map/while/body/eval_jaxpr/reduce_sum | solution.py:213
  904.7 27.6 %multiply_reduce_fusion.5 = (f32[8,512]{1,0:T(8,128)S(1)}, f32[8,512,2048]{2,1,0:T(8,128)}) fusion(f32[8,512,2048]{2,1,0:T(8,128)} %fusion.143, f32[8,512]{1,0:T(8,128)S(1)} %dynamic-slice_bitcast_fusion.2, f32[8]{0:T(128)S(1)} %get-tuple-element.681, f32[8]{0:T(128)S(1)} %get-tuple-element.682, pred[512,2048]{1,0:T(8,128)(4,1)S(1)} %get-tuple-element.680, ...), kind=kOutput, calls=%fused_computation.20.clone.1 | convolution fusion | flops 1132457984 | bytes 71860288 | tf_op jit(solution)/shard_map/while/body/eval_jaxpr/qhd,khd->hqk/dot_general | solution.py:129
  932.3 27.8 %select_reduce_fusion.3 = (f32[8]{0:T(128)S(1)}, f32[8]{0:T(128)S(1)}, bf16[8,512,2048]{2,1,0:T(8,128)(2,1)}) fusion(pred[512,2048]{1,0:T(8,128)(4,1)S(1)} %get-tuple-element.680, f32[8,512,2048]{2,1,0:T(8,128)} %get-tuple-element.684, f32[8,512,2048]{2,1,0:T(8,128)} %fusion.143, f32[8,512]{1,0:T(8,128)S(1)} %get-tuple-element.685), kind=kLoop, calls=%fused_computation.18.clone.1 | loop fusion | flops 58720240 | bytes 84951104 | tf_op jit(solution)/shard_map/while/body/eval_jaxpr/reduce_sum | solution.py:213
  1019.5 27.6 %multiply_reduce_fusion.5 = (f32[8,512]{1,0:T(8,128)S(1)}, f32[8,512,2048]{2,1,0:T(8,128)}) fusion(f32[8,512,2048]{2,1,0:T(8,128)} %fusion.143, f32[8,512]{1,0:T(8,128)S(1)} %dynamic-slice_bitcast_fusion.2, f32[8]{0:T(128)S(1)} %get-tuple-element.681, f32[8]{0:T(128)S(1)} %get-tuple-element.682, pred[512,2048]{1,0:T(8,128)(4,1)S(1)} %get-tuple-element.680, ...), kind=kOutput, calls=%fused_computation.20.clone.1 | convolution fusion | flops 1132457984 | bytes 71860288 | tf_op jit(solution)/shard_map/while/body/eval_jaxpr/qhd,khd->hqk/dot_general | solution.py:129
  1047.1 27.8 %select_reduce_fusion.3 = (f32[8]{0:T(128)S(1)}, f32[8]{0:T(128)S(1)}, bf16[8,512,2048]{2,1,0:T(8,128)(2,1)}) fusion(pred[512,2048]{1,0:T(8,128)(4,1)S(1)} %get-tuple-element.680, f32[8,512,2048]{2,1,0:T(8,128)} %get-tuple-element.684, f32[8,512,2048]{2,1,0:T(8,128)} %fusion.143, f32[8,512]{1,0:T(8,128)S(1)} %get-tuple-element.685), kind=kLoop, calls=%fused_computation.18.clone.1 | loop fusion | flops 58720240 | bytes 84951104 | tf_op jit(solution)/shard_map/while/body/eval_jaxpr/reduce_sum | solution.py:213
  1161.0 82.9 %all-to-all-done.3 = bf16[2048,3,512]{2,1,0:T(4,128)(2,1)} async-done(((bf16[2048,3,512]{2,1,0:T(4,128)(2,1)}), bf16[2048,3,512]{2,1,0:T(4,128)(2,1)}, u32[]{:S(2)}, u32[]{:S(2)}) %all-to-all-start.3) | async-done | bytes 6291488 | tf_op jit(solution)/shard_map/all_to_all | solution.py:244
  1320.2 27.9 %fusion.44 = f32[1024,8192]{1,0:T(8,128)} fusion(bf16[1024,4096]{1,0:T(8,128)(2,1)} %get-tuple-element.457, bf16[1024,4096]{1,0:T(8,128)(2,1)} %get-tuple-element.456, f32[1024,1024]{0,1:T(8,128)} %get-tuple-element.489, f32[1024]{0:T(1024)S(1)} %copy-done.27, f32[1024]{0:T(1024)S(1)} %copy-done.29), kind=kOutput, calls=%fused_computation.59 | convolution fusion | flops 17216569344 | bytes 54534144 | tf_op jit(solution)/shard_map/dot_general | solution.py:37
  1348.8 84.6 %reduce-scatter.5.cloned.1.call-done = f32[64,3072]{1,0:T(8,128)} async-done(((f32[1024,3072]{1,0:T(8,128)}), f32[64,3072]{1,0:T(8,128)}) %reduce-scatter.5.cloned.1.call-update) | async-done | bytes 786448 | tf_op jit(solution)/shard_map/reduce_scatter | solution.py:268
  1433.4 182.4 %reduce-scatter.11.cloned.1.call-done = f32[256,1024]{1,0:T(8,128)} async-done(((f32[4096,1024]{1,0:T(8,128)}), f32[256,1024]{1,0:T(8,128)}) %reduce-scatter.11.cloned.1.call-update) | async-done | bytes 1048592 | tf_op jit(solution)/shard_map/reduce_scatter | solution.py:271
  1615.8 336.6 %reduce-scatter.9.cloned.1.call-done = f32[64,8192]{1,0:T(8,128)} async-done(((f32[1024,8192]{1,0:T(8,128)}), f32[64,8192]{1,0:T(8,128)}) %reduce-scatter.9.cloned.1.call-update) | async-done | bytes 2097168 | tf_op jit(solution)/shard_map/reduce_scatter | solution.py:270
  1992.4 32.0 %all-reduce.5 = (f32[1024]{0:T(1024)S(1)}, f32[1024]{0:T(1024)S(1)}) all-reduce(f32[1024]{0:T(1024)S(1)} %get-tuple-element.374, f32[1024]{0:T(1024)S(1)} %copy-done.39), channel_id=6, replica_groups=mesh['dp'=16,'seq'=2] {'dp'}, use_global_device_ids=true, to_apply=%region_26.27.clone | all-reduce | flops 2048 | bytes 16384
  2024.6 37.4 %all-reduce.4 = (f32[64]{0:T(128)}, f32[64]{0:T(128)}, f32[16,2]{0,1:T(2,128)}) all-reduce(f32[64]{0:T(128)S(1)} %get-tuple-element.369, f32[64]{0:T(128)S(1)} %get-tuple-element.364, f32[16,2]{0,1:T(2,128)S(1)} %dynamic_update_slice.14), channel_id=1, replica_groups=mesh['dp'=16,'seq'=2] {'dp','seq'}, use_global_device_ids=true, to_apply=%region_32.33 | all-reduce | flops 160 | bytes 1280 | tf_op jit(solution)/shard_map/psum | solution.py:279
  (312 shorter events, 784.2 us)
Async XLA Ops:
  7.2 114.5 %copy-start = (f32[16,2]{0,1:T(2,128)S(1)}, f32[16,2]{0,1:T(2,128)}, u32[]{:S(2)}) copy-start(f32[16,2]{0,1:T(2,128)} %param.30) | copy-start | bytes 388
  7.2 43.1 %copy-start.38 = (s32[1024]{0:T(1024)S(1)}, s32[1024]{0:T(1024)}, u32[]{:S(2)}) copy-start(s32[1024]{0:T(1024)} %param.21) | copy-start | bytes 12292
  7.2 67.8 %all-gather.5.cloned.1.call-start = ((), (), s32[]{:S(2)}) async-start(), calls=%async_computation.8 | async-start | bytes 6684672 | tf_op jit(solution)/shard_map/all_gather | solution.py:77
  8.0 482.3 %all-gather.7.cloned.1.call-start = ((), (), s32[]{:S(2)}) async-start(), calls=%async_computation.9 | async-start | bytes 2228224 | tf_op jit(solution)/shard_map/all_gather | solution.py:78
  8.7 509.3 %all-gather.9.cloned.1.call-start = ((), (), s32[]{:S(2)}) async-start(), calls=%async_computation.10 | async-start | bytes 17825792 | tf_op jit(solution)/shard_map/all_gather | solution.py:79
  12.3 72.3 %copy-start.4 = (bf16[1024,1024]{0,1:T(8,128)(2,1)}, bf16[1024,1024]{0,1:T(8,128)(2,1)S(1)}, u32[]{:S(2)}) copy-start(bf16[1024,1024]{0,1:T(8,128)(2,1)S(1)} %copy.100) | copy-start | bytes 6291460
  50.3 34.3 %copy-start.30 = (f32[1024]{0:T(1024)}, f32[1024]{0:T(1024)S(1)}, u32[]{:S(2)}) copy-start(f32[1024]{0:T(1024)S(1)} %convert_element_type.100) | copy-start | bytes 12292
  50.8 33.8 %copy-start.32 = (f32[1024]{0:T(1024)}, f32[1024]{0:T(1024)S(1)}, u32[]{:S(2)}) copy-start(f32[1024]{0:T(1024)S(1)} %add_rsqrt_fusion.3) | copy-start | bytes 12292
  111.9 100.2 %all-to-all-start = ((bf16[1024,3,1024]{0,1,2:T(4,128)(2,1)}), bf16[1024,3,1024]{0,1,2:T(4,128)(2,1)}, u32[]{:S(2)}, u32[]{:S(2)}) async-start(bf16[1024,3,1024]{0,1,2:T(4,128)(2,1)} %copy.102), calls=%async_computation | async-start | bytes 16777216 | tf_op jit(solution)/shard_map/all_to_all | solution.py:116
  119.1 427.4 %all-gather.11.cloned.1.call-start = ((), (), s32[]{:S(2)}) async-start(), calls=%async_computation.11 | async-start | bytes 8912896 | tf_op jit(solution)/shard_map/all_gather | solution.py:80
  481.0 29.5 %all-to-all-start.1 = ((bf16[2,1024,512]{1,2,0:T(8,128)(2,1)}), bf16[2,1024,512]{1,2,0:T(8,128)(2,1)}, u32[]{:S(2)}, u32[]{:S(2)}) async-start(bf16[2,1024,512]{1,2,0:T(8,128)(2,1)} %copy.107), calls=%async_computation.1 | async-start | bytes 4194304 | tf_op jit(solution)/shard_map/all_to_all | solution.py:153
  485.9 119.3 %copy-start.26 = (f32[1024]{0:T(1024)}, f32[1024]{0:T(1024)S(1)}, u32[]{:S(2)}) copy-start(f32[1024]{0:T(1024)S(1)} %convert_element_type.103) | copy-start | bytes 12292
  490.3 115.0 %copy-start.24 = (f32[1024]{0:T(1024)}, f32[1024]{0:T(1024)S(1)}, u32[]{:S(2)}) copy-start(f32[1024]{0:T(1024)S(1)} %fusion.87) | copy-start | bytes 12292
  518.0 87.2 %copy-start.28 = (f32[1024]{0:T(1024)}, f32[1024]{0:T(1024)S(1)}, u32[]{:S(2)}) copy-start(f32[1024]{0:T(1024)S(1)} %add_rsqrt_fusion.2) | copy-start | bytes 12292
  577.6 27.6 %copy-start.9 = (bf16[1024,1024]{0,1:T(8,128)(2,1)S(1)}, bf16[1024,1024]{0,1:T(8,128)(2,1)}, u32[]{:S(2)}) copy-start(bf16[1024,1024]{0,1:T(8,128)(2,1)} %copy.109) | copy-start | bytes 6291460
  577.6 27.6 %copy-start.12 = (f32[1024,1024]{0,1:T(8,128)S(1)}, f32[1024,1024]{0,1:T(8,128)}, u32[]{:S(2)}) copy-start(f32[1024,1024]{0,1:T(8,128)} %get-tuple-element.489) | copy-start | bytes 12582916
  612.7 28.6 %all-to-all-start.2 = ((bf16[1024,2,512]{0,2,1:T(8,128)(2,1)}), bf16[1024,2,512]{0,2,1:T(8,128)(2,1)}, u32[]{:S(2)}, u32[]{:S(2)}) async-start(bf16[1024,2,512]{0,2,1:T(8,128)(2,1)} %bitcast.224), calls=%async_computation.2 | async-start | bytes 4194304 | tf_op jit(solution)/shard_map/all_to_all | solution.py:192
  774.3 15.8 copy-start.13
  1146.7 97.3 %all-to-all-start.3 = ((bf16[2048,3,512]{2,1,0:T(4,128)(2,1)}), bf16[2048,3,512]{2,1,0:T(4,128)(2,1)}, u32[]{:S(2)}, u32[]{:S(2)}) async-start(bf16[2048,3,512]{2,1,0:T(4,128)(2,1)} %copy.115), calls=%async_computation.3 | async-start | bytes 16777216 | tf_op jit(solution)/shard_map/all_to_all | solution.py:244
  1153.7 195.1 %reduce-scatter.7.cloned.1.call-start = ((), (), s32[]{:S(2)}) async-start(), calls=%async_computation.13 | async-start | bytes 4456448 | tf_op jit(solution)/shard_map/reduce_scatter | solution.py:269
  1161.0 272.4 %reduce-scatter.5.cloned.1.call-start = ((), (), s32[]{:S(2)}) async-start(), calls=%async_computation.12 | async-start | bytes 13369344 | tf_op jit(solution)/shard_map/reduce_scatter | solution.py:268
  1300.9 314.9 %reduce-scatter.11.cloned.1.call-start = ((), (), s32[]{:S(2)}) async-start(), calls=%async_computation.15 | async-start | bytes 17825792 | tf_op jit(solution)/shard_map/reduce_scatter | solution.py:271
  1319.5 632.9 %reduce-scatter.9.cloned.1.call-start = ((), (), s32[]{:S(2)}) async-start(), calls=%async_computation.14 | async-start | bytes 35651584 | tf_op jit(solution)/shard_map/reduce_scatter | solution.py:270
  1348.1 719.7 %all-reduce.11.cloned.1.call-start = ((), (), s32[]{:S(2)}) async-start(), calls=%async_computation.16 | async-start | bytes 8388608 | tf_op jit(solution)/shard_map/psum | solution.py:275
  (47 other events, 286.1 us)
Sparse Core Ops, SparseCore 0:
  10.4 64.6 all-gather.4
  77.2 40.0 all-gather.6
  119.4 125.6 all-gather.8
  247.1 73.0 all-gather.10
  1161.1 71.7 reduce-scatter.6
  1301.0 132.3 reduce-scatter.4
  1438.1 177.6 reduce-scatter.10
  1620.6 331.7 reduce-scatter.8
  1955.2 109.4 all-reduce.10
where the time goes:
time: 2090 us; the launch traced here: 2080 us
  waiting for transfers between devices  845 us (40%)
  matrix products  648 us (31%)
  other arithmetic  230 us (11%)
  local copies, waits for them, and re-layouts  190 us (9%)
  blocking collectives  111 us (5%)
  starting transfers between devices  24.2 us (1%)
    reduce_scatter x1, waiting for transfers between devices, body(): lax.psum_scatter(gate_up_grad, 'dp', scatter_dimension=0, tiled=True)  337 us
    reduce_scatter x1, waiting for transfers between devices, body(): lax.psum_scatter(down_grad, 'dp', scatter_dimension=0, tiled=True)  182 us
    dot_general x8, matrix products, block_scores(): jnp.einsum('qhd,khd->hqk', query_block, head_key, preferred_element_type=...  181 us
    reduce_sum x4, other arithmetic, backward_block(): same_terms = jnp.sum(jnp.where(same_var, score_grad, 0.0), axis=(1, 2))  111 us
    all_to_all x1, waiting for transfers between devices, body(): lax.all_to_all(packed, 'seq', split_axis=2, concat_axis=0, tiled=True)  89.8 us
    reduce_scatter x1, waiting for transfers between devices, body(): lax.psum_scatter(in_proj_grad, 'dp', scatter_dimension=0, tiled=True)  84.6 us
    all_to_all x1, waiting for transfers between devices, body(): lax.all_to_all(grads_heads, 'seq', split_axis=0, concat_axis=2, tiled=True)  82.9 us
    dot_general x4, matrix products, cols_product(): lax.dot_general(left, right, (((1,), (1,)), ((), ())), preferred_element_...  74 us
  transfers between devices with their start and end apart: 13, of which 8 were waited for; matrix products, arithmetic and copies ran while one was open for 23% of the time, Pallas kernels for 0%

commit v1 on v0

v1 whole, which is shorter than its diff:
```python
import functools
import math

import jax
import jax.numpy as jnp
from jax import lax
from jax.experimental import pallas as pl
from jax.experimental.pallas import tpu as pltpu
from jax.sharding import PartitionSpec as P

EPSILON = 1e-06
ROPE_BASE = 10000.0
NEG_FILL = -1e30
PAIR = 128
KEY_ROWS = 256
VMEM_BYTES = 48 * 2**20
bf16 = jnp.bfloat16
f32 = jnp.float32
NN = (((1,), (0,)), ((), ()))
NT = (((1,), (1,)), ((), ()))
TN = (((0,), (0,)), ((), ()))


def dot(left, right, dims=NN):
    return lax.dot_general(left, right, dims, preferred_element_type=f32)


def split_two(values):
    high = values.astype(bf16)
    return high, (values - high.astype(f32)).astype(bf16)


def lane_index():
    return lax.broadcasted_iota(jnp.int32, (1, PAIR), 1)


def half_ones(same):
    rows = lax.broadcasted_iota(jnp.int32, (2 * PAIR, PAIR), 0) % PAIR
    cols = lax.broadcasted_iota(jnp.int32, (2 * PAIR, PAIR), 1)
    match = (rows < 64) == (cols < 64)
    return jnp.where(match if same else jnp.logical_not(match), 1.0, 0.0).astype(bf16)


def head_sums(values, ones):
    return dot(jnp.concatenate(split_two(values), axis=1), ones)


def swap_halves(values):
    first = lane_index() % 64 < 32
    return jnp.where(first, pltpu.roll(values, PAIR - 32, 1), pltpu.roll(values, 32, 1))


def qkv_kernel(
    tokens_ref, gain_ref, weight_ref, cos_ref, sin_ref, qgain_ref, kgain_ref,
    q_ref, k_ref, v_ref, raw_ref, normed_ref,
):
    width = tokens_ref.shape[1]
    values = tokens_ref[...].astype(f32)
    inv = lax.rsqrt(jnp.mean(values * values, axis=-1, keepdims=True) + EPSILON)
    normed = (values * inv * gain_ref[...]).astype(bf16)
    normed_ref[...] = normed
    ones = half_ones(True)
    cosine, sine = cos_ref[...], sin_ref[...]
    for part, (out_ref, head_gain, scale) in enumerate(
        ((q_ref, qgain_ref[...], 0.125), (k_ref, kgain_ref[...], 1.0))
    ):
        for chunk in range(width // 256):
            start = part * width + chunk * 256
            raw = dot(normed, weight_ref[:, start : start + 256])
            raw_ref[:, start : start + 256] = raw
            for tile in range(2):
                u = raw[:, tile * PAIR : (tile + 1) * PAIR]
                unit = lax.rsqrt(head_sums(u * u, ones) * (1.0 / 64) + EPSILON)
                u = u * unit * head_gain
                u = u * cosine + swap_halves(u) * sine
                at = chunk * 256 + tile * PAIR
                out_ref[:, at : at + PAIR] = (u * scale).astype(bf16)
    for chunk in range(width // 256):
        start = 2 * width + chunk * 256
        v_ref[:, chunk * 256 : (chunk + 1) * 256] = dot(
            normed, weight_ref[:, start : start + 256]
        ).astype(bf16)


def project(tokens, gain, weight, cosine, sine, qgain, kgain, block=256):
    rows, width = tokens.shape
    by_rows = lambda i: (i, 0)
    whole = lambda i: (0, 0)
    return pl.pallas_call(
        qkv_kernel,
        grid=(rows // block,),
        in_specs=[
            pl.BlockSpec((block, width), by_rows),
            pl.BlockSpec((1, width), whole),
            pl.BlockSpec(weight.shape, whole),
            pl.BlockSpec((block, PAIR), by_rows),
            pl.BlockSpec((block, PAIR), by_rows),
            pl.BlockSpec((1, PAIR), whole),
            pl.BlockSpec((1, PAIR), whole),
        ],
        out_specs=[
            pl.BlockSpec((block, width), by_rows),
            pl.BlockSpec((block, width), by_rows),
            pl.BlockSpec((block, width), by_rows),
            pl.BlockSpec((block, 2 * width), by_rows),
            pl.BlockSpec((block, width), by_rows),
        ],
        out_shape=[
            jax.ShapeDtypeStruct((rows, width), bf16),
            jax.ShapeDtypeStruct((rows, width), bf16),
            jax.ShapeDtypeStruct((rows, width), bf16),
            jax.ShapeDtypeStruct((rows, 2 * width), f32),
            jax.ShapeDtypeStruct((rows, width), bf16),
        ],
        compiler_params=pltpu.CompilerParams(vmem_limit_bytes=VMEM_BYTES),
        cost_estimate=pl.CostEstimate(
            flops=6 * rows * width * width, bytes_accessed=20 * rows * width, transcendentals=0
        ),
    )(tokens, gain, weight, cosine, sine, qgain, kgain)


def merge_kernel(sources, parts, *refs):
    dq_refs = refs[:parts]
    dk_refs = refs[parts : parts + sources]
    dv_refs = refs[parts + sources : parts + 2 * sources]
    raw_ref, cos_ref, sin_ref, qgain_ref, kgain_ref, out_ref, gains_ref = refs[parts + 2 * sources :]
    width = dq_refs[0].shape[1]
    ones = half_ones(True)
    cosine, sine = cos_ref[...], sin_ref[...]

    @pl.when(pl.program_id(0) == 0)
    def _():
        gains_ref[...] = jnp.zeros_like(gains_ref)

    for part, (grad_refs, head_gain) in enumerate(((dq_refs, qgain_ref[...]), (dk_refs, kgain_ref[...]))):
        for tile in range(width // PAIR):
            at = slice(tile * PAIR, (tile + 1) * PAIR)
            grad = grad_refs[0][:, at].astype(f32)
            for ref in grad_refs[1:]:
                grad = grad + ref[:, at].astype(f32)
            grad = grad.astype(bf16).astype(f32)
            grad = grad * cosine - swap_halves(grad) * sine
            there = slice(part * width + tile * PAIR, part * width + (tile + 1) * PAIR)
            raw = raw_ref[:, there]
            unit = lax.rsqrt(head_sums(raw * raw, ones) * (1.0 / 64) + EPSILON)
            hat = raw * unit
            gains_ref[part : part + 1, at] += jnp.sum(grad * hat, axis=0, keepdims=True)
            weighted = grad * head_gain
            inner = head_sums(weighted * hat, ones) * (1.0 / 64)
            out_ref[:, there] = (unit * (weighted - hat * inner)).astype(bf16)
    total = dv_refs[0][...].astype(f32)
    for ref in dv_refs[1:]:
        total = total + ref[...].astype(f32)
    out_ref[:, 2 * width :] = total.astype(bf16)


def merge_grads(dqs, dks, dvs, raw, cosine, sine, qgain, kgain, block=256):
    rows, width = dqs[0].shape
    by_rows = lambda i: (i, 0)
    whole = lambda i: (0, 0)
    grads = list(dqs) + list(dks) + list(dvs)
    return pl.pallas_call(
        functools.partial(merge_kernel, len(dks), len(dqs)),
        grid=(rows // block,),
        in_specs=[pl.BlockSpec((block, width), by_rows)] * len(grads)
        + [
            pl.BlockSpec((block, 2 * width), by_rows),
            pl.BlockSpec((block, PAIR), by_rows),
            pl.BlockSpec((block, PAIR), by_rows),
            pl.BlockSpec((1, PAIR), whole),
            pl.BlockSpec((1, PAIR), whole),
        ],
        out_specs=[pl.BlockSpec((block, 3 * width), by_rows), pl.BlockSpec((8, width), whole)],
        out_shape=[
            jax.ShapeDtypeStruct((rows, 3 * width), bf16),
            jax.ShapeDtypeStruct((8, width), f32),
        ],
        compiler_params=pltpu.CompilerParams(vmem_limit_bytes=VMEM_BYTES),
        cost_estimate=pl.CostEstimate(
            flops=100 * rows * width, bytes_accessed=40 * rows * width, transcendentals=0
        ),
    )(*grads, raw, cosine, sine, qgain, kgain)


def forward_kernel(sources, query_rows, flags, q_ref, aq_ref, coef_ref, *refs):
    keyed = refs[: 3 * sources]
    out_ref, full_ref, query, total = refs[3 * sources :]
    rows = q_ref.shape[0]
    lane = lane_index()
    half = lane < 64
    mine = (half, jnp.logical_not(half))
    both = q_ref[...]
    extra = aq_ref[...]
    for h in range(2):
        query[h] = jnp.where(mine[h], both, extra * coef_ref[0, h : h + 1, :])
        total[h] = jnp.zeros_like(total[h])
    blocks = keyed[0].shape[0] // KEY_ROWS
    for j in range(sources):
        k_ref, v_ref, ak_ref = keyed[3 * j : 3 * j + 3]
        for b in range(blocks):

            @pl.when(flags[j * blocks + b] != 0)
            def _():
                at = slice(b * KEY_ROWS, (b + 1) * KEY_ROWS)
                keys, values, columns = k_ref[at, :], v_ref[at, :], ak_ref[at, :]
                ones = jnp.ones_like(values)
                keys2 = [jnp.where(mine[h], keys, columns) for h in range(2)]
                values2 = [jnp.where(mine[h], values, ones) for h in range(2)]
                for i in range(rows // query_rows):
                    part = slice(i * query_rows, (i + 1) * query_rows)
                    for h in range(2):
                        probs = jnp.exp(dot(query[h, part, :], keys2[h], NT)).astype(bf16)
                        total[h, part, :] += dot(probs, values2[h])

    outs = []
    for h in range(2):
        summed = total[h]
        outs.append(summed / pltpu.roll(summed, 64, 1))
        log_total = jnp.log(jnp.maximum(summed, 1e-30))
        high = log_total.astype(bf16)
        mid, low = split_two(log_total - high.astype(f32))
        base = lane - 64 if h == 0 else lane
        full_ref[:, h * PAIR : (h + 1) * PAIR] = jnp.where(
            base == 11, -high, jnp.where(base == 12, -mid, jnp.where(base == 13, -low, query[h]))
        )
    out_ref[...] = jnp.where(half, outs[0], outs[1]).astype(bf16)


def attend(flags, queries, query_columns, coefficients, keyed):
    rows, width = queries.shape
    pairs = width // PAIR
    key_rows = keyed[0][0].shape[0]
    sources = len(keyed)
    by_pair = lambda p, f: (0, p)
    whole = lambda p, f: (0, 0)
    in_specs = [
        pl.BlockSpec((rows, PAIR), by_pair),
        pl.BlockSpec((rows, PAIR), whole),
        pl.BlockSpec((1, 2, PAIR), lambda p, f: (p, 0, 0)),
    ]
    operands = [queries, query_columns, coefficients]
    for keys, values, columns in keyed:
        in_specs += [
            pl.BlockSpec((key_rows, PAIR), by_pair),
            pl.BlockSpec((key_rows, PAIR), by_pair),
            pl.BlockSpec((key_rows, PAIR), whole),
        ]
        operands += [keys, values, columns]
    return pl.pallas_call(
        functools.partial(forward_kernel, sources, min(512, rows)),
        grid_spec=pltpu.PrefetchScalarGridSpec(
            num_scalar_prefetch=1,
            grid=(pairs,),
            in_specs=in_specs,
            out_specs=[
                pl.BlockSpec((rows, PAIR), by_pair),
                pl.BlockSpec((rows, 2 * PAIR), by_pair),
            ],
            scratch_shapes=[
                pltpu.VMEM((2, rows, PAIR), bf16),
                pltpu.VMEM((2, rows, PAIR), f32),
            ],
        ),
        out_shape=[
            jax.ShapeDtypeStruct((rows, width), bf16),
            jax.ShapeDtypeStruct((rows, 2 * width), bf16),
        ],
        compiler_params=pltpu.CompilerParams(vmem_limit_bytes=VMEM_BYTES),
        cost_estimate=pl.CostEstimate(
            flops=8 * rows * key_rows * sources * width,
            bytes_accessed=12 * rows * width,
            transcendentals=rows * key_rows * sources * 2 * pairs,
        ),
    )(flags, *operands)


def backward_kernel(
    flags, full_ref, grad_ref, out_ref, aq_ref, k_ref, v_ref, ak_ref,
    dq_ref, dk_ref, dv_ref, bias_ref, grads, dq_total,
):
    rows = grad_ref.shape[0]
    lane = lane_index()
    half = lane < 64
    mine = (half, jnp.logical_not(half))
    base = (lane - 64, lane)
    both = grad_ref[...]
    row_total = head_sums(both.astype(f32) * out_ref[...].astype(f32), half_ones(False))
    high, low = split_two(row_total)
    zero = jnp.zeros_like(high)
    for h in range(2):
        extra = jnp.where(base[h] == 0, -high, jnp.where(base[h] == 1, -low, zero))
        grads[h] = jnp.where(mine[h], both, extra)
        dq_total[h] = jnp.zeros_like(dq_total[h])
    for b in range(k_ref.shape[0] // KEY_ROWS):
        at = slice(b * KEY_ROWS, (b + 1) * KEY_ROWS)

        @pl.when(flags[b] != 0)
        def _():
            keys, values, columns = k_ref[at, :], v_ref[at, :], ak_ref[at, :]
            ones = jnp.ones_like(values)
            dks, dvs = [], []
            for h in range(2):
                keys2 = jnp.where(mine[h], keys, columns)
                pick = (base[h] >= 0) & (base[h] < 2)
                values2 = jnp.where(mine[h], values, jnp.where(pick, ones, jnp.zeros_like(ones)))
                full = full_ref[:, h * PAIR : (h + 1) * PAIR]
                probs = jnp.exp(dot(keys2, full, NT))
                score_low = (probs * dot(values2, grads[h], NT)).astype(bf16)
                dks.append(dot(score_low, full))
                dvs.append(dot(probs.astype(bf16), grads[h]))
                dq_total[h] += dot(keys2, score_low, TN)
            dk_ref[at, :] = jnp.where(half, dks[0], dks[1]).astype(dk_ref.dtype)
            dv_ref[at, :] = jnp.where(half, dvs[0], dvs[1]).astype(dv_ref.dtype)

        @pl.when(flags[b] == 0)
        def _():
            dk_ref[at, :] = jnp.zeros((KEY_ROWS, PAIR), dk_ref.dtype)
            dv_ref[at, :] = jnp.zeros((KEY_ROWS, PAIR), dv_ref.dtype)

    dq = [dq_total[h].T for h in range(2)]
    dq_ref[...] = jnp.where(half, dq[0], dq[1]) * 0.125
    variates = aq_ref[...].astype(f32)
    for h in range(2):
        pick = (base[h] >= 0) & (base[h] < 4)
        bias_ref[0, h : h + 1, :] = jnp.sum(
            jnp.where(pick, dq[h] * variates, 0.0), axis=0, keepdims=True
        )


def attend_back(flags, full, grad, out, query_columns, keys, values, key_columns):
    rows, width = grad.shape
    pairs = width // PAIR
    key_rows = keys.shape[0]
    by_pair = lambda p, f: (0, p)
    whole = lambda p, f: (0, 0)
    return pl.pallas_call(
        backward_kernel,
        grid_spec=pltpu.PrefetchScalarGridSpec(
            num_scalar_prefetch=1,
            grid=(pairs,),
            in_specs=[
                pl.BlockSpec((rows, 2 * PAIR), by_pair),
                pl.BlockSpec((rows, PAIR), by_pair),
                pl.BlockSpec((rows, PAIR), by_pair),
                pl.BlockSpec((rows, PAIR), whole),
                pl.BlockSpec((key_rows, PAIR), by_pair),
                pl.BlockSpec((key_rows, PAIR), by_pair),
                pl.BlockSpec((key_rows, PAIR), whole),
            ],
            out_specs=[
                pl.BlockSpec((rows, PAIR), by_pair),
                pl.BlockSpec((key_rows, PAIR), by_pair),
                pl.BlockSpec((key_rows, PAIR), by_pair),
                pl.BlockSpec((1, 2, PAIR), lambda p, f: (p, 0, 0)),
            ],
            scratch_shapes=[
                pltpu.VMEM((2, rows, PAIR), bf16),
                pltpu.VMEM((2, PAIR, rows), f32),
            ],
        ),
        out_shape=[
            jax.ShapeDtypeStruct((rows, width), f32),
            jax.ShapeDtypeStruct((key_rows, width), bf16),
            jax.ShapeDtypeStruct((key_rows, width), bf16),
            jax.ShapeDtypeStruct((pairs, 2, PAIR), f32),
        ],
        compiler_params=pltpu.CompilerParams(vmem_limit_bytes=VMEM_BYTES),
        cost_estimate=pl.CostEstimate(
            flops=20 * rows * key_rows * width,
            bytes_accessed=20 * rows * width,
            transcendentals=rows * key_rows * 2 * pairs,
        ),
    )(flags, full, grad, out, query_columns, keys, values, key_columns)


def slot_columns(segment, variates):
    rows = segment.shape[0]
    same_var = (variates[:, None] == jnp.arange(4, dtype=jnp.int32)[None, :]).astype(f32)
    in_seg = (segment[:, None] == jnp.arange(3, dtype=jnp.int32)[None, :]).astype(f32)
    three = jnp.ones((rows, 3), f32)
    rest = jnp.zeros((rows, 50), f32)
    query = jnp.concatenate([same_var, same_var, (1.0 - in_seg) * NEG_FILL, 0.0 * three, rest], 1)
    key = jnp.concatenate([same_var, same_var, in_seg, three, rest], 1)
    return (
        jnp.concatenate([query, query], 1).astype(bf16),
        jnp.concatenate([key, key], 1).astype(bf16),
    )


def bias_columns(head_bias):
    delta = head_bias[:, 0] - head_bias[:, 1]
    high, low = split_two(delta)
    heads = delta.shape[0]
    row = jnp.concatenate(
        [
            jnp.broadcast_to(high[:, None], (heads, 4)),
            jnp.broadcast_to(low[:, None], (heads, 4)),
            jnp.ones((heads, 3), bf16),
            jnp.zeros((heads, 53), bf16),
        ],
        1,
    )
    return jnp.concatenate([row, row], 1).reshape(heads // 2, 2, PAIR)


def rms_forward(values, gain_vec):
    inv_rms = lax.rsqrt(jnp.mean(values * values, axis=-1, keepdims=True) + EPSILON)
    return (values * inv_rms * gain_vec, inv_rms)


def rms_backward(values, inv_rms, gain_vec, upstream):
    weighted = upstream * gain_vec
    inner_sum = jnp.mean(weighted * values, axis=-1, keepdims=True)
    value_grad = inv_rms * weighted - values * inv_rms * inv_rms * inv_rms * inner_sum
    return (value_grad, upstream * values * inv_rms)


def rows_product(left, right):
    return dot(left, right, TN).astype(bf16)


def shift_by(values, count, step):
    return lax.ppermute(values, "seq", [(i, (i + step) % count) for i in range(count)])


def sum_seq(values, count):
    if count == 2:
        return values.astype(f32) + shift_by(values, count, 1).astype(f32)
    return lax.psum(values.astype(f32), "seq")


def body(
    tokens, doc_lengths, variate_ids, time_ids, in_proj, out_proj, gate_up, down_proj,
    attn_gain, ffn_gain, query_gain, key_gain, head_bias, cotangent,
):
    seq_count = lax.axis_size("seq")
    seq_rank = lax.axis_index("seq")
    local_rows, width = tokens.shape
    pack_rows = local_rows * seq_count
    head_dim = query_gain.shape[0]
    hidden_width = gate_up.shape[1] // 2

    gains = jnp.stack([attn_gain, ffn_gain], axis=1)
    in_wide = jnp.concatenate([in_proj, jnp.pad(gains, ((0, 0), (0, PAIR - 2)))], axis=1)
    gather = lambda w: lax.all_gather(w, "dp", axis=0, tiled=True)
    in_full = gather(in_wide)
    out_full, gate_full, down_full = gather(out_proj), gather(gate_up), gather(down_proj)
    attn_gain_f = in_full[:, 3 * width].astype(f32)[None, :]
    ffn_gain_f = in_full[:, 3 * width + 1].astype(f32)[None, :]

    positions = jnp.arange(pack_rows, dtype=jnp.int32)
    first_end = doc_lengths[0, 0]
    second_end = first_end + doc_lengths[0, 1]
    segment = (positions >= first_end).astype(jnp.int32) + (positions >= second_end).astype(jnp.int32)
    query_columns, key_columns = slot_columns(segment, variate_ids[0])
    coefficients = bias_columns(head_bias)
    start = seq_rank * local_rows
    query_columns = lax.dynamic_slice_in_dim(query_columns, start, local_rows)
    local_segment = lax.dynamic_slice_in_dim(segment, start, local_rows)
    valid_rows = (local_segment < 2).astype(f32)
    source_columns, source_flags = [], []
    for step in range(seq_count):
        begin = ((seq_rank + step) % seq_count) * local_rows
        source_columns.append(lax.dynamic_slice_in_dim(key_columns, begin, local_rows))
        there = lax.dynamic_slice_in_dim(segment, begin, local_rows).reshape(-1, KEY_ROWS)
        source_flags.append(
            ((there[:, 0] <= local_segment[-1]) & (there[:, -1] >= local_segment[0])).astype(jnp.int32)
        )

    half_dim = head_dim // 2
    frequency = jnp.exp(jnp.arange(half_dim, dtype=f32) * (-math.log(ROPE_BASE) / half_dim))
    angles = time_ids.astype(f32)[:, None] * frequency[None, :]
    cosine, sine = jnp.cos(angles), jnp.sin(angles)
    cosine = jnp.concatenate([cosine] * 4, axis=1)
    sine = jnp.concatenate([-sine, sine] * 2, axis=1)
    qgain = jnp.tile(query_gain, 2)[None, :]
    kgain = jnp.tile(key_gain, 2)[None, :]

    queries, keys, values, raw, normed_low = project(
        tokens, attn_gain_f, in_full, cosine, sine, qgain, kgain
    )
    keyed = [(keys, values, source_columns[0])]
    for step in range(1, seq_count):
        keyed.append(
            (
                shift_by(keys, seq_count, -step),
                shift_by(values, seq_count, -step),
                source_columns[step],
            )
        )
    attended, full_query = attend(
        jnp.concatenate(source_flags), queries, query_columns, coefficients, keyed
    )

    inputs_f = tokens.astype(f32)
    residual = inputs_f + dot(attended, out_full)
    normed_ffn, ffn_scale = rms_forward(residual, ffn_gain_f)
    normed_ffn_low = normed_ffn.astype(bf16)
    gate_vals = dot(normed_ffn_low, gate_full)
    gate_part = gate_vals[:, :hidden_width]
    up_part = gate_vals[:, hidden_width:]
    sigmoid_gate = jax.nn.sigmoid(gate_part)
    silu_gate = gate_part * sigmoid_gate
    hidden = (silu_gate * up_part).astype(bf16)
    layer_out = (residual + dot(hidden, down_full)).astype(bf16)

    seed_grad = cotangent.astype(f32) * valid_rows[:, None]
    seed_low = seed_grad.astype(bf16)
    down_grad = rows_product(hidden, seed_low)
    hidden_grad = dot(seed_low, down_full, NT)
    gate_grad_part = hidden_grad * up_part * sigmoid_gate * (1.0 + gate_part * (1.0 - sigmoid_gate))
    up_grad_part = hidden_grad * silu_gate
    gate_vals_grad = jnp.concatenate([gate_grad_part, up_grad_part], axis=1).astype(bf16)
    gate_up_grad = rows_product(normed_ffn_low, gate_vals_grad)
    normed_ffn_grad = dot(gate_vals_grad, gate_full, NT)
    resid_norm_grad, ffn_gain_terms = rms_backward(residual, ffn_scale, ffn_gain_f, normed_ffn_grad)
    residual_grad = seed_grad + resid_norm_grad
    mixed_low = residual_grad.astype(bf16)
    out_proj_grad = rows_product(attended, mixed_low)
    attended_grad = dot(mixed_low, out_full, NT).astype(bf16)

    scatter = lambda g: sum_seq(
        lax.psum_scatter(g, "dp", scatter_dimension=0, tiled=True), seq_count
    )
    dqs, dks, dvs, biases = [], [], [], []
    for step in list(range(1, seq_count)) + [0]:
        there_keys, there_values, there_columns = keyed[step]
        dq, dk, dv, bias = attend_back(
            source_flags[step], full_query, attended_grad, attended, query_columns,
            there_keys, there_values, there_columns,
        )
        dqs.append(dq)
        dks.append(shift_by(dk, seq_count, step) if step else dk)
        dvs.append(shift_by(dv, seq_count, step) if step else dv)
        biases.append(bias)
    merged_grad, head_gain_terms = merge_grads(dqs, dks, dvs, raw, cosine, sine, qgain, kgain)
    in_proj_grad = rows_product(normed_low, merged_grad)
    normed_grad = dot(merged_grad, in_full[:, : 3 * width], NT)
    norm_scale = lax.rsqrt(jnp.mean(inputs_f * inputs_f, axis=-1, keepdims=True) + EPSILON)
    input_norm_grad, attn_gain_terms = rms_backward(inputs_f, norm_scale, attn_gain_f, normed_grad)
    input_grad = residual_grad + input_norm_grad

    same_bias = jnp.sum(sum(biases), axis=-1).reshape(-1)
    heads = same_bias.shape[0]
    head_gains = jnp.sum(head_gain_terms[:2].reshape(2, -1, head_dim), axis=1)
    small = lax.psum(
        jnp.concatenate(
            [
                jnp.sum(attn_gain_terms, axis=0),
                jnp.sum(ffn_gain_terms, axis=0),
                head_gains[0],
                head_gains[1],
                same_bias,
            ]
        ),
        ("dp", "seq"),
    )
    gain_rows = attn_gain.shape[0]
    here = lax.axis_index("dp") * gain_rows
    tail = small[2 * width :]
    same_bias = tail[2 * head_dim : 2 * head_dim + heads]
    return (
        layer_out,
        input_grad,
        scatter(in_proj_grad),
        scatter(out_proj_grad),
        scatter(gate_up_grad),
        scatter(down_grad),
        lax.dynamic_slice_in_dim(small, here, gain_rows),
        lax.dynamic_slice_in_dim(small, width + here, gain_rows),
        tail[:head_dim],
        tail[head_dim : 2 * head_dim],
        jnp.stack([same_bias, -same_bias], axis=1),
    )


def solution(mesh):
    in_specs = (
        P(("dp", "seq"), None),
        P("dp", None),
        P("dp", None),
        P(("dp", "seq")),
        P("dp", None),
        P("dp", None),
        P("dp", None),
        P("dp", None),
        P("dp"),
        P("dp"),
        P(),
        P(),
        P(),
        P(("dp", "seq"), None),
    )
    out_specs = (
        P(("dp", "seq"), None),
        P(("dp", "seq"), None),
        P("dp", None),
        P("dp", None),
        P("dp", None),
        P("dp", None),
        P("dp"),
        P("dp"),
        P(),
        P(),
        P(),
    )
    return jax.shard_map(body, mesh=mesh, in_specs=in_specs, out_specs=out_specs, check_vma=False)
```

time: 2090 us -> 966 us (0.46)
  matrix products: 648 us -> 181 us
  waiting for transfers between devices: 845 us -> 432 us
  Pallas kernels: 0 us -> 210 us
  other arithmetic: 230 us -> 27.9 us
  local copies, waits for them, and re-layouts: 190 us -> 42.4 us
  blocking collectives: 111 us -> 38.2 us
    dot_general x40 -> x11, matrix products: 648 us -> 181 us  [dot(): return lax.dot_general(left, right, dims, preferred_element_type=f32)]
    reduce_scatter x4, waiting for transfers between devices: 604 us -> 239 us  [body(): lax.psum_scatter(g, 'dp', scatter_dimension=0, tiled=True)]
    all_to_all x4 -> x0, waiting for transfers between devices: 217 us -> none  [the longest x1 89.8 us: body(): lax.all_to_all(packed, 'seq', split_axis=2, concat_axis=0, tiled=True)]
    pallas_call x0 -> x5, Pallas kernels: none -> 210 us  [the longest x2 110 us: attend_back(): pl.pallas_call(backward_kernel, grid_spec=pltpu.PrefetchScalarGridSpec(nu...]
    reduce_sum x11 -> x3, other arithmetic: 170 us -> 0.58 us  [the longest x1 0.48 us: body(): jnp.mean(inputs_f * inputs_f, axis=-1, keepdims=True) + EPSILON]
    ppermute x0 -> x8, waiting for transfers between devices: none -> 115 us  [shift_by(): lax.ppermute(values, 'seq', [(i, (i + step) % count) for i in range(count)])]
    unnamed x2 -> x0, blocking collectives: 68.1 us -> none
    all_gather x4, waiting for transfers between devices: 22.4 us -> 76.1 us  [body(): gather = lambda w: lax.all_gather(w, 'dp', axis=0, tiled=True)]
  transfers between devices with their start and end apart: 13 -> 16, of which waited for: 8 -> 8; matrix products, arithmetic and copies ran while one was open for 23% -> 18% of each run, Pallas kernels for 0% -> 16%
where the time goes in v1:
time: 966 us; the launch traced here: 957 us
  waiting for transfers between devices  432 us (45%)
  Pallas kernels  210 us (22%)
  matrix products  181 us (19%)
  local copies, waits for them, and re-layouts  42.4 us (4%)
  blocking collectives  38.2 us (4%)
  other arithmetic  27.9 us (3%)
  between operations  16.3 us (2%)
  starting transfers between devices  9.75 us (1%)
    reduce_scatter x4, waiting for transfers between devices, body(): lax.psum_scatter(g, 'dp', scatter_dimension=0, tiled=True)  239 us
    dot_general x11, matrix products, dot(): return lax.dot_general(left, right, dims, preferred_element_type=f32)  181 us
    ppermute x8, waiting for transfers between devices, shift_by(): lax.ppermute(values, 'seq', [(i, (i + step) % count) for i in range(count)])  115 us
    pallas_call x2, Pallas kernels, attend_back(): pl.pallas_call(backward_kernel, grid_spec=pltpu.PrefetchScalarGridSpec(nu...  110 us
    all_gather x4, waiting for transfers between devices, body(): gather = lambda w: lax.all_gather(w, 'dp', axis=0, tiled=True)  76.1 us
    pallas_call x1, Pallas kernels, attend(): pl.pallas_call(functools.partial(forward_kernel, sources, min(512, rows))...  62.7 us
    psum x1, blocking collectives, body(): lax.psum(jnp.concatenate([jnp.sum(attn_gain_terms, axis=0), jnp.sum(ffn_g...  38.2 us
    unnamed x70, local copies, waits for them, and re-layouts  24.8 us
  transfers between devices with their start and end apart: 16, of which 8 were waited for; matrix products, arithmetic and copies ran while one was open for 18% of the time, Pallas kernels for 16%

profile of v1, /device:TPU:0, one launch (start us, length us, event | category | flops | bytes accessed | tf_op | source)
XLA Modules:
  0.0 957.4 jit_solution(6433703924746490428)
XLA Ops:
  26.9 50.1 %all-gather.5.cloned.1.call-done.weight_ref = bf16[1024,3200]{1,0:T(8,128)(2,1)} async-done(((bf16[64,3200]{1,0:T(8,128)(2,1)}), bf16[1024,3200]{1,0:T(8,128)(2,1)}) %all-gather.5.cloned.1.call-update) | async-done | bytes 6553616 | tf_op jit(solution)/shard_map/all_gather | solution.py:445
  78.4 22.3 %shard_map.221 = (bf16[1024,1024]{1,0:T(8,128)(2,1)S(1)}, bf16[1024,1024]{1,0:T(8,128)(2,1)}, bf16[1024,1024]{1,0:T(8,128)(2,1)}, f32[1024,2048]{1,0:T(8,128)}, bf16[1024,1024]{1,0:T(8,128)(2,1)}) custom-call(bf16[1024,1024]{1,0:T(8,128)(2,1)} %tokens_ref.1, f32[1,1024]{1,0:T(1,128)S(1)} %bitcast.34, ...), custom_call_target="tpu_custom_call" | custom-call | flops 6442450944 | bytes 20971520 | tf_op jit(solution)/shard_map/pallas_call | solution.py:89
  121.2 29.7 %collective-permute-done.refs_3_.k_ref = bf16[1024,1024]{1,0:T(8,128)(2,1)} collective-permute-done((bf16[1024,1024]{1,0:T(8,128)(2,1)}, bf16[1024,1024]{1,0:T(8,128)(2,1)}, u32[]{:S(2)}, u32[]{:S(2)}) %collective-permute-start) | collective-permute-done | bytes 2097184 | tf_op jit(solution)/shard_map/ppermute | solution.py:423
  150.8 44.3 %collective-permute-done.1.refs_4_.v_ref = bf16[1024,1024]{1,0:T(8,128)(2,1)} collective-permute-done((bf16[1024,1024]{1,0:T(8,128)(2,1)}, bf16[1024,1024]{1,0:T(8,128)(2,1)}, u32[]{:S(2)}, u32[]{:S(2)}) %collective-permute-start.1) | collective-permute-done | bytes 2097184 | tf_op jit(solution)/shard_map/ppermute | solution.py:423
  196.7 62.7 %shard_map.222 = (bf16[1024,1024]{1,0:T(8,128)(2,1)S(1)}, bf16[1024,2048]{1,0:T(8,128)(2,1)}) custom-call(s32[8]{0:T(128)S(1)} %pad_add_fusion.flags, bf16[1024,1024]{1,0:T(8,128)(2,1)S(1)} %copy-done.18, bf16[1024,128]{1,0:T(8,128)(2,1)S(1)} %get-tuple-element.140.aq_ref, bf16[8,2,128]{2,1,0:T(2,128)(2,1)S(1)} %bitcast.35, ...), custom_call_target="tpu_custom_call" | custom-call | flops 17179869184 | bytes 12582912 | tf_op jit(solution)/shard_map/pallas_call | solution.py:249
  259.4 7.6 multiply_reduce_fusion.2
  267.0 29.1 %fusion.28 = f32[1024,8192]{1,0:T(8,128)} fusion(bf16[1024,8192]{1,0:T(8,128)(2,1)} %all-gather.9.cloned.1.call-done, f32[1024,1024]{0,1:T(8,128)} %get-tuple-element.133, f32[1024]{0:T(1024)S(1)} %get-tuple-element.102, f32[1024]{0:T(1024)S(1)} %add_rsqrt_fusion.1), kind=kOutput, calls=%fused_computation.93 | convolution fusion | flops 17183014912 | bytes 54534144 | tf_op jit(solution)/shard_map/dot_general | solution.py:25
  296.2 26.0 %all-gather.11.cloned.1.call-done = bf16[4096,1024]{1,0:T(8,128)(2,1)} async-done(((bf16[256,1024]{1,0:T(8,128)(2,1)}), bf16[4096,1024]{1,0:T(8,128)(2,1)}) %all-gather.11.cloned.1.call-update) | async-done | bytes 8388624 | tf_op jit(solution)/shard_map/all_gather | solution.py:445
  322.2 27.8 %multiply_convert_fusion.1 = (bf16[1024,4096]{1,0:T(8,128)(2,1)}, bf16[1024,4096]{1,0:T(8,128)(2,1)}, bf16[1024,4096]{1,0:T(8,128)(2,1)}) fusion(f32[1024,8192]{1,0:T(8,128)} %fusion.28, bf16[4096,1024]{1,0:T(8,128)(2,1)} %all-gather.11.cloned.1.call-done, bf16[1024,1024]{0,1:T(8,128)(2,1)S(1)} %copy-done.21, f32[1024]{0:T(1024)S(1)} %get-tuple-element.106), kind=kOutput, calls=%fused_computation.2 | convolution fusion | flops 8655994880 | bytes 69210112 | tf_op jit(solution)/shard_map/dot_general | solution.py:25
  350.0 27.8 %multiply_reduce_fusion = (f32[1024]{0:T(1024)}, f32[1024]{0:T(1024)S(1)}, f32[1024,1024]{0,1:T(8,128)}) fusion(f32[1024,1024]{0,1:T(8,128)} %get-tuple-element.133, f32[1024]{0:T(1024)S(1)} %add_rsqrt_fusion.1, f32[1024]{0:T(1024)S(1)} %get-tuple-element.102, bf16[1024,8192]{1,0:T(8,128)(2,1)} %all-gather.9.cloned.1.call-done, ...), kind=kOutput, calls=%fused_computation.26 | convolution fusion | flops 17219715072 | bytes 41959424 | tf_op jit(solution)/shard_map/dot_general | solution.py:25
  385.3 54.6 %shard_map.223 = (f32[1024,1024]{1,0:T(8,128)}, bf16[1024,1024]{1,0:T(8,128)(2,1)}, bf16[1024,1024]{1,0:T(8,128)(2,1)}, f32[8,2,128]{2,1,0:T(2,128)S(1)}) custom-call(s32[4]{0:T(128)S(1)} %get-tuple-element.136.flags, bf16[1024,2048]{1,0:T(8,128)(2,1)} %get-tuple-element.32.full_ref, bf16[1024,1024]{1,0:T(8,128)(2,1)} %convolution_convert_fusion.4.grad_ref, ...), custom_call_target="tpu_custom_call" | custom-call | flops 21474836480 | bytes 20971520 | tf_op jit(solution)/shard_map/pallas_call | solution.py:336
  446.9 55.1 %shard_map.224 = (f32[1024,1024]{1,0:T(8,128)}, bf16[1024,1024]{1,0:T(8,128)(2,1)S(1)}, bf16[1024,1024]{1,0:T(8,128)(2,1)S(1)}, f32[8,2,128]{2,1,0:T(2,128)S(1)}) custom-call(s32[4]{0:T(128)S(1)} %copy-done.14, bf16[1024,2048]{1,0:T(8,128)(2,1)} %get-tuple-element.32.full_ref, bf16[1024,1024]{1,0:T(8,128)(2,1)} %convolution_convert_fusion.4.grad_ref, ...), custom_call_target="tpu_custom_call" | custom-call | flops 21474836480 | bytes 20971520 | tf_op jit(solution)/shard_map/pallas_call | solution.py:336
  503.4 29.7 %collective-permute-done.3.refs_4_ = bf16[1024,1024]{1,0:T(8,128)(2,1)} collective-permute-done((bf16[1024,1024]{1,0:T(8,128)(2,1)}, bf16[1024,1024]{1,0:T(8,128)(2,1)}, u32[]{:S(2)}, u32[]{:S(2)}) %collective-permute-start.3) | collective-permute-done | bytes 2097184 | tf_op jit(solution)/shard_map/ppermute | solution.py:423
  533.1 15.1 %shard_map.225 = (bf16[1024,3072]{1,0:T(8,128)(2,1)}, f32[8,1024]{1,0:T(8,128)S(1)}) custom-call(f32[1024,1024]{1,0:T(8,128)} %get-tuple-element.33.refs_0_, f32[1024,1024]{1,0:T(8,128)} %get-tuple-element.34.refs_1_, bf16[1024,1024]{1,0:T(8,128)(2,1)S(1)} %collective-permute-done.2.refs_2_, bf16[1024,1024]{1,0:T(8,128)(2,1)S(1)} %get-tuple-element.36.refs_3_, ...), custom_call_target="tpu_custom_call" | custom-call | flops 104857600 | bytes 41943040 | tf_op jit(solution)/shard_map/pallas_call | solution.py:162
  548.2 11.6 %convolution_convert_fusion.2 = bf16[1024,3072]{1,0:T(8,128)(2,1)} fusion(bf16[1024,1024]{1,0:T(8,128)(2,1)S(1)} %copy-done.32, bf16[1024,3072]{1,0:T(8,128)(2,1)} %get-tuple-element.40), kind=kOutput, calls=%fused_computation.16 | convolution fusion | flops 6445596672 | bytes 14680064 | tf_op jit(solution)/shard_map/dot_general | solution.py:25
  559.9 25.5 %convolution_convert_fusion = bf16[1024,8192]{1,0:T(8,128)(2,1)} fusion(bf16[1024,4096]{1,0:T(8,128)(2,1)} %get-tuple-element.109, bf16[1024,4096]{1,0:T(8,128)(2,1)} %get-tuple-element.108, f32[1024,1024]{0,1:T(8,128)} %get-tuple-element.133, f32[1024]{0:T(1024)S(1)} %get-tuple-element.102, f32[1024]{0:T(1024)S(1)} %add_rsqrt_fusion.1), kind=kOutput, calls=%fused_computation.6 | convolution fusion | flops 17224957952 | bytes 37756928 | tf_op jit(solution)/shard_map/dot_general | solution.py:25
  587.0 15.7 %convolution_convert_fusion.1 = bf16[4096,1024]{1,0:T(8,128)(2,1)} fusion(bf16[1024,4096]{1,0:T(8,128)(2,1)} %get-tuple-element.110, bf16[1024,1024]{0,1:T(8,128)(2,1)S(1)} %copy-done.22, f32[1024]{0:T(1024)S(1)} %get-tuple-element.106), kind=kOutput, calls=%fused_computation.13 | convolution fusion | flops 8597274624 | bytes 18878464 | tf_op jit(solution)/shard_map/dot_general | solution.py:25
  604.9 15.6 %add_convert_fusion = bf16[1024,1024]{0,1:T(8,128)(2,1)} fusion(f32[1024,1024]{0,1:T(8,128)} %get-tuple-element.133, bf16[1024,4096]{1,0:T(8,128)(2,1)} %get-tuple-element.110, bf16[4096,1024]{1,0:T(8,128)(2,1)} %all-gather.11.cloned.1.call-done), kind=kOutput, calls=%fused_computation.31 | convolution fusion | flops 8592031744 | bytes 23068672 | tf_op jit(solution)/shard_map/dot_general | solution.py:25
  624.6 13.0 %fusion.12 = (f32[1024]{0:T(1024)S(1)}, f32[1024]{0:T(1024)S(1)}, f32[1024,1024]{0,1:T(8,128)}) fusion(bf16[1024,1024]{0,1:T(8,128)(2,1)S(1)} %copy-done.19, f32[1024]{0:T(1024)S(1)} %add_rsqrt_fusion, f32[1024]{0:T(1024)S(1)} %copy-done.8, bf16[1024,3072]{1,0:T(8,128)(2,1)} %get-tuple-element.40, bf16[1024,3200]{1,0:T(8,128)(2,1)} %all-gather.5.cloned.1.call-done.weight_ref), kind=kOutput, calls=%fused_computation.25 | convolution fusion | flops 6449788928 | bytes 18890752 | tf_op jit(solution)/shard_map/dot_general | solution.py:25
  637.7 38.2 %psum.7 = f32[2192]{0:T(1024)S(1)} all-reduce(f32[2192]{0:T(1024)S(1)} %concatenate.44), channel_id=1, replica_groups=mesh['dp'=16,'seq'=2] {'dp','seq'}, use_global_device_ids=true, to_apply=%region_12.13 | all-reduce | flops 2192 | bytes 17536 | tf_op jit(solution)/shard_map/psum | solution.py:546
  676.5 6.8 fusion.9
  691.7 132.9 %reduce-scatter.9.cloned.1.call-done = bf16[64,8192]{1,0:T(8,128)(2,1)} async-done(((bf16[1024,8192]{1,0:T(8,128)(2,1)}), bf16[64,8192]{1,0:T(8,128)(2,1)}) %reduce-scatter.9.cloned.1.call-update) | async-done | bytes 1048592 | tf_op jit(solution)/shard_map/reduce_scatter | solution.py:523
  826.9 105.6 %reduce-scatter.11.cloned.1.call-done = bf16[256,1024]{1,0:T(8,128)(2,1)} async-done(((bf16[4096,1024]{1,0:T(8,128)(2,1)}), bf16[256,1024]{1,0:T(8,128)(2,1)}) %reduce-scatter.11.cloned.1.call-update) | async-done | bytes 524304 | tf_op jit(solution)/shard_map/reduce_scatter | solution.py:523
  934.9 11.5 %collective-permute-done.7 = bf16[256,1024]{1,0:T(8,128)(2,1)S(1)} collective-permute-done((bf16[256,1024]{1,0:T(8,128)(2,1)}, bf16[256,1024]{1,0:T(8,128)(2,1)S(1)}, u32[]{:S(2)}, u32[]{:S(2)}) %collective-permute-start.7) | collective-permute-done | bytes 524320 | tf_op jit(solution)/shard_map/ppermute | solution.py:423
  (160 shorter events, 82.8 us)
Async XLA Ops:
  7.2 69.8 %all-gather.5.cloned.1.call-start = ((), (), s32[]{:S(2)}) async-start(), calls=%async_computation.4 | async-start | bytes 6963200 | tf_op jit(solution)/shard_map/all_gather | solution.py:445
  10.0 249.4 %all-gather.7.cloned.1.call-start = ((), (), s32[]{:S(2)}) async-start(), calls=%async_computation.5 | async-start | bytes 2228224 | tf_op jit(solution)/shard_map/all_gather | solution.py:445
  10.7 256.3 %all-gather.9.cloned.1.call-start = ((), (), s32[]{:S(2)}) async-start(), calls=%async_computation.6 | async-start | bytes 17825792 | tf_op jit(solution)/shard_map/all_gather | solution.py:445
  11.5 310.7 %all-gather.11.cloned.1.call-start = ((), (), s32[]{:S(2)}) async-start(), calls=%async_computation.7 | async-start | bytes 8912896 | tf_op jit(solution)/shard_map/all_gather | solution.py:445
  12.0 671.3 %reduce-scatter.7.cloned.1.call-start = ((), (), s32[]{:S(2)}) async-start(), calls=%async_computation.9 | async-start | bytes 2228224 | tf_op jit(solution)/shard_map/reduce_scatter | solution.py:523
  102.1 48.8 %collective-permute-start = (bf16[1024,1024]{1,0:T(8,128)(2,1)}, bf16[1024,1024]{1,0:T(8,128)(2,1)}, u32[]{:S(2)}, u32[]{:S(2)}) collective-permute-start(bf16[1024,1024]{1,0:T(8,128)(2,1)} %get-tuple-element.29.refs_0_.k_ref), channel_id=1, source_target_pairs={{0,1},{1,0},{2,3},{3,2},{4,5},{5,4},{6,7},{7,6},{8,9},{9,8},{10,11... | collective-permute-start | bytes 6291464 | tf_op jit(solution)/shard_map/ppermute | solution.py:423
  103.6 91.6 %collective-permute-start.1 = (bf16[1024,1024]{1,0:T(8,128)(2,1)}, bf16[1024,1024]{1,0:T(8,128)(2,1)}, u32[]{:S(2)}, u32[]{:S(2)}) collective-permute-start(bf16[1024,1024]{1,0:T(8,128)(2,1)} %get-tuple-element.30.refs_1_.v_ref), channel_id=1, source_target_pairs={{0,1},{1,0},{2,3},{3,2},{4,5},{5,4},{6,7},{7,6},{8,9},{9,8},{10,11... | collective-permute-start | bytes 6291464 | tf_op jit(solution)/shard_map/ppermute | solution.py:423
  121.2 264.1 %copy-start.5 = (bf16[1024,128]{1,0:T(8,128)(2,1)}, bf16[1024,128]{1,0:T(8,128)(2,1)S(1)}, u32[]{:S(2)}) copy-start(bf16[1024,128]{1,0:T(8,128)(2,1)S(1)} %get-tuple-element.140.aq_ref) | copy-start | bytes 786436
  439.9 63.4 %collective-permute-start.2 = (bf16[1024,1024]{1,0:T(8,128)(2,1)}, bf16[1024,1024]{1,0:T(8,128)(2,1)S(1)}, u32[]{:S(2)}, u32[]{:S(2)}) collective-permute-start(bf16[1024,1024]{1,0:T(8,128)(2,1)} %get-tuple-element.35), channel_id=1, source_target_pairs={{0,1},{1,0},{2,3},{3,2},{4,5},{5,4},{6,7},{7,6},{8,9},{9,8},{10,11... | collective-permute-start | bytes 6291464 | tf_op jit(solution)/shard_map/ppermute | solution.py:423
  440.0 93.0 %collective-permute-start.3 = (bf16[1024,1024]{1,0:T(8,128)(2,1)}, bf16[1024,1024]{1,0:T(8,128)(2,1)}, u32[]{:S(2)}, u32[]{:S(2)}) collective-permute-start(bf16[1024,1024]{1,0:T(8,128)(2,1)} %get-tuple-element.37), channel_id=1, source_target_pairs={{0,1},{1,0},{2,3},{3,2},{4,5},{5,4},{6,7},{7,6},{8,9},{9,8},{10,11... | collective-permute-start | bytes 6291464 | tf_op jit(solution)/shard_map/ppermute | solution.py:423
  445.8 87.3 %copy-start.2 = (f32[1024,128]{1,0:T(8,128)S(1)}, f32[1024,128]{1,0:T(8,128)}, u32[]{:S(2)}) copy-start(f32[1024,128]{1,0:T(8,128)} %copy-done.1) | copy-start | bytes 1572868
  445.8 87.3 %copy-start.4 = (f32[1024,128]{1,0:T(8,128)S(1)}, f32[1024,128]{1,0:T(8,128)}, u32[]{:S(2)}) copy-start(f32[1024,128]{1,0:T(8,128)} %copy-done.3) | copy-start | bytes 1572868
  445.8 239.9 %reduce-scatter.5.cloned.1.call-start = ((), (), s32[]{:S(2)}) async-start(), calls=%async_computation.8 | async-start | bytes 6684672 | tf_op jit(solution)/shard_map/reduce_scatter | solution.py:523
  446.9 86.2 %copy-start.10 = (f32[1,128]{1,0:T(1,128)S(1)}, f32[1,128]{1,0:T(1,128)}, u32[]{:S(2)}) copy-start(f32[1,128]{1,0:T(1,128)} %copy-done.9) | copy-start | bytes 1540
  446.9 86.2 %copy-start.12 = (f32[1,128]{1,0:T(1,128)S(1)}, f32[1,128]{1,0:T(1,128)}, u32[]{:S(2)}) copy-start(f32[1,128]{1,0:T(1,128)} %copy-done.11) | copy-start | bytes 1540
  559.8 264.9 %reduce-scatter.9.cloned.1.call-start = ((), (), s32[]{:S(2)}) async-start(), calls=%async_computation.10 | async-start | bytes 17825792 | tf_op jit(solution)/shard_map/reduce_scatter | solution.py:523
  585.4 347.1 %reduce-scatter.11.cloned.1.call-start = ((), (), s32[]{:S(2)}) async-start(), calls=%async_computation.11 | async-start | bytes 8912896 | tf_op jit(solution)/shard_map/reduce_scatter | solution.py:523
  683.4 142.8 %collective-permute-start.5 = (bf16[64,1024]{1,0:T(8,128)(2,1)}, bf16[64,1024]{1,0:T(8,128)(2,1)S(1)}, u32[]{:S(2)}, u32[]{:S(2)}) collective-permute-start(bf16[64,1024]{1,0:T(8,128)(2,1)} %reduce-scatter.7.cloned.1.call-done), channel_id=1, source_target_pairs={{0,1},{1,0},{2,3},{3,2},{4,5},{5,4},{6,7},{7,6},{8,9},{9,8},{10,11... | collective-permute-start | bytes 393224 | tf_op jit(solution)/shard_map/ppermute | solution.py:423
  685.7 248.3 %collective-permute-start.4 = (bf16[64,3072]{1,0:T(8,128)(2,1)}, bf16[64,3072]{1,0:T(8,128)(2,1)S(1)}, u32[]{:S(2)}, u32[]{:S(2)}) collective-permute-start(bf16[64,3072]{1,0:T(8,128)(2,1)} %reduce-scatter.5.cloned.1.call-done), channel_id=1, source_target_pairs={{0,1},{1,0},{2,3},{3,2},{4,5},{5,4},{6,7},{7,6},{8,9},{9,8},{10,11... | collective-permute-start | bytes 1179656 | tf_op jit(solution)/shard_map/ppermute | solution.py:423
  685.8 140.4 %copy-start.27 = (bf16[64,1024]{1,0:T(8,128)(2,1)S(1)}, bf16[64,1024]{1,0:T(8,128)(2,1)}, u32[]{:S(2)}) copy-start(bf16[64,1024]{1,0:T(8,128)(2,1)} %reduce-scatter.7.cloned.1.call-done) | copy-start | bytes 393220
  685.8 248.2 %copy-start.26 = (bf16[64,3072]{1,0:T(8,128)(2,1)S(1)}, bf16[64,3072]{1,0:T(8,128)(2,1)}, u32[]{:S(2)}) copy-start(bf16[64,3072]{1,0:T(8,128)(2,1)} %reduce-scatter.5.cloned.1.call-done) | copy-start | bytes 1179652
  824.7 123.9 %copy-start.25 = (bf16[64,8192]{1,0:T(8,128)(2,1)S(1)}, bf16[64,8192]{1,0:T(8,128)(2,1)}, u32[]{:S(2)}) copy-start(bf16[64,8192]{1,0:T(8,128)(2,1)} %reduce-scatter.9.cloned.1.call-done) | copy-start | bytes 3145732
  824.7 123.9 %collective-permute-start.6 = (bf16[64,8192]{1,0:T(8,128)(2,1)}, bf16[64,8192]{1,0:T(8,128)(2,1)S(1)}, u32[]{:S(2)}, u32[]{:S(2)}) collective-permute-start(bf16[64,8192]{1,0:T(8,128)(2,1)} %reduce-scatter.9.cloned.1.call-done), channel_id=1, source_target_pairs={{0,1},{1,0},{2,3},{3,2},{4,5},{5,4},{6,7},{7,6},{8,9},{9,8},{10,11... | collective-permute-start | bytes 3145736 | tf_op jit(solution)/shard_map/ppermute | solution.py:423
  932.5 13.9 %collective-permute-start.7 = (bf16[256,1024]{1,0:T(8,128)(2,1)}, bf16[256,1024]{1,0:T(8,128)(2,1)S(1)}, u32[]{:S(2)}, u32[]{:S(2)}) collective-permute-start(bf16[256,1024]{1,0:T(8,128)(2,1)} %reduce-scatter.11.cloned.1.call-done), channel_id=1, source_target_pairs={{0,1},{1,0},{2,3},{3,2},{4,5},{5,4},{6,7},{7,6},{8,9},{9,8},{10,11... | collective-permute-start | bytes 1572872 | tf_op jit(solution)/shard_map/ppermute | solution.py:423
  (25 other events, 598.2 us)
Sparse Core Ops, SparseCore 0:
  10.9 66.0 all-gather.4
  79.2 39.9 all-gather.6
  121.3 125.6 all-gather.8
  249.1 73.0 all-gather.10
  445.9 59.7 reduce-scatter.6
  559.9 82.7 reduce-scatter.4
  646.9 177.7 reduce-scatter.8
  828.7 103.6 reduce-scatter.10

commit v2 on v1

v2 whole, which is shorter than its diff:
```python
import functools
import math

import jax
import jax.numpy as jnp
from jax import lax
from jax.experimental import pallas as pl
from jax.experimental.pallas import tpu as pltpu
from jax.sharding import PartitionSpec as P

EPSILON = 1e-06
ROPE_BASE = 10000.0
NEG_FILL = -1e30
PAIR = 128
CHUNKS = 2
KEY_ROWS = 256
VMEM_BYTES = 48 * 2**20
NO_COST = pl.CostEstimate(flops=1, bytes_accessed=1, transcendentals=0)
bf16 = jnp.bfloat16
f32 = jnp.float32
NN = (((1,), (0,)), ((), ()))
NT = (((1,), (1,)), ((), ()))
TN = (((0,), (0,)), ((), ()))


def dot(left, right, dims=NN):
    return lax.dot_general(left, right, dims, preferred_element_type=f32)


def split_two(values):
    high = values.astype(bf16)
    return high, (values - high.astype(f32)).astype(bf16)


def lane_index():
    return lax.broadcasted_iota(jnp.int32, (1, PAIR), 1)


def half_ones(same):
    rows = lax.broadcasted_iota(jnp.int32, (2 * PAIR, PAIR), 0) % PAIR
    cols = lax.broadcasted_iota(jnp.int32, (2 * PAIR, PAIR), 1)
    match = (rows < 64) == (cols < 64)
    return jnp.where(match if same else jnp.logical_not(match), 1.0, 0.0).astype(bf16)


def head_sums(values, ones):
    return dot(jnp.concatenate(split_two(values), axis=1), ones)


def swap_halves(values):
    first = lane_index() % 64 < 32
    return jnp.where(first, pltpu.roll(values, PAIR - 32, 1), pltpu.roll(values, 32, 1))


def gather_kernel(shard_ref, tokens_ref, times_ref, wide_ref, there_tokens_ref, there_times_ref, arrived, sent, keep):
    place, rank = lax.axis_index("dp"), lax.axis_index("seq")
    z, x, core = place // 4, place // 2 % 2, place % 2
    rows = shard_ref.shape[0]
    lines = 4

    def device(z, x, core, seq):
        return {"dp": z * 4 + x * 2 + core, "seq": seq}

    up, down = device(z + 1, x, core, rank), device(z - 1, x, core, rank)
    over, twin = device(z, 1 - x, core, rank), device(z, x, 1 - core, rank)
    other = device(z, x, core, 1 - rank)
    barrier = pltpu.get_barrier_semaphore()

    def greet(target):
        pl.semaphore_signal(barrier, inc=1, device_id=target, device_id_type=pl.DeviceIdType.MESH)

    for target in (over, twin, other):
        greet(target)
    pl.when(z < lines - 1)(lambda: greet(up))
    pl.when(z > 0)(lambda: greet(down))
    ends = (z == 0).astype(jnp.int32) + (z == lines - 1).astype(jnp.int32)
    pl.semaphore_wait(barrier, 5 - ends)

    def block(z, x, core):
        return z * 4 + x * 2 + core

    def rows_of(which):
        return wide_ref.at[pl.ds(pl.multiple_of(which * rows, rows), rows)]

    def copy(which, path, target, own=False):
        return pltpu.make_async_remote_copy(
            src_ref=shard_ref if own else rows_of(which),
            dst_ref=rows_of(which),
            send_sem=sent.at[path, which],
            recv_sem=arrived.at[which],
            device_id=target,
            device_id_type=pl.DeviceIdType.MESH,
        )

    def swap(source, target, index):
        return pltpu.make_async_remote_copy(
            src_ref=source,
            dst_ref=target,
            send_sem=keep.at[index],
            recv_sem=keep.at[index + 1],
            device_id=other,
            device_id_type=pl.DeviceIdType.MESH,
        )

    me = block(z, x, core)
    pl.when(z < lines - 1)(lambda: copy(me, 0, up, True).start())
    pl.when(z > 0)(lambda: copy(me, 3, down, True).start())
    copy(me, 1, over, True).start()
    copy(me, 2, twin, True).start()
    swaps = [swap(tokens_ref, there_tokens_ref, 0), swap(times_ref, there_times_ref, 2)]
    for each in swaps:
        each.start()
    here = pltpu.make_async_copy(shard_ref, rows_of(me), keep.at[4])
    here.start()

    def pass_over(which):
        copy(which, 2, twin).start()

    for step in range(1, lines):

        @pl.when(z >= step)
        def _():
            which = block(z - step, x, core)
            copy(which, 0, up).wait_recv()
            pl.when(z < lines - 1)(lambda: copy(which, 0, up).start())
            copy(which, 1, over).start()
            pass_over(which)

        @pl.when(z + step < lines)
        def _():
            which = block(z + step, x, core)
            copy(which, 3, down).wait_recv()
            pl.when(z > 0)(lambda: copy(which, 3, down).start())
            copy(which, 1, over).start()
            pass_over(which)

    for line in range(lines):
        which = block(line, 1 - x, core)
        copy(which, 1, over).wait_recv()
        pass_over(which)
    for line in range(lines):
        for side in range(2):
            copy(block(line, side, 1 - core), 2, twin).wait_recv()
    for line in range(lines):
        which = block(line, x, core)
        copy(which, 1, over).wait_send()
        copy(which, 2, twin).wait_send()
        copy(block(line, 1 - x, core), 2, twin).wait_send()
        pl.when((line <= z) & (z < lines - 1))(lambda: copy(which, 0, up).wait_send())
        pl.when((line >= z) & (z > 0))(lambda: copy(which, 3, down).wait_send())
    for each in swaps:
        each.wait()
    here.wait()


def gather_first(shard, tokens, times, places):
    anywhere = pl.BlockSpec(memory_space=pl.ANY)
    return pl.pallas_call(
        gather_kernel,
        in_specs=[anywhere] * 3,
        out_specs=[anywhere] * 3,
        out_shape=[
            jax.ShapeDtypeStruct((shard.shape[0] * places, shard.shape[1]), shard.dtype),
            jax.ShapeDtypeStruct(tokens.shape, tokens.dtype),
            jax.ShapeDtypeStruct(times.shape, times.dtype),
        ],
        scratch_shapes=[
            pltpu.SemaphoreType.DMA((places,)),
            pltpu.SemaphoreType.DMA((4, places)),
            pltpu.SemaphoreType.DMA((5,)),
        ],
        compiler_params=pltpu.CompilerParams(collective_id=0, has_side_effects=True),
        cost_estimate=NO_COST,
    )(shard, tokens, times)


def column_of(part, column, width):
    size = width // CHUNKS
    return (column // size * 3 + part) * size + column % size


def qkv_kernel(
    tokens_ref, gain_ref, weight_ref, cos_ref, sin_ref, qgain_ref, kgain_ref,
    k_ref, v_ref, *own_refs,
):
    width = tokens_ref.shape[1]
    values = tokens_ref[...].astype(f32)
    inv = lax.rsqrt(jnp.mean(values * values, axis=-1, keepdims=True) + EPSILON)
    normed = (values * inv * gain_ref[...]).astype(bf16)
    ones = half_ones(True)
    cosine, sine = cos_ref[...], sin_ref[...]
    turned = [(1, k_ref, kgain_ref[...], 1.0)]
    if own_refs:
        q_ref, raw_ref, normed_ref = own_refs
        normed_ref[...] = normed
        turned.append((0, q_ref, qgain_ref[...], 0.125))
    for part, out_ref, head_gain, scale in turned:
        for chunk in range(width // 256):
            start = column_of(part, chunk * 256, width)
            raw = dot(normed, weight_ref[:, start : start + 256])
            if own_refs:
                raw_ref[:, part * width + chunk * 256 : part * width + (chunk + 1) * 256] = raw
            for tile in range(2):
                u = raw[:, tile * PAIR : (tile + 1) * PAIR]
                unit = lax.rsqrt(head_sums(u * u, ones) * (1.0 / 64) + EPSILON)
                u = u * unit * head_gain
                u = u * cosine + swap_halves(u) * sine
                at = chunk * 256 + tile * PAIR
                out_ref[:, at : at + PAIR] = (u * scale).astype(bf16)
    for chunk in range(width // 256):
        start = column_of(2, chunk * 256, width)
        v_ref[:, chunk * 256 : (chunk + 1) * 256] = dot(
            normed, weight_ref[:, start : start + 256]
        ).astype(bf16)


def project(tokens, gain, weight, cosine, sine, qgain, kgain, own, block=256):
    rows, width = tokens.shape
    sizes = [(width, bf16), (width, bf16)]
    if own:
        sizes += [(width, bf16), (2 * width, f32), (width, bf16)]
    by_rows = lambda i: (i, 0)
    whole = lambda i: (0, 0)
    return pl.pallas_call(
        qkv_kernel,
        grid=(rows // block,),
        in_specs=[
            pl.BlockSpec((block, width), by_rows),
            pl.BlockSpec((1, width), whole),
            pl.BlockSpec((width, 3 * width), whole, pipeline_mode=pl.Buffered(1)),
            pl.BlockSpec((block, PAIR), by_rows),
            pl.BlockSpec((block, PAIR), by_rows),
            pl.BlockSpec((1, PAIR), whole),
            pl.BlockSpec((1, PAIR), whole),
        ],
        out_specs=[pl.BlockSpec((block, size), by_rows) for size, _ in sizes],
        out_shape=[jax.ShapeDtypeStruct((rows, size), kind) for size, kind in sizes],
        compiler_params=pltpu.CompilerParams(vmem_limit_bytes=VMEM_BYTES),
        cost_estimate=NO_COST,
    )(tokens, gain, weight, cosine, sine, qgain, kgain)


def merge_kernel(sources, parts, *refs):
    dq_refs = refs[:parts]
    dkv_refs = refs[parts : parts + sources]
    rawq_ref, rawk_ref, cos_ref, sin_ref, qgain_ref, kgain_ref, out_ref, gains_ref = refs[parts + sources :]
    width = dq_refs[0].shape[1]
    ones = half_ones(True)
    cosine, sine = cos_ref[...], sin_ref[...]

    @pl.when(pl.program_id(0) == 0)
    def _():
        gains_ref[...] = jnp.zeros_like(gains_ref)

    def read(part, at):
        found = [ref[:, at] for ref in dq_refs] if part == 0 else [ref[part - 1, :, at] for ref in dkv_refs]
        return sum(value.astype(f32) for value in found).astype(bf16)

    for part, (raw_ref, head_gain) in enumerate(((rawq_ref, qgain_ref[...]), (rawk_ref, kgain_ref[...]))):
        for tile in range(width // PAIR):
            at = slice(tile * PAIR, (tile + 1) * PAIR)
            grad = read(part, at).astype(f32)
            grad = grad * cosine - swap_halves(grad) * sine
            raw = raw_ref[:, at]
            unit = lax.rsqrt(head_sums(raw * raw, ones) * (1.0 / 64) + EPSILON)
            hat = raw * unit
            gains_ref[part : part + 1, at] += jnp.sum(grad * hat, axis=0, keepdims=True)
            weighted = grad * head_gain
            inner = head_sums(weighted * hat, ones) * (1.0 / 64)
            there = slice(part * width + tile * PAIR, part * width + (tile + 1) * PAIR)
            out_ref[:, there] = (unit * (weighted - hat * inner)).astype(bf16)
    out_ref[:, 2 * width :] = read(2, slice(0, width))


def merge_grads(chunk, dqs, dkvs, raw, cosine, sine, qgain, kgain, block=256):
    rows, width = dqs[0].shape
    by_rows = lambda i: (i, 0)
    whole = lambda i: (0, 0)
    return pl.pallas_call(
        functools.partial(merge_kernel, len(dkvs), len(dqs)),
        grid=(rows // block,),
        in_specs=[pl.BlockSpec((block, width), by_rows)] * len(dqs)
        + [pl.BlockSpec((2, block, width), lambda i: (0, i, 0))] * len(dkvs)
        + [
            pl.BlockSpec((block, width), lambda i: (i, chunk)),
            pl.BlockSpec((block, width), lambda i: (i, CHUNKS + chunk)),
            pl.BlockSpec((block, PAIR), by_rows),
            pl.BlockSpec((block, PAIR), by_rows),
            pl.BlockSpec((1, PAIR), whole),
            pl.BlockSpec((1, PAIR), whole),
        ],
        out_specs=[pl.BlockSpec((block, 3 * width), by_rows), pl.BlockSpec((8, width), whole)],
        out_shape=[
            jax.ShapeDtypeStruct((rows, 3 * width), bf16),
            jax.ShapeDtypeStruct((8, width), f32),
        ],
        compiler_params=pltpu.CompilerParams(vmem_limit_bytes=VMEM_BYTES),
        cost_estimate=NO_COST,
    )(*dqs, *dkvs, raw, raw, cosine, sine, qgain, kgain)


def forward_kernel(sources, query_rows, flags, q_ref, aq_ref, coef_ref, *refs):
    keyed = refs[: 3 * sources]
    out_ref, full_ref, query, total = refs[3 * sources :]
    rows = q_ref.shape[0]
    lane = lane_index()
    half = lane < 64
    mine = (half, jnp.logical_not(half))
    both = q_ref[...]
    extra = aq_ref[...]
    for h in range(2):
        query[h] = jnp.where(mine[h], both, extra * coef_ref[0, h : h + 1, :])
        total[h] = jnp.zeros_like(total[h])
    blocks = keyed[0].shape[0] // KEY_ROWS
    for j in range(sources):
        k_ref, v_ref, ak_ref = keyed[3 * j : 3 * j + 3]
        for b in range(blocks):

            @pl.when(flags[j * blocks + b] != 0)
            def _():
                at = slice(b * KEY_ROWS, (b + 1) * KEY_ROWS)
                keys, values, columns = k_ref[at, :], v_ref[at, :], ak_ref[at, :]
                ones = jnp.ones_like(values)
                keys2 = [jnp.where(mine[h], keys, columns) for h in range(2)]
                values2 = [jnp.where(mine[h], values, ones) for h in range(2)]
                for i in range(rows // query_rows):
                    part = slice(i * query_rows, (i + 1) * query_rows)
                    for h in range(2):
                        probs = jnp.exp(dot(query[h, part, :], keys2[h], NT)).astype(bf16)
                        total[h, part, :] += dot(probs, values2[h])

    outs = []
    for h in range(2):
        summed = total[h]
        outs.append(summed / pltpu.roll(summed, 64, 1))
        log_total = jnp.log(jnp.maximum(summed, 1e-30))
        high = log_total.astype(bf16)
        mid, low = split_two(log_total - high.astype(f32))
        base = lane - 64 if h == 0 else lane
        full_ref[:, h * PAIR : (h + 1) * PAIR] = jnp.where(
            base == 11, -high, jnp.where(base == 12, -mid, jnp.where(base == 13, -low, query[h]))
        )
    out_ref[...] = jnp.where(half, outs[0], outs[1]).astype(bf16)


def attend(flags, queries, query_columns, coefficients, keyed):
    rows, width = queries.shape
    pairs = width // PAIR
    key_rows = keyed[0][0].shape[0]
    sources = len(keyed)
    by_pair = lambda p, f: (0, p)
    whole = lambda p, f: (0, 0)
    in_specs = [
        pl.BlockSpec((rows, PAIR), by_pair),
        pl.BlockSpec((rows, PAIR), whole),
        pl.BlockSpec((1, 2, PAIR), lambda p, f: (p, 0, 0)),
    ]
    operands = [queries, query_columns, coefficients]
    for keys, values, columns in keyed:
        in_specs += [
            pl.BlockSpec((key_rows, PAIR), by_pair),
            pl.BlockSpec((key_rows, PAIR), by_pair),
            pl.BlockSpec((key_rows, PAIR), whole),
        ]
        operands += [keys, values, columns]
    return pl.pallas_call(
        functools.partial(forward_kernel, sources, min(512, rows)),
        grid_spec=pltpu.PrefetchScalarGridSpec(
            num_scalar_prefetch=1,
            grid=(pairs,),
            in_specs=in_specs,
            out_specs=[
                pl.BlockSpec((rows, PAIR), by_pair),
                pl.BlockSpec((rows, 2 * PAIR), by_pair),
            ],
            scratch_shapes=[
                pltpu.VMEM((2, rows, PAIR), bf16),
                pltpu.VMEM((2, rows, PAIR), f32),
            ],
        ),
        out_shape=[
            jax.ShapeDtypeStruct((rows, width), bf16),
            jax.ShapeDtypeStruct((rows, 2 * width), bf16),
        ],
        compiler_params=pltpu.CompilerParams(vmem_limit_bytes=VMEM_BYTES),
        cost_estimate=NO_COST,
    )(flags, *operands)


def backward_kernel(
    flags, full_ref, grad_ref, out_ref, aq_ref, k_ref, v_ref, ak_ref,
    dq_ref, dkv_ref, bias_ref, grads, dq_total,
):
    rows = grad_ref.shape[0]
    lane = lane_index()
    half = lane < 64
    mine = (half, jnp.logical_not(half))
    base = (lane - 64, lane)
    both = grad_ref[...]
    row_total = head_sums(both.astype(f32) * out_ref[...].astype(f32), half_ones(False))
    high, low = split_two(row_total)
    zero = jnp.zeros_like(high)
    for h in range(2):
        extra = jnp.where(base[h] == 0, -high, jnp.where(base[h] == 1, -low, zero))
        grads[h] = jnp.where(mine[h], both, extra)
        dq_total[h] = jnp.zeros_like(dq_total[h])
    for b in range(k_ref.shape[0] // KEY_ROWS):
        at = slice(b * KEY_ROWS, (b + 1) * KEY_ROWS)

        @pl.when(flags[b] != 0)
        def _():
            keys, values, columns = k_ref[at, :], v_ref[at, :], ak_ref[at, :]
            ones = jnp.ones_like(values)
            dks, dvs = [], []
            for h in range(2):
                keys2 = jnp.where(mine[h], keys, columns)
                pick = (base[h] >= 0) & (base[h] < 2)
                values2 = jnp.where(mine[h], values, jnp.where(pick, ones, jnp.zeros_like(ones)))
                full = full_ref[:, h * PAIR : (h + 1) * PAIR]
                probs = jnp.exp(dot(keys2, full, NT))
                score_low = (probs * dot(values2, grads[h], NT)).astype(bf16)
                dks.append(dot(score_low, full))
                dvs.append(dot(probs.astype(bf16), grads[h]))
                dq_total[h] += dot(keys2, score_low, TN)
            dkv_ref[0, at, :] = jnp.where(half, dks[0], dks[1]).astype(bf16)
            dkv_ref[1, at, :] = jnp.where(half, dvs[0], dvs[1]).astype(bf16)

        @pl.when(flags[b] == 0)
        def _():
            dkv_ref[:, at, :] = jnp.zeros((2, KEY_ROWS, PAIR), bf16)

    dq = [dq_total[h].T for h in range(2)]
    dq_ref[...] = jnp.where(half, dq[0], dq[1]) * 0.125
    variates = aq_ref[...].astype(f32)
    for h in range(2):
        pick = (base[h] >= 0) & (base[h] < 4)
        bias_ref[0, h : h + 1, :] = jnp.sum(
            jnp.where(pick, dq[h] * variates, 0.0), axis=0, keepdims=True
        )


def attend_back(chunk, flags, full, grad, out, query_columns, keys, values, key_columns):
    rows, width = grad.shape
    pairs = width // PAIR // CHUNKS
    width = width // CHUNKS
    key_rows = keys.shape[0]
    by_pair = lambda p, f: (0, p)
    from_pair = lambda p, f: (0, chunk * pairs + p)
    whole = lambda p, f: (0, 0)
    return pl.pallas_call(
        backward_kernel,
        grid_spec=pltpu.PrefetchScalarGridSpec(
            num_scalar_prefetch=1,
            grid=(pairs,),
            in_specs=[
                pl.BlockSpec((rows, 2 * PAIR), from_pair),
                pl.BlockSpec((rows, PAIR), from_pair),
                pl.BlockSpec((rows, PAIR), from_pair),
                pl.BlockSpec((rows, PAIR), whole),
                pl.BlockSpec((key_rows, PAIR), from_pair),
                pl.BlockSpec((key_rows, PAIR), from_pair),
                pl.BlockSpec((key_rows, PAIR), whole),
            ],
            out_specs=[
                pl.BlockSpec((rows, PAIR), by_pair),
                pl.BlockSpec((2, key_rows, PAIR), lambda p, f: (0, 0, p)),
                pl.BlockSpec((1, 2, PAIR), lambda p, f: (p, 0, 0)),
            ],
            scratch_shapes=[
                pltpu.VMEM((2, rows, PAIR), bf16),
                pltpu.VMEM((2, PAIR, rows), f32),
            ],
        ),
        out_shape=[
            jax.ShapeDtypeStruct((rows, width), f32),
            jax.ShapeDtypeStruct((2, key_rows, width), bf16),
            jax.ShapeDtypeStruct((pairs, 2, PAIR), f32),
        ],
        compiler_params=pltpu.CompilerParams(vmem_limit_bytes=VMEM_BYTES),
        cost_estimate=NO_COST,
    )(flags, full, grad, out, query_columns, keys, values, key_columns)


def slot_columns(segment, variates):
    column = jnp.arange(PAIR, dtype=jnp.int32)[None, :] % 64
    same_var = (column < 8) & (variates[:, None] == column % 4)
    in_seg = (column >= 8) & (column < 11)
    same_seg = segment[:, None] == column - 8
    three = (column >= 11) & (column < 14)
    query = jnp.where(in_seg & jnp.logical_not(same_seg), NEG_FILL, same_var.astype(f32))
    key = (same_var | (in_seg & same_seg) | three).astype(f32)
    return query.astype(bf16), key.astype(bf16)


def bias_columns(head_bias):
    delta = head_bias[:, 0] - head_bias[:, 1]
    high, low = split_two(delta)
    heads = delta.shape[0]
    row = jnp.concatenate(
        [
            jnp.broadcast_to(high[:, None], (heads, 4)),
            jnp.broadcast_to(low[:, None], (heads, 4)),
            jnp.ones((heads, 3), bf16),
            jnp.zeros((heads, 53), bf16),
        ],
        1,
    )
    return jnp.concatenate([row, row], 1).reshape(heads // 2, 2, PAIR)


def arrange_rows(places, spot, left_ref, turned, arranged):
    shard = left_ref.shape[1] // places
    turned[...] = left_ref[...].T
    for i in range(places):
        at = pl.multiple_of(spot[2 + i] * shard, shard)
        arranged[i * shard : (i + 1) * shard, :] = turned[pl.ds(at, shard), :]


def ffn_kernel(
    places, first, spot, nf_ref, seed_ref, start_ref, nfstart_ref, wg_ref, wu_ref, wd_ref,
    branch_ref, nfgrad_ref, down_far, down_cross, down_own, gate_far, gate_cross, gate_own,
    turned, arranged, branch,
):
    step = pl.program_id(0)
    rows, width = nf_ref.shape
    shard = width // places
    chunk = wg_ref.shape[1]

    @pl.when(step == 0)
    def _():
        arrange_rows(places, spot, nf_ref, turned, arranged)
        branch[...] = start_ref[...]
        nfgrad_ref[...] = jnp.zeros_like(nfgrad_ref) if first else nfstart_ref[...]

    wg, wu = wg_ref[...], wu_ref[...]
    wd = jnp.concatenate(
        [
            wd_ref[i * shard : (i + 1) * shard, k * width : (k + 1) * width]
            for i in range(2)
            for k in range(chunk // 2 // shard)
        ],
        axis=0,
    )
    hiddens, gates, ups = [], [], []
    part_rows = min(256, rows)
    for i in range(rows // part_rows):
        at = slice(i * part_rows, (i + 1) * part_rows)
        nf = nf_ref[at, :]
        g, u = dot(nf, wg), dot(nf, wu)
        hidden_grad = dot(seed_ref[at, :], wd, NT)
        sg = 1.0 / (1.0 + jnp.exp(-g))
        silu = g * sg
        hidden = (silu * u).astype(bf16)
        gate = (hidden_grad * u * sg * (1.0 + g * (1.0 - sg))).astype(bf16)
        up = (hidden_grad * silu).astype(bf16)
        branch[at, :] += dot(hidden, wd)
        nfgrad_ref[at, :] += dot(gate, wg, NT) + dot(up, wu, NT)
        hiddens.append(hidden)
        gates.append(gate)
        ups.append(up)
    hidden = jnp.concatenate(hiddens, axis=0)
    gate = jnp.concatenate(gates, axis=0)
    up = jnp.concatenate(ups, axis=0)
    down = dot(hidden, seed_ref[...], TN).astype(bf16)
    lower, upper = down[: chunk // 2, :], down[chunk // 2 :, :]
    on_upper = spot[0] == 1
    far = jnp.where(on_upper, lower, upper)
    near = jnp.where(on_upper, upper, lower)
    folds = [slice(k * shard, (k + 1) * shard) for k in range(chunk // 2 // shard)]
    for k, at in enumerate(folds):
        down_far[k] = far[at, :]

    @pl.when(step % 2 != spot[1])
    def _():
        for k, at in enumerate(folds):
            down_cross[k] = near[at, :]

    @pl.when(step % 2 == spot[1])
    def _():
        for k, at in enumerate(folds):
            down_own[k] = near[at, :]

    half = width // 2
    for part, grad in enumerate((gate, up)):
        gate_far[part, 0] = dot(arranged[:half, :], grad).astype(bf16)
        gate_cross[part, 0] = dot(arranged[half : half + half // 2, :], grad).astype(bf16)
        gate_own[part, 0] = dot(arranged[half + half // 2 :, :], grad).astype(bf16)

    @pl.when(step == pl.num_programs(0) - 1)
    def _():
        branch_ref[...] = branch[...].astype(branch_ref.dtype)


def feed_forward(spot, normed, seed, start, nfstart, weights):
    rows, width = normed.shape
    places = spot.shape[0] - 2
    groups = places // 4
    first = nfstart is None
    hidden = weights.shape[1] // 3
    chunk = 2 * hidden // places
    steps = places // 2
    whole = lambda t, o: (0, 0)
    once = pl.Buffered(1)
    shard = width // places
    folds = chunk // 2 // shard
    spans = hidden // width
    per_span = steps // spans
    by_cols = lambda t, o: (0, t // per_span, 0, t % per_span)
    return pl.pallas_call(
        functools.partial(ffn_kernel, places, first),
        grid_spec=pltpu.PrefetchScalarGridSpec(
            num_scalar_prefetch=1,
            grid=(steps,),
            in_specs=[
                pl.BlockSpec((rows, width), whole, pipeline_mode=once),
                pl.BlockSpec((rows, width), whole, pipeline_mode=once),
                pl.BlockSpec((rows, width), whole, pipeline_mode=once),
                pl.BlockSpec((8, 128) if first else (rows, width), whole, pipeline_mode=once),
                pl.BlockSpec((width, chunk), lambda t, o: (0, t)),
                pl.BlockSpec((width, chunk), lambda t, o: (0, steps + t)),
                pl.BlockSpec((2 * width // places, hidden), lambda t, o: (t, 2)),
            ],
            out_specs=[
                pl.BlockSpec((rows, width), whole),
                pl.BlockSpec((rows, width), whole),
                pl.BlockSpec(
                    (folds, shard, width),
                    lambda t, o: (0, jnp.where(t % 2 == o[1], groups, 0) + t // 2, 0),
                ),
                pl.BlockSpec((folds, shard, width), lambda t, o: (0, t // 2, 0)),
                pl.BlockSpec((folds, shard, width), lambda t, o: (0, t // 2, 0)),
                pl.BlockSpec((2, 1, width // 2, chunk), by_cols),
                pl.BlockSpec((2, 1, width // 4, chunk), by_cols),
                pl.BlockSpec((2, 1, width // 4, chunk), by_cols),
            ],
            scratch_shapes=[
                pltpu.VMEM((width, rows), bf16),
                pltpu.VMEM((width, rows), bf16),
                pltpu.VMEM((rows, width), f32),
            ],
        ),
        out_shape=[
            jax.ShapeDtypeStruct((rows, width), f32 if first else bf16),
            jax.ShapeDtypeStruct((rows, width), f32),
            jax.ShapeDtypeStruct((folds, width // 2, width), bf16),
            jax.ShapeDtypeStruct((folds, width // 4, width), bf16),
            jax.ShapeDtypeStruct((folds, width // 4, width), bf16),
            jax.ShapeDtypeStruct((2, spans, width // 2, width), bf16),
            jax.ShapeDtypeStruct((2, spans, width // 4, width), bf16),
            jax.ShapeDtypeStruct((2, spans, width // 4, width), bf16),
        ],
        compiler_params=pltpu.CompilerParams(vmem_limit_bytes=56 * 2**20),
        cost_estimate=NO_COST,
    )(spot, normed, seed, start, start if first else nfstart, weights, weights, weights)


def outer_kernel(places, spot, left_ref, right_ref, far_ref, cross_ref, own_ref, turned, arranged):
    width = left_ref.shape[1]

    @pl.when(pl.program_id(0) == 0)
    def _():
        arrange_rows(places, spot, left_ref, turned, arranged)

    right = right_ref[...]
    half = width // 2
    far_ref[0] = dot(arranged[:half, :], right).astype(bf16)
    cross_ref[0] = dot(arranged[half : half + half // 2, :], right).astype(bf16)
    own_ref[0] = dot(arranged[half + half // 2 :, :], right).astype(bf16)


def outer(spot, left, right, block):
    rows, width = left.shape
    columns = right.shape[1]
    places = spot.shape[0] - 2
    by_cols = lambda t, o: (0, t)
    one_block = lambda t, o: (t, 0, 0)
    return pl.pallas_call(
        functools.partial(outer_kernel, places),
        grid_spec=pltpu.PrefetchScalarGridSpec(
            num_scalar_prefetch=1,
            grid=(columns // block,),
            in_specs=[
                pl.BlockSpec((rows, width), lambda t, o: (0, 0)),
                pl.BlockSpec((rows, block), by_cols),
            ],
            out_specs=[
                pl.BlockSpec((1, width // 2, block), one_block),
                pl.BlockSpec((1, width // 4, block), one_block),
                pl.BlockSpec((1, width // 4, block), one_block),
            ],
            scratch_shapes=[pltpu.VMEM((width, rows), bf16), pltpu.VMEM((width, rows), bf16)],
        ),
        out_shape=[
            jax.ShapeDtypeStruct((columns // block, width // 2, block), bf16),
            jax.ShapeDtypeStruct((columns // block, width // 4, block), bf16),
            jax.ShapeDtypeStruct((columns // block, width // 4, block), bf16),
        ],
        compiler_params=pltpu.CompilerParams(vmem_limit_bytes=VMEM_BYTES),
        cost_estimate=NO_COST,
    )(spot, left, right)


def rms_forward(values, gain_vec):
    inv_rms = lax.rsqrt(jnp.mean(values * values, axis=-1, keepdims=True) + EPSILON)
    return (values * inv_rms * gain_vec, inv_rms)


def rms_backward(values, inv_rms, gain_vec, upstream):
    weighted = upstream * gain_vec
    inner_sum = jnp.mean(weighted * values, axis=-1, keepdims=True)
    value_grad = inv_rms * weighted - values * inv_rms * inv_rms * inv_rms * inner_sum
    return (value_grad, upstream * values * inv_rms)


def shift_by(values, count, step):
    return lax.ppermute(values, "seq", [(i, (i + step) % count) for i in range(count)])


def cross_core(values, places):
    return lax.ppermute(values, "dp", [(i, i ^ 1) for i in range(places)])


def cross_x(values, places):
    return lax.ppermute(values, "dp", [(i, i ^ 2) for i in range(places)])


def core_sum(pieces, places):
    crossed, terms = [], []
    for far, cross, own in pieces:
        quarter = own.shape[1]
        far = cross_core(far, places)
        crossed.append(cross + far[:, :quarter])
        terms.append([own, far[:, quarter:]])
    return jnp.concatenate(crossed, axis=0), terms


def add_received(terms, received):
    start, longer = 0, []
    for held in terms:
        count = held[0].shape[0]
        longer.append(held + [received[start : start + count]])
        start += count
    return longer


def total_of(terms):
    return jnp.concatenate([sum(term.astype(f32) for term in held) for held in terms], axis=0).astype(bf16)


def halve(terms, step, places):
    mine = lax.axis_index("dp") // 4 // 2**step % 2

    def cut(value, which):
        blocks, rows, columns = value.shape
        left = places // 4 // 2**step
        value = value.reshape(blocks, left // 2, 2, rows // left, columns)
        value = lax.dynamic_index_in_dim(value, which, 2, keepdims=False)
        return value.reshape(blocks, rows // 2, columns)

    sent = total_of([[cut(term, 1 - mine) for term in held] for held in terms])
    return sent, [[cut(term, mine) for term in held] for held in terms]


def cross_z(values, step, places):
    return lax.ppermute(values, "dp", [(i, i ^ (4 * 2**step)) for i in range(places)])


def sum_seq(values, count):
    if count == 2:
        return values.astype(f32) + shift_by(values, count, 1).astype(f32)
    return lax.psum(values.astype(f32), "seq")


def after(value, *before):
    return lax.optimization_barrier((value, before))[0]


def sum_small(values, places, seq_count):
    step = 1
    while step < places:
        values = values + lax.ppermute(values, "dp", [(i, i ^ step) for i in range(places)])
        step *= 2
    if seq_count == 2:
        return values + shift_by(values, 2, 1)
    return lax.psum(values, "seq")


def body(
    tokens, doc_lengths, variate_ids, time_ids, in_proj, out_proj, gate_up, down_proj,
    attn_gain, ffn_gain, query_gain, key_gain, head_bias, cotangent,
):
    seq_count = lax.axis_size("seq")
    seq_rank = lax.axis_index("seq")
    local_rows, width = tokens.shape
    pack_rows = local_rows * seq_count
    head_dim = query_gain.shape[0]
    places = lax.axis_size("dp")
    place = lax.axis_index("dp")
    core, across = place % 2, place // 2 % 2
    groups = places // 4
    spot = jnp.stack(
        [core, across]
        + [
            group * 4 + (across + 1 - near_x) % 2 * 2 + (core + 1 - near_core) % 2
            for near_core in range(2)
            for near_x in range(2)
            for group in range(groups)
        ]
    ).astype(jnp.int32)

    gains = jnp.stack([attn_gain, ffn_gain], axis=1)
    gather = lambda w: lax.all_gather(w, "dp", axis=0, tiled=True)
    in_chunks = in_proj.reshape(-1, 3, CHUNKS, width // CHUNKS).transpose(0, 2, 1, 3)
    in_chunks = in_chunks.reshape(in_proj.shape)
    first_shard = jnp.concatenate(
        [in_chunks, out_proj, jnp.pad(gains, ((0, 0), (0, PAIR - 2)))], axis=1
    )
    if places == 16 and seq_count == 2:
        wide, *there = gather_first(first_shard, tokens, time_ids.reshape(-1, PAIR), places)
        slots = [(tokens, time_ids), (there[0], there[1].reshape(-1))]
    else:
        wide = gather(first_shard)
        slots = [(tokens, time_ids)]
        for step in range(1, seq_count):
            slots.append(tuple(shift_by(array, seq_count, -step) for array in slots[0]))
    out_full = wide[:, 3 * width : 4 * width]
    attn_gain_f = wide[:, 4 * width].astype(f32)[None, :]
    ffn_gain_f = wide[:, 4 * width + 1].astype(f32)[None, :]
    shard = in_proj.shape[0]
    hidden_part = down_proj.shape[0] // 2
    columns = gate_up.reshape(shard, 2, places, 2, hidden_part)
    folds = down_proj.reshape(2, hidden_part // shard, shard, width)
    ffn_weights = []
    for part in range(2):
        piece = jnp.concatenate(
            [columns[:, 0, :, part].reshape(shard, -1), columns[:, 1, :, part].reshape(shard, -1)]
            + [folds[part, k] for k in range(hidden_part // shard)],
            axis=1,
        )
        ffn_weights.append(piece)
    ffn_weights[0] = gather(after(ffn_weights[0], wide))

    positions = jnp.arange(pack_rows, dtype=jnp.int32)
    first_end = doc_lengths[0, 0]
    second_end = first_end + doc_lengths[0, 1]
    segment = (positions >= first_end).astype(jnp.int32) + (positions >= second_end).astype(jnp.int32)
    query_columns, key_columns = slot_columns(segment, variate_ids[0])
    coefficients = bias_columns(head_bias)
    start = seq_rank * local_rows
    query_columns = lax.dynamic_slice_in_dim(query_columns, start, local_rows)
    local_segment = lax.dynamic_slice_in_dim(segment, start, local_rows)
    valid_rows = (local_segment < 2).astype(f32)
    source_columns, source_flags = [], []
    for step in range(seq_count):
        begin = ((seq_rank + step) % seq_count) * local_rows
        source_columns.append(lax.dynamic_slice_in_dim(key_columns, begin, local_rows))
        there = lax.dynamic_slice_in_dim(segment, begin, local_rows).reshape(-1, KEY_ROWS)
        source_flags.append(
            ((there[:, 0] <= local_segment[-1]) & (there[:, -1] >= local_segment[0])).astype(jnp.int32)
        )

    half_dim = head_dim // 2
    frequency = jnp.exp(jnp.arange(half_dim, dtype=f32) * (-math.log(ROPE_BASE) / half_dim))
    qgain = jnp.tile(query_gain, 2)[None, :]
    kgain = jnp.tile(key_gain, 2)[None, :]

    def rope_tables(times):
        angles = times.astype(f32)[:, None] * jnp.tile(frequency, 4)[None, :]
        sign = jnp.where(jnp.arange(PAIR) % head_dim < half_dim, -1.0, 1.0)
        return jnp.cos(angles), jnp.sin(angles) * sign[None, :]

    tables = [rope_tables(times) for _, times in slots]
    seed_grad = cotangent.astype(f32) * valid_rows[:, None]
    seed_low = seed_grad.astype(bf16)
    keyed = []
    for step, (there_tokens, _) in enumerate(slots):
        keys, values, *own = project(
            there_tokens, attn_gain_f, wide, *tables[step], qgain, kgain, step == 0
        )
        keyed.append((keys, values, source_columns[step]))
        if step == 0:
            cosine, sine = tables[0]
            queries, raw, normed_low = own
            ffn_weights[1] = gather(after(ffn_weights[1], queries))
    attended, full_query = attend(
        jnp.concatenate(source_flags), queries, query_columns, coefficients, keyed
    )

    inputs_f = tokens.astype(f32)
    residual = inputs_f + dot(attended, out_full)
    normed_ffn, ffn_scale = rms_forward(residual, ffn_gain_f)
    normed_ffn_low = normed_ffn.astype(bf16)
    def ffn_pieces(arrays):
        gates = [array.reshape(-1, *array.shape[2:]) for array in arrays[3:]]
        return [gates, arrays[:3]]

    branch, normed_ffn_grad, *pieces = feed_forward(
        spot, normed_ffn_low, seed_low, residual, None, ffn_weights[0]
    )
    crossed, first_terms = core_sum(ffn_pieces(pieces), places)
    layer_out, normed_ffn_grad, *pieces = feed_forward(
        spot, after(normed_ffn_low, crossed), seed_low, branch, normed_ffn_grad, ffn_weights[1]
    )
    across = cross_x(crossed, places)
    normed_ffn_grad = after(normed_ffn_grad, across)
    first_terms = add_received(first_terms, across)
    resid_norm_grad, ffn_gain_terms = rms_backward(residual, ffn_scale, ffn_gain_f, normed_ffn_grad)
    residual_grad = seed_grad + resid_norm_grad
    mixed_low = residual_grad.astype(bf16)
    attended_grad = dot(mixed_low, out_full, NT).astype(bf16)

    attended_grad = dot(mixed_low, out_full, NT).astype(bf16)
    crossed, second_terms = core_sum(
        ffn_pieces(pieces) + [outer(spot, attended, mixed_low, width)], places
    )
    steps = (places // 4).bit_length() - 1
    sent, first_terms = halve(first_terms, 0, places)
    attended_grad = after(attended_grad, crossed, sent)

    remote = list(range(1, seq_count))
    dqs = [[] for _ in range(CHUNKS)]
    dkvs = [[] for _ in range(CHUNKS)]
    biases = [0.0] * CHUNKS

    def back(chunk, sources, grad):
        for step in sources:
            dq, dkv, bias = attend_back(
                chunk, source_flags[step], full_query, grad, attended, query_columns, *keyed[step]
            )
            grad = after(grad, dkv)
            dqs[chunk].append(dq)
            dkvs[chunk].append(shift_by(dkv, seq_count, step) if step else dkv)
            biases[chunk] = biases[chunk] + bias
        return grad

    def merge(chunk):
        return merge_grads(chunk, dqs[chunk], dkvs[chunk], raw, cosine, sine, qgain, kgain)

    def chunk_weights(chunk):
        return wide[:, chunk * 3 * width // CHUNKS : (chunk + 1) * 3 * width // CHUNKS]

    def finish_line(terms, sent, first):
        for step in range(first, steps):
            terms = add_received(terms, cross_z(sent, step, places))
            if step + 1 < steps:
                sent, terms = halve(terms, step + 1, places)
        return total_of(terms)

    second_across = cross_x(crossed, places)
    first_received = cross_z(sent, 0, places)
    grad = back(0, remote, attended_grad)
    grad = back(1, remote, after(grad, first_received))
    first_terms = add_received(first_terms, first_received)
    sent, first_terms = halve(first_terms, 1, places)
    grad = after(grad, sent)
    first_received = cross_z(sent, 1, places)
    grad = back(0, [0], grad)

    second_across = after(second_across, grad)
    second_terms = add_received(second_terms, second_across)
    sent, second_terms = halve(second_terms, 0, places)
    second_received = cross_z(sent, 0, places)
    dqs[0][0] = after(dqs[0][0], grad, sent)
    merged_0, gains_0 = merge(0)
    crossed, in_terms_0 = core_sum([outer(spot, normed_low, merged_0, width // CHUNKS)], places)
    normed_grad_0 = dot(merged_0, chunk_weights(0), NT)
    grad = after(grad, crossed, normed_grad_0)
    in_across_0 = cross_x(crossed, places)
    grad = back(1, [0], grad)
    dqs[1][0] = after(dqs[1][0], grad, in_across_0, second_received, first_received)

    merged_1, gains_1 = merge(1)
    crossed, in_terms_1 = core_sum([outer(spot, normed_low, merged_1, width // CHUNKS)], places)
    in_terms_1 = add_received(in_terms_1, cross_x(crossed, places))
    normed_grad = normed_grad_0 + dot(after(merged_1, crossed), chunk_weights(1), NT)
    first_terms = add_received(first_terms, first_received)
    first_total = finish_line(*halve(first_terms, 2, places)[::-1], 2) if steps > 2 else total_of(first_terms)
    second_terms = add_received(second_terms, second_received)
    sent, second_terms = halve(second_terms, 1, places)
    second_total = finish_line(second_terms, sent, 1)
    sent, in_terms_0 = halve(add_received(in_terms_0, in_across_0), 0, places)
    in_total_0 = finish_line(in_terms_0, sent, 0)
    sent, in_terms_1 = halve(in_terms_1, 0, places)
    in_total_1 = finish_line(in_terms_1, sent, 0)
    first_sum = sum_seq(first_total, seq_count)
    second_sum = sum_seq(second_total, seq_count)
    in_sum = jnp.concatenate(
        [sum_seq(in_total_0, seq_count), sum_seq(in_total_1, seq_count)], axis=2
    )
    norm_scale = lax.rsqrt(jnp.mean(inputs_f * inputs_f, axis=-1, keepdims=True) + EPSILON)
    input_norm_grad, attn_gain_terms = rms_backward(inputs_f, norm_scale, attn_gain_f, normed_grad)
    input_grad = residual_grad + input_norm_grad

    same_bias = jnp.concatenate([jnp.sum(bias, axis=-1).reshape(-1) for bias in biases])
    heads = same_bias.shape[0]
    head_gains = sum(jnp.sum(part[:2].reshape(2, -1, head_dim), axis=1) for part in (gains_0, gains_1))
    small = sum_small(
        jnp.concatenate(
            [
                jnp.sum(attn_gain_terms, axis=0),
                jnp.sum(ffn_gain_terms, axis=0),
                head_gains[0],
                head_gains[1],
                same_bias,
            ]
        ),
        places,
        seq_count,
    )
    in_proj_grad = in_sum.transpose(1, 0, 2).reshape(in_proj.shape)
    spans = places * hidden_part // width
    gates = 2 * spans
    down_grad = jnp.concatenate(
        [part[gates : gates + hidden_part // shard].reshape(-1, width) for part in (first_sum, second_sum)]
    )
    gate_up_grad = jnp.stack(
        [
            part[:gates].reshape(2, spans, shard, -1, hidden_part).transpose(2, 0, 1, 3, 4)
            for part in (first_sum, second_sum)
        ],
        axis=4,
    ).reshape(gate_up.shape)
    gain_rows = attn_gain.shape[0]
    here = place * gain_rows
    tail = small[2 * width :]
    same_bias = tail[2 * head_dim : 2 * head_dim + heads]
    return (
        layer_out,
        input_grad,
        in_proj_grad,
        second_sum[-1],
        gate_up_grad,
        down_grad,
        lax.dynamic_slice_in_dim(small, here, gain_rows),
        lax.dynamic_slice_in_dim(small, width + here, gain_rows),
        tail[:head_dim],
        tail[head_dim : 2 * head_dim],
        jnp.stack([same_bias, -same_bias], axis=1),
    )


def solution(mesh):
    in_specs = (
        P(("dp", "seq"), None),
        P("dp", None),
        P("dp", None),
        P(("dp", "seq")),
        P("dp", None),
        P("dp", None),
        P("dp", None),
        P("dp", None),
        P("dp"),
        P("dp"),
        P(),
        P(),
        P(),
        P(("dp", "seq"), None),
    )
    out_specs = (
        P(("dp", "seq"), None),
        P(("dp", "seq"), None),
        P("dp", None),
        P("dp", None),
        P("dp", None),
        P("dp", None),
        P("dp"),
        P("dp"),
        P(),
        P(),
        P(),
    )
    return jax.shard_map(body, mesh=mesh, in_specs=in_specs, out_specs=out_specs, check_vma=False)
```

time: 966 us -> 765 us (0.79)
  waiting for transfers between devices: 432 us -> 117 us
  Pallas kernels: 210 us -> 403 us
  matrix products: 181 us -> 25.3 us
  other arithmetic: 27.9 us -> 86.5 us
  starting transfers between devices: 9.75 us -> 48.5 us
  blocking collectives: 38.2 us -> 0 us
  local copies, waits for them, and re-layouts: 42.4 us -> 60.9 us
    reduce_scatter x4 -> x0, waiting for transfers between devices: 239 us -> none  [body(): lax.psum_scatter(g, 'dp', scatter_dimension=0, tiled=True)]
    pallas_call x1 -> x8, Pallas kernels: 15.1 us -> 207 us  [the longest x2 113 us: feed_forward(): pl.pallas_call(functools.partial(ffn_kernel, places, first), grid_spec=pl...]
    dot_general x11 -> x4, matrix products: 181 us -> 25.3 us  [dot(): return lax.dot_general(left, right, dims, preferred_element_type=f32)]
    ppermute x0 -> x23, waiting for transfers between devices: none -> 95 us  [the longest x8 60.4 us: cross_z(): lax.ppermute(values, 'dp', [(i, i ^ 4 * 2 ** step) for i in range(places)])]
    ppermute x8 -> x7, waiting for transfers between devices: 115 us -> 22.4 us  [shift_by(): lax.ppermute(values, 'seq', [(i, (i + step) % count) for i in range(count)])]
    all_gather x4 -> x2, waiting for transfers between devices: 76.1 us -> 0.01 us  [body(): gather = lambda w: lax.all_gather(w, 'dp', axis=0, tiled=True)]
    psum x1 -> x0, blocking collectives: 38.2 us -> none  [body(): lax.psum(jnp.concatenate([jnp.sum(attn_gain_terms, axis=0), jnp.sum(ffn_g...]
    ppermute x0 -> x23, starting transfers between devices: none -> 30 us  [the longest x8 11.7 us: cross_z(): lax.ppermute(values, 'dp', [(i, i ^ 4 * 2 ** step) for i in range(places)])]
  transfers between devices with their start and end apart: 16 -> 32, of which waited for: 8 -> 11; matrix products, arithmetic and copies ran while one was open for 18% -> 17% of each run, Pallas kernels for 16% -> 43%
where the time goes in v2:
time: 765 us; the launch traced here: 759 us
  Pallas kernels  403 us (53%)
  waiting for transfers between devices  117 us (15%)
  other arithmetic  86.5 us (11%)
  local copies, waits for them, and re-layouts  60.9 us (8%)
  starting transfers between devices  48.5 us (6%)
  matrix products  25.3 us (3%)
  between operations  17.1 us (2%)
    pallas_call x2, Pallas kernels, feed_forward(): pl.pallas_call(functools.partial(ffn_kernel, places, first), grid_spec=pl...  113 us
    pallas_call x4, Pallas kernels, attend_back(): pl.pallas_call(backward_kernel, grid_spec=pltpu.PrefetchScalarGridSpec(nu...  104 us
    ppermute x8, waiting for transfers between devices, cross_z(): lax.ppermute(values, 'dp', [(i, i ^ 4 * 2 ** step) for i in range(places)])  60.4 us
    pallas_call x1, Pallas kernels, gather_first(): pl.pallas_call(gather_kernel, in_specs=[anywhere] * 3, out_specs=[anywher...  57.4 us
    pallas_call x1, Pallas kernels, attend(): pl.pallas_call(functools.partial(forward_kernel, sources, min(512, rows))...  56.3 us
    pallas_call x2, Pallas kernels, project(): pl.pallas_call(qkv_kernel, grid=(rows // block,), in_specs=[pl.BlockSpec(...  35.5 us
    dot_general x4, matrix products, dot(): return lax.dot_general(left, right, dims, preferred_element_type=f32)  25.3 us
    unnamed x170, local copies, waits for them, and re-layouts  23.1 us
  transfers between devices with their start and end apart: 32, of which 11 were waited for; matrix products, arithmetic and copies ran while one was open for 17% of the time, Pallas kernels for 43%

profile of v2, /device:TPU:0, one launch (start us, length us, event | category | flops | bytes accessed | tf_op | source)
XLA Modules:
  0.0 758.6 jit_solution(1153126225562847671)
XLA Ops:
  18.7 57.4 %shard_map.221 = (bf16[1024,4224]{1,0:T(8,128)(2,1)}, bf16[1024,1024]{1,0:T(8,128)(2,1)}, s32[8,128]{1,0:T(8,128)}) custom-call(bf16[64,4224]{1,0:T(8,128)(2,1)} %fusion.22.shard_ref, bf16[1024,1024]{1,0:T(8,128)(2,1)} %tokens_ref.3, s32[8,128]{1,0:T(8,128)} %bitcast.361), custom_call_target="tpu_custom_call" | custom-call | flops 1 | bytes 1 | tf_op jit(solution)/shard_map/pallas_call | solution.py:158
  83.0 22.4 %shard_map.222 = (bf16[1024,1024]{1,0:T(8,128)(2,1)S(1)}, bf16[1024,1024]{1,0:T(8,128)(2,1)S(1)}, bf16[1024,1024]{1,0:T(8,128)(2,1)}, f32[1024,2048]{1,0:T(8,128)}, bf16[1024,1024]{1,0:T(8,128)(2,1)}) custom-call(bf16[1024,1024]{1,0:T(8,128)(2,1)} %tokens_ref.3, f32[1,1024]{1,0:T(1,128)S(1)} %bitcast.272, bf16[1024,4224]{1,0:T(8,128)(2,1)} %get-tuple-element.79.weight_ref, ...), custom_call_target="tpu_custom_call" | custom-call | flops 1 | bytes 1 | tf_op jit(solution)/shard_map/pallas_call | solution.py:224
  108.1 13.1 %shard_map.223 = (bf16[1024,1024]{1,0:T(8,128)(2,1)S(1)}, bf16[1024,1024]{1,0:T(8,128)(2,1)S(1)}) custom-call(bf16[1024,1024]{1,0:T(8,128)(2,1)} %get-tuple-element.83.tokens_ref, f32[1,1024]{1,0:T(1,128)S(1)} %bitcast.273, bf16[1024,4224]{1,0:T(8,128)(2,1)} %get-tuple-element.79.weight_ref, f32[1024,128]{1,0:T(8,128)S(1)} %get-tuple-element.193.cos_ref, ...), custom_call_target="tpu_custom_call" | custom-call | flops 1 | bytes 1 | tf_op jit(solution)/shard_map/pallas_call | solution.py:224
  132.7 56.3 %shard_map.224 = (bf16[1024,1024]{1,0:T(8,128)(2,1)S(1)}, bf16[1024,2048]{1,0:T(8,128)(2,1)}) custom-call(s32[8]{0:T(128)S(1)} %pad_add_fusion.flags, bf16[1024,1024]{1,0:T(8,128)(2,1)S(1)} %copy-done.17, bf16[1024,128]{1,0:T(8,128)(2,1)S(1)} %select_convert_fusion.aq_ref, bf16[8,2,128]{2,1,0:T(2,128)(2,1)S(1)} %bitcast.274, bf16[1024,1024]{1,0:T(8,128)(2,1)} %copy-done.1, ...), custom_call_target="tpu_custom_call" | custom-call | flops 1 | bytes 1 | tf_op jit(solution)/shard_map/pallas_call | solution.py:366
  199.1 56.5 %shard_map.225 = (f32[1024,1024]{1,0:T(8,128)}, f32[1024,1024]{1,0:T(8,128)}, bf16[2,512,1024]{2,1,0:T(8,128)(2,1)}, bf16[2,256,1024]{2,1,0:T(8,128)(2,1)}, bf16...) custom-call(s32[18]{0:T(128)} %stack.102.spot, ...), custom_call_target="tpu_custom_call" | custom-call | flops 1 | bytes 1 | tf_op jit(solution)/shard_map/pallas_call | solution.py:609
  255.6 7.1 collective-permute-start
  262.8 11.6 %collective-permute-done.1 = bf16[2,512,1024]{2,1,0:T(8,128)(2,1)S(1)} collective-permute-done((bf16[2,512,1024]{2,1,0:T(8,128)(2,1)}, bf16[2,512,1024]{2,1,0:T(8,128)(2,1)S(1)}, u32[]{:S(2)}, u32[]{:S(2)}) %collective-permute-start.1) | collective-permute-done | bytes 2097184 | tf_op jit(solution)/shard_map/ppermute | solution.py:720
  281.0 56.9 %shard_map.226 = (bf16[1024,1024]{1,0:T(8,128)(2,1)}, f32[1024,1024]{1,0:T(8,128)}, bf16[2,512,1024]{2,1,0:T(8,128)(2,1)}, bf16[2,256,1024]{2,1,0:T(8,128)(2,1)}...) custom-call(s32[18]{0:T(128)} %stack.102.spot, ...), custom_call_target="tpu_custom_call" | custom-call | flops 1 | bytes 1 | tf_op jit(solution)/shard_map/pallas_call | solution.py:609
  338.5 12.9 %collective-permute-done.2 = bf16[6,256,1024]{2,1,0:T(8,128)(2,1)} collective-permute-done((bf16[6,256,1024]{2,1,0:T(8,128)(2,1)}, bf16[6,256,1024]{2,1,0:T(8,128)(2,1)}, u32[]{:S(2)}, u32[]{:S(2)}) %collective-permute-start.2) | collective-permute-done | bytes 3145760 | tf_op jit(solution)/shard_map/ppermute | solution.py:724
  389.3 23.2 %shard_map.228 = (f32[1024,512]{1,0:T(8,128)S(1)}, bf16[2,1024,512]{2,1,0:T(8,128)(2,1)}, f32[4,2,128]{2,1,0:T(2,128)S(1)}) custom-call(s32[4]{0:T(128)S(1)} %get-tuple-element.209.flags, bf16[1024,2048]{1,0:T(8,128)(2,1)} %get-tuple-element.100.full_ref, bf16[1024,1024]{1,0:T(8,128)(2,1)} %convolution_convert_fusion.grad_ref, bf16[1024,1024]{1,0:T(8,128)(2,1)} %copy-done, ...), custom_call_target="tpu_custom_call" | custom-call | flops 1 | bytes 1 | tf_op jit(solution)/shard_map/pallas_call | solution.py:450
  413.9 7.8 %collective-permute-start.8 = (bf16[2,1024,512]{2,1,0:T(8,128)(2,1)}, bf16[2,1024,512]{2,1,0:T(8,128)(2,1)}, u32[]{:S(2)}, u32[]{:S(2)}) collective-permute-start(bf16[2,1024,512]{2,1,0:T(8,128)(2,1)} %get-tuple-element.111), channel_id=1, source_target_pairs={{0,1},{1,0},{2,3},{3,2},{4,5},{5,4},{6,7},{7,6},{8,9},{9,8},{10,11... | collective-permute-start | bytes 6291464 | tf_op jit(solution)/shard_map/ppermute | solution.py:716
  421.6 23.6 %shard_map.229 = (f32[1024,512]{1,0:T(8,128)S(1)}, bf16[2,1024,512]{2,1,0:T(8,128)(2,1)}, f32[4,2,128]{2,1,0:T(2,128)S(1)}) custom-call(s32[4]{0:T(128)S(1)} %get-tuple-element.209.flags, bf16[1024,2048]{1,0:T(8,128)(2,1)} %get-tuple-element.100.full_ref, bf16[1024,1024]{1,0:T(8,128)(2,1)} %convolution_convert_fusion.grad_ref, bf16[1024,1024]{1,0:T(8,128)(2,1)} %copy-done, ...), custom_call_target="tpu_custom_call" | custom-call | flops 1 | bytes 1 | tf_op jit(solution)/shard_map/pallas_call | solution.py:450
  452.6 28.5 %shard_map.230 = (f32[1024,512]{1,0:T(8,128)S(1)}, bf16[2,1024,512]{2,1,0:T(8,128)(2,1)S(1)}, f32[4,2,128]{2,1,0:T(2,128)S(1)}) custom-call(s32[4]{0:T(128)S(1)} %get-tuple-element.210.flags, bf16[1024,2048]{1,0:T(8,128)(2,1)} %get-tuple-element.100.full_ref, bf16[1024,1024]{1,0:T(8,128)(2,1)} %convolution_convert_fusion.grad_ref, ...), custom_call_target="tpu_custom_call" | custom-call | flops 1 | bytes 1 | tf_op jit(solution)/shard_map/pallas_call | solution.py:450
  491.8 8.7 %shard_map.231 = (bf16[1024,1536]{1,0:T(8,128)(2,1)}, f32[8,512]{1,0:T(8,128)S(1)}) custom-call(f32[1024,512]{1,0:T(8,128)S(1)} %copy-done.14, f32[1024,512]{1,0:T(8,128)S(1)} %get-tuple-element.124.refs_1_, bf16[2,1024,512]{2,1,0:T(8,128)(2,1)} %collective-permute-done.8.refs_2_, bf16[2,1024,512]{2,1,0:T(8,128)(2,1)} %copy-done.15, ...), custom_call_target="tpu_custom_call" | custom-call | flops 1 | bytes 1 | tf_op jit(solution)/shard_map/pallas_call | solution.py:279
  500.5 7.1 shard_map.232
  520.7 49.5 %collective-permute-done.12 = bf16[6,64,1024]{2,1,0:T(8,128)(2,1)} collective-permute-done((bf16[6,64,1024]{2,1,0:T(8,128)(2,1)}, bf16[6,64,1024]{2,1,0:T(8,128)(2,1)}, u32[]{:S(2)}, u32[]{:S(2)}) %collective-permute-start.12) | collective-permute-done | bytes 786464 | tf_op jit(solution)/shard_map/ppermute | solution.py:765
  599.2 7.0 fusion.12
  606.2 28.4 %shard_map.233 = (f32[1024,512]{1,0:T(8,128)S(1)}, bf16[2,1024,512]{2,1,0:T(8,128)(2,1)S(1)}, f32[4,2,128]{2,1,0:T(2,128)S(1)}) custom-call(s32[4]{0:T(128)S(1)} %get-tuple-element.210.flags, bf16[1024,2048]{1,0:T(8,128)(2,1)} %get-tuple-element.100.full_ref, bf16[1024,1024]{1,0:T(8,128)(2,1)} %convolution_convert_fusion.grad_ref, ...), custom_call_target="tpu_custom_call" | custom-call | flops 1 | bytes 1 | tf_op jit(solution)/shard_map/pallas_call | solution.py:450
  635.9 8.7 %shard_map.234 = (bf16[1024,1536]{1,0:T(8,128)(2,1)}, f32[8,512]{1,0:T(8,128)S(1)}) custom-call(f32[1024,512]{1,0:T(8,128)S(1)} %copy-done.12, f32[1024,512]{1,0:T(8,128)S(1)} %get-tuple-element.133.refs_1_, bf16[2,1024,512]{2,1,0:T(8,128)(2,1)} %collective-permute-done.13.refs_2_, bf16[2,1024,512]{2,1,0:T(8,128)(2,1)} %copy-done.16, ...), custom_call_target="tpu_custom_call" | custom-call | flops 1 | bytes 1 | tf_op jit(solution)/shard_map/pallas_call | solution.py:279
  644.6 6.9 shard_map.235
  667.5 17.9 %collective-permute-done.17 = bf16[3,64,512]{2,1,0:T(8,128)(2,1)S(1)} collective-permute-done((bf16[3,64,512]{2,1,0:T(8,128)(2,1)S(1)}, bf16[3,64,512]{2,1,0:T(8,128)(2,1)S(1)}, u32[]{:S(2)}, u32[]{:S(2)}) %collective-permute-start.17) | collective-permute-done | bytes 196640 | tf_op jit(solution)/shard_map/ppermute | solution.py:716
  691.4 8.2 %fusion.8 = (f32[1024]{0:T(1024)S(1)}, f32[1024]{0:T(1024)S(1)}, f32[1024,1024]{1,0:T(8,128)}) fusion(bf16[1024,1024]{1,0:T(8,128)(2,1)S(1)} %copy-done.30, f32[1024]{0:T(1024)S(1)} %add_rsqrt_fusion, f32[1024]{0:T(1024)S(1)} %get-tuple-element.148, f32[1024,1024]{1,0:T(8,128)} %fusion.12, bf16[1024,1536]{1,0:T(8,128)(2,1)S(1)} %copy-done.50, ...), kind=kOutput, calls=%fused_computation.13 | convolution fusion | flops 3229612032 | bytes 16793600 | tf_op jit(solution)/shard_map/dot_general | solution.py:27
  702.8 6.4 collective-permute-done.26
  736.3 7.1 collective-permute-done.20
  (370 shorter events, 208.3 us)
Async XLA Ops:
  7.2 191.9 %all-gather.3.cloned.1.call-start = ((), (), s32[]{:S(2)}) async-start(), calls=%async_computation | async-start | bytes 13369344 | tf_op jit(solution)/shard_map/all_gather | solution.py:812
  77.4 203.7 %all-gather.5.cloned.1.call-start = ((), (), s32[]{:S(2)}) async-start(), calls=%async_computation.1 | async-start | bytes 13369344 | tf_op jit(solution)/shard_map/all_gather | solution.py:812
  255.6 21.5 %collective-permute-start = (bf16[4,512,1024]{2,1,0:T(8,128)(2,1)}, bf16[4,512,1024]{2,1,0:T(8,128)(2,1)S(1)}, u32[]{:S(2)}, u32[]{:S(2)}) collective-permute-start(bf16[4,512,1024]{2,1,0:T(8,128)(2,1)} %bitcast.364), channel_id=1, source_target_pairs={{0,2},{2,0},{4,6},{6,4},{8,10},{10,8},{12,14},{14,12},{16,18},{18,... | collective-permute-start | bytes 12582920 | tf_op jit(solution)/shard_map/ppermute | solution.py:720
  262.8 11.7 %collective-permute-start.1 = (bf16[2,512,1024]{2,1,0:T(8,128)(2,1)}, bf16[2,512,1024]{2,1,0:T(8,128)(2,1)S(1)}, u32[]{:S(2)}, u32[]{:S(2)}) collective-permute-start(bf16[2,512,1024]{2,1,0:T(8,128)(2,1)} %get-tuple-element.92), channel_id=1, source_target_pairs={{0,2},{2,0},{4,6},{6,4},{8,10},{10,8},{12,14},{14,12},{16,18},{18,... | collective-permute-start | bytes 6291464 | tf_op jit(solution)/shard_map/ppermute | solution.py:720
  280.9 70.6 %collective-permute-start.2 = (bf16[6,256,1024]{2,1,0:T(8,128)(2,1)}, bf16[6,256,1024]{2,1,0:T(8,128)(2,1)}, u32[]{:S(2)}, u32[]{:S(2)}) collective-permute-start(bf16[6,256,1024]{2,1,0:T(8,128)(2,1)} %pad_maximum_fusion.1), channel_id=1, source_target_pairs={{0,4},{2,6},{4,0},{6,2},{8,12},{10,14},{12,8},{14,10},{16,20},{18,... | collective-permute-start | bytes 9437192 | tf_op jit(solution)/shard_map/ppermute | solution.py:724
  337.9 30.1 %collective-permute-start.3 = (bf16[4,512,1024]{2,1,0:T(8,128)(2,1)}, bf16[4,512,1024]{2,1,0:T(8,128)(2,1)}, u32[]{:S(2)}, u32[]{:S(2)}) collective-permute-start(bf16[4,512,1024]{2,1,0:T(8,128)(2,1)} %bitcast.363), channel_id=1, source_target_pairs={{0,2},{2,0},{4,6},{6,4},{8,10},{10,8},{12,14},{14,12},{16,18},{18,... | collective-permute-start | bytes 12582920 | tf_op jit(solution)/shard_map/ppermute | solution.py:720
  338.1 26.5 %collective-permute-start.4 = (bf16[2,512,1024]{2,1,0:T(8,128)(2,1)}, bf16[2,512,1024]{2,1,0:T(8,128)(2,1)S(1)}, u32[]{:S(2)}, u32[]{:S(2)}) collective-permute-start(bf16[2,512,1024]{2,1,0:T(8,128)(2,1)} %get-tuple-element.104), channel_id=1, source_target_pairs={{0,2},{2,0},{4,6},{6,4},{8,10},{10,8},{12,14},{14,12},{16,18},{18,... | collective-permute-start | bytes 6291464 | tf_op jit(solution)/shard_map/ppermute | solution.py:720
  374.7 106.4 %collective-permute-start.7 = (bf16[7,256,1024]{2,1,0:T(8,128)(2,1)}, bf16[7,256,1024]{2,1,0:T(8,128)(2,1)}, u32[]{:S(2)}, u32[]{:S(2)}) collective-permute-start(bf16[7,256,1024]{2,1,0:T(8,128)(2,1)} %pad_maximum_fusion), channel_id=1, source_target_pairs={{0,4},{2,6},{4,0},{6,2},{8,12},{10,14},{12,8},{14,10},{16,20},{18,... | collective-permute-start | bytes 11010056 | tf_op jit(solution)/shard_map/ppermute | solution.py:724
  383.1 38.5 %collective-permute-start.6 = (bf16[6,128,1024]{2,1,0:T(8,128)(2,1)}, bf16[6,128,1024]{2,1,0:T(8,128)(2,1)}, u32[]{:S(2)}, u32[]{:S(2)}) collective-permute-start(bf16[6,128,1024]{2,1,0:T(8,128)(2,1)} %pad_maximum_fusion.4), channel_id=1, source_target_pairs={{0,8},{2,10},{4,12},{6,14},{8,0},{10,2},{12,4},{14,6},{16,24},{18,... | collective-permute-start | bytes 4718600 | tf_op jit(solution)/shard_map/ppermute | solution.py:765
  413.9 77.2 %collective-permute-start.8 = (bf16[2,1024,512]{2,1,0:T(8,128)(2,1)}, bf16[2,1024,512]{2,1,0:T(8,128)(2,1)}, u32[]{:S(2)}, u32[]{:S(2)}) collective-permute-start(bf16[2,1024,512]{2,1,0:T(8,128)(2,1)} %get-tuple-element.111), channel_id=1, source_target_pairs={{0,1},{1,0},{2,3},{3,2},{4,5},{5,4},{6,7},{7,6},{8,9},{9,8},{10,11... | collective-permute-start | bytes 6291464 | tf_op jit(solution)/shard_map/ppermute | solution.py:716
  509.4 63.0 %collective-permute-start.9 = (bf16[3,512,512]{2,1,0:T(8,128)(2,1)}, bf16[3,512,512]{2,1,0:T(8,128)(2,1)}, u32[]{:S(2)}, u32[]{:S(2)}) collective-permute-start(bf16[3,512,512]{2,1,0:T(8,128)(2,1)} %get-tuple-element.130), channel_id=1, source_target_pairs={{0,2},{2,0},{4,6},{6,4},{8,10},{10,8},{12,14},{14,12},{16,18},{18,... | collective-permute-start | bytes 4718600 | tf_op jit(solution)/shard_map/ppermute | solution.py:720
  512.8 68.3 %collective-permute-start.11 = (bf16[7,128,1024]{2,1,0:T(8,128)(2,1)}, bf16[7,128,1024]{2,1,0:T(8,128)(2,1)}, u32[]{:S(2)}, u32[]{:S(2)}) collective-permute-start(bf16[7,128,1024]{2,1,0:T(8,128)(2,1)} %pad_maximum_fusion.3), channel_id=1, source_target_pairs={{0,8},{2,10},{4,12},{6,14},{8,0},{10,2},{12,4},{14,6},{16,24},{18,... | collective-permute-start | bytes 5505032 | tf_op jit(solution)/shard_map/ppermute | solution.py:765
  513.6 56.6 %collective-permute-start.12 = (bf16[6,64,1024]{2,1,0:T(8,128)(2,1)}, bf16[6,64,1024]{2,1,0:T(8,128)(2,1)}, u32[]{:S(2)}, u32[]{:S(2)}) collective-permute-start(bf16[6,64,1024]{2,1,0:T(8,128)(2,1)} %pad_maximum_fusion.10), channel_id=1, source_target_pairs={{0,16},{2,18},{4,20},{6,22},{8,24},{10,26},{12,28},{14,30},{16,0},... | collective-permute-start | bytes 2359304 | tf_op jit(solution)/shard_map/ppermute | solution.py:765
  517.7 118.2 %collective-permute-start.13 = (bf16[2,1024,512]{2,1,0:T(8,128)(2,1)}, bf16[2,1024,512]{2,1,0:T(8,128)(2,1)}, u32[]{:S(2)}, u32[]{:S(2)}) collective-permute-start(bf16[2,1024,512]{2,1,0:T(8,128)(2,1)} %get-tuple-element.114), channel_id=1, source_target_pairs={{0,1},{1,0},{2,3},{3,2},{4,5},{5,4},{6,7},{7,6},{8,9},{9,8},{10,11... | collective-permute-start | bytes 6291464 | tf_op jit(solution)/shard_map/ppermute | solution.py:716
  574.0 19.7 %collective-permute-start.10 = (bf16[3,256,512]{2,1,0:T(8,128)(2,1)S(1)}, bf16[3,256,512]{2,1,0:T(8,128)(2,1)S(1)}, u32[]{:S(2)}, u32[]{:S(2)}) collective-permute-start(bf16[3,256,512]{2,1,0:T(8,128)(2,1)S(1)} %get-tuple-element.170), channel_id=1, source_target_pairs={{0,4},{2,6},{4,0},{6,2},{8,12},{10,14},{12,8},{14,10},{16,20},{18,... | collective-permute-start | bytes 2359304 | tf_op jit(solution)/shard_map/ppermute | solution.py:724
  578.4 81.5 %collective-permute-start.24 = (bf16[6,64,1024]{2,1,0:T(8,128)(2,1)}, bf16[6,64,1024]{2,1,0:T(8,128)(2,1)}, u32[]{:S(2)}, u32[]{:S(2)}) collective-permute-start(bf16[6,64,1024]{2,1,0:T(8,128)(2,1)} %pad_maximum_fusion.11), channel_id=1, source_target_pairs={{0,1},{1,0},{2,3},{3,2},{4,5},{5,4},{6,7},{7,6},{8,9},{9,8},{10,11... | collective-permute-start | bytes 2359304 | tf_op jit(solution)/shard_map/ppermute | solution.py:716
  590.2 63.1 %collective-permute-start.22 = (bf16[7,64,1024]{2,1,0:T(8,128)(2,1)}, bf16[7,64,1024]{2,1,0:T(8,128)(2,1)}, u32[]{:S(2)}, u32[]{:S(2)}) collective-permute-start(bf16[7,64,1024]{2,1,0:T(8,128)(2,1)} %pad_maximum_fusion.6), channel_id=1, source_target_pairs={{0,16},{2,18},{4,20},{6,22},{8,24},{10,26},{12,28},{14,30},{16,0},... | collective-permute-start | bytes 2752520 | tf_op jit(solution)/shard_map/ppermute | solution.py:765
  594.7 56.9 %collective-permute-start.15 = (bf16[3,128,512]{2,1,0:T(8,128)(2,1)}, bf16[3,128,512]{2,1,0:T(8,128)(2,1)}, u32[]{:S(2)}, u32[]{:S(2)}) collective-permute-start(bf16[3,128,512]{2,1,0:T(8,128)(2,1)} %bitcast.67), channel_id=1, source_target_pairs={{0,8},{2,10},{4,12},{6,14},{8,0},{10,2},{12,4},{14,6},{16,24},{18,... | collective-permute-start | bytes 1179656 | tf_op jit(solution)/shard_map/ppermute | solution.py:765
  651.6 35.5 %collective-permute-start.14 = (bf16[3,512,512]{2,1,0:T(8,128)(2,1)}, bf16[3,512,512]{2,1,0:T(8,128)(2,1)}, u32[]{:S(2)}, u32[]{:S(2)}) collective-permute-start(bf16[3,512,512]{2,1,0:T(8,128)(2,1)} %get-tuple-element.137), channel_id=1, source_target_pairs={{0,2},{2,0},{4,6},{6,4},{8,10},{10,8},{12,14},{14,12},{16,18},{18,... | collective-permute-start | bytes 4718600 | tf_op jit(solution)/shard_map/ppermute | solution.py:720
  653.2 11.7 %collective-permute-start.16 = (bf16[3,64,512]{2,1,0:T(8,128)(2,1)S(1)}, bf16[3,64,512]{2,1,0:T(8,128)(2,1)S(1)}, u32[]{:S(2)}, u32[]{:S(2)}) collective-permute-start(bf16[3,64,512]{2,1,0:T(8,128)(2,1)S(1)} %fusion.35), channel_id=1, source_target_pairs={{0,16},{2,18},{4,20},{6,22},{8,24},{10,26},{12,28},{14,30},{16,0},... | collective-permute-start | bytes 589832 | tf_op jit(solution)/shard_map/ppermute | solution.py:765
  658.6 26.9 %collective-permute-start.23 = (bf16[7,64,1024]{2,1,0:T(8,128)(2,1)}, bf16[7,64,1024]{2,1,0:T(8,128)(2,1)S(1)}, u32[]{:S(2)}, u32[]{:S(2)}) collective-permute-start(bf16[7,64,1024]{2,1,0:T(8,128)(2,1)} %pad_maximum_fusion.7), channel_id=1, source_target_pairs={{0,1},{1,0},{2,3},{3,2},{4,5},{5,4},{6,7},{7,6},{8,9},{9,8},{10,11... | collective-permute-start | bytes 2752520 | tf_op jit(solution)/shard_map/ppermute | solution.py:716
  666.2 19.3 %collective-permute-start.17 = (bf16[3,64,512]{2,1,0:T(8,128)(2,1)S(1)}, bf16[3,64,512]{2,1,0:T(8,128)(2,1)S(1)}, u32[]{:S(2)}, u32[]{:S(2)}) collective-permute-start(bf16[3,64,512]{2,1,0:T(8,128)(2,1)S(1)} %fusion.31), channel_id=1, source_target_pairs={{0,1},{1,0},{2,3},{3,2},{4,5},{5,4},{6,7},{7,6},{8,9},{9,8},{10,11... | collective-permute-start | bytes 589832 | tf_op jit(solution)/shard_map/ppermute | solution.py:716
  689.9 34.7 %collective-permute-start.18 = (bf16[3,256,512]{2,1,0:T(8,128)(2,1)}, bf16[3,256,512]{2,1,0:T(8,128)(2,1)}, u32[]{:S(2)}, u32[]{:S(2)}) collective-permute-start(bf16[3,256,512]{2,1,0:T(8,128)(2,1)} %get-tuple-element.172), channel_id=1, source_target_pairs={{0,4},{2,6},{4,0},{6,2},{8,12},{10,14},{12,8},{14,10},{16,20},{18,... | collective-permute-start | bytes 2359304 | tf_op jit(solution)/shard_map/ppermute | solution.py:724
  709.2 9.2 %collective-permute-start.27 = (f32[2192]{0:T(1024)S(1)}, f32[2192]{0:T(1024)S(1)}, u32[]{:S(2)}, u32[]{:S(2)}) collective-permute-start(f32[2192]{0:T(1024)S(1)} %add.1189), channel_id=1, source_target_pairs={{0,8},{2,10},{4,12},{6,14},{8,0},{10,2},{12,4},{14,6},{16,24},{18,... | collective-permute-start | bytes 26312 | tf_op jit(solution)/shard_map/ppermute | solution.py:781
  (93 other events, 1030.4 us)
Sparse Core Ops, SparseCore 0:
  77.5 100.8 all-gather.2
  180.7 99.0 all-gather.4

commit v3 on v2

--- a/solution.py
+++ b/solution.py
@@ -517,27 +517,101 @@
 
 
 def ffn_kernel(
-    places, first, spot, nf_ref, seed_ref, start_ref, nfstart_ref, wg_ref, wu_ref, wd_ref,
-    branch_ref, nfgrad_ref, down_far, down_cross, down_own, gate_far, gate_cross, gate_own,
-    turned, arranged, branch,
+    places, first, nf_ref, seed_ref, start_ref, nfstart_ref, wg_ref, wu_ref, wd_ref, *refs
 ):
+    if first:
+        branch_ref, nfgrad_ref, far_ref, cross_ref, own_ref, *refs = refs
+    else:
+        across_ref, branch_ref, nfgrad_ref, far_ref, cross_ref, own_ref, got_ref, *refs = refs
+    turned, branch, columns_out, rows_out, sems, arrived, *x_sems = refs
     step = pl.program_id(0)
+    steps = pl.num_programs(0)
     rows, width = nf_ref.shape
     shard = width // places
     chunk = wg_ref.shape[1]
+    folds = chunk // 2 // shard
+
+    place = lax.axis_index("dp")
+    groups = places // 4
+
+    twin = {"dp": place + 1 - place % 2 * 2}
+    over = {"dp": place + 2 - place // 2 % 2 * 4}
+    mesh_id = pl.DeviceIdType.MESH
+
+    def carry():
+        return pltpu.make_async_remote_copy(
+            src_ref=across_ref, dst_ref=got_ref, send_sem=x_sems[0].at[0], recv_sem=x_sems[0].at[1],
+            device_id=over, device_id_type=mesh_id,
+        )
 
     @pl.when(step == 0)
     def _():
-        arrange_rows(places, spot, nf_ref, turned, arranged)
+        barrier = pltpu.get_barrier_semaphore()
+        for target in (twin,) if first else (twin, over):
+            pl.semaphore_signal(barrier, inc=1, device_id=target, device_id_type=mesh_id)
+        pl.semaphore_wait(barrier, 1 if first else 2)
+        if not first:
+            carry().start()
+        turned[...] = nf_ref[...].T
         branch[...] = start_ref[...]
         nfgrad_ref[...] = jnp.zeros_like(nfgrad_ref) if first else nfstart_ref[...]
 
+    def spot_of(line, x, core):
+        near_core = (core == place % 2).astype(jnp.int32)
+        near_x = (x == place // 2 % 2).astype(jnp.int32)
+        return (near_core * 2 + near_x) * groups + line
+
+    def to_twin(source, target, send_sem, recv_sem):
+        return pltpu.make_async_remote_copy(
+            src_ref=source, dst_ref=target, send_sem=send_sem, recv_sem=recv_sem,
+            device_id=twin, device_id_type=mesh_id,
+        )
+
+    def column_copies(at):
+        slot = lax.rem(at, 2)
+        start = pl.multiple_of(at * chunk, chunk)
+        made, begin = [], 0
+        for k, ref in enumerate((far_ref, cross_ref, own_ref)):
+            count = ref.shape[0]
+            source = columns_out.at[slot, pl.ds(begin, count)]
+            target = ref.at[:, pl.ds(0, 2), :, pl.ds(start, chunk)]
+            if k == 0:
+                made.append(to_twin(source, target, sems.at[slot, k], arrived.at[at, 0]))
+            else:
+                made.append(pltpu.make_async_copy(source, target, sems.at[slot, k]))
+            begin += count
+        return made
+
+    def row_copies(at, ref, index, k):
+        slot = lax.rem(at, 2)
+        source, target = rows_out.at[slot, k], ref.at[index, 2]
+        if k == 0:
+            return to_twin(source, target, sems.at[slot, 3], arrived.at[at, 1])
+        return pltpu.make_async_copy(source, target, sems.at[slot, 4])
+
+    def sent(copy):
+        copy.wait_send() if copy.is_remote else copy.wait()
+
+    def each_copy(at, act):
+        for copy in column_copies(at):
+            act(copy)
+        line, x = at // 2, lax.rem(at, 2)
+        near = x == place // 2 % 2
+        act(row_copies(at, far_ref, near.astype(jnp.int32) * groups + line, 0))
+        pl.when(near)(lambda: act(row_copies(at, own_ref, line, 1)))
+        pl.when(jnp.logical_not(near))(lambda: act(row_copies(at, cross_ref, line, 1)))
+
+    @pl.when(step >= 2)
+    def _():
+        each_copy(step - 2, sent)
+
+    slot = lax.rem(step, 2)
     wg, wu = wg_ref[...], wu_ref[...]
     wd = jnp.concatenate(
         [
             wd_ref[i * shard : (i + 1) * shard, k * width : (k + 1) * width]
             for i in range(2)
-            for k in range(chunk // 2 // shard)
+            for k in range(folds)
         ],
         axis=0,
     )
@@ -559,99 +633,81 @@
         gates.append(gate)
         ups.append(up)
     hidden = jnp.concatenate(hiddens, axis=0)
-    gate = jnp.concatenate(gates, axis=0)
-    up = jnp.concatenate(ups, axis=0)
     down = dot(hidden, seed_ref[...], TN).astype(bf16)
+    on_upper = place % 2 == 1
     lower, upper = down[: chunk // 2, :], down[chunk // 2 :, :]
-    on_upper = spot[0] == 1
-    far = jnp.where(on_upper, lower, upper)
-    near = jnp.where(on_upper, upper, lower)
-    folds = [slice(k * shard, (k + 1) * shard) for k in range(chunk // 2 // shard)]
-    for k, at in enumerate(folds):
-        down_far[k] = far[at, :]
-
-    @pl.when(step % 2 != spot[1])
-    def _():
-        for k, at in enumerate(folds):
-            down_cross[k] = near[at, :]
-
-    @pl.when(step % 2 == spot[1])
-    def _():
-        for k, at in enumerate(folds):
-            down_own[k] = near[at, :]
-
-    half = width // 2
-    for part, grad in enumerate((gate, up)):
-        gate_far[part, 0] = dot(arranged[:half, :], grad).astype(bf16)
-        gate_cross[part, 0] = dot(arranged[half : half + half // 2, :], grad).astype(bf16)
-        gate_own[part, 0] = dot(arranged[half + half // 2 :, :], grad).astype(bf16)
-
-    @pl.when(step == pl.num_programs(0) - 1)
+    for i, part in enumerate((jnp.where(on_upper, lower, upper), jnp.where(on_upper, upper, lower))):
+        for k in range(folds):
+            rows_out[slot, i, :, k * width : (k + 1) * width] = part[k * shard : (k + 1) * shard, :]
+    for part, grad in enumerate((gates, ups)):
+        columns = dot(turned[...], jnp.concatenate(grad, axis=0)).astype(bf16)
+        for j in range(places):
+            spot = spot_of(j // 4, j // 2 % 2, j % 2)
+            columns_out[slot, spot, part] = columns[j * shard : (j + 1) * shard, :]
+    each_copy(step, lambda copy: copy.start())
+
+    @pl.when(step == steps - 1)
     def _():
         branch_ref[...] = branch[...].astype(branch_ref.dtype)
-
-
-def feed_forward(spot, normed, seed, start, nfstart, weights):
+        each_copy(step - 1, sent)
+        each_copy(step, sent)
+        for at in range(places // 2):
+            column_copies(at)[0].wait_recv()
+            near = (at % 2 == place // 2 % 2).astype(jnp.int32)
+            row_copies(at, far_ref, near * groups + at // 2, 0).wait_recv()
+        if not first:
+            carry().wait()
+
+
+def feed_forward(places, normed, seed, start, nfstart, weights, across=None):
     rows, width = normed.shape
-    places = spot.shape[0] - 2
-    groups = places // 4
     first = nfstart is None
     hidden = weights.shape[1] // 3
     chunk = 2 * hidden // places
     steps = places // 2
-    whole = lambda t, o: (0, 0)
+    shard = width // places
+    whole = lambda t: (0, 0)
     once = pl.Buffered(1)
-    shard = width // places
-    folds = chunk // 2 // shard
-    spans = hidden // width
-    per_span = steps // spans
-    by_cols = lambda t, o: (0, t // per_span, 0, t % per_span)
     return pl.pallas_call(
         functools.partial(ffn_kernel, places, first),
-        grid_spec=pltpu.PrefetchScalarGridSpec(
-            num_scalar_prefetch=1,
-            grid=(steps,),
-            in_specs=[
-                pl.BlockSpec((rows, width), whole, pipeline_mode=once),
-                pl.BlockSpec((rows, width), whole, pipeline_mode=once),
-                pl.BlockSpec((rows, width), whole, pipeline_mode=once),
-                pl.BlockSpec((8, 128) if first else (rows, width), whole, pipeline_mode=once),
-                pl.BlockSpec((width, chunk), lambda t, o: (0, t)),
-                pl.BlockSpec((width, chunk), lambda t, o: (0, steps + t)),
-                pl.BlockSpec((2 * width // places, hidden), lambda t, o: (t, 2)),
-            ],
-            out_specs=[
-                pl.BlockSpec((rows, width), whole),
-                pl.BlockSpec((rows, width), whole),
-                pl.BlockSpec(
-                    (folds, shard, width),
-                    lambda t, o: (0, jnp.where(t % 2 == o[1], groups, 0) + t // 2, 0),
-                ),
-                pl.BlockSpec((folds, shard, width), lambda t, o: (0, t // 2, 0)),
-                pl.BlockSpec((folds, shard, width), lambda t, o: (0, t // 2, 0)),
-                pl.BlockSpec((2, 1, width // 2, chunk), by_cols),
-                pl.BlockSpec((2, 1, width // 4, chunk), by_cols),
-                pl.BlockSpec((2, 1, width // 4, chunk), by_cols),
-            ],
-            scratch_shapes=[
-                pltpu.VMEM((width, rows), bf16),
-                pltpu.VMEM((width, rows), bf16),
-                pltpu.VMEM((rows, width), f32),
-            ],
-        ),
+        grid=(steps,),
+        in_specs=[
+            pl.BlockSpec((rows, width), whole, pipeline_mode=once),
+            pl.BlockSpec((rows, width), whole, pipeline_mode=once),
+            pl.BlockSpec((rows, width), whole, pipeline_mode=once),
+            pl.BlockSpec((8, 128) if first else (rows, width), whole, pipeline_mode=once),
+            pl.BlockSpec((width, chunk), lambda t: (0, t)),
+            pl.BlockSpec((width, chunk), lambda t: (0, steps + t)),
+            pl.BlockSpec((2 * shard, hidden), lambda t: (t, 2)),
+        ]
+        + [pl.BlockSpec(memory_space=pl.ANY)] * (not first),
+        out_specs=[
+            pl.BlockSpec((rows, width), whole),
+            pl.BlockSpec((rows, width), whole),
+        ]
+        + [pl.BlockSpec(memory_space=pl.ANY)] * (3 if first else 4),
+        scratch_shapes=[
+            pltpu.VMEM((width, rows), bf16),
+            pltpu.VMEM((rows, width), f32),
+            pltpu.VMEM((2, places, 2, shard, chunk), bf16),
+            pltpu.VMEM((2, 2, shard, hidden), bf16),
+            pltpu.SemaphoreType.DMA((2, 5)),
+            pltpu.SemaphoreType.DMA((steps, 2)),
+        ]
+        + [pltpu.SemaphoreType.DMA((2,))] * (not first),
         out_shape=[
             jax.ShapeDtypeStruct((rows, width), f32 if first else bf16),
             jax.ShapeDtypeStruct((rows, width), f32),
-            jax.ShapeDtypeStruct((folds, width // 2, width), bf16),
-            jax.ShapeDtypeStruct((folds, width // 4, width), bf16),
-            jax.ShapeDtypeStruct((folds, width // 4, width), bf16),
-            jax.ShapeDtypeStruct((2, spans, width // 2, width), bf16),
-            jax.ShapeDtypeStruct((2, spans, width // 4, width), bf16),
-            jax.ShapeDtypeStruct((2, spans, width // 4, width), bf16),
-        ],
-        compiler_params=pltpu.CompilerParams(vmem_limit_bytes=56 * 2**20),
+        ]
+        + [jax.ShapeDtypeStruct((places // part, 3, shard, hidden), bf16) for part in ((2, 4, 4) if first else (2, 4, 4, 4))],
+        compiler_params=pltpu.CompilerParams(
+            vmem_limit_bytes=56 * 2**20, collective_id=1 if first else 2, has_side_effects=True
+        ),
         cost_estimate=NO_COST,
-    )(spot, normed, seed, start, start if first else nfstart, weights, weights, weights)
+    )(
+        normed, seed, start, start if first else nfstart, weights, weights, weights,
+        *(() if first else (across,)),
+    )
 
 
 def outer_kernel(places, spot, left_ref, right_ref, far_ref, cross_ref, own_ref, turned, arranged):
@@ -890,32 +946,35 @@
     residual = inputs_f + dot(attended, out_full)
     normed_ffn, ffn_scale = rms_forward(residual, ffn_gain_f)
     normed_ffn_low = normed_ffn.astype(bf16)
-    def ffn_pieces(arrays):
-        gates = [array.reshape(-1, *array.shape[2:]) for array in arrays[3:]]
-        return [gates, arrays[:3]]
-
-    branch, normed_ffn_grad, *pieces = feed_forward(
-        spot, normed_ffn_low, seed_low, residual, None, ffn_weights[0]
-    )
-    crossed, first_terms = core_sum(ffn_pieces(pieces), places)
-    layer_out, normed_ffn_grad, *pieces = feed_forward(
-        spot, after(normed_ffn_low, crossed), seed_low, branch, normed_ffn_grad, ffn_weights[1]
-    )
-    across = cross_x(crossed, places)
-    normed_ffn_grad = after(normed_ffn_grad, across)
-    first_terms = add_received(first_terms, across)
+    def x_part(received, own, far):
+        total = received.astype(f32) + own.astype(f32) + far[groups:].astype(f32)
+        return total.astype(bf16)
+
+    def scatter_line(parts):
+        lines = [[line * 4 + k for line in range(groups)] for k in range(4)]
+        return lax.psum_scatter(parts, "dp", scatter_dimension=0, axis_index_groups=lines, tiled=True)[0]
+
+    branch, normed_ffn_grad, *grads = feed_forward(
+        places, normed_ffn_low, seed_low, residual, None, ffn_weights[0]
+    )
+    far, cross, own = grads
+    layer_out, normed_ffn_grad, *grads, received = feed_forward(
+        places, normed_ffn_low, seed_low, branch, normed_ffn_grad, ffn_weights[1], cross + far[:groups]
+    )
+    first_total = scatter_line(x_part(received, own, far))
+    far, cross, own = grads
+    second_crossed = cross + far[:groups]
     resid_norm_grad, ffn_gain_terms = rms_backward(residual, ffn_scale, ffn_gain_f, normed_ffn_grad)
     residual_grad = seed_grad + resid_norm_grad
     mixed_low = residual_grad.astype(bf16)
     attended_grad = dot(mixed_low, out_full, NT).astype(bf16)
 
     attended_grad = dot(mixed_low, out_full, NT).astype(bf16)
-    crossed, second_terms = core_sum(
-        ffn_pieces(pieces) + [outer(spot, attended, mixed_low, width)], places
-    )
+    out_crossed, out_terms = core_sum([outer(spot, attended, mixed_low, width)], places)
     steps = (places // 4).bit_length() - 1
-    sent, first_terms = halve(first_terms, 0, places)
-    attended_grad = after(attended_grad, crossed, sent)
+    attended_grad = after(attended_grad, out_crossed, second_crossed)
+    second_across = cross_x(second_crossed, places)
+    out_across = cross_x(out_crossed, places)
 
     remote = list(range(1, seq_count))
     dqs = [[] for _ in range(CHUNKS)]
@@ -946,42 +1005,40 @@
                 sent, terms = halve(terms, step + 1, places)
         return total_of(terms)
 
-    second_across = cross_x(crossed, places)
-    first_received = cross_z(sent, 0, places)
+    def line_of(terms):
+        total = total_of(terms)
+        blocks, rows, columns = total.shape
+        return total.reshape(blocks, groups, rows // groups, columns).transpose(1, 0, 2, 3)
+
     grad = back(0, remote, attended_grad)
-    grad = back(1, remote, after(grad, first_received))
-    first_terms = add_received(first_terms, first_received)
-    sent, first_terms = halve(first_terms, 1, places)
-    grad = after(grad, sent)
-    first_received = cross_z(sent, 1, places)
+    grad = back(1, remote, grad)
     grad = back(0, [0], grad)
-
     second_across = after(second_across, grad)
-    second_terms = add_received(second_terms, second_across)
-    sent, second_terms = halve(second_terms, 0, places)
-    second_received = cross_z(sent, 0, places)
-    dqs[0][0] = after(dqs[0][0], grad, sent)
+    second = x_part(second_across, own, far).reshape(groups, -1, second_across.shape[-1])
+    out_total = line_of(add_received(out_terms, out_across))
+    folds = second.shape[-1] // width
+    out_total = out_total.reshape(groups, folds, -1, width).transpose(0, 2, 1, 3)
+    out_total = out_total.reshape(groups, -1, folds * width)
+    second = scatter_line(jnp.concatenate([second, out_total], axis=1))
+    dqs[0][0] = after(dqs[0][0], grad)
     merged_0, gains_0 = merge(0)
     crossed, in_terms_0 = core_sum([outer(spot, normed_low, merged_0, width // CHUNKS)], places)
     normed_grad_0 = dot(merged_0, chunk_weights(0), NT)
     grad = after(grad, crossed, normed_grad_0)
     in_across_0 = cross_x(crossed, places)
     grad = back(1, [0], grad)
-    dqs[1][0] = after(dqs[1][0], grad, in_across_0, second_received, first_received)
+    dqs[1][0] = after(dqs[1][0], grad, in_across_0)
+    in_total_0 = scatter_line(line_of(add_received(in_terms_0, in_across_0)))
 
     merged_1, gains_1 = merge(1)
     crossed, in_terms_1 = core_sum([outer(spot, normed_low, merged_1, width // CHUNKS)], places)
     in_terms_1 = add_received(in_terms_1, cross_x(crossed, places))
     normed_grad = normed_grad_0 + dot(after(merged_1, crossed), chunk_weights(1), NT)
-    first_terms = add_received(first_terms, first_received)
-    first_total = finish_line(*halve(first_terms, 2, places)[::-1], 2) if steps > 2 else total_of(first_terms)
-    second_terms = add_received(second_terms, second_received)
-    sent, second_terms = halve(second_terms, 1, places)
-    second_total = finish_line(second_terms, sent, 1)
-    sent, in_terms_0 = halve(add_received(in_terms_0, in_across_0), 0, places)
-    in_total_0 = finish_line(in_terms_0, sent, 0)
     sent, in_terms_1 = halve(in_terms_1, 0, places)
     in_total_1 = finish_line(in_terms_1, sent, 0)
+    second_total = second[: 3 * shard].reshape(3, shard, -1)
+    out_total = second[3 * shard :].reshape(-1, folds, width).transpose(1, 0, 2).reshape(shard, width)
+    out_proj_grad = sum_seq(out_total, seq_count)
     first_sum = sum_seq(first_total, seq_count)
     second_sum = sum_seq(second_total, seq_count)
     in_sum = jnp.concatenate(
@@ -1008,17 +1065,18 @@
         seq_count,
     )
     in_proj_grad = in_sum.transpose(1, 0, 2).reshape(in_proj.shape)
-    spans = places * hidden_part // width
-    gates = 2 * spans
     down_grad = jnp.concatenate(
-        [part[gates : gates + hidden_part // shard].reshape(-1, width) for part in (first_sum, second_sum)]
+        [
+            part[2].reshape(shard, -1, width).transpose(1, 0, 2).reshape(hidden_part, width)
+            for part in (first_sum, second_sum)
+        ]
     )
     gate_up_grad = jnp.stack(
         [
-            part[:gates].reshape(2, spans, shard, -1, hidden_part).transpose(2, 0, 1, 3, 4)
+            part[:2].reshape(2, shard, places, hidden_part).transpose(1, 0, 2, 3)
             for part in (first_sum, second_sum)
         ],
-        axis=4,
+        axis=3,
     ).reshape(gate_up.shape)
     gain_rows = attn_gain.shape[0]
     here = place * gain_rows
@@ -1028,7 +1086,7 @@
         layer_out,
         input_grad,
         in_proj_grad,
-        second_sum[-1],
+        out_proj_grad,
         gate_up_grad,
         down_grad,
         lax.dynamic_slice_in_dim(small, here, gain_rows),

time: 765 us -> 780 us (1.020)
  Pallas kernels: 403 us -> 440 us
  waiting for transfers between devices: 117 us -> 151 us
  starting transfers between devices: 48.5 us -> 20.7 us
  other arithmetic: 86.5 us -> 66.3 us
    ppermute x4, waiting for transfers between devices: 13.1 us -> 89.8 us  [cross_x(): return lax.ppermute(values, 'dp', [(i, i ^ 2) for i in range(places)])]
    ppermute x8 -> x2, waiting for transfers between devices: 60.4 us -> 6.77 us  [cross_z(): lax.ppermute(values, 'dp', [(i, i ^ 4 * 2 ** step) for i in range(places)])]
    pallas_call x2, Pallas kernels: 113 us -> 135 us  [feed_forward(): pl.pallas_call(functools.partial(ffn_kernel, places, first), grid=(steps,...]
    all_gather x2, waiting for transfers between devices: 0.01 us -> 14.1 us  [body(): gather = lambda w: lax.all_gather(w, 'dp', axis=0, tiled=True)]
    slice x17 -> x7, local copies, waits for them, and re-layouts: 15.3 us -> 2.3 us  [the longest x1 1.22 us: body(): second_total = second[:3 * shard].reshape(3, shard, -1)]
    slice x7 -> x1, other arithmetic: 14.9 us -> 2.93 us  [core_sum(): terms.append([own, far[:, quarter:]])]
    convert_element_type x0 -> x2, other arithmetic: none -> 11.9 us  [x_part(): return total.astype(bf16)]
    ppermute x7 -> x3, starting transfers between devices: 11.2 us -> 0.08 us  [cross_core(): return lax.ppermute(values, 'dp', [(i, i ^ 1) for i in range(places)])]
  transfers between devices with their start and end apart: 32 -> 26, of which waited for: 11 -> 13; matrix products, arithmetic and copies ran while one was open for 17% -> 13% of each run, Pallas kernels for 43% -> 38%
where the time goes in v3:
time: 780 us; the launch traced here: 775 us
  Pallas kernels  440 us (56%)
  waiting for transfers between devices  151 us (19%)
  other arithmetic  66.3 us (8%)
  local copies, waits for them, and re-layouts  53.1 us (7%)
  matrix products  27.6 us (4%)
  starting transfers between devices  20.7 us (3%)
  between operations  16.2 us (2%)
    pallas_call x2, Pallas kernels, feed_forward(): pl.pallas_call(functools.partial(ffn_kernel, places, first), grid=(steps,...  135 us
    pallas_call x4, Pallas kernels, attend_back(): pl.pallas_call(backward_kernel, grid_spec=pltpu.PrefetchScalarGridSpec(nu...  114 us
    ppermute x4, waiting for transfers between devices, cross_x(): return lax.ppermute(values, 'dp', [(i, i ^ 2) for i in range(places)])  89.8 us
    pallas_call x1, Pallas kernels, attend(): pl.pallas_call(functools.partial(forward_kernel, sources, min(512, rows))...  63 us
    pallas_call x1, Pallas kernels, gather_first(): pl.pallas_call(gather_kernel, in_specs=[anywhere] * 3, out_specs=[anywher...  57.4 us
    pallas_call x2, Pallas kernels, project(): pl.pallas_call(qkv_kernel, grid=(rows // block,), in_specs=[pl.BlockSpec(...  35.1 us
    dot_general x4, matrix products, dot(): return lax.dot_general(left, right, dims, preferred_element_type=f32)  27.6 us
    unnamed x111, local copies, waits for them, and re-layouts  22.7 us
  transfers between devices with their start and end apart: 26, of which 13 were waited for; matrix products, arithmetic and copies ran while one was open for 13% of the time, Pallas kernels for 38%

profile of v3, /device:TPU:0, one launch (start us, length us, event | category | flops | bytes accessed | tf_op | source)
XLA Modules:
  0.0 774.8 jit_solution(4505394549188536759)
XLA Ops:
  17.7 57.4 %shard_map.221 = (bf16[1024,4224]{1,0:T(8,128)(2,1)}, bf16[1024,1024]{1,0:T(8,128)(2,1)}, s32[8,128]{1,0:T(8,128)}) custom-call(bf16[64,4224]{1,0:T(8,128)(2,1)} %fusion.20.shard_ref, bf16[1024,1024]{1,0:T(8,128)(2,1)} %tokens_ref.3, s32[8,128]{1,0:T(8,128)} %bitcast.188), custom_call_target="tpu_custom_call" | custom-call | flops 1 | bytes 1 | tf_op jit(solution)/shard_map/pallas_call | solution.py:158
  82.1 22.1 %shard_map.222 = (bf16[1024,1024]{1,0:T(8,128)(2,1)S(1)}, bf16[1024,1024]{1,0:T(8,128)(2,1)S(1)}, bf16[1024,1024]{1,0:T(8,128)(2,1)}, f32[1024,2048]{1,0:T(8,128)}, bf16[1024,1024]{1,0:T(8,128)(2,1)}) custom-call(bf16[1024,1024]{1,0:T(8,128)(2,1)} %tokens_ref.3, f32[1,1024]{1,0:T(1,128)S(1)} %bitcast.148, bf16[1024,4224]{1,0:T(8,128)(2,1)} %get-tuple-element.70.weight_ref, ...), custom_call_target="tpu_custom_call" | custom-call | flops 1 | bytes 1 | tf_op jit(solution)/shard_map/pallas_call | solution.py:224
  107.4 13.0 %shard_map.223 = (bf16[1024,1024]{1,0:T(8,128)(2,1)S(1)}, bf16[1024,1024]{1,0:T(8,128)(2,1)S(1)}) custom-call(bf16[1024,1024]{1,0:T(8,128)(2,1)} %get-tuple-element.74.tokens_ref, f32[1,1024]{1,0:T(1,128)S(1)} %bitcast.149, bf16[1024,4224]{1,0:T(8,128)(2,1)} %get-tuple-element.70.weight_ref, f32[1024,128]{1,0:T(8,128)S(1)} %get-tuple-element.163.cos_ref, ...), custom_call_target="tpu_custom_call" | custom-call | flops 1 | bytes 1 | tf_op jit(solution)/shard_map/pallas_call | solution.py:224
  131.9 63.0 %shard_map.224 = (bf16[1024,1024]{1,0:T(8,128)(2,1)S(1)}, bf16[1024,2048]{1,0:T(8,128)(2,1)}) custom-call(s32[8]{0:T(128)S(1)} %pad_add_fusion.flags, bf16[1024,1024]{1,0:T(8,128)(2,1)S(1)} %copy-done.15, bf16[1024,128]{1,0:T(8,128)(2,1)S(1)} %select_convert_fusion.aq_ref, bf16[8,2,128]{2,1,0:T(2,128)(2,1)S(1)} %bitcast.150, bf16[1024,1024]{1,0:T(8,128)(2,1)} %copy-done.1, ...), custom_call_target="tpu_custom_call" | custom-call | flops 1 | bytes 1 | tf_op jit(solution)/shard_map/pallas_call | solution.py:366
  204.8 55.5 %shard_map.225 = (f32[1024,1024]{1,0:T(8,128)}, f32[1024,1024]{1,0:T(8,128)}, bf16[8,3,64,2048]{3,2,1,0:T(8,128)(2,1)}, bf16[4,3,64,2048]{3,2,1,0:T(8,128)(2,1)}, bf16[4,3,64,2048]{3,2,1,0:T(8,128)(2,1)}) custom-call(bf16[1024,1024]{1,0:T(8,128)(2,1)} %multiply_convert_fusion.nf_ref, bf16[1024,1024]{1,0:T(8,128)(2,1)} %fusion.9.seed_ref, ...), custom_call_target="tpu_custom_call" | custom-call | flops 1 | bytes 1 | tf_op jit(solution)/shard_map/pallas_call | solution.py:671
  265.2 14.1 %all-gather.5.cloned.1.call-done.wg_ref.wu_ref.wd_ref = bf16[1024,6144]{1,0:T(8,128)(2,1)} async-done(((bf16[64,6144]{1,0:T(8,128)(2,1)}), bf16[1024,6144]{1,0:T(8,128)(2,1)}) %all-gather.5.cloned.1.call-update) | async-done | bytes 12582928 | tf_op jit(solution)/shard_map/all_gather | solution.py:868
  279.3 79.2 %shard_map.226 = (bf16[1024,1024]{1,0:T(8,128)(2,1)}, f32[1024,1024]{1,0:T(8,128)}, bf16[8,3,64,2048]{3,2,1,0:T(8,128)(2,1)}, bf16[4,3,64,2048]{3,2,1,0:T(8,128)...) custom-call(bf16[1024,1024]{1,0:T(8,128)(2,1)} %multiply_convert_fusion.nf_ref, ...), custom_call_target="tpu_custom_call" | custom-call | flops 1 | bytes 1 | tf_op jit(solution)/shard_map/pallas_call | solution.py:671
  373.6 5.9 add_convert_fusion
  392.4 28.5 %shard_map.228 = (f32[1024,512]{1,0:T(8,128)S(1)}, bf16[2,1024,512]{2,1,0:T(8,128)(2,1)S(1)}, f32[4,2,128]{2,1,0:T(2,128)S(1)}) custom-call(s32[4]{0:T(128)S(1)} %get-tuple-element.179.flags, bf16[1024,2048]{1,0:T(8,128)(2,1)} %get-tuple-element.87.full_ref, bf16[1024,1024]{1,0:T(8,128)(2,1)} %convolution_convert_fusion.grad_ref, ...), custom_call_target="tpu_custom_call" | custom-call | flops 1 | bytes 1 | tf_op jit(solution)/shard_map/pallas_call | solution.py:450
  421.0 28.7 %shard_map.229 = (f32[1024,512]{1,0:T(8,128)S(1)}, bf16[2,1024,512]{2,1,0:T(8,128)(2,1)S(1)}, f32[4,2,128]{2,1,0:T(2,128)S(1)}) custom-call(s32[4]{0:T(128)S(1)} %get-tuple-element.179.flags, bf16[1024,2048]{1,0:T(8,128)(2,1)} %get-tuple-element.87.full_ref, bf16[1024,1024]{1,0:T(8,128)(2,1)} %convolution_convert_fusion.grad_ref, ...), custom_call_target="tpu_custom_call" | custom-call | flops 1 | bytes 1 | tf_op jit(solution)/shard_map/pallas_call | solution.py:450
  452.4 28.4 %shard_map.230 = (f32[1024,512]{1,0:T(8,128)S(1)}, bf16[2,1024,512]{2,1,0:T(8,128)(2,1)S(1)}, f32[4,2,128]{2,1,0:T(2,128)S(1)}) custom-call(s32[4]{0:T(128)S(1)} %get-tuple-element.180.flags, bf16[1024,2048]{1,0:T(8,128)(2,1)} %get-tuple-element.87.full_ref, bf16[1024,1024]{1,0:T(8,128)(2,1)} %convolution_convert_fusion.grad_ref, ...), custom_call_target="tpu_custom_call" | custom-call | flops 1 | bytes 1 | tf_op jit(solution)/shard_map/pallas_call | solution.py:450
  483.6 8.6 %shard_map.231 = (bf16[1024,1536]{1,0:T(8,128)(2,1)}, f32[8,512]{1,0:T(8,128)S(1)}) custom-call(f32[1024,512]{1,0:T(8,128)S(1)} %get-tuple-element.100.refs_0_, f32[1024,512]{1,0:T(8,128)S(1)} %get-tuple-element.101.refs_1_, bf16[2,1024,512]{2,1,0:T(8,128)(2,1)} %copy-done.35, bf16[2,1024,512]{2,1,0:T(8,128)(2,1)} %copy-done.14, ...), custom_call_target="tpu_custom_call" | custom-call | flops 1 | bytes 1 | tf_op jit(solution)/shard_map/pallas_call | solution.py:279
  492.1 6.3 shard_map.232
  504.1 82.5 %collective-permute-done.3 = bf16[3,256,512]{2,1,0:T(8,128)(2,1)S(1)} collective-permute-done((bf16[3,256,512]{2,1,0:T(8,128)(2,1)S(1)}, bf16[3,256,512]{2,1,0:T(8,128)(2,1)S(1)}, u32[]{:S(2)}, u32[]{:S(2)}) %collective-permute-start.3) | collective-permute-done | bytes 786464 | tf_op jit(solution)/shard_map/ppermute | solution.py:780
  590.1 7.3 collective-permute-done.12
  602.7 5.9 add_convert_fusion.1
  610.8 8.3 %fusion.12 = f32[1024,1024]{1,0:T(8,128)} fusion(bf16[1024,1536]{1,0:T(8,128)(2,1)} %get-tuple-element.103.right_ref, bf16[1024,4224]{1,0:T(8,128)(2,1)} %get-tuple-element.70.weight_ref), kind=kOutput, calls=%fused_computation.26 | convolution fusion | flops 3221225472 | bytes 10485760 | tf_op jit(solution)/shard_map/dot_general | solution.py:27
  619.1 28.3 %shard_map.233 = (f32[1024,512]{1,0:T(8,128)S(1)}, bf16[2,1024,512]{2,1,0:T(8,128)(2,1)S(1)}, f32[4,2,128]{2,1,0:T(2,128)S(1)}) custom-call(s32[4]{0:T(128)S(1)} %get-tuple-element.180.flags, bf16[1024,2048]{1,0:T(8,128)(2,1)} %get-tuple-element.87.full_ref, bf16[1024,1024]{1,0:T(8,128)(2,1)} %convolution_convert_fusion.grad_ref, ...), custom_call_target="tpu_custom_call" | custom-call | flops 1 | bytes 1 | tf_op jit(solution)/shard_map/pallas_call | solution.py:450
  648.8 8.4 %shard_map.234 = (bf16[1024,1536]{1,0:T(8,128)(2,1)}, f32[8,512]{1,0:T(8,128)S(1)}) custom-call(f32[1024,512]{1,0:T(8,128)S(1)} %copy-done.12, f32[1024,512]{1,0:T(8,128)S(1)} %get-tuple-element.110.refs_1_, bf16[2,1024,512]{2,1,0:T(8,128)(2,1)} %collective-permute-done.4.refs_2_, bf16[2,1024,512]{2,1,0:T(8,128)(2,1)} %copy-done.13, ...), custom_call_target="tpu_custom_call" | custom-call | flops 1 | bytes 1 | tf_op jit(solution)/shard_map/pallas_call | solution.py:279
  657.2 7.0 shard_map.235
  671.8 8.5 %fusion.8 = (f32[1024]{0:T(1024)S(1)}, f32[1024]{0:T(1024)S(1)}, f32[1024,1024]{1,0:T(8,128)}) fusion(bf16[1024,1024]{1,0:T(8,128)(2,1)S(1)} %copy-done.24, f32[1024]{0:T(1024)S(1)} %add_rsqrt_fusion, f32[1024]{0:T(1024)S(1)} %get-tuple-element.130, f32[1024,1024]{1,0:T(8,128)} %fusion.12, bf16[1024,1536]{1,0:T(8,128)(2,1)S(1)} %copy-done.30, ...), kind=kOutput, calls=%fused_computation.15 | convolution fusion | flops 3229612032 | bytes 16793600 | tf_op jit(solution)/shard_map/dot_general | solution.py:27
  688.5 12.4 %collective-permute-done.17 = f32[2192]{0:T(1024)S(1)} collective-permute-done((f32[2192]{0:T(1024)S(1)}, f32[2192]{0:T(1024)S(1)}, u32[]{:S(2)}, u32[]{:S(2)}) %collective-permute-start.17) | collective-permute-done | bytes 8800 | tf_op jit(solution)/shard_map/ppermute | solution.py:837
  727.9 5.9 collective-permute-done.9
  745.7 11.9 %collective-permute-done.13 = bf16[64,1024]{1,0:T(8,128)(2,1)S(1)} collective-permute-done((bf16[64,1024]{1,0:T(8,128)(2,1)S(1)}, bf16[64,1024]{1,0:T(8,128)(2,1)S(1)}, u32[]{:S(2)}, u32[]{:S(2)}) %collective-permute-start.13) | collective-permute-done | bytes 131104 | tf_op jit(solution)/shard_map/ppermute | solution.py:772
  (281 shorter events, 161.1 us)
Async XLA Ops:
  7.2 197.6 %all-gather.3.cloned.1.call-start = ((), (), s32[]{:S(2)}) async-start(), calls=%async_computation.3 | async-start | bytes 13369344 | tf_op jit(solution)/shard_map/all_gather | solution.py:868
  76.4 202.9 %all-gather.5.cloned.1.call-start = ((), (), s32[]{:S(2)}) async-start(), calls=%async_computation.4 | async-start | bytes 13369344 | tf_op jit(solution)/shard_map/all_gather | solution.py:868
  107.0 559.2 %reduce-scatter.8.cloned.1.call-start = ((), (), s32[]{:S(2)}) async-start(), calls=%async_computation.7 | async-start | bytes 3932160 | tf_op jit(solution)/shard_map/reduce_scatter | solution.py:955
  373.6 16.9 %collective-permute-start = (bf16[1,512,1024]{2,1,0:T(8,128)(2,1)}, bf16[1,512,1024]{2,1,0:T(8,128)(2,1)}, u32[]{:S(2)}, u32[]{:S(2)}) collective-permute-start(bf16[1,512,1024]{2,1,0:T(8,128)(2,1)} %get-tuple-element.89), channel_id=1, source_target_pairs={{0,2},{2,0},{4,6},{6,4},{8,10},{10,8},{12,14},{14,12},{16,18},{18,... | collective-permute-start | bytes 3145736 | tf_op jit(solution)/shard_map/ppermute | solution.py:776
  379.6 327.9 %reduce-scatter.4.cloned.1.call-start = ((), (), s32[]{:S(2)}) async-start(), calls=%async_computation.5 | async-start | bytes 983040 | tf_op jit(solution)/shard_map/reduce_scatter | solution.py:955
  420.9 61.3 %collective-permute-start.1 = (bf16[2,1024,512]{2,1,0:T(8,128)(2,1)S(1)}, bf16[2,1024,512]{2,1,0:T(8,128)(2,1)S(1)}, u32[]{:S(2)}, u32[]{:S(2)}) collective-permute-start(bf16[2,1024,512]{2,1,0:T(8,128)(2,1)S(1)} %get-tuple-element.94), channel_id=1, source_target_pairs={{0,1},{1,0},{2,3},{3,2},{4,5},{5,4},{6,7},{7,6},{8,9},{9,8},{10,11... | collective-permute-start | bytes 6291464 | tf_op jit(solution)/shard_map/ppermute | solution.py:772
  498.6 104.1 %collective-permute-start.11 = (bf16[4,3,64,2048]{3,2,1,0:T(8,128)(2,1)}, bf16[4,3,64,2048]{3,2,1,0:T(8,128)(2,1)}, u32[]{:S(2)}, u32[]{:S(2)}) collective-permute-start(bf16[4,3,64,2048]{3,2,1,0:T(8,128)(2,1)} %slice_add_fusion), channel_id=1, source_target_pairs={{0,4},{2,6},{4,0},{6,2},{8,12},{10,14},{12,8},{14,10},{16,20},{18,... | collective-permute-start | bytes 9437192 | tf_op jit(solution)/shard_map/ppermute | solution.py:780
  502.0 84.5 %collective-permute-start.3 = (bf16[3,256,512]{2,1,0:T(8,128)(2,1)S(1)}, bf16[3,256,512]{2,1,0:T(8,128)(2,1)S(1)}, u32[]{:S(2)}, u32[]{:S(2)}) collective-permute-start(bf16[3,256,512]{2,1,0:T(8,128)(2,1)S(1)} %slice_add_fusion.3), channel_id=1, source_target_pairs={{0,4},{2,6},{4,0},{6,2},{8,12},{10,14},{12,8},{14,10},{16,20},{18,... | collective-permute-start | bytes 2359304 | tf_op jit(solution)/shard_map/ppermute | solution.py:780
  502.1 95.4 %collective-permute-start.12 = (bf16[1,256,1024]{2,1,0:T(8,128)(2,1)}, bf16[1,256,1024]{2,1,0:T(8,128)(2,1)}, u32[]{:S(2)}, u32[]{:S(2)}) collective-permute-start(bf16[1,256,1024]{2,1,0:T(8,128)(2,1)} %slice_add_fusion.4), channel_id=1, source_target_pairs={{0,4},{2,6},{4,0},{6,2},{8,12},{10,14},{12,8},{14,10},{16,20},{18,... | collective-permute-start | bytes 1572872 | tf_op jit(solution)/shard_map/ppermute | solution.py:780
  587.9 148.7 %reduce-scatter.6.cloned.1.call-start = ((), (), s32[]{:S(2)}) async-start(), calls=%async_computation.6 | async-start | bytes 4587520 | tf_op jit(solution)/shard_map/reduce_scatter | solution.py:955
  588.1 60.7 %collective-permute-start.4 = (bf16[2,1024,512]{2,1,0:T(8,128)(2,1)}, bf16[2,1024,512]{2,1,0:T(8,128)(2,1)}, u32[]{:S(2)}, u32[]{:S(2)}) collective-permute-start(bf16[2,1024,512]{2,1,0:T(8,128)(2,1)} %copy-done.20), channel_id=1, source_target_pairs={{0,1},{1,0},{2,3},{3,2},{4,5},{5,4},{6,7},{7,6},{8,9},{9,8},{10,11... | collective-permute-start | bytes 6291464 | tf_op jit(solution)/shard_map/ppermute | solution.py:772
  665.1 3.8 collective-permute-start.5
  666.2 20.3 %collective-permute-start.14 = (bf16[3,64,2048]{2,1,0:T(8,128)(2,1)}, bf16[3,64,2048]{2,1,0:T(8,128)(2,1)}, u32[]{:S(2)}, u32[]{:S(2)}) collective-permute-start(bf16[3,64,2048]{2,1,0:T(8,128)(2,1)} %bitcast.181), channel_id=1, source_target_pairs={{0,1},{1,0},{2,3},{3,2},{4,5},{5,4},{6,7},{7,6},{8,9},{9,8},{10,11... | collective-permute-start | bytes 2359304 | tf_op jit(solution)/shard_map/ppermute | solution.py:772
  680.6 33.5 %collective-permute-start.7 = (bf16[3,256,512]{2,1,0:T(8,128)(2,1)}, bf16[3,256,512]{2,1,0:T(8,128)(2,1)}, u32[]{:S(2)}, u32[]{:S(2)}) collective-permute-start(bf16[3,256,512]{2,1,0:T(8,128)(2,1)} %get-tuple-element.144), channel_id=1, source_target_pairs={{0,4},{2,6},{4,0},{6,2},{8,12},{10,14},{12,8},{14,10},{16,20},{18,... | collective-permute-start | bytes 2359304 | tf_op jit(solution)/shard_map/ppermute | solution.py:780
  681.6 19.2 %collective-permute-start.17 = (f32[2192]{0:T(1024)S(1)}, f32[2192]{0:T(1024)S(1)}, u32[]{:S(2)}, u32[]{:S(2)}) collective-permute-start(f32[2192]{0:T(1024)S(1)} %add.567), channel_id=1, source_target_pairs={{0,4},{2,6},{4,0},{6,2},{8,12},{10,14},{12,8},{14,10},{16,20},{18,... | collective-permute-start | bytes 26312 | tf_op jit(solution)/shard_map/ppermute | solution.py:837
  700.9 8.0 %collective-permute-start.18 = (f32[2192]{0:T(1024)S(1)}, f32[2192]{0:T(1024)S(1)}, u32[]{:S(2)}, u32[]{:S(2)}) collective-permute-start(f32[2192]{0:T(1024)S(1)} %add.568), channel_id=1, source_target_pairs={{0,8},{2,10},{4,12},{6,14},{8,0},{10,2},{12,4},{14,6},{16,24},{18,... | collective-permute-start | bytes 26312 | tf_op jit(solution)/shard_map/ppermute | solution.py:837
  707.4 30.9 %collective-permute-start.6 = (bf16[3,64,512]{2,1,0:T(8,128)(2,1)}, bf16[3,64,512]{2,1,0:T(8,128)(2,1)S(1)}, u32[]{:S(2)}, u32[]{:S(2)}) collective-permute-start(bf16[3,64,512]{2,1,0:T(8,128)(2,1)} %bitcast.187), channel_id=1, source_target_pairs={{0,1},{1,0},{2,3},{3,2},{4,5},{5,4},{6,7},{7,6},{8,9},{9,8},{10,11... | collective-permute-start | bytes 589832 | tf_op jit(solution)/shard_map/ppermute | solution.py:772
  708.9 4.6 collective-permute-start.19
  713.5 9.2 %collective-permute-start.20 = (f32[2192]{0:T(1024)S(1)}, f32[2192]{0:T(1024)S(1)}, u32[]{:S(2)}, u32[]{:S(2)}) collective-permute-start(f32[2192]{0:T(1024)S(1)} %add.570), channel_id=1, source_target_pairs={{0,1},{1,0},{2,3},{3,2},{4,5},{5,4},{6,7},{7,6},{8,9},{9,8},{10,11... | collective-permute-start | bytes 26312 | tf_op jit(solution)/shard_map/ppermute | solution.py:772
  715.3 8.7 %collective-permute-start.8 = (bf16[3,128,512]{2,1,0:T(8,128)(2,1)S(1)}, bf16[3,128,512]{2,1,0:T(8,128)(2,1)S(1)}, u32[]{:S(2)}, u32[]{:S(2)}) collective-permute-start(bf16[3,128,512]{2,1,0:T(8,128)(2,1)S(1)} %bitcast.186), channel_id=1, source_target_pairs={{0,8},{2,10},{4,12},{6,14},{8,0},{10,2},{12,4},{14,6},{16,24},{18,... | collective-permute-start | bytes 1179656 | tf_op jit(solution)/shard_map/ppermute | solution.py:821
  725.1 8.7 %collective-permute-start.9 = (bf16[3,64,512]{2,1,0:T(8,128)(2,1)S(1)}, bf16[3,64,512]{2,1,0:T(8,128)(2,1)S(1)}, u32[]{:S(2)}, u32[]{:S(2)}) collective-permute-start(bf16[3,64,512]{2,1,0:T(8,128)(2,1)S(1)} %fusion.25), channel_id=1, source_target_pairs={{0,16},{2,18},{4,20},{6,22},{8,24},{10,26},{12,28},{14,30},{16,0},... | collective-permute-start | bytes 589832 | tf_op jit(solution)/shard_map/ppermute | solution.py:821
  734.9 7.9 %collective-permute-start.10 = (bf16[3,64,512]{2,1,0:T(8,128)(2,1)S(1)}, bf16[3,64,512]{2,1,0:T(8,128)(2,1)S(1)}, u32[]{:S(2)}, u32[]{:S(2)}) collective-permute-start(bf16[3,64,512]{2,1,0:T(8,128)(2,1)S(1)} %fusion.24), channel_id=1, source_target_pairs={{0,1},{1,0},{2,3},{3,2},{4,5},{5,4},{6,7},{7,6},{8,9},{9,8},{10,11... | collective-permute-start | bytes 589832 | tf_op jit(solution)/shard_map/ppermute | solution.py:772
  737.8 20.5 %collective-permute-start.15 = (bf16[3,64,2048]{2,1,0:T(8,128)(2,1)S(1)}, bf16[3,64,2048]{2,1,0:T(8,128)(2,1)S(1)}, u32[]{:S(2)}, u32[]{:S(2)}) collective-permute-start(bf16[3,64,2048]{2,1,0:T(8,128)(2,1)S(1)} %bitcast.159), channel_id=1, source_target_pairs={{0,1},{1,0},{2,3},{3,2},{4,5},{5,4},{6,7},{7,6},{8,9},{9,8},{10,11... | collective-permute-start | bytes 2359304 | tf_op jit(solution)/shard_map/ppermute | solution.py:772
  743.0 14.5 %collective-permute-start.13 = (bf16[64,1024]{1,0:T(8,128)(2,1)S(1)}, bf16[64,1024]{1,0:T(8,128)(2,1)S(1)}, u32[]{:S(2)}, u32[]{:S(2)}) collective-permute-start(bf16[64,1024]{1,0:T(8,128)(2,1)S(1)} %bitcast.183), channel_id=1, source_target_pairs={{0,1},{1,0},{2,3},{3,2},{4,5},{5,4},{6,7},{7,6},{8,9},{9,8},{10,11... | collective-permute-start | bytes 393224 | tf_op jit(solution)/shard_map/ppermute | solution.py:772
  (55 other events, 731.1 us)
Sparse Core Ops, SparseCore 0:
  76.5 100.9 all-gather.2
  180.3 98.9 all-gather.4
  379.7 58.5 reduce-scatter.7
  588.0 21.9 reduce-scatter.3
  612.1 67.6 reduce-scatter.5

commit v4 on v3

--- a/solution.py
+++ b/solution.py
@@ -12,7 +12,6 @@
 ROPE_BASE = 10000.0
 NEG_FILL = -1e30
 PAIR = 128
-CHUNKS = 2
 KEY_ROWS = 256
 VMEM_BYTES = 48 * 2**20
 NO_COST = pl.CostEstimate(flops=1, bytes_accessed=1, transcendentals=0)
@@ -174,11 +173,6 @@
     )(shard, tokens, times)
 
 
-def column_of(part, column, width):
-    size = width // CHUNKS
-    return (column // size * 3 + part) * size + column % size
-
-
 def qkv_kernel(
     tokens_ref, gain_ref, weight_ref, cos_ref, sin_ref, qgain_ref, kgain_ref,
     k_ref, v_ref, *own_refs,
@@ -191,15 +185,15 @@
     cosine, sine = cos_ref[...], sin_ref[...]
     turned = [(1, k_ref, kgain_ref[...], 1.0)]
     if own_refs:
-        q_ref, raw_ref, normed_ref = own_refs
+        q_ref, *raw_refs, normed_ref = own_refs
         normed_ref[...] = normed
         turned.append((0, q_ref, qgain_ref[...], 0.125))
     for part, out_ref, head_gain, scale in turned:
         for chunk in range(width // 256):
-            start = column_of(part, chunk * 256, width)
+            start = part * width + chunk * 256
             raw = dot(normed, weight_ref[:, start : start + 256])
             if own_refs:
-                raw_ref[:, part * width + chunk * 256 : part * width + (chunk + 1) * 256] = raw
+                raw_refs[part][:, chunk * 256 : (chunk + 1) * 256] = raw
             for tile in range(2):
                 u = raw[:, tile * PAIR : (tile + 1) * PAIR]
                 unit = lax.rsqrt(head_sums(u * u, ones) * (1.0 / 64) + EPSILON)
@@ -208,7 +202,7 @@
                 at = chunk * 256 + tile * PAIR
                 out_ref[:, at : at + PAIR] = (u * scale).astype(bf16)
     for chunk in range(width // 256):
-        start = column_of(2, chunk * 256, width)
+        start = 2 * width + chunk * 256
         v_ref[:, chunk * 256 : (chunk + 1) * 256] = dot(
             normed, weight_ref[:, start : start + 256]
         ).astype(bf16)
@@ -218,7 +212,7 @@
     rows, width = tokens.shape
     sizes = [(width, bf16), (width, bf16)]
     if own:
-        sizes += [(width, bf16), (2 * width, f32), (width, bf16)]
+        sizes += [(width, bf16), (width, f32), (width, f32), (width, bf16)]
     by_rows = lambda i: (i, 0)
     whole = lambda i: (0, 0)
     return pl.pallas_call(
@@ -272,18 +266,20 @@
     out_ref[:, 2 * width :] = read(2, slice(0, width))
 
 
-def merge_grads(chunk, dqs, dkvs, raw, cosine, sine, qgain, kgain, block=256):
-    rows, width = dqs[0].shape
+def merge_grads(width, at, dqs, dkvs, raws, cosine, sine, qgain, kgain, block=256):
+    rows = raws[0].shape[0]
     by_rows = lambda i: (i, 0)
     whole = lambda i: (0, 0)
+    cut = lambda index: pl.BlockSpec((block, width), lambda i: (i, index))
+    cut_two = lambda index: pl.BlockSpec((2, block, width), lambda i: (0, i, index))
     return pl.pallas_call(
         functools.partial(merge_kernel, len(dkvs), len(dqs)),
         grid=(rows // block,),
-        in_specs=[pl.BlockSpec((block, width), by_rows)] * len(dqs)
-        + [pl.BlockSpec((2, block, width), lambda i: (0, i, 0))] * len(dkvs)
+        in_specs=[cut(index) for _, index in dqs]
+        + [cut_two(index) for _, index in dkvs]
         + [
-            pl.BlockSpec((block, width), lambda i: (i, chunk)),
-            pl.BlockSpec((block, width), lambda i: (i, CHUNKS + chunk)),
+            cut(at),
+            cut(at),
             pl.BlockSpec((block, PAIR), by_rows),
             pl.BlockSpec((block, PAIR), by_rows),
             pl.BlockSpec((1, PAIR), whole),
@@ -296,7 +292,7 @@
         ],
         compiler_params=pltpu.CompilerParams(vmem_limit_bytes=VMEM_BYTES),
         cost_estimate=NO_COST,
-    )(*dqs, *dkvs, raw, raw, cosine, sine, qgain, kgain)
+    )(*[array for array, _ in dqs], *[array for array, _ in dkvs], *raws, cosine, sine, qgain, kgain)
 
 
 def forward_kernel(sources, query_rows, flags, q_ref, aq_ref, coef_ref, *refs):
@@ -387,11 +383,7 @@
     )(flags, *operands)
 
 
-def backward_kernel(
-    flags, full_ref, grad_ref, out_ref, aq_ref, k_ref, v_ref, ak_ref,
-    dq_ref, dkv_ref, bias_ref, grads, dq_total,
-):
-    rows = grad_ref.shape[0]
+def backward_start(grad_ref, out_ref, grads, dq_total):
     lane = lane_index()
     half = lane < 64
     mine = (half, jnp.logical_not(half))
@@ -404,33 +396,36 @@
         extra = jnp.where(base[h] == 0, -high, jnp.where(base[h] == 1, -low, zero))
         grads[h] = jnp.where(mine[h], both, extra)
         dq_total[h] = jnp.zeros_like(dq_total[h])
-    for b in range(k_ref.shape[0] // KEY_ROWS):
-        at = slice(b * KEY_ROWS, (b + 1) * KEY_ROWS)
-
-        @pl.when(flags[b] != 0)
-        def _():
-            keys, values, columns = k_ref[at, :], v_ref[at, :], ak_ref[at, :]
-            ones = jnp.ones_like(values)
-            dks, dvs = [], []
-            for h in range(2):
-                keys2 = jnp.where(mine[h], keys, columns)
-                pick = (base[h] >= 0) & (base[h] < 2)
-                values2 = jnp.where(mine[h], values, jnp.where(pick, ones, jnp.zeros_like(ones)))
-                full = full_ref[:, h * PAIR : (h + 1) * PAIR]
-                probs = jnp.exp(dot(keys2, full, NT))
-                score_low = (probs * dot(values2, grads[h], NT)).astype(bf16)
-                dks.append(dot(score_low, full))
-                dvs.append(dot(probs.astype(bf16), grads[h]))
-                dq_total[h] += dot(keys2, score_low, TN)
-            dkv_ref[0, at, :] = jnp.where(half, dks[0], dks[1]).astype(bf16)
-            dkv_ref[1, at, :] = jnp.where(half, dvs[0], dvs[1]).astype(bf16)
-
-        @pl.when(flags[b] == 0)
-        def _():
-            dkv_ref[:, at, :] = jnp.zeros((2, KEY_ROWS, PAIR), bf16)
-
+
+
+def backward_block(full_ref, keys, values, columns, grads, dq_total):
+    lane = lane_index()
+    half = lane < 64
+    mine = (half, jnp.logical_not(half))
+    base = (lane - 64, lane)
+    ones = jnp.ones_like(values)
+    dks, dvs = [], []
+    for h in range(2):
+        keys2 = jnp.where(mine[h], keys, columns)
+        pick = (base[h] >= 0) & (base[h] < 2)
+        values2 = jnp.where(mine[h], values, jnp.where(pick, ones, jnp.zeros_like(ones)))
+        full = full_ref[:, h * PAIR : (h + 1) * PAIR]
+        probs = jnp.exp(dot(keys2, full, NT))
+        score_low = (probs * dot(values2, grads[h], NT)).astype(bf16)
+        dks.append(dot(score_low, full))
+        dvs.append(dot(probs.astype(bf16), grads[h]))
+        dq_total[h] += dot(keys2, score_low, TN)
+    return (
+        jnp.where(half, dks[0], dks[1]).astype(bf16),
+        jnp.where(half, dvs[0], dvs[1]).astype(bf16),
+    )
+
+
+def backward_end(aq_ref, dq_ref, bias_ref, dq_total):
+    lane = lane_index()
+    base = (lane - 64, lane)
     dq = [dq_total[h].T for h in range(2)]
-    dq_ref[...] = jnp.where(half, dq[0], dq[1]) * 0.125
+    dq_ref[...] = jnp.where(lane < 64, dq[0], dq[1]) * 0.125
     variates = aq_ref[...].astype(f32)
     for h in range(2):
         pick = (base[h] >= 0) & (base[h] < 4)
@@ -439,13 +434,33 @@
         )
 
 
-def attend_back(chunk, flags, full, grad, out, query_columns, keys, values, key_columns):
-    rows, width = grad.shape
-    pairs = width // PAIR // CHUNKS
-    width = width // CHUNKS
+def backward_kernel(
+    flags, full_ref, grad_ref, out_ref, aq_ref, k_ref, v_ref, ak_ref,
+    dq_ref, dkv_ref, bias_ref, grads, dq_total,
+):
+    backward_start(grad_ref, out_ref, grads, dq_total)
+    for b in range(k_ref.shape[0] // KEY_ROWS):
+        at = slice(b * KEY_ROWS, (b + 1) * KEY_ROWS)
+
+        @pl.when(flags[b] != 0)
+        def _():
+            dkv_ref[0, at, :], dkv_ref[1, at, :] = backward_block(
+                full_ref, k_ref[at, :], v_ref[at, :], ak_ref[at, :], grads, dq_total
+            )
+
+        @pl.when(flags[b] == 0)
+        def _():
+            dkv_ref[:, at, :] = jnp.zeros((2, KEY_ROWS, PAIR), bf16)
+
+    backward_end(aq_ref, dq_ref, bias_ref, dq_total)
+
+
+def attend_back(first_pair, pairs, flags, full, grad, out, query_columns, keys, values, key_columns):
+    rows = grad.shape[0]
+    width = pairs * PAIR
     key_rows = keys.shape[0]
     by_pair = lambda p, f: (0, p)
-    from_pair = lambda p, f: (0, chunk * pairs + p)
+    from_pair = lambda p, f: (0, first_pair + p)
     whole = lambda p, f: (0, 0)
     return pl.pallas_call(
         backward_kernel,
@@ -479,6 +494,222 @@
         compiler_params=pltpu.CompilerParams(vmem_limit_bytes=VMEM_BYTES),
         cost_estimate=NO_COST,
     )(flags, full, grad, out, query_columns, keys, values, key_columns)
+
+
+LINES = 4
+STARTS = (0, 3, 7, 0)
+ARRIVALS = (7, 10, 13, 4)
+
+
+def line_device(place, line):
+    return {"dp": line * 4 + place % 4}
+
+
+def carry_kernel(
+    pairs, full_ref, grad_ref, out_ref, aq_ref,
+    far_k_ref, far_v_ref, far_ak_ref, near_k_ref, near_v_ref, near_ak_ref,
+    across_ref, own_ref, far_ref, out_across_ref, out_own_ref, out_far_ref,
+    dq_ref, bias_ref, got_ref, near_ref, line_ref, line_got_ref, across_got, out_got,
+    grads, dq_total, stage, near_stage, terms, sums,
+    send_sems, recv_sems, near_sems, across_sems, term_sems, line_send, line_recv, line_own,
+):
+    step = pl.program_id(0)
+    place, rank = lax.axis_index("dp"), lax.axis_index("seq")
+    line = place // 4
+    other = {"seq": 1 - rank}
+    over = {"dp": place + 2 - place // 2 % 2 * 4}
+    mesh_id = pl.DeviceIdType.MESH
+
+    def lanes(index):
+        return pl.ds(pl.multiple_of(index * PAIR, PAIR), PAIR)
+
+    def part_of(refs, part):
+        return refs[1] if part == 3 else refs[0].at[:, part]
+
+    def held(ref, part):
+        return ref.at[:, :, pl.ds(0, out_own_ref.shape[2])] if part == 3 else ref
+
+    def across(part):
+        return pltpu.make_async_remote_copy(
+            src_ref=part_of((across_ref, out_across_ref), part),
+            dst_ref=part_of((across_got, out_got), part),
+            send_sem=across_sems.at[part, 0], recv_sem=across_sems.at[part, 1],
+            device_id=over, device_id_type=mesh_id,
+        )
+
+    def load(part, k):
+        source = part_of(((own_ref, out_own_ref), (far_ref, out_far_ref), (across_got, out_got))[k], part)
+        return pltpu.make_async_copy(source, held(terms.at[k], part), term_sems.at[k])
+
+    def along(part, k):
+        to = lax.rem(line + k, LINES)
+        columns = pl.ds(0, out_own_ref.shape[2] if part == 3 else sums.shape[3])
+        return pltpu.make_async_remote_copy(
+            src_ref=sums.at[part, to, :, columns], dst_ref=line_got_ref.at[k - 1, part, :, columns],
+            send_sem=line_send.at[part, k - 1], recv_sem=line_recv.at[part, k - 1],
+            device_id=line_device(place, to), device_id_type=mesh_id,
+        )
+
+    def stay(part):
+        columns = pl.ds(0, out_own_ref.shape[2] if part == 3 else sums.shape[3])
+        return pltpu.make_async_copy(
+            sums.at[part, line, :, columns], line_ref.at[part, :, columns], line_own.at[part]
+        )
+
+    def to_other(pair):
+        return pltpu.make_async_remote_copy(
+            src_ref=stage.at[pair], dst_ref=got_ref.at[:, :, lanes(pair)], send_sem=send_sems.at[pair],
+            recv_sem=recv_sems.at[pair], device_id=other, device_id_type=mesh_id,
+        )
+
+    def to_near(pair):
+        slot = lax.rem(pair, 2)
+        return pltpu.make_async_copy(
+            near_stage.at[slot], near_ref.at[:, :, lanes(pair)], near_sems.at[slot]
+        )
+
+    @pl.when(step == 0)
+    def _():
+        barrier = pltpu.get_barrier_semaphore()
+        peers = [other, over] + [line_device(place, lax.rem(line + k, LINES)) for k in range(1, LINES)]
+        for target in peers:
+            pl.semaphore_signal(barrier, inc=1, device_id=target, device_id_type=mesh_id)
+        pl.semaphore_wait(barrier, len(peers))
+
+    for part in range(4):
+
+        @pl.when(step == STARTS[part])
+        def _():
+            across(part).start()
+
+        @pl.when(step == ARRIVALS[part] - 1)
+        def _():
+            load(part, 0).start()
+            load(part, 1).start()
+
+        @pl.when(step == ARRIVALS[part])
+        def _():
+            across(part).wait()
+            load(part, 2).start()
+            for k in range(3):
+                load(part, k).wait()
+            columns = out_own_ref.shape[2] if part == 3 else sums.shape[3]
+            for i in range(LINES):
+                sums[part, i, :, :columns] = sum(
+                    terms[k, i, :, :columns].astype(f32) for k in range(3)
+                ).astype(bf16)
+            for k in range(1, LINES):
+                along(part, k).start()
+            stay(part).start()
+
+    @pl.when(step >= pairs + 2)
+    def _():
+        to_near(step - pairs - 2).wait()
+
+    backward_start(grad_ref, out_ref, grads, dq_total)
+    is_far = step < pairs
+    slot = lax.rem(step - jnp.where(is_far, 0, pairs), 2)
+    for b in range(far_k_ref.shape[0] // KEY_ROWS):
+        at = slice(b * KEY_ROWS, (b + 1) * KEY_ROWS)
+        block = [
+            jnp.where(is_far, far[at, :], near[at, :])
+            for far, near in ((far_k_ref, near_k_ref), (far_v_ref, near_v_ref), (far_ak_ref, near_ak_ref))
+        ]
+        dk, dv = backward_block(full_ref, *block, grads, dq_total)
+
+        @pl.when(is_far)
+        def _():
+            stage[step, 0, at, :] = dk
+            stage[step, 1, at, :] = dv
+
+        @pl.when(jnp.logical_not(is_far))
+        def _():
+            near_stage[slot, 0, at, :] = dk
+            near_stage[slot, 1, at, :] = dv
+
+    backward_end(aq_ref, dq_ref, bias_ref, dq_total)
+    pl.when(is_far)(lambda: to_other(step).start())
+    pl.when(jnp.logical_not(is_far))(lambda: to_near(step - pairs).start())
+
+    @pl.when(step == pl.num_programs(0) - 1)
+    def _():
+        to_near(step - pairs - 1).wait()
+        to_near(step - pairs).wait()
+        for pair in range(pairs):
+            to_other(pair).wait()
+        for part in range(4):
+            for k in range(1, LINES):
+                along(part, k).wait()
+            stay(part).wait()
+
+
+def attend_back_carry(full, grad, out, query_columns, near, far, sums, out_sums):
+    rows, width = grad.shape
+    pairs = width // PAIR
+    key_rows = near[0].shape[0]
+    pair_of = lambda i: jnp.where(i < pairs, i, i - pairs)
+    by_pair = lambda i: (0, pair_of(i))
+    far_pair = lambda i: (0, jnp.minimum(i, pairs - 1))
+    near_pair = lambda i: (0, jnp.maximum(i - pairs, 0))
+    whole = lambda i: (0, 0)
+    anywhere = pl.BlockSpec(memory_space=pl.ANY)
+    shard, hidden = sums[0].shape[2:]
+
+    def key_specs(pair):
+        return [
+            pl.BlockSpec((key_rows, PAIR), pair),
+            pl.BlockSpec((key_rows, PAIR), pair),
+            pl.BlockSpec((key_rows, PAIR), whole),
+        ]
+
+    return pl.pallas_call(
+        functools.partial(carry_kernel, pairs),
+        grid=(2 * pairs,),
+        in_specs=[
+            pl.BlockSpec((rows, 2 * PAIR), by_pair),
+            pl.BlockSpec((rows, PAIR), by_pair),
+            pl.BlockSpec((rows, PAIR), by_pair),
+            pl.BlockSpec((rows, PAIR), whole),
+        ]
+        + key_specs(far_pair)
+        + key_specs(near_pair)
+        + [anywhere] * 6,
+        out_specs=[
+            pl.BlockSpec((rows, PAIR), lambda i: (0, i)),
+            pl.BlockSpec((1, 2, PAIR), lambda i: (i, 0, 0)),
+        ]
+        + [anywhere] * 6,
+        out_shape=[
+            jax.ShapeDtypeStruct((rows, 2 * width), f32),
+            jax.ShapeDtypeStruct((2 * pairs, 2, PAIR), f32),
+            jax.ShapeDtypeStruct((2, key_rows, width), bf16),
+            jax.ShapeDtypeStruct((2, key_rows, width), bf16),
+            jax.ShapeDtypeStruct((4, shard, hidden), bf16),
+            jax.ShapeDtypeStruct((LINES - 1, 4, shard, hidden), bf16),
+            jax.ShapeDtypeStruct(sums[0].shape, bf16),
+            jax.ShapeDtypeStruct(out_sums[0].shape, bf16),
+        ],
+        scratch_shapes=[
+            pltpu.VMEM((2, rows, PAIR), bf16),
+            pltpu.VMEM((2, PAIR, rows), f32),
+            pltpu.VMEM((pairs, 2, key_rows, PAIR), bf16),
+            pltpu.VMEM((2, 2, key_rows, PAIR), bf16),
+            pltpu.VMEM((3, LINES, shard, hidden), bf16),
+            pltpu.VMEM((4, LINES, shard, hidden), bf16),
+            pltpu.SemaphoreType.DMA((pairs,)),
+            pltpu.SemaphoreType.DMA((pairs,)),
+            pltpu.SemaphoreType.DMA((2,)),
+            pltpu.SemaphoreType.DMA((4, 2)),
+            pltpu.SemaphoreType.DMA((3,)),
+            pltpu.SemaphoreType.DMA((4, LINES - 1)),
+            pltpu.SemaphoreType.DMA((4, LINES - 1)),
+            pltpu.SemaphoreType.DMA((4,)),
+        ],
+        compiler_params=pltpu.CompilerParams(
+            vmem_limit_bytes=VMEM_BYTES, collective_id=3, has_side_effects=True
+        ),
+        cost_estimate=NO_COST,
+    )(full, grad, out, query_columns, *far, *near, *sums, *out_sums)
 
 
 def slot_columns(segment, variates):
@@ -756,6 +987,192 @@
     )(spot, left, right)
 
 
+def finish_kernel(
+    far_ref, cross_ref, own_ref, line_ref, line_got_ref, first_ref, small_ref,
+    merged_ref, weight_ref, tokens_ref, resid_ref, gain_ref,
+    in_ref, first_out_ref, second_out_ref, small_out_ref, grad_ref,
+    core_got, x_sent, x_got, z_sent, z_got, y_sent, y_got, first_got, second, second_got, small_sent, small_got,
+    merged, weight, tokens, resid, grad,
+    core_sems, x_sems, z_send, z_recv, y_sems, first_sems, second_sems, small_sems, load_sems, store_sem,
+):
+    place, rank = lax.axis_index("dp"), lax.axis_index("seq")
+    line = place // 4
+    mesh_id = pl.DeviceIdType.MESH
+    twin = {"dp": place + 1 - place % 2 * 2}
+    over = {"dp": place + 2 - place // 2 % 2 * 4}
+    other = {"seq": 1 - rank}
+    lines = [line_device(place, lax.rem(line + k, LINES)) for k in range(1, LINES)]
+    low = line_device(place, line + 1 - line % 2 * 2)
+    high = line_device(place, lax.rem(line + 2, LINES))
+    blocks, quarter = cross_ref.shape[:2]
+    shard = quarter // LINES
+
+    def send(source, target, sems, to):
+        return pltpu.make_async_remote_copy(
+            src_ref=source, dst_ref=target, send_sem=sems[0], recv_sem=sems[1],
+            device_id=to, device_id_type=mesh_id,
+        )
+
+    def pair_of(sems, *index):
+        return sems.at[*index, 0], sems.at[*index, 1]
+
+    to_core = [send(far_ref.at[b], core_got.at[b], pair_of(core_sems, b), twin) for b in range(blocks)]
+    to_x = [send(x_sent.at[b], x_got.at[b], pair_of(x_sems, b), over) for b in range(blocks)]
+    to_y = [send(y_sent.at[b], y_got.at[b], pair_of(y_sems, b), other) for b in range(blocks)]
+    first_y = send(first_ref, first_got, pair_of(first_sems), other)
+    second_y = send(second, second_got, pair_of(second_sems), other)
+    rounds = [
+        send(small_sent.at[k], small_got.at[k], pair_of(small_sems, k), to)
+        for k, to in enumerate((twin, over, low, high, other))
+    ]
+
+    def to_z(b, k):
+        return send(
+            z_sent.at[b, lax.rem(line + k, LINES)], z_got.at[b, k - 1],
+            (z_send.at[b, k - 1], z_recv.at[b, k - 1]), lines[k - 1],
+        )
+
+    loads = [
+        pltpu.make_async_copy(source, target, load_sems.at[k])
+        for k, (source, target) in enumerate(
+            ((merged_ref, merged), (weight_ref.at[:, pl.ds(0, weight.shape[1])], weight),
+             (tokens_ref, tokens), (resid_ref, resid))
+        )
+    ]
+    store = pltpu.make_async_copy(grad, grad_ref, store_sem.at[0])
+
+    barrier = pltpu.get_barrier_semaphore()
+    peers = [twin, over, other] + lines
+    for target in peers:
+        pl.semaphore_signal(barrier, inc=1, device_id=target, device_id_type=mesh_id)
+    pl.semaphore_wait(barrier, len(peers))
+    for copy in to_core + [first_y] + loads:
+        copy.start()
+    second[...] = sum(
+        part.astype(f32) for part in [line_ref[...]] + [line_got_ref[k] for k in range(LINES - 1)]
+    ).astype(bf16)
+    second_y.start()
+    for b in range(blocks):
+        to_core[b].wait()
+        x_sent[b] = (cross_ref[b].astype(f32) + core_got[b, :quarter].astype(f32)).astype(bf16)
+        to_x[b].start()
+
+    for copy in loads:
+        copy.wait()
+    gain = gain_ref[...]
+    rows = tokens.shape[0]
+    step = min(256, rows)
+    gain_grad = jnp.zeros_like(gain)
+    for i in range(rows // step):
+        at = slice(i * step, (i + 1) * step)
+        normed_grad = dot(merged[at, :], weight[...], NT)
+        values = tokens[at, :].astype(f32)
+        inv = lax.rsqrt(jnp.mean(values * values, axis=-1, keepdims=True) + EPSILON)
+        hat = values * inv
+        weighted = normed_grad * gain
+        inner = jnp.mean(weighted * hat, axis=-1, keepdims=True)
+        grad[at, :] = resid[at, :] + inv * (weighted - hat * inner)
+        gain_grad = gain_grad + jnp.sum(normed_grad * hat, axis=0, keepdims=True)
+    store.start()
+    small_sent[0] = small_ref[...]
+    for k in range(gain.shape[1] // PAIR):
+        small_sent[0, k : k + 1, :] = gain_grad[:, k * PAIR : (k + 1) * PAIR]
+    rounds[0].start()
+
+    def next_round(k):
+        rounds[k].wait()
+        total = small_sent[k] + small_got[k]
+        if k + 1 < len(rounds):
+            small_sent[k + 1] = total
+            rounds[k + 1].start()
+        else:
+            small_out_ref[...] = total
+
+    next_round(0)
+    for b in range(blocks):
+        to_x[b].wait()
+        total = own_ref[b].astype(f32) + core_got[b, quarter:].astype(f32) + x_got[b].astype(f32)
+        total = total.astype(bf16)
+        for k in range(LINES):
+            z_sent[b, k] = total[k * shard : (k + 1) * shard, :]
+        for k in range(1, LINES):
+            to_z(b, k).start()
+    next_round(1)
+    first_y.wait()
+    first_out_ref[...] = first_ref[...].astype(f32) + first_got[...].astype(f32)
+    second_y.wait()
+    second_out_ref[...] = second[...].astype(f32) + second_got[...].astype(f32)
+    for b in range(blocks):
+        for k in range(1, LINES):
+            to_z(b, k).wait()
+        total = z_sent[b, line].astype(f32)
+        for k in range(LINES - 1):
+            total = total + z_got[b, k].astype(f32)
+        y_sent[b] = total.astype(bf16)
+        to_y[b].start()
+    for k in range(2, len(rounds)):
+        next_round(k)
+    for b in range(blocks):
+        to_y[b].wait()
+        in_ref[b] = y_sent[b].astype(f32) + y_got[b].astype(f32)
+    store.wait()
+
+
+def finish(in_grads, line_sums, line_got, first, small, merged, weight, tokens, resid, gain):
+    far, cross, own = in_grads
+    blocks, quarter, columns = cross.shape
+    shard = quarter // LINES
+    rows, width = tokens.shape
+    vmem = pl.BlockSpec(memory_space=pltpu.VMEM)
+    anywhere = pl.BlockSpec(memory_space=pl.ANY)
+    dma = pltpu.SemaphoreType.DMA
+    return pl.pallas_call(
+        finish_kernel,
+        in_specs=[vmem] * 7 + [anywhere] * 4 + [vmem],
+        out_specs=[vmem] * 4 + [anywhere],
+        out_shape=[
+            jax.ShapeDtypeStruct((blocks, shard, columns), f32),
+            jax.ShapeDtypeStruct(first.shape, f32),
+            jax.ShapeDtypeStruct(line_sums.shape, f32),
+            jax.ShapeDtypeStruct(small.shape, f32),
+            jax.ShapeDtypeStruct((rows, width), f32),
+        ],
+        scratch_shapes=[
+            pltpu.VMEM(far.shape, bf16),
+            pltpu.VMEM(cross.shape, bf16),
+            pltpu.VMEM(cross.shape, bf16),
+            pltpu.VMEM((blocks, LINES, shard, columns), bf16),
+            pltpu.VMEM((blocks, LINES - 1, shard, columns), bf16),
+            pltpu.VMEM((blocks, shard, columns), bf16),
+            pltpu.VMEM((blocks, shard, columns), bf16),
+            pltpu.VMEM(first.shape, bf16),
+            pltpu.VMEM(line_sums.shape, bf16),
+            pltpu.VMEM(line_sums.shape, bf16),
+            pltpu.VMEM((5, *small.shape), f32),
+            pltpu.VMEM((5, *small.shape), f32),
+            pltpu.VMEM(merged.shape, bf16),
+            pltpu.VMEM(merged.shape, bf16),
+            pltpu.VMEM((rows, width), bf16),
+            pltpu.VMEM((rows, width), f32),
+            pltpu.VMEM((rows, width), f32),
+            dma((blocks, 2)),
+            dma((blocks, 2)),
+            dma((blocks, LINES - 1)),
+            dma((blocks, LINES - 1)),
+            dma((blocks, 2)),
+            dma((2,)),
+            dma((2,)),
+            dma((5, 2)),
+            dma((4,)),
+            dma((1,)),
+        ],
+        compiler_params=pltpu.CompilerParams(
+            vmem_limit_bytes=56 * 2**20, collective_id=4, has_side_effects=True
+        ),
+        cost_estimate=NO_COST,
+    )(far, cross, own, line_sums, line_got, first, small, merged, weight, tokens, resid, gain)
+
+
 def rms_forward(values, gain_vec):
     inv_rms = lax.rsqrt(jnp.mean(values * values, axis=-1, keepdims=True) + EPSILON)
     return (values * inv_rms * gain_vec, inv_rms)
@@ -801,24 +1218,6 @@
 
 def total_of(terms):
     return jnp.concatenate([sum(term.astype(f32) for term in held) for held in terms], axis=0).astype(bf16)
-
-
-def halve(terms, step, places):
-    mine = lax.axis_index("dp") // 4 // 2**step % 2
-
-    def cut(value, which):
-        blocks, rows, columns = value.shape
-        left = places // 4 // 2**step
-        value = value.reshape(blocks, left // 2, 2, rows // left, columns)
-        value = lax.dynamic_index_in_dim(value, which, 2, keepdims=False)
-        return value.reshape(blocks, rows // 2, columns)
-
-    sent = total_of([[cut(term, 1 - mine) for term in held] for held in terms])
-    return sent, [[cut(term, mine) for term in held] for held in terms]
-
-
-def cross_z(values, step, places):
-    return lax.ppermute(values, "dp", [(i, i ^ (4 * 2**step)) for i in range(places)])
 
 
 def sum_seq(values, count):
@@ -866,12 +1265,11 @@
 
     gains = jnp.stack([attn_gain, ffn_gain], axis=1)
     gather = lambda w: lax.all_gather(w, "dp", axis=0, tiled=True)
-    in_chunks = in_proj.reshape(-1, 3, CHUNKS, width // CHUNKS).transpose(0, 2, 1, 3)
-    in_chunks = in_chunks.reshape(in_proj.shape)
     first_shard = jnp.concatenate(
-        [in_chunks, out_proj, jnp.pad(gains, ((0, 0), (0, PAIR - 2)))], axis=1
+        [in_proj, out_proj, jnp.pad(gains, ((0, 0), (0, PAIR - 2)))], axis=1
     )
-    if places == 16 and seq_count == 2:
+    fused = places == 16 and seq_count == 2
+    if fused:
         wide, *there = gather_first(first_shard, tokens, time_ids.reshape(-1, PAIR), places)
         slots = [(tokens, time_ids), (there[0], there[1].reshape(-1))]
     else:
@@ -936,7 +1334,7 @@
         keyed.append((keys, values, source_columns[step]))
         if step == 0:
             cosine, sine = tables[0]
-            queries, raw, normed_low = own
+            queries, *raws, normed_low = own
             ffn_weights[1] = gather(after(ffn_weights[1], queries))
     attended, full_query = attend(
         jnp.concatenate(source_flags), queries, query_columns, coefficients, keyed
@@ -970,100 +1368,70 @@
     attended_grad = dot(mixed_low, out_full, NT).astype(bf16)
 
     attended_grad = dot(mixed_low, out_full, NT).astype(bf16)
-    out_crossed, out_terms = core_sum([outer(spot, attended, mixed_low, width)], places)
-    steps = (places // 4).bit_length() - 1
-    attended_grad = after(attended_grad, out_crossed, second_crossed)
-    second_across = cross_x(second_crossed, places)
-    out_across = cross_x(out_crossed, places)
-
-    remote = list(range(1, seq_count))
-    dqs = [[] for _ in range(CHUNKS)]
-    dkvs = [[] for _ in range(CHUNKS)]
-    biases = [0.0] * CHUNKS
-
-    def back(chunk, sources, grad):
-        for step in sources:
+    out_grads = outer(spot, attended, mixed_low, width)
+    folds = hidden_part // shard
+    ffn_gain_sum = jnp.sum(ffn_gain_terms, axis=0)
+
+    def merge(dqs, dkvs):
+        merged, gains = merge_grads(width, 0, dqs, dkvs, raws, cosine, sine, qgain, kgain)
+        return merged, jnp.sum(gains[:2].reshape(2, -1, head_dim), axis=1)
+
+    def small_parts(bias, head_gains):
+        same_bias = jnp.sum(bias, axis=-1).reshape(-1)
+        tail = jnp.concatenate([head_gains[0], head_gains[1], same_bias])
+        return jnp.concatenate([ffn_gain_sum, tail, jnp.zeros(-tail.shape[0] % 1024, f32)])
+
+    if fused:
+        (out_far,), out_cross, out_own = (cross_core(out_grads[0], places),), *out_grads[1:]
+        by_line = lambda array: array.reshape(groups, -1, width)
+        out_sums = [
+            by_line(array) for array in (out_cross + out_far[:, : shard * groups], out_own, out_far[:, shard * groups :])
+        ]
+        dq_all, bias_all, received, own_kv, line_sums, line_got, *_ = attend_back_carry(
+            full_query, attended_grad, attended, query_columns, keyed[0], keyed[1],
+            (second_crossed, own, far[groups:]), out_sums,
+        )
+        merged_grad, head_gains = merge([(dq_all, 0), (dq_all, 1)], [(received, 0), (own_kv, 0)])
+        in_grads = outer(spot, normed_low, merged_grad, width)
+        half = bias_all.shape[0] // 2
+        small = small_parts(bias_all[:half] + bias_all[half:], head_gains)
+        small = jnp.concatenate([jnp.zeros(width, f32), small]).reshape(-1, PAIR)
+        in_sum, first_sum, second_sum, small, input_grad = finish(
+            in_grads, line_sums, line_got, first_total, small, merged_grad, wide, tokens,
+            residual_grad, attn_gain_f,
+        )
+        small = small.reshape(-1)
+        out_proj_grad = second_sum[3, :, :width]
+    else:
+        second = scatter_line(x_part(cross_x(second_crossed, places), own, far))
+        dqs, dkvs, biases = [], [], 0.0
+        for step in list(range(1, seq_count)) + [0]:
             dq, dkv, bias = attend_back(
-                chunk, source_flags[step], full_query, grad, attended, query_columns, *keyed[step]
+                0, width // PAIR, source_flags[step], full_query, attended_grad, attended,
+                query_columns, *keyed[step],
             )
-            grad = after(grad, dkv)
-            dqs[chunk].append(dq)
-            dkvs[chunk].append(shift_by(dkv, seq_count, step) if step else dkv)
-            biases[chunk] = biases[chunk] + bias
-        return grad
-
-    def merge(chunk):
-        return merge_grads(chunk, dqs[chunk], dkvs[chunk], raw, cosine, sine, qgain, kgain)
-
-    def chunk_weights(chunk):
-        return wide[:, chunk * 3 * width // CHUNKS : (chunk + 1) * 3 * width // CHUNKS]
-
-    def finish_line(terms, sent, first):
-        for step in range(first, steps):
-            terms = add_received(terms, cross_z(sent, step, places))
-            if step + 1 < steps:
-                sent, terms = halve(terms, step + 1, places)
-        return total_of(terms)
-
-    def line_of(terms):
-        total = total_of(terms)
-        blocks, rows, columns = total.shape
-        return total.reshape(blocks, groups, rows // groups, columns).transpose(1, 0, 2, 3)
-
-    grad = back(0, remote, attended_grad)
-    grad = back(1, remote, grad)
-    grad = back(0, [0], grad)
-    second_across = after(second_across, grad)
-    second = x_part(second_across, own, far).reshape(groups, -1, second_across.shape[-1])
-    out_total = line_of(add_received(out_terms, out_across))
-    folds = second.shape[-1] // width
-    out_total = out_total.reshape(groups, folds, -1, width).transpose(0, 2, 1, 3)
-    out_total = out_total.reshape(groups, -1, folds * width)
-    second = scatter_line(jnp.concatenate([second, out_total], axis=1))
-    dqs[0][0] = after(dqs[0][0], grad)
-    merged_0, gains_0 = merge(0)
-    crossed, in_terms_0 = core_sum([outer(spot, normed_low, merged_0, width // CHUNKS)], places)
-    normed_grad_0 = dot(merged_0, chunk_weights(0), NT)
-    grad = after(grad, crossed, normed_grad_0)
-    in_across_0 = cross_x(crossed, places)
-    grad = back(1, [0], grad)
-    dqs[1][0] = after(dqs[1][0], grad, in_across_0)
-    in_total_0 = scatter_line(line_of(add_received(in_terms_0, in_across_0)))
-
-    merged_1, gains_1 = merge(1)
-    crossed, in_terms_1 = core_sum([outer(spot, normed_low, merged_1, width // CHUNKS)], places)
-    in_terms_1 = add_received(in_terms_1, cross_x(crossed, places))
-    normed_grad = normed_grad_0 + dot(after(merged_1, crossed), chunk_weights(1), NT)
-    sent, in_terms_1 = halve(in_terms_1, 0, places)
-    in_total_1 = finish_line(in_terms_1, sent, 0)
-    second_total = second[: 3 * shard].reshape(3, shard, -1)
-    out_total = second[3 * shard :].reshape(-1, folds, width).transpose(1, 0, 2).reshape(shard, width)
-    out_proj_grad = sum_seq(out_total, seq_count)
-    first_sum = sum_seq(first_total, seq_count)
-    second_sum = sum_seq(second_total, seq_count)
-    in_sum = jnp.concatenate(
-        [sum_seq(in_total_0, seq_count), sum_seq(in_total_1, seq_count)], axis=2
-    )
-    norm_scale = lax.rsqrt(jnp.mean(inputs_f * inputs_f, axis=-1, keepdims=True) + EPSILON)
-    input_norm_grad, attn_gain_terms = rms_backward(inputs_f, norm_scale, attn_gain_f, normed_grad)
-    input_grad = residual_grad + input_norm_grad
-
-    same_bias = jnp.concatenate([jnp.sum(bias, axis=-1).reshape(-1) for bias in biases])
-    heads = same_bias.shape[0]
-    head_gains = sum(jnp.sum(part[:2].reshape(2, -1, head_dim), axis=1) for part in (gains_0, gains_1))
-    small = sum_small(
-        jnp.concatenate(
-            [
-                jnp.sum(attn_gain_terms, axis=0),
-                jnp.sum(ffn_gain_terms, axis=0),
-                head_gains[0],
-                head_gains[1],
-                same_bias,
-            ]
-        ),
-        places,
-        seq_count,
-    )
+            dqs.append((dq, 0))
+            dkvs.append((shift_by(dkv, seq_count, step) if step else dkv, 0))
+            biases = biases + bias
+        merged_grad, head_gains = merge(dqs, dkvs)
+
+        def sum_rows(pieces):
+            crossed, terms = core_sum([pieces], places)
+            total = total_of(add_received(terms, cross_x(crossed, places)))
+            total = total.reshape(total.shape[0], groups, shard, -1).transpose(1, 0, 2, 3)
+            return sum_seq(scatter_line(total), seq_count)
+
+        in_sum = sum_rows(outer(spot, normed_low, merged_grad, width))
+        out_proj_grad = sum_rows(out_grads)[0]
+        first_sum = sum_seq(first_total, seq_count)
+        second_sum = sum_seq(second, seq_count)
+        normed_grad = dot(merged_grad, wide[:, : 3 * width], NT)
+        norm_scale = lax.rsqrt(jnp.mean(inputs_f * inputs_f, axis=-1, keepdims=True) + EPSILON)
+        input_norm_grad, attn_gain_terms = rms_backward(inputs_f, norm_scale, attn_gain_f, normed_grad)
+        input_grad = residual_grad + input_norm_grad
+        small = jnp.concatenate([jnp.sum(attn_gain_terms, axis=0), small_parts(biases, head_gains)])
+        small = sum_small(small, places, seq_count)
+    heads = head_bias.shape[0]
     in_proj_grad = in_sum.transpose(1, 0, 2).reshape(in_proj.shape)
     down_grad = jnp.concatenate(
         [

time: 780 us -> 655 us (0.84)
  waiting for transfers between devices: 151 us -> 15 us
  Pallas kernels: 440 us -> 519 us
  other arithmetic: 66.3 us -> 41.5 us
  starting transfers between devices: 20.7 us -> 0.58 us
  matrix products: 27.6 us -> 9.04 us
    ppermute x18 -> x0, waiting for transfers between devices: 132 us -> none  [the longest x4 89.8 us: cross_x(): return lax.ppermute(values, 'dp', [(i, i ^ 2) for i in range(places)])]
    pallas_call x4 -> x2, Pallas kernels: 114 us -> 198 us  [the longest x1 128 us: attend_back_carry(): pl.pallas_call(functools.partial(carry_kernel, pairs), grid=(2 * pairs,),...]
    ppermute x18 -> x0, starting transfers between devices: 19.7 us -> none  [the longest x8 9.51 us: shift_by(): lax.ppermute(values, 'seq', [(i, (i + step) % count) for i in range(count)])]
    dot_general x4 -> x2, matrix products: 27.6 us -> 9.04 us  [dot(): return lax.dot_general(left, right, dims, preferred_element_type=f32)]
    add x16 -> x0, other arithmetic: 15.1 us -> none  [the longest x1 5.57 us: body(): input_grad = residual_grad + input_norm_grad]
    pallas_call x2, Pallas kernels: 135 us -> 148 us  [feed_forward(): pl.pallas_call(functools.partial(ffn_kernel, places, first), grid=(steps,...]
    pallas_call x1, Pallas kernels: 63 us -> 49.9 us  [attend(): pl.pallas_call(functools.partial(forward_kernel, sources, min(512, rows))...]
    unnamed x111 -> x90, local copies, waits for them, and re-layouts: 22.7 us -> 19.2 us
  transfers between devices with their start and end apart: 26 -> 4, of which waited for: 13 -> 1; matrix products, arithmetic and copies ran while one was open for 13% -> 6% of each run, Pallas kernels for 38% -> 48%
where the time goes in v4:
time: 655 us; the launch traced here: 650 us
  Pallas kernels  519 us (79%)
  local copies, waits for them, and re-layouts  48.6 us (7%)
  other arithmetic  41.5 us (6%)
  between operations  16.1 us (2%)
  waiting for transfers between devices  15 us (2%)
  matrix products  9.04 us (1%)
    pallas_call x2, Pallas kernels, feed_forward(): pl.pallas_call(functools.partial(ffn_kernel, places, first), grid=(steps,...  148 us
    pallas_call x1, Pallas kernels, attend_back_carry(): pl.pallas_call(functools.partial(carry_kernel, pairs), grid=(2 * pairs,),...  128 us
    pallas_call x1, Pallas kernels, finish(): pl.pallas_call(finish_kernel, in_specs=[vmem] * 7 + [anywhere] * 4 + [vme...  69.5 us
    pallas_call x1, Pallas kernels, gather_first(): pl.pallas_call(gather_kernel, in_specs=[anywhere] * 3, out_specs=[anywher...  57.4 us
    pallas_call x1, Pallas kernels, attend(): pl.pallas_call(functools.partial(forward_kernel, sources, min(512, rows))...  49.9 us
    pallas_call x2, Pallas kernels, project(): pl.pallas_call(qkv_kernel, grid=(rows // block,), in_specs=[pl.BlockSpec(...  35.5 us
    unnamed x90, local copies, waits for them, and re-layouts  19.2 us
    pallas_call x2, Pallas kernels, outer(): pl.pallas_call(functools.partial(outer_kernel, places), grid_spec=pltpu.P...  15.8 us
  transfers between devices with their start and end apart: 4, of which 1 were waited for; matrix products, arithmetic and copies ran while one was open for 6% of the time, Pallas kernels for 48%

profile of v4, /device:TPU:0, one launch (start us, length us, event | category | flops | bytes accessed | tf_op | source)
XLA Modules:
  0.0 650.2 jit_solution(371990029047209466)
XLA Ops:
  9.9 5.9 slice_reduce_fusion.1
  16.9 57.4 %shard_map.221 = (bf16[1024,4224]{1,0:T(8,128)(2,1)}, bf16[1024,1024]{1,0:T(8,128)(2,1)}, s32[8,128]{1,0:T(8,128)}) custom-call(bf16[64,4224]{1,0:T(8,128)(2,1)} %fusion.4.shard_ref, bf16[1024,1024]{1,0:T(8,128)(2,1)} %tokens_ref.5, s32[8,128]{1,0:T(8,128)} %bitcast.136), custom_call_target="tpu_custom_call" | custom-call | flops 1 | bytes 1 | tf_op jit(solution)/shard_map/pallas_call | solution.py:157
  77.5 3.7 fusion.6
  81.3 22.4 %shard_map.222 = (bf16[1024,1024]{1,0:T(8,128)(2,1)S(1)}, bf16[1024,1024]{1,0:T(8,128)(2,1)S(1)}, bf16[1024,1024]{1,0:T(8,128)(2,1)}, f32[1024,1024]{1,0:T(8,128...) custom-call(bf16[1024,1024]{1,0:T(8,128)(2,1)} %tokens_ref.5, f32[1,1024]{1,0:T(1,128)S(1)} %bitcast.109, ...), custom_call_target="tpu_custom_call" | custom-call | flops 1 | bytes 1 | tf_op jit(solution)/shard_map/pallas_call | solution.py:218
  106.7 13.1 %shard_map.223 = (bf16[1024,1024]{1,0:T(8,128)(2,1)S(1)}, bf16[1024,1024]{1,0:T(8,128)(2,1)S(1)}) custom-call(bf16[1024,1024]{1,0:T(8,128)(2,1)} %get-tuple-element.60.tokens_ref, f32[1,1024]{1,0:T(1,128)S(1)} %bitcast.110, bf16[1024,4224]{1,0:T(8,128)(2,1)} %get-tuple-element.56.weight_ref, f32[1024,128]{1,0:T(8,128)S(1)} %get-tuple-element.131.cos_ref, ...), custom_call_target="tpu_custom_call" | custom-call | flops 1 | bytes 1 | tf_op jit(solution)/shard_map/pallas_call | solution.py:218
  130.8 49.9 %shard_map.224 = (bf16[1024,1024]{1,0:T(8,128)(2,1)S(1)}, bf16[1024,2048]{1,0:T(8,128)(2,1)}) custom-call(s32[8]{0:T(128)S(1)} %add_convert_fusion.1.flags, bf16[1024,1024]{1,0:T(8,128)(2,1)S(1)} %copy-done.11, bf16[1024,128]{1,0:T(8,128)(2,1)S(1)} %select_convert_fusion.aq_ref, bf16[8,2,128]{2,1,0:T(2,128)(2,1)S(1)} %bitcast.112, ...), custom_call_target="tpu_custom_call" | custom-call | flops 1 | bytes 1 | tf_op jit(solution)/shard_map/pallas_call | solution.py:362
  180.8 4.9 multiply_reduce_fusion.2
  190.0 68.7 %shard_map.225 = (f32[1024,1024]{1,0:T(8,128)}, f32[1024,1024]{1,0:T(8,128)}, bf16[8,3,64,2048]{3,2,1,0:T(8,128)(2,1)}, bf16[4,3,64,2048]{3,2,1,0:T(8,128)(2,1)}, bf16[4,3,64,2048]{3,2,1,0:T(8,128)(2,1)}) custom-call(bf16[1024,1024]{1,0:T(8,128)(2,1)} %multiply_convert_fusion.nf_ref, bf16[1024,1024]{1,0:T(8,128)(2,1)} %fusion.seed_ref, ...), custom_call_target="tpu_custom_call" | custom-call | flops 1 | bytes 1 | tf_op jit(solution)/shard_map/pallas_call | solution.py:902
  258.7 4.8 slice_add_fusion.1.refs_0_
  263.6 14.9 %all-gather.5.cloned.1.call-done.wg_ref.wu_ref.wd_ref = bf16[1024,6144]{1,0:T(8,128)(2,1)} async-done(((bf16[64,6144]{1,0:T(8,128)(2,1)}), bf16[1024,6144]{1,0:T(8,128)(2,1)}) %all-gather.5.cloned.1.call-update) | async-done | bytes 12582928 | tf_op jit(solution)/shard_map/all_gather | solution.py:1267
  278.5 79.2 %shard_map.226 = (bf16[1024,1024]{1,0:T(8,128)(2,1)}, f32[1024,1024]{1,0:T(8,128)}, bf16[8,3,64,2048]{3,2,1,0:T(8,128)(2,1)}, bf16[4,3,64,2048]{3,2,1,0:T(8,128)...) custom-call(bf16[1024,1024]{1,0:T(8,128)(2,1)} %multiply_convert_fusion.nf_ref, ...), custom_call_target="tpu_custom_call" | custom-call | flops 1 | bytes 1 | tf_op jit(solution)/shard_map/pallas_call | solution.py:902
  357.7 6.9 %add_convert_fusion = bf16[4,3,64,2048]{3,2,1,0:T(8,128)(2,1)} fusion(bf16[4,3,64,2048]{3,2,1,0:T(8,128)(2,1)S(1)} %copy-done.23, bf16[4,3,64,2048]{3,2,1,0:T(8,128)(2,1)} %get-tuple-element.92, bf16[8,3,64,2048]{3,2,1,0:T(8,128)(2,1)} %get-tuple-element.70), kind=kLoop, calls=%fused_computation | loop fusion | flops 9437184 | bytes 12582912 | tf_op jit(solution)/shard_map/convert_element_type | solution.py:1349
  364.8 4.6 multiply_reduce_fusion
  371.3 5.0 fusion.13
  376.3 5.2 shard_map.227
  381.7 4.1 convolution_convert_fusion.grad_ref
  386.0 2.9 fusion.14
  389.0 128.4 %shard_map.228 = (f32[1024,2048]{1,0:T(8,128)}, f32[16,2,128]{2,1,0:T(2,128)S(1)}, bf16[2,1024,1024]{2,1,0:T(8,128)(2,1)}, bf16[2,1024,1024]{2,1,0:T(8,128)(2,1)...) custom-call(bf16[1024,2048]{1,0:T(8,128)(2,1)} %get-tuple-element.73, ...), custom_call_target="tpu_custom_call" | custom-call | flops 1 | bytes 1 | tf_op jit(solution)/shard_map/pallas_call | solution.py:665
  518.5 2.2 copy-done.5
  520.6 14.9 %shard_map.229 = (bf16[1024,3072]{1,0:T(8,128)(2,1)}, f32[8,1024]{1,0:T(8,128)S(1)}) custom-call(f32[1024,2048]{1,0:T(8,128)} %get-tuple-element.81.refs_0_.refs_1_, f32[1024,2048]{1,0:T(8,128)} %get-tuple-element.81.refs_0_.refs_1_, bf16[2,1024,1024]{2,1,0:T(8,128)(2,1)S(1)} %copy-done.5, bf16[2,1024,1024]{2,1,0:T(8,128)(2,1)} %get-tuple-element.83.refs_3_, ...), custom_call_target="tpu_custom_call" | custom-call | flops 1 | bytes 1 | tf_op jit(solution)/shard_map/pallas_call | solution.py:275
  535.6 10.5 %shard_map.230 = (bf16[3,512,1024]{2,1,0:T(8,128)(2,1)}, bf16[3,256,1024]{2,1,0:T(8,128)(2,1)S(1)}, bf16[3,256,1024]{2,1,0:T(8,128)(2,1)S(1)}) custom-call(s32[18]{0:T(128)S(1)} %stack.105.spot, bf16[1024,1024]{1,0:T(8,128)(2,1)S(1)} %copy-done.10, bf16[1024,3072]{1,0:T(8,128)(2,1)} %get-tuple-element.86.right_ref.merged_ref), custom_call_target="tpu_custom_call" | custom-call | flops 1 | bytes 1 | tf_op jit(solution)/shard_map/pallas_call | solution.py:964
  549.4 69.5 %shard_map.231 = (f32[3,64,1024]{2,1,0:T(8,128)}, f32[3,64,2048]{2,1,0:T(8,128)}, f32[4,64,2048]{2,1,0:T(8,128)}, f32[24,128]{1,0:T(8,128)}, f32[1024,1024]{1,0:T(8,128)}) custom-call(bf16[3,512,1024]{2,1,0:T(8,128)(2,1)} %get-tuple-element.87.far_ref, bf16[3,256,1024]{2,1,0:T(8,128)(2,1)} %copy-done.12, bf16[3,256,1024]{2,1,0:T(8,128)(2,1)} %copy-done.13, ...), custom_call_target="tpu_custom_call" | custom-call | flops 1 | bytes 1 | tf_op jit(solution)/shard_map/pallas_call | solution.py:1129
  631.7 2.7 reshape.223
  634.4 2.2 copy.61
  (172 shorter events, 49.9 us)
Async XLA Ops:
  7.2 182.9 %all-gather.3.cloned.1.call-start = ((), (), s32[]{:S(2)}) async-start(), calls=%async_computation.1 | async-start | bytes 13369344 | tf_op jit(solution)/shard_map/all_gather | solution.py:1267
  9.8 6.2 copy-start.29
  9.8 6.2 copy-start.30
  9.8 6.2 copy-start.31
  16.9 58.9 %copy-start.32 = (s32[1024]{0:T(1024)S(1)}, s32[1024]{0:T(1024)}, u32[]{:S(2)}) copy-start(s32[1024]{0:T(1024)} %param.17) | copy-start | bytes 12292
  16.9 59.0 %copy-start.37 = (f32[64]{0:T(128)S(1)}, f32[64]{0:T(128)}, u32[]{:S(2)}) copy-start(f32[64]{0:T(128)} %param.24) | copy-start | bytes 772
  16.9 59.1 %copy-start.38 = (f32[64]{0:T(128)S(1)}, f32[64]{0:T(128)}, u32[]{:S(2)}) copy-start(f32[64]{0:T(128)} %param.25) | copy-start | bytes 772
  75.6 202.9 %all-gather.5.cloned.1.call-start = ((), (), s32[]{:S(2)}) async-start(), calls=%async_computation.2 | async-start | bytes 13369344 | tf_op jit(solution)/shard_map/all_gather | solution.py:1267
  77.5 29.2 %copy-start.15 = (f32[1024]{0:T(1024)}, f32[1024]{0:T(1024)S(1)}, u32[]{:S(2)}) copy-start(f32[1024]{0:T(1024)S(1)} %get-tuple-element.102) | copy-start | bytes 12292
  106.4 443.0 %reduce-scatter.2.cloned.1.call-start = ((), (), s32[]{:S(2)}) async-start(), calls=%async_computation.3 | async-start | bytes 3932160 | tf_op jit(solution)/shard_map/reduce_scatter | solution.py:1353
  106.7 15.8 %copy-start.35 = (s32[1,2]{1,0:T(1,128)S(1)}, s32[1,2]{1,0:T(1,128)}, u32[]{:S(2)}) copy-start(s32[1,2]{1,0:T(1,128)} %param.15) | copy-start | bytes 28
  106.7 18.3 %copy-start.36 = (f32[16,2]{0,1:T(2,128)S(1)}, f32[16,2]{0,1:T(2,128)}, u32[]{:S(2)}) copy-start(f32[16,2]{0,1:T(2,128)} %param.26) | copy-start | bytes 388
  106.7 20.8 %copy-start.33 = (s32[1,2048]{1,0:T(1,128)S(1)}, s32[1,2048]{1,0:T(1,128)}, u32[]{:S(2)}) copy-start(s32[1,2048]{1,0:T(1,128)} %param.16) | copy-start | bytes 24580
  128.9 51.8 %copy-start.6 = (bf16[1024,128]{1,0:T(8,128)(2,1)}, bf16[1024,128]{1,0:T(8,128)(2,1)S(1)}, u32[]{:S(2)}) copy-start(bf16[1024,128]{1,0:T(8,128)(2,1)S(1)} %get-tuple-element.122.refs_2_.near_ak_ref) | copy-start | bytes 786436
  129.0 51.7 %copy-start.8 = (bf16[1024,128]{1,0:T(8,128)(2,1)}, bf16[1024,128]{1,0:T(8,128)(2,1)S(1)}, u32[]{:S(2)}) copy-start(bf16[1024,128]{1,0:T(8,128)(2,1)S(1)} %select_convert_fusion.aq_ref) | copy-start | bytes 786436
  130.8 49.9 %copy-start.18 = (bf16[1024,1024]{1,0:T(8,128)(2,1)S(1)}, bf16[1024,1024]{1,0:T(8,128)(2,1)}, u32[]{:S(2)}) copy-start(bf16[1024,1024]{1,0:T(8,128)(2,1)} %tokens_ref.5) | copy-start | bytes 6291460
  180.7 195.6 %copy-start = (bf16[1024,1024]{1,0:T(8,128)(2,1)}, bf16[1024,1024]{1,0:T(8,128)(2,1)S(1)}, u32[]{:S(2)}) copy-start(bf16[1024,1024]{1,0:T(8,128)(2,1)S(1)} %get-tuple-element.64.left_ref.out_ref) | copy-start | bytes 6291460
  278.5 79.2 %copy-start.23 = (bf16[4,3,64,2048]{3,2,1,0:T(8,128)(2,1)S(1)}, bf16[4,3,64,2048]{3,2,1,0:T(8,128)(2,1)}, u32[]{:S(2)}) copy-start(bf16[4,3,64,2048]{3,2,1,0:T(8,128)(2,1)} %get-tuple-element.93) | copy-start | bytes 9437188
  364.8 6.5 %copy-start.19 = (f32[1024,1024]{1,0:T(8,128)S(1)}, f32[1024,1024]{1,0:T(8,128)}, u32[]{:S(2)}) copy-start(f32[1024,1024]{1,0:T(8,128)} %get-tuple-element.74) | copy-start | bytes 12582916
  381.6 7.3 %collective-permute-start = (bf16[1,512,1024]{2,1,0:T(8,128)(2,1)S(1)}, bf16[1,512,1024]{2,1,0:T(8,128)(2,1)S(1)}, u32[]{:S(2)}, u32[]{:S(2)}) collective-permute-start(bf16[1,512,1024]{2,1,0:T(8,128)(2,1)S(1)} %get-tuple-element.79), channel_id=1, source_target_pairs={{0,2},{2,0},{4,6},{6,4},{8,10},{10,8},{12,14},{14,12},{16,18},{18,... | collective-permute-start | bytes 3145736 | tf_op jit(solution)/shard_map/ppermute | solution.py:1193
  520.6 15.0 %copy-start.10 = (bf16[1024,1024]{1,0:T(8,128)(2,1)S(1)}, bf16[1024,1024]{1,0:T(8,128)(2,1)}, u32[]{:S(2)}) copy-start(bf16[1024,1024]{1,0:T(8,128)(2,1)} %get-tuple-element.72.left_ref) | copy-start | bytes 6291460
  631.7 5.5 copy-start.26
  631.7 5.5 copy-start.27
  634.4 5.7 copy-start.25
  (21 other events, 59.4 us)
Sparse Core Ops, SparseCore 0:
  75.7 100.9 all-gather.2
  179.5 98.9 all-gather.4
  364.7 58.4 reduce-scatter.1

commit v5 on v4

--- a/solution.py
+++ b/solution.py
@@ -51,105 +51,127 @@
     return jnp.where(first, pltpu.roll(values, PAIR - 32, 1), pltpu.roll(values, 32, 1))
 
 
-def gather_kernel(shard_ref, tokens_ref, times_ref, wide_ref, there_tokens_ref, there_times_ref, arrived, sent, keep):
-    place, rank = lax.axis_index("dp"), lax.axis_index("seq")
-    z, x, core = place // 4, place // 2 % 2, place % 2
-    rows = shard_ref.shape[0]
-    lines = 4
-
-    def device(z, x, core, seq):
-        return {"dp": z * 4 + x * 2 + core, "seq": seq}
-
-    up, down = device(z + 1, x, core, rank), device(z - 1, x, core, rank)
-    over, twin = device(z, 1 - x, core, rank), device(z, x, 1 - core, rank)
-    other = device(z, x, core, 1 - rank)
+LINES = 4
+
+
+def line_device(place, line):
+    return {"dp": line * 4 + place % 4}
+
+
+class Spread:
+    def __init__(self, shard_ref, whole_ref, arrived, sent, kept):
+        self.shard_ref, self.whole_ref = shard_ref, whole_ref
+        self.arrived, self.sent, self.kept = arrived, sent, kept
+        self.place = place = lax.axis_index("dp")
+        self.z, self.x, self.core = place // 4, place // 2 % 2, place % 2
+        self.lines = whole_ref.shape[0] // shard_ref.shape[0] // 4
+        self.ends = (self.z == 0).astype(jnp.int32) + (self.z == self.lines - 1).astype(jnp.int32)
+        self.up, self.down = {"dp": place + 4}, {"dp": place - 4}
+        self.over = {"dp": place + 2 - self.x * 4}
+        self.twin = {"dp": place + 1 - self.core * 2}
+        self.not_last, self.not_first = self.z < self.lines - 1, self.z > 0
+
+    def greet(self, barrier):
+        def one(target):
+            pl.semaphore_signal(barrier, inc=1, device_id=target, device_id_type=pl.DeviceIdType.MESH)
+
+        pl.when(self.not_last)(lambda: one(self.up))
+        pl.when(self.not_first)(lambda: one(self.down))
+
+    def block(self, z, x, core):
+        return z * 4 + x * 2 + core
+
+    def rows_of(self, which):
+        rows = self.shard_ref.shape[0]
+        return self.whole_ref.at[pl.ds(pl.multiple_of(which * rows, rows), rows)]
+
+    def copy(self, which, path, own=False):
+        return pltpu.make_async_remote_copy(
+            src_ref=self.shard_ref if own else self.rows_of(which),
+            dst_ref=self.rows_of(which),
+            send_sem=self.sent.at[path, which],
+            recv_sem=self.arrived.at[which],
+            device_id=(self.up, self.over, self.twin, self.down)[path],
+            device_id_type=pl.DeviceIdType.MESH,
+        )
+
+    def stay(self):
+        me = self.block(self.z, self.x, self.core)
+        return pltpu.make_async_copy(self.shard_ref, self.rows_of(me), self.kept.at[0])
+
+    def begin(self):
+        me = self.block(self.z, self.x, self.core)
+        pl.when(self.not_last)(lambda: self.copy(me, 0, True).start())
+        pl.when(self.not_first)(lambda: self.copy(me, 3, True).start())
+        self.copy(me, 1, True).start()
+        self.copy(me, 2, True).start()
+        self.stay().start()
+
+    def along(self, step):
+        def take(which, path, more):
+            self.copy(which, path).wait_recv()
+            pl.when(more)(lambda: self.copy(which, path).start())
+            self.copy(which, 1).start()
+            self.copy(which, 2).start()
+
+        pl.when(self.z >= step)(
+            lambda: take(self.block(self.z - step, self.x, self.core), 0, self.not_last)
+        )
+        pl.when(self.z + step < self.lines)(
+            lambda: take(self.block(self.z + step, self.x, self.core), 3, self.not_first)
+        )
+
+    def to_twin(self):
+        for line in range(self.lines):
+            which = self.block(line, 1 - self.x, self.core)
+            self.copy(which, 1).wait_recv()
+            self.copy(which, 2).start()
+
+    def end(self):
+        for line in range(self.lines):
+            for side in range(2):
+                self.copy(self.block(line, side, 1 - self.core), 2).wait_recv()
+        for line in range(self.lines):
+            which = self.block(line, self.x, self.core)
+            self.copy(which, 1).wait_send()
+            self.copy(which, 2).wait_send()
+            self.copy(self.block(line, 1 - self.x, self.core), 2).wait_send()
+            pl.when((line <= self.z) & self.not_last)(lambda: self.copy(which, 0).wait_send())
+            pl.when((line >= self.z) & self.not_first)(lambda: self.copy(which, 3).wait_send())
+        self.stay().wait()
+
+
+def gather_kernel(
+    shard_ref, tokens_ref, times_ref, wide_ref, there_tokens_ref, there_times_ref, arrived, sent, kept, swapped
+):
+    other = {"seq": 1 - lax.axis_index("seq")}
+    spread = Spread(shard_ref, wide_ref, arrived, sent, kept)
     barrier = pltpu.get_barrier_semaphore()
-
-    def greet(target):
+    for target in (spread.over, spread.twin, other):
         pl.semaphore_signal(barrier, inc=1, device_id=target, device_id_type=pl.DeviceIdType.MESH)
-
-    for target in (over, twin, other):
-        greet(target)
-    pl.when(z < lines - 1)(lambda: greet(up))
-    pl.when(z > 0)(lambda: greet(down))
-    ends = (z == 0).astype(jnp.int32) + (z == lines - 1).astype(jnp.int32)
-    pl.semaphore_wait(barrier, 5 - ends)
-
-    def block(z, x, core):
-        return z * 4 + x * 2 + core
-
-    def rows_of(which):
-        return wide_ref.at[pl.ds(pl.multiple_of(which * rows, rows), rows)]
-
-    def copy(which, path, target, own=False):
-        return pltpu.make_async_remote_copy(
-            src_ref=shard_ref if own else rows_of(which),
-            dst_ref=rows_of(which),
-            send_sem=sent.at[path, which],
-            recv_sem=arrived.at[which],
-            device_id=target,
-            device_id_type=pl.DeviceIdType.MESH,
-        )
+    spread.greet(barrier)
+    pl.semaphore_wait(barrier, 5 - spread.ends)
 
     def swap(source, target, index):
         return pltpu.make_async_remote_copy(
             src_ref=source,
             dst_ref=target,
-            send_sem=keep.at[index],
-            recv_sem=keep.at[index + 1],
+            send_sem=swapped.at[index],
+            recv_sem=swapped.at[index + 1],
             device_id=other,
             device_id_type=pl.DeviceIdType.MESH,
         )
 
-    me = block(z, x, core)
-    pl.when(z < lines - 1)(lambda: copy(me, 0, up, True).start())
-    pl.when(z > 0)(lambda: copy(me, 3, down, True).start())
-    copy(me, 1, over, True).start()
-    copy(me, 2, twin, True).start()
     swaps = [swap(tokens_ref, there_tokens_ref, 0), swap(times_ref, there_times_ref, 2)]
+    spread.begin()
     for each in swaps:
         each.start()
-    here = pltpu.make_async_copy(shard_ref, rows_of(me), keep.at[4])
-    here.start()
-
-    def pass_over(which):
-        copy(which, 2, twin).start()
-
-    for step in range(1, lines):
-
-        @pl.when(z >= step)
-        def _():
-            which = block(z - step, x, core)
-            copy(which, 0, up).wait_recv()
-            pl.when(z < lines - 1)(lambda: copy(which, 0, up).start())
-            copy(which, 1, over).start()
-            pass_over(which)
-
-        @pl.when(z + step < lines)
-        def _():
-            which = block(z + step, x, core)
-            copy(which, 3, down).wait_recv()
-            pl.when(z > 0)(lambda: copy(which, 3, down).start())
-            copy(which, 1, over).start()
-            pass_over(which)
-
-    for line in range(lines):
-        which = block(line, 1 - x, core)
-        copy(which, 1, over).wait_recv()
-        pass_over(which)
-    for line in range(lines):
-        for side in range(2):
-            copy(block(line, side, 1 - core), 2, twin).wait_recv()
-    for line in range(lines):
-        which = block(line, x, core)
-        copy(which, 1, over).wait_send()
-        copy(which, 2, twin).wait_send()
-        copy(block(line, 1 - x, core), 2, twin).wait_send()
-        pl.when((line <= z) & (z < lines - 1))(lambda: copy(which, 0, up).wait_send())
-        pl.when((line >= z) & (z > 0))(lambda: copy(which, 3, down).wait_send())
+    for step in range(1, spread.lines):
+        spread.along(step)
+    spread.to_twin()
+    spread.end()
     for each in swaps:
         each.wait()
-    here.wait()
 
 
 def gather_first(shard, tokens, times, places):
@@ -166,7 +188,8 @@
         scratch_shapes=[
             pltpu.SemaphoreType.DMA((places,)),
             pltpu.SemaphoreType.DMA((4, places)),
-            pltpu.SemaphoreType.DMA((5,)),
+            pltpu.SemaphoreType.DMA((1,)),
+            pltpu.SemaphoreType.DMA((4,)),
         ],
         compiler_params=pltpu.CompilerParams(collective_id=0, has_side_effects=True),
         cost_estimate=NO_COST,
@@ -425,7 +448,7 @@
     lane = lane_index()
     base = (lane - 64, lane)
     dq = [dq_total[h].T for h in range(2)]
-    dq_ref[...] = jnp.where(lane < 64, dq[0], dq[1]) * 0.125
+    dq_ref[...] = (jnp.where(lane < 64, dq[0], dq[1]) * 0.125).astype(dq_ref.dtype)
     variates = aq_ref[...].astype(f32)
     for h in range(2):
         pick = (base[h] >= 0) & (base[h] < 4)
@@ -496,21 +519,17 @@
     )(flags, full, grad, out, query_columns, keys, values, key_columns)
 
 
-LINES = 4
-STARTS = (0, 3, 7, 0)
-ARRIVALS = (7, 10, 13, 4)
-
-
-def line_device(place, line):
-    return {"dp": line * 4 + place % 4}
+STARTS = (0, 7, 19, 33, 47)
+ARRIVALS = (10, 23, 37, 50, 62)
 
 
 def carry_kernel(
     pairs, full_ref, grad_ref, out_ref, aq_ref,
     far_k_ref, far_v_ref, far_ak_ref, near_k_ref, near_v_ref, near_ak_ref,
-    across_ref, own_ref, far_ref, out_across_ref, out_own_ref, out_far_ref,
-    dq_ref, bias_ref, got_ref, near_ref, line_ref, line_got_ref, across_got, out_got,
-    grads, dq_total, stage, near_stage, terms, sums,
+    early_across_ref, early_own_ref, early_far_ref, across_ref, own_ref, far_ref,
+    out_across_ref, out_own_ref, out_far_ref,
+    dq_ref, bias_ref, got_ref, near_ref, line_ref, line_got_ref, late_ref, early_got, across_got, out_got,
+    grads, dq_total, stage, terms, sums,
     send_sems, recv_sems, near_sems, across_sems, term_sems, line_send, line_recv, line_own,
 ):
     step = pl.program_id(0)
@@ -523,27 +542,39 @@
     def lanes(index):
         return pl.ds(pl.multiple_of(index * PAIR, PAIR), PAIR)
 
+    last = len(STARTS) - 1
+
     def part_of(refs, part):
-        return refs[1] if part == 3 else refs[0].at[:, part]
-
-    def held(ref, part):
-        return ref.at[:, :, pl.ds(0, out_own_ref.shape[2])] if part == 3 else ref
+        if part == last:
+            return refs[0]
+        return refs[2] if part == 0 else refs[1].at[:, part - 1]
+
+    def width_of(part):
+        return out_own_ref.shape[2] if part == 0 else sums.shape[3]
 
     def across(part):
         return pltpu.make_async_remote_copy(
-            src_ref=part_of((across_ref, out_across_ref), part),
-            dst_ref=part_of((across_got, out_got), part),
+            src_ref=part_of((early_across_ref, across_ref, out_across_ref), part),
+            dst_ref=part_of((early_got, across_got, out_got), part),
             send_sem=across_sems.at[part, 0], recv_sem=across_sems.at[part, 1],
             device_id=over, device_id_type=mesh_id,
         )
 
     def load(part, k):
-        source = part_of(((own_ref, out_own_ref), (far_ref, out_far_ref), (across_got, out_got))[k], part)
-        return pltpu.make_async_copy(source, held(terms.at[k], part), term_sems.at[k])
+        if k == 0:
+            source = part_of((early_own_ref.at[:, 2], own_ref, out_own_ref), part)
+        elif k == 1:
+            near = pl.ds(LINES, LINES)
+            source = part_of((early_far_ref.at[near, 2], far_ref.at[near], out_far_ref), part)
+        else:
+            source = part_of((early_got, across_got, out_got), part)
+        return pltpu.make_async_copy(
+            source, terms.at[k, :, :, pl.ds(0, width_of(part))], term_sems.at[k]
+        )
 
     def along(part, k):
         to = lax.rem(line + k, LINES)
-        columns = pl.ds(0, out_own_ref.shape[2] if part == 3 else sums.shape[3])
+        columns = pl.ds(0, width_of(part))
         return pltpu.make_async_remote_copy(
             src_ref=sums.at[part, to, :, columns], dst_ref=line_got_ref.at[k - 1, part, :, columns],
             send_sem=line_send.at[part, k - 1], recv_sem=line_recv.at[part, k - 1],
@@ -551,7 +582,9 @@
         )
 
     def stay(part):
-        columns = pl.ds(0, out_own_ref.shape[2] if part == 3 else sums.shape[3])
+        if part == last:
+            return pltpu.make_async_copy(sums.at[part], late_ref, line_own.at[part])
+        columns = pl.ds(0, width_of(part))
         return pltpu.make_async_copy(
             sums.at[part, line, :, columns], line_ref.at[part, :, columns], line_own.at[part]
         )
@@ -563,9 +596,8 @@
         )
 
     def to_near(pair):
-        slot = lax.rem(pair, 2)
         return pltpu.make_async_copy(
-            near_stage.at[slot], near_ref.at[:, :, lanes(pair)], near_sems.at[slot]
+            stage.at[pairs + pair], near_ref.at[:, :, lanes(pair)], near_sems.at[pair]
         )
 
     @pl.when(step == 0)
@@ -576,56 +608,53 @@
             pl.semaphore_signal(barrier, inc=1, device_id=target, device_id_type=mesh_id)
         pl.semaphore_wait(barrier, len(peers))
 
-    for part in range(4):
-
-        @pl.when(step == STARTS[part])
-        def _():
-            across(part).start()
-
-        @pl.when(step == ARRIVALS[part] - 1)
-        def _():
-            load(part, 0).start()
-            load(part, 1).start()
-
-        @pl.when(step == ARRIVALS[part])
-        def _():
-            across(part).wait()
-            load(part, 2).start()
-            for k in range(3):
-                load(part, k).wait()
-            columns = out_own_ref.shape[2] if part == 3 else sums.shape[3]
-            for i in range(LINES):
-                sums[part, i, :, :columns] = sum(
-                    terms[k, i, :, :columns].astype(f32) for k in range(3)
-                ).astype(bf16)
+    def arrive(part):
+        across(part).wait()
+        load(part, 2).start()
+        for k in range(3):
+            load(part, k).wait()
+        columns = width_of(part)
+        for i in range(LINES):
+            sums[part, i, :, :columns] = sum(
+                terms[k, i, :, :columns].astype(f32) for k in range(3)
+            ).astype(bf16)
+        if part < last:
             for k in range(1, LINES):
                 along(part, k).start()
-            stay(part).start()
-
-    @pl.when(step >= pairs + 2)
-    def _():
-        to_near(step - pairs - 2).wait()
+        stay(part).start()
+
+    def go_on(quarter):
+        for part in range(last + 1):
+
+            before = ARRIVALS[part] - 3
+            if STARTS[part] % 4 == quarter:
+
+                @pl.when(step == STARTS[part] // 4)
+                def _():
+                    across(part).start()
+
+            if before % 4 == quarter:
+
+                @pl.when(step == before // 4)
+                def _():
+                    load(part, 0).start()
+                    load(part, 1).start()
+
+            if ARRIVALS[part] % 4 == quarter:
+                pl.when(step == ARRIVALS[part] // 4)(functools.partial(arrive, part))
 
     backward_start(grad_ref, out_ref, grads, dq_total)
     is_far = step < pairs
-    slot = lax.rem(step - jnp.where(is_far, 0, pairs), 2)
     for b in range(far_k_ref.shape[0] // KEY_ROWS):
         at = slice(b * KEY_ROWS, (b + 1) * KEY_ROWS)
+        go_on(b)
         block = [
             jnp.where(is_far, far[at, :], near[at, :])
             for far, near in ((far_k_ref, near_k_ref), (far_v_ref, near_v_ref), (far_ak_ref, near_ak_ref))
         ]
-        dk, dv = backward_block(full_ref, *block, grads, dq_total)
-
-        @pl.when(is_far)
-        def _():
-            stage[step, 0, at, :] = dk
-            stage[step, 1, at, :] = dv
-
-        @pl.when(jnp.logical_not(is_far))
-        def _():
-            near_stage[slot, 0, at, :] = dk
-            near_stage[slot, 1, at, :] = dv
+        stage[step, 0, at, :], stage[step, 1, at, :] = backward_block(
+            full_ref, *block, grads, dq_total
+        )
 
     backward_end(aq_ref, dq_ref, bias_ref, dq_total)
     pl.when(is_far)(lambda: to_other(step).start())
@@ -633,17 +662,17 @@
 
     @pl.when(step == pl.num_programs(0) - 1)
     def _():
-        to_near(step - pairs - 1).wait()
-        to_near(step - pairs).wait()
         for pair in range(pairs):
+            to_near(pair).wait()
             to_other(pair).wait()
-        for part in range(4):
-            for k in range(1, LINES):
-                along(part, k).wait()
+        for part in range(last + 1):
+            if part < last:
+                for k in range(1, LINES):
+                    along(part, k).wait()
             stay(part).wait()
 
 
-def attend_back_carry(full, grad, out, query_columns, near, far, sums, out_sums):
+def attend_back_carry(full, grad, out, query_columns, near, far, early, sums, out_sums):
     rows, width = grad.shape
     pairs = width // PAIR
     key_rows = near[0].shape[0]
@@ -654,6 +683,7 @@
     whole = lambda i: (0, 0)
     anywhere = pl.BlockSpec(memory_space=pl.ANY)
     shard, hidden = sums[0].shape[2:]
+    parts = len(STARTS)
 
     def key_specs(pair):
         return [
@@ -673,43 +703,44 @@
         ]
         + key_specs(far_pair)
         + key_specs(near_pair)
-        + [anywhere] * 6,
+        + [anywhere] * 9,
         out_specs=[
             pl.BlockSpec((rows, PAIR), lambda i: (0, i)),
             pl.BlockSpec((1, 2, PAIR), lambda i: (i, 0, 0)),
         ]
-        + [anywhere] * 6,
+        + [anywhere] * 8,
         out_shape=[
-            jax.ShapeDtypeStruct((rows, 2 * width), f32),
+            jax.ShapeDtypeStruct((rows, 2 * width), bf16),
             jax.ShapeDtypeStruct((2 * pairs, 2, PAIR), f32),
             jax.ShapeDtypeStruct((2, key_rows, width), bf16),
             jax.ShapeDtypeStruct((2, key_rows, width), bf16),
-            jax.ShapeDtypeStruct((4, shard, hidden), bf16),
-            jax.ShapeDtypeStruct((LINES - 1, 4, shard, hidden), bf16),
+            jax.ShapeDtypeStruct((parts - 1, shard, hidden), bf16),
+            jax.ShapeDtypeStruct((LINES - 1, parts - 1, shard, hidden), bf16),
+            jax.ShapeDtypeStruct((LINES, shard, hidden), bf16),
+            jax.ShapeDtypeStruct(early[0].shape, bf16),
             jax.ShapeDtypeStruct(sums[0].shape, bf16),
             jax.ShapeDtypeStruct(out_sums[0].shape, bf16),
         ],
         scratch_shapes=[
             pltpu.VMEM((2, rows, PAIR), bf16),
             pltpu.VMEM((2, PAIR, rows), f32),
-            pltpu.VMEM((pairs, 2, key_rows, PAIR), bf16),
-            pltpu.VMEM((2, 2, key_rows, PAIR), bf16),
+            pltpu.VMEM((2 * pairs, 2, key_rows, PAIR), bf16),
             pltpu.VMEM((3, LINES, shard, hidden), bf16),
-            pltpu.VMEM((4, LINES, shard, hidden), bf16),
+            pltpu.VMEM((parts, LINES, shard, hidden), bf16),
             pltpu.SemaphoreType.DMA((pairs,)),
             pltpu.SemaphoreType.DMA((pairs,)),
-            pltpu.SemaphoreType.DMA((2,)),
-            pltpu.SemaphoreType.DMA((4, 2)),
+            pltpu.SemaphoreType.DMA((pairs,)),
+            pltpu.SemaphoreType.DMA((parts, 2)),
             pltpu.SemaphoreType.DMA((3,)),
-            pltpu.SemaphoreType.DMA((4, LINES - 1)),
-            pltpu.SemaphoreType.DMA((4, LINES - 1)),
-            pltpu.SemaphoreType.DMA((4,)),
+            pltpu.SemaphoreType.DMA((parts - 1, LINES - 1)),
+            pltpu.SemaphoreType.DMA((parts - 1, LINES - 1)),
+            pltpu.SemaphoreType.DMA((parts,)),
         ],
         compiler_params=pltpu.CompilerParams(
             vmem_limit_bytes=VMEM_BYTES, collective_id=3, has_side_effects=True
         ),
         cost_estimate=NO_COST,
-    )(full, grad, out, query_columns, *far, *near, *sums, *out_sums)
+    )(full, grad, out, query_columns, *far, *near, *early, *sums, *out_sums)
 
 
 def slot_columns(segment, variates):
@@ -753,7 +784,8 @@
     if first:
         branch_ref, nfgrad_ref, far_ref, cross_ref, own_ref, *refs = refs
     else:
-        across_ref, branch_ref, nfgrad_ref, far_ref, cross_ref, own_ref, got_ref, *refs = refs
+        resid_ref, gain_ref, across_ref, branch_ref, nfgrad_ref, *refs = refs
+        low_ref, gain_grad_ref, far_ref, cross_ref, own_ref, got_ref, *refs = refs
     turned, branch, columns_out, rows_out, sems, arrived, *x_sems = refs
     step = pl.program_id(0)
     steps = pl.num_programs(0)
@@ -847,7 +879,7 @@
         axis=0,
     )
     hiddens, gates, ups = [], [], []
-    part_rows = min(256, rows)
+    part_rows = min(512, rows)
     for i in range(rows // part_rows):
         at = slice(i * part_rows, (i + 1) * part_rows)
         nf = nf_ref[at, :]
@@ -877,6 +909,23 @@
             columns_out[slot, spot, part] = columns[j * shard : (j + 1) * shard, :]
     each_copy(step, lambda copy: copy.start())
 
+    def through_norm():
+        gain = gain_ref[...]
+        gain_grad = jnp.zeros_like(gain)
+        part_rows = min(256, rows)
+        for i in range(rows // part_rows):
+            at = slice(i * part_rows, (i + 1) * part_rows)
+            values, upstream = resid_ref[at, :], nfgrad_ref[at, :]
+            inv = lax.rsqrt(jnp.mean(values * values, axis=-1, keepdims=True) + EPSILON)
+            hat = values * inv
+            weighted = upstream * gain
+            inner = jnp.mean(weighted * hat, axis=-1, keepdims=True)
+            gain_grad = gain_grad + jnp.sum(upstream * hat, axis=0, keepdims=True)
+            total = seed_ref[at, :].astype(f32) + inv * (weighted - hat * inner)
+            nfgrad_ref[at, :] = total
+            low_ref[at, :] = total.astype(bf16)
+        gain_grad_ref[...] = gain_grad
+
     @pl.when(step == steps - 1)
     def _():
         branch_ref[...] = branch[...].astype(branch_ref.dtype)
@@ -887,10 +936,11 @@
             near = (at % 2 == place // 2 % 2).astype(jnp.int32)
             row_copies(at, far_ref, near * groups + at // 2, 0).wait_recv()
         if not first:
+            through_norm()
             carry().wait()
 
 
-def feed_forward(places, normed, seed, start, nfstart, weights, across=None):
+def feed_forward(places, normed, seed, start, nfstart, weights, resid=None, gain=None, across=None):
     rows, width = normed.shape
     first = nfstart is None
     hidden = weights.shape[1] // 3
@@ -911,11 +961,20 @@
             pl.BlockSpec((width, chunk), lambda t: (0, steps + t)),
             pl.BlockSpec((2 * shard, hidden), lambda t: (t, 2)),
         ]
-        + [pl.BlockSpec(memory_space=pl.ANY)] * (not first),
+        + (
+            []
+            if first
+            else [
+                pl.BlockSpec((rows, width), whole, pipeline_mode=once),
+                pl.BlockSpec((1, width), whole),
+                pl.BlockSpec(memory_space=pl.ANY),
+            ]
+        ),
         out_specs=[
             pl.BlockSpec((rows, width), whole),
             pl.BlockSpec((rows, width), whole),
         ]
+        + ([] if first else [pl.BlockSpec((rows, width), whole), pl.BlockSpec((1, width), whole)])
         + [pl.BlockSpec(memory_space=pl.ANY)] * (3 if first else 4),
         scratch_shapes=[
             pltpu.VMEM((width, rows), bf16),
@@ -930,14 +989,20 @@
             jax.ShapeDtypeStruct((rows, width), f32 if first else bf16),
             jax.ShapeDtypeStruct((rows, width), f32),
         ]
-        + [jax.ShapeDtypeStruct((places // part, 3, shard, hidden), bf16) for part in ((2, 4, 4) if first else (2, 4, 4, 4))],
+        + (
+            []
+            if first
+            else [jax.ShapeDtypeStruct((rows, width), bf16), jax.ShapeDtypeStruct((1, width), f32)]
+        )
+        + [jax.ShapeDtypeStruct((places // part, 3, shard, hidden), bf16) for part in (2, 4, 4)]
+        + ([] if first else [jax.ShapeDtypeStruct(across.shape, bf16)]),
         compiler_params=pltpu.CompilerParams(
             vmem_limit_bytes=56 * 2**20, collective_id=1 if first else 2, has_side_effects=True
         ),
         cost_estimate=NO_COST,
     )(
         normed, seed, start, start if first else nfstart, weights, weights, weights,
-        *(() if first else (across,)),
+        *(() if first else (resid, gain, across)),
     )
 
 
@@ -988,12 +1053,14 @@
 
 
 def finish_kernel(
-    far_ref, cross_ref, own_ref, line_ref, line_got_ref, first_ref, small_ref,
-    merged_ref, weight_ref, tokens_ref, resid_ref, gain_ref,
-    in_ref, first_out_ref, second_out_ref, small_out_ref, grad_ref,
-    core_got, x_sent, x_got, z_sent, z_got, y_sent, y_got, first_got, second, second_got, small_sent, small_got,
-    merged, weight, tokens, resid, grad,
-    core_sems, x_sems, z_send, z_recv, y_sems, first_sems, second_sems, small_sems, load_sems, store_sem,
+    line_ref, line_got_ref, late_ref, first_ref, ffn_ref, bias_ref, cos_ref, sin_ref, qgain_ref, kgain_ref, gain_ref,
+    normed_ref, dq_ref, got_kv_ref, own_kv_ref, rawq_ref, rawk_ref, weight_ref, tokens_ref, resid_ref,
+    in_ref, out_ref, gate_up_ref, down_ref, small_out_ref, grad_ref,
+    merged, low_a, low_b, low_c, low_d, wide_a, wide_b, sums,
+    arranged, far, own, core_got, x_sent, x_got, z_sent, z_got, y_sent, y_got,
+    first_got, second, second_got, late_got, late, late_there, small_sent, small_got,
+    core_sems, x_sems, z_send, z_recv, y_sems, first_sems, second_sems, late_send, late_recv, late_sems, small_sems,
+    load_sems, store_sem,
 ):
     place, rank = lax.axis_index("dp"), lax.axis_index("seq")
     line = place // 4
@@ -1004,8 +1071,11 @@
     lines = [line_device(place, lax.rem(line + k, LINES)) for k in range(1, LINES)]
     low = line_device(place, line + 1 - line % 2 * 2)
     high = line_device(place, lax.rem(line + 2, LINES))
-    blocks, quarter = cross_ref.shape[:2]
+    blocks, quarter, columns = x_sent.shape
+    rows = merged.shape[0]
+    step = min(256, rows)
     shard = quarter // LINES
+    places = 4 * LINES
 
     def send(source, target, sems, to):
         return pltpu.make_async_remote_copy(
@@ -1016,11 +1086,19 @@
     def pair_of(sems, *index):
         return sems.at[*index, 0], sems.at[*index, 1]
 
-    to_core = [send(far_ref.at[b], core_got.at[b], pair_of(core_sems, b), twin) for b in range(blocks)]
+    to_core = [send(far.at[b], core_got.at[b], pair_of(core_sems, b), twin) for b in range(blocks)]
     to_x = [send(x_sent.at[b], x_got.at[b], pair_of(x_sems, b), over) for b in range(blocks)]
     to_y = [send(y_sent.at[b], y_got.at[b], pair_of(y_sems, b), other) for b in range(blocks)]
     first_y = send(first_ref, first_got, pair_of(first_sems), other)
     second_y = send(second, second_got, pair_of(second_sems), other)
+    late_y = send(late, late_there, pair_of(late_sems), other)
+
+    def late_z(k):
+        return send(
+            late_ref.at[lax.rem(line + k, LINES)], late_got.at[k - 1],
+            (late_send.at[k - 1], late_recv.at[k - 1]), lines[k - 1],
+        )
+
     rounds = [
         send(small_sent.at[k], small_got.at[k], pair_of(small_sems, k), to)
         for k, to in enumerate((twin, over, low, high, other))
@@ -1032,51 +1110,143 @@
             (z_send.at[b, k - 1], z_recv.at[b, k - 1]), lines[k - 1],
         )
 
-    loads = [
-        pltpu.make_async_copy(source, target, load_sems.at[k])
-        for k, (source, target) in enumerate(
-            ((merged_ref, merged), (weight_ref.at[:, pl.ds(0, weight.shape[1])], weight),
-             (tokens_ref, tokens), (resid_ref, resid))
-        )
-    ]
-    store = pltpu.make_async_copy(grad, grad_ref, store_sem.at[0])
+    def cut(ref, index):
+        return ref.at[:, pl.ds(index * columns, columns)]
+
+    def load(k):
+        source, target = (
+            (normed_ref, low_a), (own_kv_ref.at[1], low_b), (got_kv_ref.at[1], low_c),
+            (rawk_ref, wide_a), (own_kv_ref.at[0], low_d), (rawq_ref, wide_b),
+            (got_kv_ref.at[0], low_a), (cut(dq_ref, 0), low_b), (cut(dq_ref, 1), low_c),
+            (tokens_ref, low_d), (resid_ref, wide_a),
+            (cut(weight_ref, 0), low_b), (cut(weight_ref, 1), low_c), (cut(weight_ref, 2), low_a),
+        )[k]
+        return pltpu.make_async_copy(source, target, load_sems.at[k])
+
+    def start(*which):
+        for k in which:
+            load(k).start()
+
+    def ready(*which):
+        for k in which:
+            load(k).wait()
+
+    store = pltpu.make_async_copy(wide_b, grad_ref, store_sem.at[0])
 
     barrier = pltpu.get_barrier_semaphore()
     peers = [twin, over, other] + lines
     for target in peers:
         pl.semaphore_signal(barrier, inc=1, device_id=target, device_id_type=mesh_id)
     pl.semaphore_wait(barrier, len(peers))
-    for copy in to_core + [first_y] + loads:
+    start(0, 1, 2, 4, 3, 5)
+    for copy in [first_y] + [late_z(k) for k in range(1, LINES)]:
         copy.start()
-    second[...] = sum(
-        part.astype(f32) for part in [line_ref[...]] + [line_got_ref[k] for k in range(LINES - 1)]
-    ).astype(bf16)
+    ready(0)
+    turned = low_a[...].T
+    for i in range(places):
+        near_core = (i % 2 == place % 2).astype(jnp.int32)
+        near_x = (i // 2 % 2 == place // 2 % 2).astype(jnp.int32)
+        at = pl.multiple_of(((near_core * 2 + near_x) * LINES + i // 4) * shard, shard)
+        arranged[pl.ds(at, shard), :] = turned[i * shard : (i + 1) * shard, :]
+    start(6)
+
+    def product(begin, count, b):
+        return dot(arranged[begin : begin + count, :], merged[:, b * columns : (b + 1) * columns])
+
+    def send_block(b):
+        far[b] = product(0, 2 * quarter, b).astype(bf16)
+        to_core[b].start()
+        cross = product(2 * quarter, quarter, b)
+        own[b] = product(3 * quarter, quarter, b).astype(bf16)
+        to_core[b].wait()
+        x_sent[b] = (cross + core_got[b, :quarter].astype(f32)).astype(bf16)
+        to_x[b].start()
+
+    def pass_on(b):
+        to_x[b].wait()
+        total = own[b].astype(f32) + core_got[b, quarter:].astype(f32) + x_got[b].astype(f32)
+        total = total.astype(bf16)
+        for k in range(LINES):
+            z_sent[b, k] = total[k * shard : (k + 1) * shard, :]
+        for k in range(1, LINES):
+            to_z(b, k).start()
+
+    ones = half_ones(True)
+
+    def turn_back(b, left, right, raw_ref, head_gain):
+        sums[b : b + 1, :] = jnp.zeros((1, PAIR), f32)
+
+        def some_rows(i, carry):
+            at = pl.ds(pl.multiple_of(i * step, step), step)
+            cosine, sine = cos_ref[at, :], sin_ref[at, :]
+            for tile in range(columns // PAIR):
+                lanes = slice(tile * PAIR, (tile + 1) * PAIR)
+                grad = left[at, lanes].astype(f32) + right[at, lanes].astype(f32)
+                grad = grad.astype(bf16).astype(f32)
+                grad = grad * cosine - swap_halves(grad) * sine
+                raw = raw_ref[at, lanes]
+                unit = lax.rsqrt(head_sums(raw * raw, ones) * (1.0 / 64) + EPSILON)
+                hat = raw * unit
+                sums[b : b + 1, :] += jnp.sum(grad * hat, axis=0, keepdims=True)
+                weighted = grad * head_gain
+                inner = head_sums(weighted * hat, ones) * (1.0 / 64)
+                there = slice(b * columns + tile * PAIR, b * columns + (tile + 1) * PAIR)
+                merged[at, there] = (unit * (weighted - hat * inner)).astype(bf16)
+            return carry
+
+        lax.fori_loop(0, rows // step, some_rows, 0)
+
+    ready(1, 2)
+
+    def add_rows(i, carry):
+        at = pl.ds(pl.multiple_of(i * step, step), step)
+        merged[at, 2 * columns :] = (low_b[at, :].astype(f32) + low_c[at, :].astype(f32)).astype(bf16)
+        return carry
+
+    lax.fori_loop(0, rows // step, add_rows, 0)
+    start(7, 8)
+    send_block(2)
+    ready(3, 4, 6)
+    turn_back(1, low_d, low_a, wide_a, kgain_ref[...])
+    start(9, 10, 13)
+    send_block(1)
+    for i in range(line_ref.shape[0]):
+        second[i] = sum(
+            part.astype(f32) for part in [line_ref[i]] + [line_got_ref[k, i] for k in range(LINES - 1)]
+        ).astype(bf16)
     second_y.start()
-    for b in range(blocks):
-        to_core[b].wait()
-        x_sent[b] = (cross_ref[b].astype(f32) + core_got[b, :quarter].astype(f32)).astype(bf16)
-        to_x[b].start()
-
-    for copy in loads:
-        copy.wait()
+    ready(5, 7, 8)
+    turn_back(0, low_b, low_c, wide_b, qgain_ref[...])
+    start(11, 12)
+    pass_on(2)
+    send_block(0)
+    pass_on(1)
+
+    ready(9, 10, 11, 12, 13)
     gain = gain_ref[...]
-    rows = tokens.shape[0]
-    step = min(256, rows)
     gain_grad = jnp.zeros_like(gain)
     for i in range(rows // step):
         at = slice(i * step, (i + 1) * step)
-        normed_grad = dot(merged[at, :], weight[...], NT)
-        values = tokens[at, :].astype(f32)
+        normed_grad = sum(
+            dot(merged[at, b * columns : (b + 1) * columns], part[...], NT)
+            for b, part in enumerate((low_b, low_c, low_a))
+        )
+        values = low_d[at, :].astype(f32)
         inv = lax.rsqrt(jnp.mean(values * values, axis=-1, keepdims=True) + EPSILON)
         hat = values * inv
         weighted = normed_grad * gain
         inner = jnp.mean(weighted * hat, axis=-1, keepdims=True)
-        grad[at, :] = resid[at, :] + inv * (weighted - hat * inner)
+        wide_b[at, :] = wide_a[at, :] + inv * (weighted - hat * inner)
         gain_grad = gain_grad + jnp.sum(normed_grad * hat, axis=0, keepdims=True)
     store.start()
-    small_sent[0] = small_ref[...]
-    for k in range(gain.shape[1] // PAIR):
+    tiles = columns // PAIR
+    for k in range(tiles):
         small_sent[0, k : k + 1, :] = gain_grad[:, k * PAIR : (k + 1) * PAIR]
+    small_sent[0, tiles : 2 * tiles, :] = ffn_ref[...]
+    small_sent[0, 2 * tiles : 2 * tiles + 8, :] = sums[...]
+    for pair in range(tiles):
+        at = 2 * tiles + 8 + 2 * pair
+        small_sent[0, at : at + 2, :] = bias_ref[pair] + bias_ref[tiles + pair]
     rounds[0].start()
 
     def next_round(k):
@@ -1088,21 +1258,7 @@
         else:
             small_out_ref[...] = total
 
-    next_round(0)
-    for b in range(blocks):
-        to_x[b].wait()
-        total = own_ref[b].astype(f32) + core_got[b, quarter:].astype(f32) + x_got[b].astype(f32)
-        total = total.astype(bf16)
-        for k in range(LINES):
-            z_sent[b, k] = total[k * shard : (k + 1) * shard, :]
-        for k in range(1, LINES):
-            to_z(b, k).start()
-    next_round(1)
-    first_y.wait()
-    first_out_ref[...] = first_ref[...].astype(f32) + first_got[...].astype(f32)
-    second_y.wait()
-    second_out_ref[...] = second[...].astype(f32) + second_got[...].astype(f32)
-    for b in range(blocks):
+    def to_last(b):
         for k in range(1, LINES):
             to_z(b, k).wait()
         total = z_sent[b, line].astype(f32)
@@ -1110,37 +1266,90 @@
             total = total + z_got[b, k].astype(f32)
         y_sent[b] = total.astype(bf16)
         to_y[b].start()
-    for k in range(2, len(rounds)):
-        next_round(k)
-    for b in range(blocks):
+
+    for k in range(1, LINES):
+        late_z(k).wait()
+    late[...] = sum(
+        part.astype(f32) for part in [late_ref[line]] + [late_got[k] for k in range(LINES - 1)]
+    ).astype(bf16)
+    late_y.start()
+    next_round(0)
+    pass_on(0)
+    next_round(1)
+    to_last(2)
+    to_last(1)
+    next_round(2)
+    first_y.wait()
+    second_y.wait()
+    part_columns = second.shape[2] // places
+    hidden = second.shape[2] * 2
+    for part in range(2):
+        halves = [
+            first_ref[part].astype(f32) + first_got[part].astype(f32),
+            second[1 + part].astype(f32) + second_got[1 + part].astype(f32),
+        ]
+        for j in range(places):
+            for h in range(2):
+                at = part * hidden + (2 * j + h) * part_columns
+                gate_up_ref[:, at : at + part_columns] = halves[h][:, j * part_columns : (j + 1) * part_columns]
+    next_round(3)
+    to_last(0)
+    out_ref[...] = second[0, :, :columns].astype(f32) + second_got[0, :, :columns].astype(f32)
+    late_y.wait()
+    for h in range(2):
+        if h == 0:
+            total = late[...].astype(f32) + late_there[...].astype(f32)
+        else:
+            total = second[3].astype(f32) + second_got[3].astype(f32)
+        for k in range(total.shape[1] // columns):
+            at = h * down_ref.shape[0] // 2 + k * shard
+            down_ref[at : at + shard, :] = total[:, k * columns : (k + 1) * columns]
+    next_round(4)
+    for b in (2, 1, 0):
         to_y[b].wait()
-        in_ref[b] = y_sent[b].astype(f32) + y_got[b].astype(f32)
+        in_ref[:, b * columns : (b + 1) * columns] = y_sent[b].astype(f32) + y_got[b].astype(f32)
     store.wait()
 
 
-def finish(in_grads, line_sums, line_got, first, small, merged, weight, tokens, resid, gain):
-    far, cross, own = in_grads
-    blocks, quarter, columns = cross.shape
-    shard = quarter // LINES
+def finish(
+    places, line_sums, line_got, late, first, ffn_gain, bias, cosine, sine, qgain, kgain, gain,
+    normed, dq, got_kv, own_kv, raws, weight, tokens, resid,
+):
     rows, width = tokens.shape
+    blocks = 3
+    quarter, shard, columns = width // 4, width // places, width
+    hidden = line_sums.shape[2]
+    small = (4 * width // PAIR + 8, PAIR)
     vmem = pl.BlockSpec(memory_space=pltpu.VMEM)
     anywhere = pl.BlockSpec(memory_space=pl.ANY)
     dma = pltpu.SemaphoreType.DMA
     return pl.pallas_call(
         finish_kernel,
-        in_specs=[vmem] * 7 + [anywhere] * 4 + [vmem],
-        out_specs=[vmem] * 4 + [anywhere],
+        in_specs=[vmem] * 11 + [anywhere] * 9,
+        out_specs=[vmem] * 5 + [anywhere],
         out_shape=[
-            jax.ShapeDtypeStruct((blocks, shard, columns), f32),
-            jax.ShapeDtypeStruct(first.shape, f32),
-            jax.ShapeDtypeStruct(line_sums.shape, f32),
-            jax.ShapeDtypeStruct(small.shape, f32),
+            jax.ShapeDtypeStruct((shard, blocks * columns), f32),
+            jax.ShapeDtypeStruct((shard, columns), f32),
+            jax.ShapeDtypeStruct((shard, 4 * hidden), f32),
+            jax.ShapeDtypeStruct((2 * hidden // places, columns), f32),
+            jax.ShapeDtypeStruct(small, f32),
             jax.ShapeDtypeStruct((rows, width), f32),
         ],
         scratch_shapes=[
-            pltpu.VMEM(far.shape, bf16),
-            pltpu.VMEM(cross.shape, bf16),
-            pltpu.VMEM(cross.shape, bf16),
+            pltpu.VMEM((rows, blocks * columns), bf16),
+            pltpu.VMEM((rows, columns), bf16),
+            pltpu.VMEM((rows, columns), bf16),
+            pltpu.VMEM((rows, columns), bf16),
+            pltpu.VMEM((rows, columns), bf16),
+            pltpu.VMEM((rows, columns), f32),
+            pltpu.VMEM((rows, columns), f32),
+            pltpu.VMEM((8, PAIR), f32),
+            pltpu.VMEM((width, rows), bf16),
+            pltpu.VMEM((blocks, 2 * quarter, columns), bf16),
+            pltpu.VMEM((blocks, quarter, columns), bf16),
+            pltpu.VMEM((blocks, 2 * quarter, columns), bf16),
+            pltpu.VMEM((blocks, quarter, columns), bf16),
+            pltpu.VMEM((blocks, quarter, columns), bf16),
             pltpu.VMEM((blocks, LINES, shard, columns), bf16),
             pltpu.VMEM((blocks, LINES - 1, shard, columns), bf16),
             pltpu.VMEM((blocks, shard, columns), bf16),
@@ -1148,13 +1357,11 @@
             pltpu.VMEM(first.shape, bf16),
             pltpu.VMEM(line_sums.shape, bf16),
             pltpu.VMEM(line_sums.shape, bf16),
-            pltpu.VMEM((5, *small.shape), f32),
-            pltpu.VMEM((5, *small.shape), f32),
-            pltpu.VMEM(merged.shape, bf16),
-            pltpu.VMEM(merged.shape, bf16),
-            pltpu.VMEM((rows, width), bf16),
-            pltpu.VMEM((rows, width), f32),
-            pltpu.VMEM((rows, width), f32),
+            pltpu.VMEM((LINES - 1, *late.shape[1:]), bf16),
+            pltpu.VMEM(late.shape[1:], bf16),
+            pltpu.VMEM(late.shape[1:], bf16),
+            pltpu.VMEM((5, *small), f32),
+            pltpu.VMEM((5, *small), f32),
             dma((blocks, 2)),
             dma((blocks, 2)),
             dma((blocks, LINES - 1)),
@@ -1162,15 +1369,21 @@
             dma((blocks, 2)),
             dma((2,)),
             dma((2,)),
+            dma((LINES - 1,)),
+            dma((LINES - 1,)),
+            dma((2,)),
             dma((5, 2)),
-            dma((4,)),
+            dma((14,)),
             dma((1,)),
         ],
         compiler_params=pltpu.CompilerParams(
-            vmem_limit_bytes=56 * 2**20, collective_id=4, has_side_effects=True
+            vmem_limit_bytes=60 * 2**20, collective_id=4, has_side_effects=True
         ),
         cost_estimate=NO_COST,
-    )(far, cross, own, line_sums, line_got, first, small, merged, weight, tokens, resid, gain)
+    )(
+        line_sums, line_got, late, first, ffn_gain, bias, cosine, sine, qgain, kgain, gain,
+        normed, dq, got_kv, own_kv, *raws, weight, tokens, resid,
+    )
 
 
 def rms_forward(values, gain_vec):
@@ -1263,12 +1476,10 @@
         ]
     ).astype(jnp.int32)
 
+    fused = places == 16 and seq_count == 2
     gains = jnp.stack([attn_gain, ffn_gain], axis=1)
     gather = lambda w: lax.all_gather(w, "dp", axis=0, tiled=True)
-    first_shard = jnp.concatenate(
-        [in_proj, out_proj, jnp.pad(gains, ((0, 0), (0, PAIR - 2)))], axis=1
-    )
-    fused = places == 16 and seq_count == 2
+    first_shard = jnp.concatenate([in_proj, out_proj, jnp.pad(gains, ((0, 0), (0, PAIR - 2)))], axis=1)
     if fused:
         wide, *there = gather_first(first_shard, tokens, time_ids.reshape(-1, PAIR), places)
         slots = [(tokens, time_ids), (there[0], there[1].reshape(-1))]
@@ -1282,16 +1493,18 @@
     ffn_gain_f = wide[:, 4 * width + 1].astype(f32)[None, :]
     shard = in_proj.shape[0]
     hidden_part = down_proj.shape[0] // 2
+    folds = hidden_part // shard
+
     columns = gate_up.reshape(shard, 2, places, 2, hidden_part)
-    folds = down_proj.reshape(2, hidden_part // shard, shard, width)
-    ffn_weights = []
-    for part in range(2):
-        piece = jnp.concatenate(
+    fold_rows = down_proj.reshape(2, folds, shard, width)
+    ffn_weights = [
+        jnp.concatenate(
             [columns[:, 0, :, part].reshape(shard, -1), columns[:, 1, :, part].reshape(shard, -1)]
-            + [folds[part, k] for k in range(hidden_part // shard)],
+            + [fold_rows[part, k] for k in range(folds)],
             axis=1,
         )
-        ffn_weights.append(piece)
+        for part in range(2)
+    ]
     ffn_weights[0] = gather(after(ffn_weights[0], wide))
 
     positions = jnp.arange(pack_rows, dtype=jnp.int32)
@@ -1342,35 +1555,30 @@
 
     inputs_f = tokens.astype(f32)
     residual = inputs_f + dot(attended, out_full)
-    normed_ffn, ffn_scale = rms_forward(residual, ffn_gain_f)
+    normed_ffn, _ = rms_forward(residual, ffn_gain_f)
     normed_ffn_low = normed_ffn.astype(bf16)
-    def x_part(received, own, far):
-        total = received.astype(f32) + own.astype(f32) + far[groups:].astype(f32)
-        return total.astype(bf16)
-
     def scatter_line(parts):
         lines = [[line * 4 + k for line in range(groups)] for k in range(4)]
         return lax.psum_scatter(parts, "dp", scatter_dimension=0, axis_index_groups=lines, tiled=True)[0]
 
-    branch, normed_ffn_grad, *grads = feed_forward(
+    def total3(first, *others):
+        return sum((other.astype(f32) for other in others), first.astype(f32)).astype(bf16)
+
+    branch, normed_ffn_grad, early_far, early_cross, early_own = feed_forward(
         places, normed_ffn_low, seed_low, residual, None, ffn_weights[0]
     )
-    far, cross, own = grads
-    layer_out, normed_ffn_grad, *grads, received = feed_forward(
-        places, normed_ffn_low, seed_low, branch, normed_ffn_grad, ffn_weights[1], cross + far[:groups]
+    crossed = early_cross[:, :2] + early_far[:groups, :2]
+    early_crossed = early_cross[:, 2] + early_far[:groups, 2]
+    layer_out, residual_grad, mixed_low, ffn_gain_sum, far, cross, own, received = feed_forward(
+        places, after(normed_ffn_low, early_crossed), seed_low, branch, normed_ffn_grad,
+        ffn_weights[1], residual, ffn_gain_f, crossed,
     )
-    first_total = scatter_line(x_part(received, own, far))
-    far, cross, own = grads
+    first_total = scatter_line(total3(received, early_own[:, :2], early_far[groups:, :2]))
     second_crossed = cross + far[:groups]
-    resid_norm_grad, ffn_gain_terms = rms_backward(residual, ffn_scale, ffn_gain_f, normed_ffn_grad)
-    residual_grad = seed_grad + resid_norm_grad
-    mixed_low = residual_grad.astype(bf16)
     attended_grad = dot(mixed_low, out_full, NT).astype(bf16)
 
     attended_grad = dot(mixed_low, out_full, NT).astype(bf16)
     out_grads = outer(spot, attended, mixed_low, width)
-    folds = hidden_part // shard
-    ffn_gain_sum = jnp.sum(ffn_gain_terms, axis=0)
 
     def merge(dqs, dkvs):
         merged, gains = merge_grads(width, 0, dqs, dkvs, raws, cosine, sine, qgain, kgain)
@@ -1379,7 +1587,7 @@
     def small_parts(bias, head_gains):
         same_bias = jnp.sum(bias, axis=-1).reshape(-1)
         tail = jnp.concatenate([head_gains[0], head_gains[1], same_bias])
-        return jnp.concatenate([ffn_gain_sum, tail, jnp.zeros(-tail.shape[0] % 1024, f32)])
+        return jnp.concatenate([ffn_gain_sum[0], tail, jnp.zeros(-tail.shape[0] % 1024, f32)])
 
     if fused:
         (out_far,), out_cross, out_own = (cross_core(out_grads[0], places),), *out_grads[1:]
@@ -1387,23 +1595,23 @@
         out_sums = [
             by_line(array) for array in (out_cross + out_far[:, : shard * groups], out_own, out_far[:, shard * groups :])
         ]
-        dq_all, bias_all, received, own_kv, line_sums, line_got, *_ = attend_back_carry(
+        dq_all, bias_all, received, own_kv, line_sums, line_got, late, *_ = attend_back_carry(
             full_query, attended_grad, attended, query_columns, keyed[0], keyed[1],
-            (second_crossed, own, far[groups:]), out_sums,
-        )
-        merged_grad, head_gains = merge([(dq_all, 0), (dq_all, 1)], [(received, 0), (own_kv, 0)])
-        in_grads = outer(spot, normed_low, merged_grad, width)
-        half = bias_all.shape[0] // 2
-        small = small_parts(bias_all[:half] + bias_all[half:], head_gains)
-        small = jnp.concatenate([jnp.zeros(width, f32), small]).reshape(-1, PAIR)
-        in_sum, first_sum, second_sum, small, input_grad = finish(
-            in_grads, line_sums, line_got, first_total, small, merged_grad, wide, tokens,
-            residual_grad, attn_gain_f,
-        )
-        small = small.reshape(-1)
-        out_proj_grad = second_sum[3, :, :width]
+            (early_crossed, early_own, early_far), (second_crossed, own, far), out_sums,
+        )
+        in_proj_grad, out_proj_grad, gate_up_grad, down_grad, small, input_grad = finish(
+            places, line_sums, line_got, late, first_total, ffn_gain_sum.reshape(-1, PAIR), bias_all,
+            cosine, sine, qgain, kgain, attn_gain_f, normed_low, dq_all, received, own_kv, raws,
+            wide, tokens, residual_grad,
+        )
+        rows_done = 2 * width // PAIR
+        head_gains = jnp.sum(small[rows_done : rows_done + 2].reshape(2, 2, head_dim), axis=1)
+        same_bias = jnp.sum(small[rows_done + 8 :], axis=1)
+        small = jnp.concatenate([small[:rows_done].reshape(-1), head_gains.reshape(-1), same_bias])
     else:
-        second = scatter_line(x_part(cross_x(second_crossed, places), own, far))
+        second = scatter_line(total3(cross_x(second_crossed, places), own, far[groups:]))
+        early_down = total3(cross_x(early_crossed, places), early_own[:, 2], early_far[groups:, 2])
+        early_down = scatter_line(early_down)
         dqs, dkvs, biases = [], [], 0.0
         for step in list(range(1, seq_count)) + [0]:
             dq, dkv, bias = attend_back(
@@ -1423,8 +1631,20 @@
 
         in_sum = sum_rows(outer(spot, normed_low, merged_grad, width))
         out_proj_grad = sum_rows(out_grads)[0]
-        first_sum = sum_seq(first_total, seq_count)
+        in_proj_grad = in_sum.transpose(1, 0, 2).reshape(in_proj.shape)
+        first_gates = sum_seq(first_total, seq_count)
         second_sum = sum_seq(second, seq_count)
+        downs = [sum_seq(early_down, seq_count), second_sum[2]]
+        down_grad = jnp.concatenate(
+            [part.reshape(shard, -1, width).transpose(1, 0, 2).reshape(hidden_part, width) for part in downs]
+        )
+        gate_up_grad = jnp.stack(
+            [
+                part.reshape(2, shard, places, hidden_part).transpose(1, 0, 2, 3)
+                for part in (first_gates, second_sum[:2])
+            ],
+            axis=3,
+        ).reshape(gate_up.shape)
         normed_grad = dot(merged_grad, wide[:, : 3 * width], NT)
         norm_scale = lax.rsqrt(jnp.mean(inputs_f * inputs_f, axis=-1, keepdims=True) + EPSILON)
         input_norm_grad, attn_gain_terms = rms_backward(inputs_f, norm_scale, attn_gain_f, normed_grad)
@@ -1432,20 +1652,6 @@
         small = jnp.concatenate([jnp.sum(attn_gain_terms, axis=0), small_parts(biases, head_gains)])
         small = sum_small(small, places, seq_count)
     heads = head_bias.shape[0]
-    in_proj_grad = in_sum.transpose(1, 0, 2).reshape(in_proj.shape)
-    down_grad = jnp.concatenate(
-        [
-            part[2].reshape(shard, -1, width).transpose(1, 0, 2).reshape(hidden_part, width)
-            for part in (first_sum, second_sum)
-        ]
-    )
-    gate_up_grad = jnp.stack(
-        [
-            part[:2].reshape(2, shard, places, hidden_part).transpose(1, 0, 2, 3)
-            for part in (first_sum, second_sum)
-        ],
-        axis=3,
-    ).reshape(gate_up.shape)
     gain_rows = attn_gain.shape[0]
     here = place * gain_rows
     tail = small[2 * width :]

time: 655 us -> 573 us (0.87)
  Pallas kernels: 519 us -> 451 us
  local copies, waits for them, and re-layouts: 48.6 us -> 32 us
  waiting for transfers between devices: 15 us -> 27.3 us
  other arithmetic: 41.5 us -> 30.2 us
    pallas_call x2, Pallas kernels: 148 us -> 114 us  [feed_forward(): pl.pallas_call(functools.partial(ffn_kernel, places, first), grid=(steps,...]
    all_gather x2, waiting for transfers between devices: 14.9 us -> 27.2 us  [body(): gather = lambda w: lax.all_gather(w, 'dp', axis=0, tiled=True)]
    pallas_call x2 -> x1, Pallas kernels: 84.5 us -> 72.9 us  [finish(): pl.pallas_call(finish_kernel, in_specs=[vmem] * 11 + [anywhere] * 9, out_...]
    pallas_call x1, Pallas kernels: 128 us -> 117 us  [attend_back_carry(): pl.pallas_call(functools.partial(carry_kernel, pairs), grid=(2 * pairs,),...]
    pallas_call x2 -> x1, Pallas kernels: 15.8 us -> 5.08 us  [outer(): pl.pallas_call(functools.partial(outer_kernel, places), grid_spec=pltpu.P...]
    convert_element_type x2 -> x1, other arithmetic: 11.9 us -> 4.99 us  [total3(): sum((other.astype(f32) for other in others), first.astype(f32)).astype(bf16)]
    unnamed x90 -> x88, local copies, waits for them, and re-layouts: 19.2 us -> 20.7 us
  transfers between devices with their start and end apart: 4 -> 4, of which waited for: 1 -> 1; matrix products, arithmetic and copies ran while one was open for 6% -> 6% of each run, Pallas kernels for 48% -> 46%
where the time goes in v5:
time: 573 us; the launch traced here: 569 us
  Pallas kernels  451 us (79%)
  local copies, waits for them, and re-layouts  32 us (6%)
  other arithmetic  30.2 us (5%)
  waiting for transfers between devices  27.3 us (5%)
  between operations  15.9 us (3%)
  matrix products  11 us (2%)
    pallas_call x1, Pallas kernels, attend_back_carry(): pl.pallas_call(functools.partial(carry_kernel, pairs), grid=(2 * pairs,),...  117 us
    pallas_call x2, Pallas kernels, feed_forward(): pl.pallas_call(functools.partial(ffn_kernel, places, first), grid=(steps,...  114 us
    pallas_call x1, Pallas kernels, finish(): pl.pallas_call(finish_kernel, in_specs=[vmem] * 11 + [anywhere] * 9, out_...  72.9 us
    pallas_call x1, Pallas kernels, gather_first(): pl.pallas_call(gather_kernel, in_specs=[anywhere] * 3, out_specs=[anywher...  57.4 us
    pallas_call x1, Pallas kernels, attend(): pl.pallas_call(functools.partial(forward_kernel, sources, min(512, rows))...  49.7 us
    pallas_call x2, Pallas kernels, project(): pl.pallas_call(qkv_kernel, grid=(rows // block,), in_specs=[pl.BlockSpec(...  35.6 us
    all_gather x2, waiting for transfers between devices, body(): gather = lambda w: lax.all_gather(w, 'dp', axis=0, tiled=True)  27.2 us
    unnamed x88, local copies, waits for them, and re-layouts  20.7 us
  transfers between devices with their start and end apart: 4, of which 1 were waited for; matrix products, arithmetic and copies ran while one was open for 6% of the time, Pallas kernels for 46%

profile of v5, /device:TPU:0, one launch (start us, length us, event | category | flops | bytes accessed | tf_op | source)
XLA Modules:
  0.0 568.6 jit_solution(4461707228653562745)
XLA Ops:
  8.0 1.8 reshape.207
  9.8 5.6 slice_reduce_fusion.1
  17.3 57.4 %shard_map.221 = (bf16[1024,4224]{1,0:T(8,128)(2,1)}, bf16[1024,1024]{1,0:T(8,128)(2,1)}, s32[8,128]{1,0:T(8,128)}) custom-call(bf16[64,4224]{1,0:T(8,128)(2,1)} %fusion.4.shard_ref, bf16[1024,1024]{1,0:T(8,128)(2,1)} %tokens_ref.5, s32[8,128]{1,0:T(8,128)} %bitcast.97), custom_call_target="tpu_custom_call" | custom-call | flops 1 | bytes 1 | tf_op jit(solution)/shard_map/pallas_call | solution.py:179
  77.9 3.7 fusion.6
  81.6 22.5 %shard_map.222 = (bf16[1024,1024]{1,0:T(8,128)(2,1)S(1)}, bf16[1024,1024]{1,0:T(8,128)(2,1)S(1)}, bf16[1024,1024]{1,0:T(8,128)(2,1)}, f32[1024,1024]{1,0:T(8,128...) custom-call(bf16[1024,1024]{1,0:T(8,128)(2,1)} %tokens_ref.5, f32[1,1024]{1,0:T(1,128)S(1)} %bitcast.80, ...), custom_call_target="tpu_custom_call" | custom-call | flops 1 | bytes 1 | tf_op jit(solution)/shard_map/pallas_call | solution.py:241
  107.2 13.1 %shard_map.223 = (bf16[1024,1024]{1,0:T(8,128)(2,1)S(1)}, bf16[1024,1024]{1,0:T(8,128)(2,1)S(1)}) custom-call(bf16[1024,1024]{1,0:T(8,128)(2,1)} %get-tuple-element.60.tokens_ref, f32[1,1024]{1,0:T(1,128)S(1)} %bitcast.81, bf16[1024,4224]{1,0:T(8,128)(2,1)} %get-tuple-element.56.weight_ref, f32[1024,128]{1,0:T(8,128)S(1)} %get-tuple-element.127.cos_ref, ...), custom_call_target="tpu_custom_call" | custom-call | flops 1 | bytes 1 | tf_op jit(solution)/shard_map/pallas_call | solution.py:241
  129.6 1.6 copy-done.7
  131.2 49.7 %shard_map.224 = (bf16[1024,1024]{1,0:T(8,128)(2,1)S(1)}, bf16[1024,2048]{1,0:T(8,128)(2,1)}) custom-call(s32[8]{0:T(128)S(1)} %add_convert_fusion.1.flags, bf16[1024,1024]{1,0:T(8,128)(2,1)S(1)} %copy-done.7, bf16[1024,128]{1,0:T(8,128)(2,1)S(1)} %select_convert_fusion.aq_ref, bf16[8,2,128]{2,1,0:T(2,128)(2,1)S(1)} %bitcast.83, ...), custom_call_target="tpu_custom_call" | custom-call | flops 1 | bytes 1 | tf_op jit(solution)/shard_map/pallas_call | solution.py:385
  181.0 4.9 multiply_reduce_fusion
  185.9 2.0 multiply_convert_fusion.seed_ref
  188.5 1.7 multiply_convert_fusion.1.nf_ref
  190.2 54.5 %shard_map.225 = (f32[1024,1024]{1,0:T(8,128)}, f32[1024,1024]{1,0:T(8,128)}, bf16[8,3,64,2048]{3,2,1,0:T(8,128)(2,1)}, bf16[4,3,64,2048]{3,2,1,0:T(8,128)(2,1)}, bf16[4,3,64,2048]{3,2,1,0:T(8,128)(2,1)}) custom-call(bf16[1024,1024]{1,0:T(8,128)(2,1)} %multiply_convert_fusion.1.nf_ref, bf16[1024,1024]{1,0:T(8,128)(2,1)} %multiply_convert_fusion.seed_ref, ...), custom_call_target="tpu_custom_call" | custom-call | flops 1 | bytes 1 | tf_op jit(solution)/shard_map/pallas_call | solution.py:952
  244.7 3.1 fusion.3.early_across_ref
  247.8 3.2 slice_add_fusion.1.refs_2_
  251.0 27.2 %all-gather.5.cloned.1.call-done.wg_ref.wu_ref.wd_ref = bf16[1024,6144]{1,0:T(8,128)(2,1)} async-done(((bf16[64,6144]{1,0:T(8,128)(2,1)}), bf16[1024,6144]{1,0:T(8,128)(2,1)}) %all-gather.5.cloned.1.call-update) | async-done | bytes 12582928 | tf_op jit(solution)/shard_map/all_gather | solution.py:1481
  278.3 59.1 %shard_map.226 = (bf16[1024,1024]{1,0:T(8,128)(2,1)}, f32[1024,1024]{1,0:T(8,128)}, bf16[1024,1024]{1,0:T(8,128)(2,1)}, f32[1,1024]{1,0:T(1,128)}, bf16[8,3,64,2...) custom-call(bf16[1024,1024]{1,0:T(8,128)(2,1)} %multiply_convert_fus, ...), custom_call_target="tpu_custom_call" | custom-call | flops 1 | bytes 1 | tf_op jit(solution)/shard_map/pallas_call | solution.py:952
  337.5 5.0 add_convert_fusion
  342.7 5.1 shard_map.227
  348.2 6.1 %convolution_convert_fusion.grad_ref = bf16[1024,1024]{1,0:T(8,128)(2,1)} fusion(bf16[1024,1024]{1,0:T(8,128)(2,1)} %get-tuple-element.74.right_ref, bf16[1024,4224]{1,0:T(8,128)(2,1)} %get-tuple-element.56.weight_ref), kind=kOutput, calls=%fused_computation.7 | convolution fusion | flops 2148532224 | bytes 6291456 | tf_op jit(solution)/shard_map/dot_general | solution.py:26
  354.3 2.0 slice_add_fusion.across_ref
  356.4 117.1 %shard_map.228 = (bf16[1024,2048]{1,0:T(8,128)(2,1)}, f32[16,2,128]{2,1,0:T(2,128)S(1)}, bf16[2,1024,1024]{2,1,0:T(8,128)(2,1)}, bf16[2,1024,1024]{2,1,0:T(8,128...) custom-call(bf16[1024,2048]{1,0:T(8,128)(2,1)} %get-tuple-element.73, ...), custom_call_target="tpu_custom_call" | custom-call | flops 1 | bytes 1 | tf_op jit(solution)/shard_map/pallas_call | solution.py:695
  476.0 72.9 %shard_map.229 = (f32[64,3072]{1,0:T(8,128)}, f32[64,1024]{1,0:T(8,128)}, f32[64,8192]{1,0:T(8,128)}, f32[256,1024]{1,0:T(8,128)}, f32[40,128]{1,0:T(8,128)}, /*index=5*/f32[1024,1024]{1,0:T(8,128)}) custom-call(bf16[4,64,2048]{2,1,0:T(8,128)(2,1)} %copy-done.8, bf16[3,4,64,2048]{3,2,1,0:T(8,128)(2,1)} %get-tuple-element.83.line_got_ref, ...), custom_call_target="tpu_custom_call" | custom-call | flops 1 | bytes 1 | tf_op jit(solution)/shard_map/pallas_call | solution.py:1326
  553.6 1.6 copy-done.17
  555.2 2.1 copy.79
  (146 shorter events, 29.6 us)
Async XLA Ops:
  7.2 183.1 %all-gather.3.cloned.1.call-start = ((), (), s32[]{:S(2)}) async-start(), calls=%async_computation.1 | async-start | bytes 13369344 | tf_op jit(solution)/shard_map/all_gather | solution.py:1481
  9.8 5.9 %copy-start.25 = (bf16[256,1024]{1,0:T(8,128)(2,1)S(1)}, bf16[256,1024]{1,0:T(8,128)(2,1)}, u32[]{:S(2)}) copy-start(bf16[256,1024]{1,0:T(8,128)(2,1)} %param.21) | copy-start | bytes 1572868
  74.7 3.2 copy-start.32
  76.0 202.3 %all-gather.5.cloned.1.call-start = ((), (), s32[]{:S(2)}) async-start(), calls=%async_computation.2 | async-start | bytes 13369344 | tf_op jit(solution)/shard_map/all_gather | solution.py:1481
  76.4 30.7 %copy-start.12 = (f32[1,128]{1,0:T(1,128)}, f32[1,128]{1,0:T(1,128)S(1)}, u32[]{:S(2)}) copy-start(f32[1,128]{1,0:T(1,128)S(1)} %broadcast_in_dim_tile.8.qgain_ref) | copy-start | bytes 1540
  76.5 30.6 %copy-start.13 = (f32[1,128]{1,0:T(1,128)}, f32[1,128]{1,0:T(1,128)S(1)}, u32[]{:S(2)}) copy-start(f32[1,128]{1,0:T(1,128)S(1)} %broadcast_in_dim_tile.9.kgain_ref) | copy-start | bytes 1540
  77.9 29.3 %copy-start.10 = (f32[1024]{0:T(1024)}, f32[1024]{0:T(1024)S(1)}, u32[]{:S(2)}) copy-start(f32[1024]{0:T(1024)S(1)} %get-tuple-element.102) | copy-start | bytes 12292
  77.9 110.1 %copy-start.29 = (f32[1024]{0:T(1024)}, f32[1024]{0:T(1024)S(1)}, u32[]{:S(2)}) copy-start(f32[1024]{0:T(1024)S(1)} %get-tuple-element.101) | copy-start | bytes 12292
  81.6 22.5 %copy-start.5 = (f32[1024,128]{1,0:T(8,128)}, f32[1024,128]{1,0:T(8,128)S(1)}, u32[]{:S(2)}) copy-start(f32[1024,128]{1,0:T(8,128)S(1)} %get-tuple-element.134.cos_ref) | copy-start | bytes 1572868
  81.6 22.5 %copy-start.6 = (f32[1024,128]{1,0:T(8,128)}, f32[1024,128]{1,0:T(8,128)S(1)}, u32[]{:S(2)}) copy-start(f32[1024,128]{1,0:T(8,128)S(1)} %get-tuple-element.135.sin_ref) | copy-start | bytes 1572868
  106.8 369.2 %reduce-scatter.2.cloned.1.call-start = ((), (), s32[]{:S(2)}) async-start(), calls=%async_computation.3 | async-start | bytes 2621440 | tf_op jit(solution)/shard_map/reduce_scatter | solution.py:1562
  107.1 15.9 %copy-start.33 = (s32[1,2]{1,0:T(1,128)S(1)}, s32[1,2]{1,0:T(1,128)}, u32[]{:S(2)}) copy-start(s32[1,2]{1,0:T(1,128)} %param.15) | copy-start | bytes 28
  107.1 18.4 %copy-start.34 = (f32[16,2]{0,1:T(2,128)S(1)}, f32[16,2]{0,1:T(2,128)}, u32[]{:S(2)}) copy-start(f32[16,2]{0,1:T(2,128)} %param.26) | copy-start | bytes 388
  107.1 20.9 %copy-start.31 = (s32[1,2048]{1,0:T(1,128)S(1)}, s32[1,2048]{1,0:T(1,128)}, u32[]{:S(2)}) copy-start(s32[1,2048]{1,0:T(1,128)} %param.16) | copy-start | bytes 24580
  131.2 49.8 %copy-start.15 = (bf16[1024,1024]{1,0:T(8,128)(2,1)S(1)}, bf16[1024,1024]{1,0:T(8,128)(2,1)}, u32[]{:S(2)}) copy-start(bf16[1024,1024]{1,0:T(8,128)(2,1)} %tokens_ref.5) | copy-start | bytes 6291460
  180.9 161.7 %copy-start = (bf16[1024,1024]{1,0:T(8,128)(2,1)}, bf16[1024,1024]{1,0:T(8,128)(2,1)S(1)}, u32[]{:S(2)}) copy-start(bf16[1024,1024]{1,0:T(8,128)(2,1)S(1)} %get-tuple-element.64.left_ref.out_ref) | copy-start | bytes 6291460
  181.0 4.9 copy-start.20
  278.3 59.2 %copy-start.16 = (bf16[4,3,64,2048]{3,2,1,0:T(8,128)(2,1)S(1)}, bf16[4,3,64,2048]{3,2,1,0:T(8,128)(2,1)}, u32[]{:S(2)}) copy-start(bf16[4,3,64,2048]{3,2,1,0:T(8,128)(2,1)} %get-tuple-element.75.early_own_ref) | copy-start | bytes 9437188
  347.8 8.5 %collective-permute-start = (bf16[1,512,1024]{2,1,0:T(8,128)(2,1)S(1)}, bf16[1,512,1024]{2,1,0:T(8,128)(2,1)S(1)}, u32[]{:S(2)}, u32[]{:S(2)}) collective-permute-start(bf16[1,512,1024]{2,1,0:T(8,128)(2,1)S(1)} %get-tuple-element.80), channel_id=1, source_target_pairs={{0,2},{2,0},{4,6},{6,4},{8,10},{10,8},{12,14},{14,12},{16,18},{18,... | collective-permute-start | bytes 3145736 | tf_op jit(solution)/shard_map/ppermute | solution.py:1406
  348.2 6.1 %slice-start = ((s8[6291456]{0:T(1024)(128)(4,1)}), s8[4194304]{0:T(1024)(128)(4,1)S(1)}, s32[]{:S(2)}) async-start(s8[6291456]{0:T(1024)(128)(4,1)} %bitcast.84), calls=%async_computation.4 | async-start | bytes 8388608
  348.2 6.1 %slice-start.1 = ((s8[6291456]{0:T(1024)(128)(4,1)}), s8[2097152]{0:T(1024)(128)(4,1)S(1)}, s32[]{:S(2)}) async-start(s8[6291456]{0:T(1024)(128)(4,1)} %bitcast.84), calls=%async_computation.5 | async-start | bytes 4194304
  348.2 6.1 %copy-start.19 = (bf16[4,3,64,2048]{3,2,1,0:T(8,128)(2,1)S(1)}, bf16[4,3,64,2048]{3,2,1,0:T(8,128)(2,1)}, u32[]{:S(2)}) copy-start(bf16[4,3,64,2048]{3,2,1,0:T(8,128)(2,1)} %get-tuple-element.76) | copy-start | bytes 9437188
  476.0 76.3 %copy-start.21 = (bf16[1024,1024]{1,0:T(8,128)(2,1)S(1)}, bf16[1024,1024]{1,0:T(8,128)(2,1)}, u32[]{:S(2)}) copy-start(bf16[1024,1024]{1,0:T(8,128)(2,1)} %get-tuple-element.161) | copy-start | bytes 6291460
  555.2 3.7 copy-start.22
  (19 other events, 32.3 us)
Sparse Core Ops, SparseCore 0:
  76.1 100.9 all-gather.2
  179.3 98.9 all-gather.4
  342.6 46.6 reduce-scatter.1

commit v6 on v5

--- a/solution.py
+++ b/solution.py
@@ -209,7 +209,7 @@
     turned = [(1, k_ref, kgain_ref[...], 1.0)]
     if own_refs:
         q_ref, *raw_refs, normed_ref = own_refs
-        normed_ref[...] = normed
+        normed_ref[...] = normed.T
         turned.append((0, q_ref, qgain_ref[...], 0.125))
     for part, out_ref, head_gain, scale in turned:
         for chunk in range(width // 256):
@@ -235,7 +235,7 @@
     rows, width = tokens.shape
     sizes = [(width, bf16), (width, bf16)]
     if own:
-        sizes += [(width, bf16), (width, f32), (width, f32), (width, bf16)]
+        sizes += [(width, bf16), (width, f32), (width, f32)]
     by_rows = lambda i: (i, 0)
     whole = lambda i: (0, 0)
     return pl.pallas_call(
@@ -250,8 +250,10 @@
             pl.BlockSpec((1, PAIR), whole),
             pl.BlockSpec((1, PAIR), whole),
         ],
-        out_specs=[pl.BlockSpec((block, size), by_rows) for size, _ in sizes],
-        out_shape=[jax.ShapeDtypeStruct((rows, size), kind) for size, kind in sizes],
+        out_specs=[pl.BlockSpec((block, size), by_rows) for size, _ in sizes]
+        + [pl.BlockSpec((width, block), lambda i: (0, i))] * own,
+        out_shape=[jax.ShapeDtypeStruct((rows, size), kind) for size, kind in sizes]
+        + [jax.ShapeDtypeStruct((width, rows), bf16)] * own,
         compiler_params=pltpu.CompilerParams(vmem_limit_bytes=VMEM_BYTES),
         cost_estimate=NO_COST,
     )(tokens, gain, weight, cosine, sine, qgain, kgain)
@@ -645,9 +647,12 @@
 
     backward_start(grad_ref, out_ref, grads, dq_total)
     is_far = step < pairs
-    for b in range(far_k_ref.shape[0] // KEY_ROWS):
-        at = slice(b * KEY_ROWS, (b + 1) * KEY_ROWS)
-        go_on(b)
+    key_rows = min(512, far_k_ref.shape[0])
+    key_blocks = far_k_ref.shape[0] // key_rows
+    for b in range(key_blocks):
+        at = slice(b * key_rows, (b + 1) * key_rows)
+        for quarter in range(4 * b // key_blocks, 4 * (b + 1) // key_blocks):
+            go_on(quarter)
         block = [
             jnp.where(is_far, far[at, :], near[at, :])
             for far, near in ((far_k_ref, near_k_ref), (far_v_ref, near_v_ref), (far_ak_ref, near_ak_ref))
@@ -1053,14 +1058,14 @@
 
 
 def finish_kernel(
-    line_ref, line_got_ref, late_ref, first_ref, ffn_ref, bias_ref, cos_ref, sin_ref, qgain_ref, kgain_ref, gain_ref,
-    normed_ref, dq_ref, got_kv_ref, own_kv_ref, rawq_ref, rawk_ref, weight_ref, tokens_ref, resid_ref,
+    line_ref, late_ref, first_ref, ffn_ref, bias_ref, cos_ref, sin_ref, qgain_ref, kgain_ref, gain_ref,
+    line_got_ref, normed_ref, dq_ref, got_kv_ref, own_kv_ref, rawq_ref, rawk_ref, weight_ref, tokens_ref, resid_ref,
     in_ref, out_ref, gate_up_ref, down_ref, small_out_ref, grad_ref,
     merged, low_a, low_b, low_c, low_d, wide_a, wide_b, sums,
-    arranged, far, own, core_got, x_sent, x_got, z_sent, z_got, y_sent, y_got,
+    line_there, arranged, far, own, core_got, x_sent, x_got, z_sent, z_got, y_sent, y_got,
     first_got, second, second_got, late_got, late, late_there, small_sent, small_got,
     core_sems, x_sems, z_send, z_recv, y_sems, first_sems, second_sems, late_send, late_recv, late_sems, small_sems,
-    load_sems, store_sem,
+    load_sems, row_sems, store_sem,
 ):
     place, rank = lax.axis_index("dp"), lax.axis_index("seq")
     line = place // 4
@@ -1072,7 +1077,7 @@
     low = line_device(place, line + 1 - line % 2 * 2)
     high = line_device(place, lax.rem(line + 2, LINES))
     blocks, quarter, columns = x_sent.shape
-    rows = merged.shape[0]
+    rows, width = merged.shape[0], low_a.shape[1]
     step = min(256, rows)
     shard = quarter // LINES
     places = 4 * LINES
@@ -1111,11 +1116,11 @@
         )
 
     def cut(ref, index):
-        return ref.at[:, pl.ds(index * columns, columns)]
+        return ref.at[:, pl.ds(index * width, width)]
 
     def load(k):
         source, target = (
-            (normed_ref, low_a), (own_kv_ref.at[1], low_b), (got_kv_ref.at[1], low_c),
+            (line_got_ref, line_there), (own_kv_ref.at[1], low_b), (got_kv_ref.at[1], low_c),
             (rawk_ref, wide_a), (own_kv_ref.at[0], low_d), (rawq_ref, wide_b),
             (got_kv_ref.at[0], low_a), (cut(dq_ref, 0), low_b), (cut(dq_ref, 1), low_c),
             (tokens_ref, low_d), (resid_ref, wide_a),
@@ -1138,17 +1143,20 @@
     for target in peers:
         pl.semaphore_signal(barrier, inc=1, device_id=target, device_id_type=mesh_id)
     pl.semaphore_wait(barrier, len(peers))
-    start(0, 1, 2, 4, 3, 5)
-    for copy in [first_y] + [late_z(k) for k in range(1, LINES)]:
-        copy.start()
-    ready(0)
-    turned = low_a[...].T
-    for i in range(places):
+    def arrange(i):
         near_core = (i % 2 == place % 2).astype(jnp.int32)
         near_x = (i // 2 % 2 == place // 2 % 2).astype(jnp.int32)
         at = pl.multiple_of(((near_core * 2 + near_x) * LINES + i // 4) * shard, shard)
-        arranged[pl.ds(at, shard), :] = turned[i * shard : (i + 1) * shard, :]
-    start(6)
+        return pltpu.make_async_copy(
+            normed_ref.at[pl.ds(i * shard, shard)], arranged.at[pl.ds(at, shard)], row_sems.at[i]
+        )
+
+    start(1, 2)
+    for i in range(places):
+        arrange(i).start()
+    for copy in [first_y] + [late_z(k) for k in range(1, LINES)]:
+        copy.start()
+    start(4, 3, 6, 0, 5)
 
     def product(begin, count, b):
         return dot(arranged[begin : begin + count, :], merged[:, b * columns : (b + 1) * columns])
@@ -1179,7 +1187,7 @@
         def some_rows(i, carry):
             at = pl.ds(pl.multiple_of(i * step, step), step)
             cosine, sine = cos_ref[at, :], sin_ref[at, :]
-            for tile in range(columns // PAIR):
+            for tile in range(width // PAIR):
                 lanes = slice(tile * PAIR, (tile + 1) * PAIR)
                 grad = left[at, lanes].astype(f32) + right[at, lanes].astype(f32)
                 grad = grad.astype(bf16).astype(f32)
@@ -1190,7 +1198,7 @@
                 sums[b : b + 1, :] += jnp.sum(grad * hat, axis=0, keepdims=True)
                 weighted = grad * head_gain
                 inner = head_sums(weighted * hat, ones) * (1.0 / 64)
-                there = slice(b * columns + tile * PAIR, b * columns + (tile + 1) * PAIR)
+                there = slice(b * width + tile * PAIR, b * width + (tile + 1) * PAIR)
                 merged[at, there] = (unit * (weighted - hat * inner)).astype(bf16)
             return carry
 
@@ -1200,27 +1208,35 @@
 
     def add_rows(i, carry):
         at = pl.ds(pl.multiple_of(i * step, step), step)
-        merged[at, 2 * columns :] = (low_b[at, :].astype(f32) + low_c[at, :].astype(f32)).astype(bf16)
+        merged[at, 2 * width :] = (low_b[at, :].astype(f32) + low_c[at, :].astype(f32)).astype(bf16)
         return carry
 
     lax.fori_loop(0, rows // step, add_rows, 0)
     start(7, 8)
-    send_block(2)
+    for i in range(places):
+        arrange(i).wait()
+    send_block(4)
+    send_block(5)
     ready(3, 4, 6)
     turn_back(1, low_d, low_a, wide_a, kgain_ref[...])
     start(9, 10, 13)
-    send_block(1)
+    send_block(2)
+    send_block(3)
+    ready(0)
     for i in range(line_ref.shape[0]):
         second[i] = sum(
-            part.astype(f32) for part in [line_ref[i]] + [line_got_ref[k, i] for k in range(LINES - 1)]
+            part.astype(f32) for part in [line_ref[i]] + [line_there[k, i] for k in range(LINES - 1)]
         ).astype(bf16)
     second_y.start()
+    pass_on(4)
     ready(5, 7, 8)
     turn_back(0, low_b, low_c, wide_b, qgain_ref[...])
     start(11, 12)
+    pass_on(5)
+    send_block(0)
+    send_block(1)
     pass_on(2)
-    send_block(0)
-    pass_on(1)
+    pass_on(3)
 
     ready(9, 10, 11, 12, 13)
     gain = gain_ref[...]
@@ -1228,7 +1244,7 @@
     for i in range(rows // step):
         at = slice(i * step, (i + 1) * step)
         normed_grad = sum(
-            dot(merged[at, b * columns : (b + 1) * columns], part[...], NT)
+            dot(merged[at, b * width : (b + 1) * width], part[...], NT)
             for b, part in enumerate((low_b, low_c, low_a))
         )
         values = low_d[at, :].astype(f32)
@@ -1239,7 +1255,7 @@
         wide_b[at, :] = wide_a[at, :] + inv * (weighted - hat * inner)
         gain_grad = gain_grad + jnp.sum(normed_grad * hat, axis=0, keepdims=True)
     store.start()
-    tiles = columns // PAIR
+    tiles = width // PAIR
     for k in range(tiles):
         small_sent[0, k : k + 1, :] = gain_grad[:, k * PAIR : (k + 1) * PAIR]
     small_sent[0, tiles : 2 * tiles, :] = ffn_ref[...]
@@ -1275,9 +1291,10 @@
     late_y.start()
     next_round(0)
     pass_on(0)
+    pass_on(1)
     next_round(1)
-    to_last(2)
-    to_last(1)
+    for b in (4, 5, 2, 3):
+        to_last(b)
     next_round(2)
     first_y.wait()
     second_y.wait()
@@ -1294,18 +1311,19 @@
                 gate_up_ref[:, at : at + part_columns] = halves[h][:, j * part_columns : (j + 1) * part_columns]
     next_round(3)
     to_last(0)
-    out_ref[...] = second[0, :, :columns].astype(f32) + second_got[0, :, :columns].astype(f32)
+    to_last(1)
+    out_ref[...] = second[0, :, :width].astype(f32) + second_got[0, :, :width].astype(f32)
     late_y.wait()
     for h in range(2):
         if h == 0:
             total = late[...].astype(f32) + late_there[...].astype(f32)
         else:
             total = second[3].astype(f32) + second_got[3].astype(f32)
-        for k in range(total.shape[1] // columns):
+        for k in range(total.shape[1] // width):
             at = h * down_ref.shape[0] // 2 + k * shard
-            down_ref[at : at + shard, :] = total[:, k * columns : (k + 1) * columns]
+            down_ref[at : at + shard, :] = total[:, k * width : (k + 1) * width]
     next_round(4)
-    for b in (2, 1, 0):
+    for b in (4, 5, 2, 3, 0, 1):
         to_y[b].wait()
         in_ref[:, b * columns : (b + 1) * columns] = y_sent[b].astype(f32) + y_got[b].astype(f32)
     store.wait()
@@ -1316,8 +1334,8 @@
     normed, dq, got_kv, own_kv, raws, weight, tokens, resid,
 ):
     rows, width = tokens.shape
-    blocks = 3
-    quarter, shard, columns = width // 4, width // places, width
+    blocks, columns = 6, width // 2
+    quarter, shard = width // 4, width // places
     hidden = line_sums.shape[2]
     small = (4 * width // PAIR + 8, PAIR)
     vmem = pl.BlockSpec(memory_space=pltpu.VMEM)
@@ -1325,25 +1343,26 @@
     dma = pltpu.SemaphoreType.DMA
     return pl.pallas_call(
         finish_kernel,
-        in_specs=[vmem] * 11 + [anywhere] * 9,
+        in_specs=[vmem] * 10 + [anywhere] * 10,
         out_specs=[vmem] * 5 + [anywhere],
         out_shape=[
             jax.ShapeDtypeStruct((shard, blocks * columns), f32),
-            jax.ShapeDtypeStruct((shard, columns), f32),
+            jax.ShapeDtypeStruct((shard, width), f32),
             jax.ShapeDtypeStruct((shard, 4 * hidden), f32),
-            jax.ShapeDtypeStruct((2 * hidden // places, columns), f32),
+            jax.ShapeDtypeStruct((2 * hidden // places, width), f32),
             jax.ShapeDtypeStruct(small, f32),
             jax.ShapeDtypeStruct((rows, width), f32),
         ],
         scratch_shapes=[
             pltpu.VMEM((rows, blocks * columns), bf16),
-            pltpu.VMEM((rows, columns), bf16),
-            pltpu.VMEM((rows, columns), bf16),
-            pltpu.VMEM((rows, columns), bf16),
-            pltpu.VMEM((rows, columns), bf16),
-            pltpu.VMEM((rows, columns), f32),
-            pltpu.VMEM((rows, columns), f32),
+            pltpu.VMEM((rows, width), bf16),
+            pltpu.VMEM((rows, width), bf16),
+            pltpu.VMEM((rows, width), bf16),
+            pltpu.VMEM((rows, width), bf16),
+            pltpu.VMEM((rows, width), f32),
+            pltpu.VMEM((rows, width), f32),
             pltpu.VMEM((8, PAIR), f32),
+            pltpu.VMEM(line_got.shape, bf16),
             pltpu.VMEM((width, rows), bf16),
             pltpu.VMEM((blocks, 2 * quarter, columns), bf16),
             pltpu.VMEM((blocks, quarter, columns), bf16),
@@ -1374,6 +1393,7 @@
             dma((2,)),
             dma((5, 2)),
             dma((14,)),
+            dma((places,)),
             dma((1,)),
         ],
         compiler_params=pltpu.CompilerParams(
@@ -1381,8 +1401,8 @@
         ),
         cost_estimate=NO_COST,
     )(
-        line_sums, line_got, late, first, ffn_gain, bias, cosine, sine, qgain, kgain, gain,
-        normed, dq, got_kv, own_kv, *raws, weight, tokens, resid,
+        line_sums, late, first, ffn_gain, bias, cosine, sine, qgain, kgain, gain,
+        line_got, normed, dq, got_kv, own_kv, *raws, weight, tokens, resid,
     )
 
 
@@ -1495,17 +1515,19 @@
     hidden_part = down_proj.shape[0] // 2
     folds = hidden_part // shard
 
-    columns = gate_up.reshape(shard, 2, places, 2, hidden_part)
-    fold_rows = down_proj.reshape(2, folds, shard, width)
-    ffn_weights = [
-        jnp.concatenate(
+    def weights_part(part, gate_up, down_proj):
+        columns = gate_up.reshape(shard, 2, places, 2, hidden_part)
+        fold_rows = down_proj.reshape(2, folds, shard, width)
+        return jnp.concatenate(
             [columns[:, 0, :, part].reshape(shard, -1), columns[:, 1, :, part].reshape(shard, -1)]
             + [fold_rows[part, k] for k in range(folds)],
             axis=1,
         )
-        for part in range(2)
+
+    ffn_weights = [
+        gather(after(weights_part(0, gate_up, down_proj), wide)),
+        weights_part(1, *after((gate_up, down_proj), wide)),
     ]
-    ffn_weights[0] = gather(after(ffn_weights[0], wide))
 
     positions = jnp.arange(pack_rows, dtype=jnp.int32)
     first_end = doc_lengths[0, 0]
@@ -1629,7 +1651,7 @@
             total = total.reshape(total.shape[0], groups, shard, -1).transpose(1, 0, 2, 3)
             return sum_seq(scatter_line(total), seq_count)
 
-        in_sum = sum_rows(outer(spot, normed_low, merged_grad, width))
+        in_sum = sum_rows(outer(spot, normed_low.T, merged_grad, width))
         out_proj_grad = sum_rows(out_grads)[0]
         in_proj_grad = in_sum.transpose(1, 0, 2).reshape(in_proj.shape)
         first_gates = sum_seq(first_total, seq_count)

time: 573 us -> 564 us (0.984)
  waiting for transfers between devices: 27.3 us -> 6.07 us
  Pallas kernels: 451 us -> 459 us
    all_gather x2, waiting for transfers between devices: 27.2 us -> 6.02 us  [body(): gather = lambda w: lax.all_gather(w, 'dp', axis=0, tiled=True)]
    pallas_call x1, Pallas kernels: 49.7 us -> 62.9 us  [attend(): pl.pallas_call(functools.partial(forward_kernel, sources, min(512, rows))...]
    unnamed x88 -> x86, local copies, waits for them, and re-layouts: 20.7 us -> 19.8 us
  transfers between devices with their start and end apart: 4 -> 4, of which waited for: 1 -> 1; matrix products, arithmetic and copies ran while one was open for 6% -> 7% of each run, Pallas kernels for 46% -> 49%
where the time goes in v6:
time: 564 us; the launch traced here: 559 us
  Pallas kernels  459 us (81%)
  local copies, waits for them, and re-layouts  35.4 us (6%)
  other arithmetic  30.9 us (5%)
  between operations  15.9 us (3%)
  matrix products  11 us (2%)
  waiting for transfers between devices  6.07 us (1%)
    pallas_call x1, Pallas kernels, attend_back_carry(): pl.pallas_call(functools.partial(carry_kernel, pairs), grid=(2 * pairs,),...  114 us
    pallas_call x2, Pallas kernels, feed_forward(): pl.pallas_call(functools.partial(ffn_kernel, places, first), grid=(steps,...  113 us
    pallas_call x1, Pallas kernels, finish(): pl.pallas_call(finish_kernel, in_specs=[vmem] * 10 + [anywhere] * 10, out...  69.8 us
    pallas_call x1, Pallas kernels, attend(): pl.pallas_call(functools.partial(forward_kernel, sources, min(512, rows))...  62.9 us
    pallas_call x1, Pallas kernels, gather_first(): pl.pallas_call(gather_kernel, in_specs=[anywhere] * 3, out_specs=[anywher...  57.4 us
    pallas_call x2, Pallas kernels, project(): pl.pallas_call(qkv_kernel, grid=(rows // block,), in_specs=[pl.BlockSpec(...  35.9 us
    unnamed x86, local copies, waits for them, and re-layouts  19.8 us
  transfers between devices with their start and end apart: 4, of which 1 were waited for; matrix products, arithmetic and copies ran while one was open for 7% of the time, Pallas kernels for 49%

profile of v6, /device:TPU:0, one launch (start us, length us, event | category | flops | bytes accessed | tf_op | source)
XLA Modules:
  0.0 559.0 jit_solution(11778302177781999799)
XLA Ops:
  8.1 1.8 reshape.213
  9.9 2.8 slice_reduce_fusion.3
  13.7 57.4 %shard_map.221 = (bf16[1024,4224]{1,0:T(8,128)(2,1)}, bf16[1024,1024]{1,0:T(8,128)(2,1)}, s32[8,128]{1,0:T(8,128)}) custom-call(bf16[64,4224]{1,0:T(8,128)(2,1)} %fusion.4.shard_ref, bf16[1024,1024]{1,0:T(8,128)(2,1)} %tokens_ref.5, s32[8,128]{1,0:T(8,128)} %bitcast.91), custom_call_target="tpu_custom_call" | custom-call | flops 1 | bytes 1 | tf_op jit(solution)/shard_map/pallas_call | solution.py:179
  74.1 3.7 fusion.6
  77.8 22.8 %shard_map.222 = (bf16[1024,1024]{1,0:T(8,128)(2,1)S(1)}, bf16[1024,1024]{1,0:T(8,128)(2,1)S(1)}, bf16[1024,1024]{1,0:T(8,128)(2,1)}, f32[1024,1024]{1,0:T(8,128...) custom-call(bf16[1024,1024]{1,0:T(8,128)(2,1)} %tokens_ref.5, f32[1,1024]{1,0:T(1,128)S(1)} %bitcast.77, ...), custom_call_target="tpu_custom_call" | custom-call | flops 1 | bytes 1 | tf_op jit(solution)/shard_map/pallas_call | solution.py:241
  105.8 4.4 slice_reduce_fusion.1
  111.6 13.1 %shard_map.223 = (bf16[1024,1024]{1,0:T(8,128)(2,1)S(1)}, bf16[1024,1024]{1,0:T(8,128)(2,1)S(1)}) custom-call(bf16[1024,1024]{1,0:T(8,128)(2,1)} %get-tuple-element.62.tokens_ref, f32[1,1024]{1,0:T(1,128)S(1)} %bitcast.78, bf16[1024,4224]{1,0:T(8,128)(2,1)} %get-tuple-element.58.weight_ref, f32[1024,128]{1,0:T(8,128)S(1)} %get-tuple-element.131.cos_ref, ...), custom_call_target="tpu_custom_call" | custom-call | flops 1 | bytes 1 | tf_op jit(solution)/shard_map/pallas_call | solution.py:241
  133.9 1.7 copy-done.7
  135.6 62.9 %shard_map.224 = (bf16[1024,1024]{1,0:T(8,128)(2,1)S(1)}, bf16[1024,2048]{1,0:T(8,128)(2,1)}) custom-call(s32[8]{0:T(128)S(1)} %add_convert_fusion.1.flags, bf16[1024,1024]{1,0:T(8,128)(2,1)S(1)} %copy-done.7, bf16[1024,128]{1,0:T(8,128)(2,1)S(1)} %select_convert_fusion.aq_ref, bf16[8,2,128]{2,1,0:T(2,128)(2,1)S(1)} %bitcast.80, ...), custom_call_target="tpu_custom_call" | custom-call | flops 1 | bytes 1 | tf_op jit(solution)/shard_map/pallas_call | solution.py:387
  198.5 4.9 multiply_reduce_fusion
  203.4 2.0 multiply_convert_fusion.seed_ref
  206.0 1.7 multiply_convert_fusion.1.nf_ref
  207.8 54.3 %shard_map.225 = (f32[1024,1024]{1,0:T(8,128)}, f32[1024,1024]{1,0:T(8,128)}, bf16[8,3,64,2048]{3,2,1,0:T(8,128)(2,1)}, bf16[4,3,64,2048]{3,2,1,0:T(8,128)(2,1)}, bf16[4,3,64,2048]{3,2,1,0:T(8,128)(2,1)}) custom-call(bf16[1024,1024]{1,0:T(8,128)(2,1)} %multiply_convert_fusion.1.nf_ref, bf16[1024,1024]{1,0:T(8,128)(2,1)} %multiply_convert_fusion.seed_ref, ...), custom_call_target="tpu_custom_call" | custom-call | flops 1 | bytes 1 | tf_op jit(solution)/shard_map/pallas_call | solution.py:957
  262.0 3.1 fusion.3.early_across_ref
  265.1 3.3 slice_add_fusion.1.refs_2_
  268.4 6.0 %all-gather.5.cloned.1.call-done.wg_ref.wu_ref.wd_ref = bf16[1024,6144]{1,0:T(8,128)(2,1)} async-done(((bf16[64,6144]{1,0:T(8,128)(2,1)}), bf16[1024,6144]{1,0:T(8,128)(2,1)}) %all-gather.5.cloned.1.call-update) | async-done | bytes 12582928 | tf_op jit(solution)/shard_map/all_gather | solution.py:1501
  274.4 59.1 %shard_map.226 = (bf16[1024,1024]{1,0:T(8,128)(2,1)}, f32[1024,1024]{1,0:T(8,128)}, bf16[1024,1024]{1,0:T(8,128)(2,1)}, f32[1,1024]{1,0:T(1,128)}, bf16[8,3,64,2...) custom-call(bf16[1024,1024]{1,0:T(8,128)(2,1)} %multiply_convert_fus, ...), custom_call_target="tpu_custom_call" | custom-call | flops 1 | bytes 1 | tf_op jit(solution)/shard_map/pallas_call | solution.py:957
  333.5 5.0 add_convert_fusion
  338.7 5.1 shard_map.227
  344.2 6.1 %convolution_convert_fusion.grad_ref = bf16[1024,1024]{1,0:T(8,128)(2,1)} fusion(bf16[1024,1024]{1,0:T(8,128)(2,1)} %get-tuple-element.78.right_ref, bf16[1024,4224]{1,0:T(8,128)(2,1)} %get-tuple-element.58.weight_ref), kind=kOutput, calls=%fused_computation.7 | convolution fusion | flops 2148532224 | bytes 6291456 | tf_op jit(solution)/shard_map/dot_general | solution.py:26
  350.3 2.0 slice_add_fusion.across_ref
  352.4 114.5 %shard_map.228 = (bf16[1024,2048]{1,0:T(8,128)(2,1)}, f32[16,2,128]{2,1,0:T(2,128)S(1)}, bf16[2,1024,1024]{2,1,0:T(8,128)(2,1)}, bf16[2,1024,1024]{2,1,0:T(8,128...) custom-call(bf16[1024,2048]{1,0:T(8,128)(2,1)} %get-tuple-element.77, ...), custom_call_target="tpu_custom_call" | custom-call | flops 1 | bytes 1 | tf_op jit(solution)/shard_map/pallas_call | solution.py:700
  469.5 69.8 %shard_map.229 = (f32[64,3072]{1,0:T(8,128)}, f32[64,1024]{1,0:T(8,128)}, f32[64,8192]{1,0:T(8,128)}, f32[256,1024]{1,0:T(8,128)}, f32[40,128]{1,0:T(8,128)}, /*index=5*/f32[1024,1024]{1,0:T(8,128)}) custom-call(bf16[4,64,2048]{2,1,0:T(8,128)(2,1)} %copy-done.8, bf16[4,64,2048]{2,1,0:T(8,128)(2,1)} %copy-done.9, bf16[2,64,2048]{2,1,0:T(8,128)(2,1)} %bitcast.87, ...), custom_call_target="tpu_custom_call" | custom-call | flops 1 | bytes 1 | tf_op jit(solution)/shard_map/pallas_call | solution.py:1344
  545.7 2.1 copy.75
  (150 shorter events, 33.7 us)
Async XLA Ops:
  7.2 200.6 %all-gather.3.cloned.1.call-start = ((), (), s32[]{:S(2)}) async-start(), calls=%async_computation.1 | async-start | bytes 13369344 | tf_op jit(solution)/shard_map/all_gather | solution.py:1501
  13.7 58.6 %copy-start.31 = (s32[1024]{0:T(1024)S(1)}, s32[1024]{0:T(1024)}, u32[]{:S(2)}) copy-start(s32[1024]{0:T(1024)} %param.17) | copy-start | bytes 12292
  13.7 58.7 %copy-start.36 = (f32[64]{0:T(128)S(1)}, f32[64]{0:T(128)}, u32[]{:S(2)}) copy-start(f32[64]{0:T(128)} %param.24) | copy-start | bytes 772
  13.7 58.8 %copy-start.37 = (f32[64]{0:T(128)S(1)}, f32[64]{0:T(128)}, u32[]{:S(2)}) copy-start(f32[64]{0:T(128)} %param.25) | copy-start | bytes 772
  72.1 202.3 %all-gather.5.cloned.1.call-start = ((), (), s32[]{:S(2)}) async-start(), calls=%async_computation.2 | async-start | bytes 13369344 | tf_op jit(solution)/shard_map/all_gather | solution.py:1501
  72.5 38.9 %copy-start.12 = (f32[1,128]{1,0:T(1,128)}, f32[1,128]{1,0:T(1,128)S(1)}, u32[]{:S(2)}) copy-start(f32[1,128]{1,0:T(1,128)S(1)} %broadcast_in_dim_tile.8.qgain_ref) | copy-start | bytes 1540
  72.6 38.9 %copy-start.13 = (f32[1,128]{1,0:T(1,128)}, f32[1,128]{1,0:T(1,128)S(1)}, u32[]{:S(2)}) copy-start(f32[1,128]{1,0:T(1,128)S(1)} %broadcast_in_dim_tile.9.kgain_ref) | copy-start | bytes 1540
  74.0 37.5 %copy-start.10 = (f32[1024]{0:T(1024)}, f32[1024]{0:T(1024)S(1)}, u32[]{:S(2)}) copy-start(f32[1024]{0:T(1024)S(1)} %get-tuple-element.106) | copy-start | bytes 12292
  74.0 131.4 %copy-start.30 = (f32[1024]{0:T(1024)}, f32[1024]{0:T(1024)S(1)}, u32[]{:S(2)}) copy-start(f32[1024]{0:T(1024)S(1)} %get-tuple-element.105) | copy-start | bytes 12292
  77.8 22.8 %copy-start.5 = (f32[1024,128]{1,0:T(8,128)}, f32[1024,128]{1,0:T(8,128)S(1)}, u32[]{:S(2)}) copy-start(f32[1024,128]{1,0:T(8,128)S(1)} %get-tuple-element.138.cos_ref) | copy-start | bytes 1572868
  77.8 22.8 %copy-start.6 = (f32[1024,128]{1,0:T(8,128)}, f32[1024,128]{1,0:T(8,128)S(1)}, u32[]{:S(2)}) copy-start(f32[1024,128]{1,0:T(8,128)S(1)} %get-tuple-element.139.sin_ref) | copy-start | bytes 1572868
  77.8 25.5 %copy-start.18 = (bf16[64,8192]{1,0:T(8,128)(2,1)S(1)}, bf16[64,8192]{1,0:T(8,128)(2,1)}, u32[]{:S(2)}) copy-start(bf16[64,8192]{1,0:T(8,128)(2,1)} %param.20) | copy-start | bytes 3145732
  111.2 358.2 %reduce-scatter.2.cloned.1.call-start = ((), (), s32[]{:S(2)}) async-start(), calls=%async_computation.3 | async-start | bytes 2621440 | tf_op jit(solution)/shard_map/reduce_scatter | solution.py:1584
  111.5 15.8 %copy-start.34 = (s32[1,2]{1,0:T(1,128)S(1)}, s32[1,2]{1,0:T(1,128)}, u32[]{:S(2)}) copy-start(s32[1,2]{1,0:T(1,128)} %param.15) | copy-start | bytes 28
  111.5 18.4 %copy-start.35 = (f32[16,2]{0,1:T(2,128)S(1)}, f32[16,2]{0,1:T(2,128)}, u32[]{:S(2)}) copy-start(f32[16,2]{0,1:T(2,128)} %param.26) | copy-start | bytes 388
  111.5 20.9 %copy-start.32 = (s32[1,2048]{1,0:T(1,128)S(1)}, s32[1,2048]{1,0:T(1,128)}, u32[]{:S(2)}) copy-start(s32[1,2048]{1,0:T(1,128)} %param.16) | copy-start | bytes 24580
  135.6 62.9 %copy-start.15 = (bf16[1024,1024]{1,0:T(8,128)(2,1)S(1)}, bf16[1024,1024]{1,0:T(8,128)(2,1)}, u32[]{:S(2)}) copy-start(bf16[1024,1024]{1,0:T(8,128)(2,1)} %tokens_ref.5) | copy-start | bytes 6291460
  198.4 140.3 %copy-start = (bf16[1024,1024]{1,0:T(8,128)(2,1)}, bf16[1024,1024]{1,0:T(8,128)(2,1)S(1)}, u32[]{:S(2)}) copy-start(bf16[1024,1024]{1,0:T(8,128)(2,1)S(1)} %get-tuple-element.66.left_ref.out_ref) | copy-start | bytes 6291460
  274.4 59.1 %copy-start.16 = (bf16[4,3,64,2048]{3,2,1,0:T(8,128)(2,1)S(1)}, bf16[4,3,64,2048]{3,2,1,0:T(8,128)(2,1)}, u32[]{:S(2)}) copy-start(bf16[4,3,64,2048]{3,2,1,0:T(8,128)(2,1)} %get-tuple-element.79.early_own_ref) | copy-start | bytes 9437188
  343.8 8.5 %collective-permute-start = (bf16[1,512,1024]{2,1,0:T(8,128)(2,1)S(1)}, bf16[1,512,1024]{2,1,0:T(8,128)(2,1)S(1)}, u32[]{:S(2)}, u32[]{:S(2)}) collective-permute-start(bf16[1,512,1024]{2,1,0:T(8,128)(2,1)S(1)} %get-tuple-element.84), channel_id=1, source_target_pairs={{0,2},{2,0},{4,6},{6,4},{8,10},{10,8},{12,14},{14,12},{16,18},{18,... | collective-permute-start | bytes 3145736 | tf_op jit(solution)/shard_map/ppermute | solution.py:1426
  344.2 6.1 %slice-start = ((s8[6291456]{0:T(1024)(128)(4,1)}), s8[4194304]{0:T(1024)(128)(4,1)S(1)}, s32[]{:S(2)}) async-start(s8[6291456]{0:T(1024)(128)(4,1)} %bitcast.81), calls=%async_computation.4 | async-start | bytes 8388608
  344.2 6.1 %slice-start.1 = ((s8[6291456]{0:T(1024)(128)(4,1)}), s8[2097152]{0:T(1024)(128)(4,1)S(1)}, s32[]{:S(2)}) async-start(s8[6291456]{0:T(1024)(128)(4,1)} %bitcast.81), calls=%async_computation.5 | async-start | bytes 4194304
  344.2 6.1 %copy-start.20 = (bf16[4,3,64,2048]{3,2,1,0:T(8,128)(2,1)S(1)}, bf16[4,3,64,2048]{3,2,1,0:T(8,128)(2,1)}, u32[]{:S(2)}) copy-start(bf16[4,3,64,2048]{3,2,1,0:T(8,128)(2,1)} %get-tuple-element.80) | copy-start | bytes 9437188
  469.5 73.2 %copy-start.22 = (bf16[1024,1024]{1,0:T(8,128)(2,1)S(1)}, bf16[1024,1024]{1,0:T(8,128)(2,1)}, u32[]{:S(2)}) copy-start(bf16[1024,1024]{1,0:T(8,128)(2,1)} %get-tuple-element.167) | copy-start | bytes 6291460
  (20 other events, 48.5 us)
Sparse Core Ops, SparseCore 0:
  72.2 100.9 all-gather.2
  175.4 98.9 all-gather.4
  338.6 47.7 reduce-scatter.1

commit v7 on v6

--- a/solution.py
+++ b/solution.py
@@ -522,7 +522,7 @@
 
 
 STARTS = (0, 7, 19, 33, 47)
-ARRIVALS = (10, 23, 37, 50, 62)
+ARRIVALS = (10, 23, 37, 50, 64)
 
 
 def carry_kernel(
@@ -642,7 +642,7 @@
                     load(part, 0).start()
                     load(part, 1).start()
 
-            if ARRIVALS[part] % 4 == quarter:
+            if part < last and ARRIVALS[part] % 4 == quarter:
                 pl.when(step == ARRIVALS[part] // 4)(functools.partial(arrive, part))
 
     backward_start(grad_ref, out_ref, grads, dq_total)
@@ -667,6 +667,7 @@
 
     @pl.when(step == pl.num_programs(0) - 1)
     def _():
+        arrive(last)
         for pair in range(pairs):
             to_near(pair).wait()
             to_other(pair).wait()
@@ -893,8 +894,9 @@
         sg = 1.0 / (1.0 + jnp.exp(-g))
         silu = g * sg
         hidden = (silu * u).astype(bf16)
-        gate = (hidden_grad * u * sg * (1.0 + g * (1.0 - sg))).astype(bf16)
-        up = (hidden_grad * silu).astype(bf16)
+        slope = hidden_grad * sg
+        gate = (slope * u * (1.0 + (g - silu))).astype(bf16)
+        up = (slope * g).astype(bf16)
         branch[at, :] += dot(hidden, wd)
         nfgrad_ref[at, :] += dot(gate, wg, NT) + dot(up, wu, NT)
         hiddens.append(hidden)

time: 564 us -> 562 us (level)
  no operation moved by 1% of the time
where the time goes in v7:
time: 562 us; the launch traced here: 557 us
  Pallas kernels  456 us (81%)
  local copies, waits for them, and re-layouts  35.4 us (6%)
  other arithmetic  30.8 us (5%)
  between operations  15.9 us (3%)
  matrix products  11 us (2%)
  waiting for transfers between devices  6.59 us (1%)
    pallas_call x1, Pallas kernels, attend_back_carry(): pl.pallas_call(functools.partial(carry_kernel, pairs), grid=(2 * pairs,),...  113 us
    pallas_call x2, Pallas kernels, feed_forward(): pl.pallas_call(functools.partial(ffn_kernel, places, first), grid=(steps,...  112 us
    pallas_call x1, Pallas kernels, finish(): pl.pallas_call(finish_kernel, in_specs=[vmem] * 10 + [anywhere] * 10, out...  69.8 us
    pallas_call x1, Pallas kernels, attend(): pl.pallas_call(functools.partial(forward_kernel, sources, min(512, rows))...  62.9 us
    pallas_call x1, Pallas kernels, gather_first(): pl.pallas_call(gather_kernel, in_specs=[anywhere] * 3, out_specs=[anywher...  57.4 us
    pallas_call x2, Pallas kernels, project(): pl.pallas_call(qkv_kernel, grid=(rows // block,), in_specs=[pl.BlockSpec(...  35.9 us
    unnamed x86, local copies, waits for them, and re-layouts  19.8 us
  transfers between devices with their start and end apart: 4, of which 1 were waited for; matrix products, arithmetic and copies ran while one was open for 7% of the time, Pallas kernels for 49%

profile of v7, /device:TPU:0, one launch (start us, length us, event | category | flops | bytes accessed | tf_op | source)
XLA Modules:
  0.0 557.1 jit_solution(11442340843769647956)
XLA Ops:
  8.1 1.8 reshape.213
  9.9 2.8 slice_reduce_fusion.3
  13.7 57.4 %shard_map.221 = (bf16[1024,4224]{1,0:T(8,128)(2,1)}, bf16[1024,1024]{1,0:T(8,128)(2,1)}, s32[8,128]{1,0:T(8,128)}) custom-call(bf16[64,4224]{1,0:T(8,128)(2,1)} %fusion.4.shard_ref, bf16[1024,1024]{1,0:T(8,128)(2,1)} %tokens_ref.5, s32[8,128]{1,0:T(8,128)} %bitcast.91), custom_call_target="tpu_custom_call" | custom-call | flops 1 | bytes 1 | tf_op jit(solution)/shard_map/pallas_call | solution.py:179
  74.1 3.7 fusion.6
  77.8 22.8 %shard_map.222 = (bf16[1024,1024]{1,0:T(8,128)(2,1)S(1)}, bf16[1024,1024]{1,0:T(8,128)(2,1)S(1)}, bf16[1024,1024]{1,0:T(8,128)(2,1)}, f32[1024,1024]{1,0:T(8,128...) custom-call(bf16[1024,1024]{1,0:T(8,128)(2,1)} %tokens_ref.5, f32[1,1024]{1,0:T(1,128)S(1)} %bitcast.77, ...), custom_call_target="tpu_custom_call" | custom-call | flops 1 | bytes 1 | tf_op jit(solution)/shard_map/pallas_call | solution.py:241
  105.8 4.4 slice_reduce_fusion.1
  111.6 13.1 %shard_map.223 = (bf16[1024,1024]{1,0:T(8,128)(2,1)S(1)}, bf16[1024,1024]{1,0:T(8,128)(2,1)S(1)}) custom-call(bf16[1024,1024]{1,0:T(8,128)(2,1)} %get-tuple-element.62.tokens_ref, f32[1,1024]{1,0:T(1,128)S(1)} %bitcast.78, bf16[1024,4224]{1,0:T(8,128)(2,1)} %get-tuple-element.58.weight_ref, f32[1024,128]{1,0:T(8,128)S(1)} %get-tuple-element.131.cos_ref, ...), custom_call_target="tpu_custom_call" | custom-call | flops 1 | bytes 1 | tf_op jit(solution)/shard_map/pallas_call | solution.py:241
  133.9 1.7 copy-done.7
  135.6 62.9 %shard_map.224 = (bf16[1024,1024]{1,0:T(8,128)(2,1)S(1)}, bf16[1024,2048]{1,0:T(8,128)(2,1)}) custom-call(s32[8]{0:T(128)S(1)} %add_convert_fusion.1.flags, bf16[1024,1024]{1,0:T(8,128)(2,1)S(1)} %copy-done.7, bf16[1024,128]{1,0:T(8,128)(2,1)S(1)} %select_convert_fusion.aq_ref, bf16[8,2,128]{2,1,0:T(2,128)(2,1)S(1)} %bitcast.80, ...), custom_call_target="tpu_custom_call" | custom-call | flops 1 | bytes 1 | tf_op jit(solution)/shard_map/pallas_call | solution.py:387
  198.5 4.9 multiply_reduce_fusion
  203.4 2.0 multiply_convert_fusion.seed_ref
  206.0 1.7 multiply_convert_fusion.1.nf_ref
  207.8 53.8 %shard_map.225 = (f32[1024,1024]{1,0:T(8,128)}, f32[1024,1024]{1,0:T(8,128)}, bf16[8,3,64,2048]{3,2,1,0:T(8,128)(2,1)}, bf16[4,3,64,2048]{3,2,1,0:T(8,128)(2,1)}, bf16[4,3,64,2048]{3,2,1,0:T(8,128)(2,1)}) custom-call(bf16[1024,1024]{1,0:T(8,128)(2,1)} %multiply_convert_fusion.1.nf_ref, bf16[1024,1024]{1,0:T(8,128)(2,1)} %multiply_convert_fusion.seed_ref, ...), custom_call_target="tpu_custom_call" | custom-call | flops 1 | bytes 1 | tf_op jit(solution)/shard_map/pallas_call | solution.py:959
  261.6 3.1 fusion.3.early_across_ref
  264.6 3.2 slice_add_fusion.1.refs_2_
  267.9 6.5 %all-gather.5.cloned.1.call-done.wg_ref.wu_ref.wd_ref = bf16[1024,6144]{1,0:T(8,128)(2,1)} async-done(((bf16[64,6144]{1,0:T(8,128)(2,1)}), bf16[1024,6144]{1,0:T(8,128)(2,1)}) %all-gather.5.cloned.1.call-update) | async-done | bytes 12582928 | tf_op jit(solution)/shard_map/all_gather | solution.py:1503
  274.4 58.6 %shard_map.226 = (bf16[1024,1024]{1,0:T(8,128)(2,1)}, f32[1024,1024]{1,0:T(8,128)}, bf16[1024,1024]{1,0:T(8,128)(2,1)}, f32[1,1024]{1,0:T(1,128)}, bf16[8,3,64,2...) custom-call(bf16[1024,1024]{1,0:T(8,128)(2,1)} %multiply_convert_fus, ...), custom_call_target="tpu_custom_call" | custom-call | flops 1 | bytes 1 | tf_op jit(solution)/shard_map/pallas_call | solution.py:959
  333.0 5.0 add_convert_fusion
  338.2 5.1 shard_map.227
  343.7 6.1 %convolution_convert_fusion.grad_ref = bf16[1024,1024]{1,0:T(8,128)(2,1)} fusion(bf16[1024,1024]{1,0:T(8,128)(2,1)} %get-tuple-element.78.right_ref, bf16[1024,4224]{1,0:T(8,128)(2,1)} %get-tuple-element.58.weight_ref), kind=kOutput, calls=%fused_computation.7 | convolution fusion | flops 2148532224 | bytes 6291456 | tf_op jit(solution)/shard_map/dot_general | solution.py:26
  349.8 2.0 slice_add_fusion.across_ref
  351.9 113.0 %shard_map.228 = (bf16[1024,2048]{1,0:T(8,128)(2,1)}, f32[16,2,128]{2,1,0:T(2,128)S(1)}, bf16[2,1024,1024]{2,1,0:T(8,128)(2,1)}, bf16[2,1024,1024]{2,1,0:T(8,128...) custom-call(bf16[1024,2048]{1,0:T(8,128)(2,1)} %get-tuple-element.77, ...), custom_call_target="tpu_custom_call" | custom-call | flops 1 | bytes 1 | tf_op jit(solution)/shard_map/pallas_call | solution.py:701
  467.5 69.8 %shard_map.229 = (f32[64,3072]{1,0:T(8,128)}, f32[64,1024]{1,0:T(8,128)}, f32[64,8192]{1,0:T(8,128)}, f32[256,1024]{1,0:T(8,128)}, f32[40,128]{1,0:T(8,128)}, /*index=5*/f32[1024,1024]{1,0:T(8,128)}) custom-call(bf16[4,64,2048]{2,1,0:T(8,128)(2,1)} %copy-done.8, bf16[4,64,2048]{2,1,0:T(8,128)(2,1)} %copy-done.9, bf16[2,64,2048]{2,1,0:T(8,128)(2,1)} %bitcast.87, ...), custom_call_target="tpu_custom_call" | custom-call | flops 1 | bytes 1 | tf_op jit(solution)/shard_map/pallas_call | solution.py:1346
  543.7 2.1 copy.75
  (150 shorter events, 33.7 us)
Async XLA Ops:
  7.2 200.6 %all-gather.3.cloned.1.call-start = ((), (), s32[]{:S(2)}) async-start(), calls=%async_computation.1 | async-start | bytes 13369344 | tf_op jit(solution)/shard_map/all_gather | solution.py:1503
  13.7 58.6 %copy-start.31 = (s32[1024]{0:T(1024)S(1)}, s32[1024]{0:T(1024)}, u32[]{:S(2)}) copy-start(s32[1024]{0:T(1024)} %param.17) | copy-start | bytes 12292
  13.7 58.7 %copy-start.36 = (f32[64]{0:T(128)S(1)}, f32[64]{0:T(128)}, u32[]{:S(2)}) copy-start(f32[64]{0:T(128)} %param.24) | copy-start | bytes 772
  13.7 58.8 %copy-start.37 = (f32[64]{0:T(128)S(1)}, f32[64]{0:T(128)}, u32[]{:S(2)}) copy-start(f32[64]{0:T(128)} %param.25) | copy-start | bytes 772
  72.1 202.3 %all-gather.5.cloned.1.call-start = ((), (), s32[]{:S(2)}) async-start(), calls=%async_computation.2 | async-start | bytes 13369344 | tf_op jit(solution)/shard_map/all_gather | solution.py:1503
  72.5 38.9 %copy-start.12 = (f32[1,128]{1,0:T(1,128)}, f32[1,128]{1,0:T(1,128)S(1)}, u32[]{:S(2)}) copy-start(f32[1,128]{1,0:T(1,128)S(1)} %broadcast_in_dim_tile.8.qgain_ref) | copy-start | bytes 1540
  72.6 38.9 %copy-start.13 = (f32[1,128]{1,0:T(1,128)}, f32[1,128]{1,0:T(1,128)S(1)}, u32[]{:S(2)}) copy-start(f32[1,128]{1,0:T(1,128)S(1)} %broadcast_in_dim_tile.9.kgain_ref) | copy-start | bytes 1540
  74.0 37.5 %copy-start.10 = (f32[1024]{0:T(1024)}, f32[1024]{0:T(1024)S(1)}, u32[]{:S(2)}) copy-start(f32[1024]{0:T(1024)S(1)} %get-tuple-element.106) | copy-start | bytes 12292
  74.0 131.4 %copy-start.30 = (f32[1024]{0:T(1024)}, f32[1024]{0:T(1024)S(1)}, u32[]{:S(2)}) copy-start(f32[1024]{0:T(1024)S(1)} %get-tuple-element.105) | copy-start | bytes 12292
  77.8 22.8 %copy-start.5 = (f32[1024,128]{1,0:T(8,128)}, f32[1024,128]{1,0:T(8,128)S(1)}, u32[]{:S(2)}) copy-start(f32[1024,128]{1,0:T(8,128)S(1)} %get-tuple-element.138.cos_ref) | copy-start | bytes 1572868
  77.8 22.8 %copy-start.6 = (f32[1024,128]{1,0:T(8,128)}, f32[1024,128]{1,0:T(8,128)S(1)}, u32[]{:S(2)}) copy-start(f32[1024,128]{1,0:T(8,128)S(1)} %get-tuple-element.139.sin_ref) | copy-start | bytes 1572868
  77.8 25.5 %copy-start.18 = (bf16[64,8192]{1,0:T(8,128)(2,1)S(1)}, bf16[64,8192]{1,0:T(8,128)(2,1)}, u32[]{:S(2)}) copy-start(bf16[64,8192]{1,0:T(8,128)(2,1)} %param.20) | copy-start | bytes 3145732
  111.2 356.3 %reduce-scatter.2.cloned.1.call-start = ((), (), s32[]{:S(2)}) async-start(), calls=%async_computation.3 | async-start | bytes 2621440 | tf_op jit(solution)/shard_map/reduce_scatter | solution.py:1586
  111.5 15.8 %copy-start.34 = (s32[1,2]{1,0:T(1,128)S(1)}, s32[1,2]{1,0:T(1,128)}, u32[]{:S(2)}) copy-start(s32[1,2]{1,0:T(1,128)} %param.15) | copy-start | bytes 28
  111.5 18.4 %copy-start.35 = (f32[16,2]{0,1:T(2,128)S(1)}, f32[16,2]{0,1:T(2,128)}, u32[]{:S(2)}) copy-start(f32[16,2]{0,1:T(2,128)} %param.26) | copy-start | bytes 388
  111.5 20.9 %copy-start.32 = (s32[1,2048]{1,0:T(1,128)S(1)}, s32[1,2048]{1,0:T(1,128)}, u32[]{:S(2)}) copy-start(s32[1,2048]{1,0:T(1,128)} %param.16) | copy-start | bytes 24580
  135.6 62.9 %copy-start.15 = (bf16[1024,1024]{1,0:T(8,128)(2,1)S(1)}, bf16[1024,1024]{1,0:T(8,128)(2,1)}, u32[]{:S(2)}) copy-start(bf16[1024,1024]{1,0:T(8,128)(2,1)} %tokens_ref.5) | copy-start | bytes 6291460
  198.4 139.8 %copy-start = (bf16[1024,1024]{1,0:T(8,128)(2,1)}, bf16[1024,1024]{1,0:T(8,128)(2,1)S(1)}, u32[]{:S(2)}) copy-start(bf16[1024,1024]{1,0:T(8,128)(2,1)S(1)} %get-tuple-element.66.left_ref.out_ref) | copy-start | bytes 6291460
  274.4 58.6 %copy-start.16 = (bf16[4,3,64,2048]{3,2,1,0:T(8,128)(2,1)S(1)}, bf16[4,3,64,2048]{3,2,1,0:T(8,128)(2,1)}, u32[]{:S(2)}) copy-start(bf16[4,3,64,2048]{3,2,1,0:T(8,128)(2,1)} %get-tuple-element.79.early_own_ref) | copy-start | bytes 9437188
  343.3 8.5 %collective-permute-start = (bf16[1,512,1024]{2,1,0:T(8,128)(2,1)S(1)}, bf16[1,512,1024]{2,1,0:T(8,128)(2,1)S(1)}, u32[]{:S(2)}, u32[]{:S(2)}) collective-permute-start(bf16[1,512,1024]{2,1,0:T(8,128)(2,1)S(1)} %get-tuple-element.84), channel_id=1, source_target_pairs={{0,2},{2,0},{4,6},{6,4},{8,10},{10,8},{12,14},{14,12},{16,18},{18,... | collective-permute-start | bytes 3145736 | tf_op jit(solution)/shard_map/ppermute | solution.py:1428
  343.7 6.1 %slice-start = ((s8[6291456]{0:T(1024)(128)(4,1)}), s8[4194304]{0:T(1024)(128)(4,1)S(1)}, s32[]{:S(2)}) async-start(s8[6291456]{0:T(1024)(128)(4,1)} %bitcast.81), calls=%async_computation.4 | async-start | bytes 8388608
  343.7 6.1 %slice-start.1 = ((s8[6291456]{0:T(1024)(128)(4,1)}), s8[2097152]{0:T(1024)(128)(4,1)S(1)}, s32[]{:S(2)}) async-start(s8[6291456]{0:T(1024)(128)(4,1)} %bitcast.81), calls=%async_computation.5 | async-start | bytes 4194304
  343.7 6.1 %copy-start.20 = (bf16[4,3,64,2048]{3,2,1,0:T(8,128)(2,1)S(1)}, bf16[4,3,64,2048]{3,2,1,0:T(8,128)(2,1)}, u32[]{:S(2)}) copy-start(bf16[4,3,64,2048]{3,2,1,0:T(8,128)(2,1)} %get-tuple-element.80) | copy-start | bytes 9437188
  467.5 73.2 %copy-start.22 = (bf16[1024,1024]{1,0:T(8,128)(2,1)S(1)}, bf16[1024,1024]{1,0:T(8,128)(2,1)}, u32[]{:S(2)}) copy-start(bf16[1024,1024]{1,0:T(8,128)(2,1)} %get-tuple-element.167) | copy-start | bytes 6291460
  (20 other events, 48.5 us)
Sparse Core Ops, SparseCore 0:
  72.2 100.9 all-gather.2
  175.4 98.9 all-gather.4
  338.2 47.8 reduce-scatter.1
